TPU v7x, 32 devices: a whole 2x2x4 slice. The times are simulated.
32 devices in a mesh: dp: 8 (over z, y), tensor: 4 (over x, core).
Axes of the slice: x: 2, y: 2, z: 4, core: 2. Of those that a mesh axis runs over, the one named last changes fastest.
Arguments:
- hidden_in: bfloat16 [2, 2048, 1536], P(None, ('dp', 'tensor')), may hold values from -6 to 6
- out_grad: bfloat16 [2, 2048, 1536], P(None, ('dp', 'tensor')), may hold values from -6 to 6
- segment_ids: int32 [2, 2048], P(None, 'dp'), may hold values from 0 to 255, as said below
- norm_gains: bfloat16 [4, 1536], P(None, 'dp'), may hold values from 0.5 to 1.5
- w_mixer_in: bfloat16 [1536, 2, 3072], P('dp', None, 'tensor'), may hold values from -0.15625 to 0.15625
- w_xproj: bfloat16 [3072, 128], P(('tensor', 'dp')), may hold values from -0.109375 to 0.109375
- w_dtproj: bfloat16 [96, 3072], P(None, ('tensor', 'dp')), may hold values from -0.625 to 0.625
- mixer_params: bfloat16 [23, 3072], P(None, ('tensor', 'dp')), may hold values from -7 to 3
- w_mixer_out: bfloat16 [3072, 1536], P(('tensor', 'dp')), may hold values from -0.109375 to 0.109375
- w_ffn_a_in: bfloat16 [1536, 2, 4096], P('dp', None, 'tensor'), may hold values from -0.15625 to 0.15625
- w_ffn_a_out: bfloat16 [4096, 1536], P(('tensor', 'dp')), may hold values from -0.09375 to 0.09375
- w_qkv: bfloat16 [1536, 3, 1536], P('dp', None, 'tensor'), may hold values from -0.15625 to 0.15625
- w_attn_out: bfloat16 [1536, 1536], P(('tensor', 'dp')), may hold values from -0.625 to 0.625
- w_ffn_b_in: bfloat16 [1536, 2, 4096], P('dp', None, 'tensor'), may hold values from -0.15625 to 0.15625
- w_ffn_b_out: bfloat16 [4096, 1536], P(('tensor', 'dp')), may hold values from -0.09375 to 0.09375
Outputs:
- block_out: bfloat16 [2, 2048, 1536], P(None, ('dp', 'tensor'))
- input_grad: bfloat16 [2, 2048, 1536], P(None, ('dp', 'tensor'))
- grad_norm_gains: float32 [4, 1536], P(None, 'dp')
- grad_w_mixer_in: float32 [1536, 2, 3072], P('dp', None, 'tensor')
- grad_w_xproj: float32 [3072, 128], P(('tensor', 'dp'))
- grad_w_dtproj: float32 [96, 3072], P(None, ('tensor', 'dp'))
- grad_mixer_params: float32 [23, 3072], P(None, ('tensor', 'dp'))
- grad_w_mixer_out: float32 [3072, 1536], P(('tensor', 'dp'))
- grad_w_ffn_a_in: float32 [1536, 2, 4096], P('dp', None, 'tensor')
- grad_w_ffn_a_out: float32 [4096, 1536], P(('tensor', 'dp'))
- grad_w_qkv: float32 [1536, 3, 1536], P('dp', None, 'tensor')
- grad_w_attn_out: float32 [1536, 1536], P(('tensor', 'dp'))
- grad_w_ffn_b_in: float32 [1536, 2, 4096], P('dp', None, 'tensor')
- grad_w_ffn_b_out: float32 [4096, 1536], P(('tensor', 'dp'))
Inputs may be any that keep to these rules, and one draw needn't show every extreme that they name: `segment_ids`: within each packed sequence of 256 rows a token's number is the position where its document starts, so the numbers start at 0, never fall, and a document starts where the number changes; the last position is always a document of its own; in every sequence one document starts before position 64 and runs past position 192.
All inputs are finite; a program needn't handle non-finite values.
Results may differ from a plain program's by a relative error of at most 0.04.
Values may be sent and summed in bfloat16 or wider, within the bound.
No kernel may reach another device: no remote copies, remote signals or barrier semaphores. Data moves between devices by JAX's collectives and lax.ppermute only.
A program may use at most 384 MiB of HBM per device.

v0:
```python
import math

import jax
import jax.numpy as jnp
from jax import lax
from jax.sharding import PartitionSpec as P

STATE = 16
CONV = 4
RANK = 96
HEAD = 128
MICRO = 2


epsilon = 1e-05
floor_score = -1e30


def matmul(left_side, right_side):
    return jnp.dot(left_side, right_side, preferred_element_type=jnp.float32)


def contract_rows(left_side, right_side):
    return lax.dot_general(
        left_side, right_side, (((0,), (0,)), ((), ())), preferred_element_type=jnp.float32
    )


def times_transpose(left_side, right_side):
    return lax.dot_general(
        left_side, right_side, (((1,), (1,)), ((), ())), preferred_element_type=jnp.float32
    )


def silu_gate(inputs):
    return inputs * jax.nn.sigmoid(inputs)


def soft_plus(inputs):
    return jnp.maximum(inputs, 0.0) + jnp.log1p(jnp.exp(-jnp.abs(inputs)))


def gate_product(gate_part, up_part):
    return silu_gate(gate_part) * up_part


def rms_piece(row_block, gain):
    return (
        row_block
        * lax.rsqrt(jnp.mean(row_block * row_block, axis=-1, keepdims=True) + epsilon)
        * gain[None, :]
    )


def reset_taps(seg_ids, taps_count):
    length = seg_ids.shape[0]
    padded = jnp.concatenate([jnp.full((taps_count - 1,), -1, jnp.int32), seg_ids])
    mask_rows = []
    for offset in range(taps_count):
        earlier = padded[taps_count - 1 - offset : taps_count - 1 - offset + length]
        mask_rows.append((earlier == seg_ids).astype(jnp.float32))
    return jnp.stack(mask_rows)


def doc_mask(seg_ids):
    position = lax.iota(jnp.int32, seg_ids.shape[0])
    return (position[None, :] <= position[:, None]) & (seg_ids[None, :] == seg_ids[:, None])


def conv_piece(inputs, conv_weights, conv_bias, tap_masks):
    length = inputs.shape[0]
    taps_count = conv_weights.shape[0]
    padded = jnp.pad(inputs, ((taps_count - 1, 0), (0, 0)))
    running = jnp.broadcast_to(conv_bias[None, :], inputs.shape)
    for offset in range(taps_count):
        shifted = padded[taps_count - 1 - offset : taps_count - 1 - offset + length]
        running = running + conv_weights[offset][None, :] * shifted * tap_masks[offset][:, None]
    return silu_gate(running)


def to_blocks(array_in, count, block):
    moved = array_in.reshape((count, block) + array_in.shape[1:])
    return jnp.swapaxes(moved, 0, 1)


def mix_piece(dt_lin, values, input_coef, output_coef, gate_pre, mixer_rest, keep_mask):
    step_sizes = soft_plus(dt_lin + mixer_rest[0][None, :])
    decay_rate = -jnp.exp(mixer_rest[2:])
    length, channels = dt_lin.shape
    block = math.gcd(length, 64)
    count = length // block

    def advance(carried, inputs_t):
        state, product = carried
        step_t, value_t, input_t, output_t, keep_t = inputs_t
        factor = jnp.exp(step_t[:, None, :] * decay_rate[None]) * keep_t[:, None, None]
        state = factor * state + (step_t * value_t)[:, None, :] * input_t[:, :, None]
        product = factor * product
        return (
            (state, product),
            (jnp.sum(output_t[:, :, None] * state, axis=1), output_t[:, :, None] * product),
        )

    shape_state = (count,) + decay_rate.shape
    initial = (jnp.zeros(shape_state, jnp.float32), jnp.ones(shape_state, jnp.float32))
    inputs_all = (
        to_blocks(step_sizes, count, block),
        to_blocks(values, count, block),
        to_blocks(input_coef, count, block),
        to_blocks(output_coef, count, block),
        to_blocks(keep_mask, count, block),
    )
    (ends, end_products), (local_out, weighted) = lax.scan(
        jax.checkpoint(advance), initial, inputs_all, unroll=min(8, block)
    )

    def link(carried, pieces):
        end_state, end_product = pieces
        return (end_product * carried + end_state, carried)

    _, starts = lax.scan(link, jnp.zeros(decay_rate.shape, jnp.float32), (ends, end_products))
    blocked = local_out + jnp.sum(weighted * starts[None], axis=2)
    scanned = jnp.swapaxes(blocked, 0, 1).reshape(length, channels)
    return (scanned + mixer_rest[1][None, :] * values) * silu_gate(gate_pre)


def rope_piece(head_rows):
    length = head_rows.shape[0]
    half_size = head_rows.shape[2] // 2
    frequency = jnp.exp(
        lax.iota(jnp.float32, half_size) * (-2.0 * math.log(10000.0) / head_rows.shape[2])
    )
    angles = lax.iota(jnp.float32, length)[:, None] * frequency[None, :]
    cosine = jnp.cos(angles)[:, None, :]
    sine_part = jnp.sin(angles)[:, None, :]
    first_half = head_rows[..., :half_size]
    second_half = head_rows[..., half_size:]
    return jnp.concatenate(
        [
            first_half * cosine - second_half * sine_part,
            second_half * cosine + first_half * sine_part,
        ],
        axis=-1,
    )


def gather_rows(normed):
    return lax.all_gather(normed, "tensor", axis=0, tiled=True)


def scatter_rows(partial_value):
    return lax.psum_scatter(
        partial_value.astype(jnp.bfloat16), "tensor", scatter_dimension=0, tiled=True
    ).astype(jnp.float32)


def gather_grads(gradient):
    return lax.all_gather(gradient, "tensor", axis=0, tiled=True)


def scatter_grads(partial_value):
    return lax.psum_scatter(
        partial_value.astype(jnp.bfloat16), "tensor", scatter_dimension=0, tiled=True
    ).astype(jnp.float32)


def gather_weights(
    norm_gains,
    w_mixer_in,
    w_xproj,
    w_dtproj,
    mixer_params,
    w_mixer_out,
    w_ffn_a_in,
    w_ffn_a_out,
    w_qkv,
    w_attn_out,
    w_ffn_b_in,
    w_ffn_b_out,
):
    return (
        lax.all_gather(norm_gains, "dp", axis=1, tiled=True),
        lax.all_gather(w_mixer_in, "dp", axis=0, tiled=True),
        lax.all_gather(w_xproj, "dp", axis=0, tiled=True),
        lax.all_gather(w_dtproj, "dp", axis=1, tiled=True),
        lax.all_gather(mixer_params, "dp", axis=1, tiled=True),
        lax.all_gather(w_mixer_out, "dp", axis=0, tiled=True),
        lax.all_gather(w_ffn_a_in, "dp", axis=0, tiled=True),
        lax.all_gather(w_ffn_a_out, "dp", axis=0, tiled=True),
        lax.all_gather(w_qkv, "dp", axis=0, tiled=True),
        lax.all_gather(w_attn_out, "dp", axis=0, tiled=True),
        lax.all_gather(w_ffn_b_in, "dp", axis=0, tiled=True),
        lax.all_gather(w_ffn_b_out, "dp", axis=0, tiled=True),
    )


def mixer_forward(gathered, mixer_in, mixer_x, mixer_dt, mixer_table, mixer_out, tap_masks):
    channels = mixer_in.shape[2]
    projected = matmul(gathered, mixer_in.reshape(mixer_in.shape[0], 2 * channels))
    param_rows = mixer_table.astype(jnp.float32)

    def conv_local(inputs, conv_weights, conv_bias):
        return conv_piece(inputs, conv_weights, conv_bias, tap_masks)

    conv_out, conv_back = jax.vjp(
        conv_local, projected[:, :channels], param_rows[:CONV], param_rows[CONV]
    )
    values = conv_out.astype(jnp.bfloat16)
    extended = lax.psum(matmul(values, mixer_x).astype(jnp.bfloat16), "tensor").astype(jnp.float32)
    dt_low = extended[:, :RANK].astype(jnp.bfloat16)
    dt_lin = matmul(dt_low, mixer_dt)

    def mix_local(step_input, value_input, input_coef, output_coef, gate_pre, mixer_rest):
        return mix_piece(
            step_input, value_input, input_coef, output_coef, gate_pre, mixer_rest, tap_masks[1]
        )

    gated_out, mix_back = jax.vjp(
        mix_local,
        dt_lin,
        values.astype(jnp.float32),
        extended[:, RANK : RANK + STATE],
        extended[:, RANK + STATE :],
        projected[:, channels:],
        param_rows[CONV + 1 :],
    )
    gated_low = gated_out.astype(jnp.bfloat16)
    return (
        matmul(gated_low, mixer_out),
        (gathered, values, dt_low, gated_low, conv_back, mix_back),
    )


def mixer_backward(grad_full, kept_state, mixer_in, mixer_x, mixer_dt, mixer_out):
    gathered, values, dt_low, gated_low, conv_back, mix_back = kept_state
    grad_out = contract_rows(gated_low, grad_full)
    d_gated = times_transpose(grad_full, mixer_out)
    d_step, d_values, d_input, d_output, d_gate, d_rest = mix_back(d_gated)
    d_step_low = d_step.astype(jnp.bfloat16)
    grad_dt = contract_rows(dt_low, d_step_low)
    d_extended = lax.psum(
        jnp.concatenate([times_transpose(d_step_low, mixer_dt), d_input, d_output], axis=1).astype(
            jnp.bfloat16
        ),
        "tensor",
    )
    grad_x = contract_rows(values, d_extended)
    d_values = d_values + times_transpose(d_extended, mixer_x)
    d_inputs, d_weights, d_bias = conv_back(d_values)
    d_projected = jnp.concatenate([d_inputs, d_gate], axis=1).astype(jnp.bfloat16)
    grad_in = contract_rows(gathered, d_projected).reshape(mixer_in.shape)
    d_normed = times_transpose(d_projected, mixer_in.reshape(mixer_in.shape[0], -1))
    grad_table = jnp.concatenate([d_weights, d_bias[None, :], d_rest], axis=0)
    return (d_normed, (grad_in, grad_x, grad_dt, grad_table, grad_out))


def ffn_forward(gathered, ffn_in, ffn_out):
    channels = ffn_in.shape[2]
    projected = matmul(gathered, ffn_in.reshape(ffn_in.shape[0], 2 * channels))
    hidden, gate_back = jax.vjp(gate_product, projected[:, :channels], projected[:, channels:])
    hidden_low = hidden.astype(jnp.bfloat16)
    return (matmul(hidden_low, ffn_out), (gathered, hidden_low, gate_back))


def ffn_backward(grad_full, kept_state, ffn_in, ffn_out):
    gathered, hidden_low, gate_back = kept_state
    grad_out = contract_rows(hidden_low, grad_full)
    d_gate, d_up = gate_back(times_transpose(grad_full, ffn_out))
    d_projected = jnp.concatenate([d_gate, d_up], axis=1).astype(jnp.bfloat16)
    grad_in = contract_rows(gathered, d_projected).reshape(ffn_in.shape)
    d_normed = times_transpose(d_projected, ffn_in.reshape(ffn_in.shape[0], -1))
    return (d_normed, (grad_in, grad_out))


def attention_forward(gathered, qkv_weight, attn_out, allowed):
    length = gathered.shape[0]
    columns = qkv_weight.shape[2]
    head_count = columns // HEAD
    score_scale = HEAD ** (-0.5)
    projected = matmul(gathered, qkv_weight.reshape(gathered.shape[1], 3 * columns))
    turned, rope_back = jax.vjp(
        rope_piece, projected[:, : 2 * columns].reshape(length, 2 * head_count, HEAD)
    )
    turned_low = turned.astype(jnp.bfloat16)
    queries = turned_low[:, :head_count]
    key_heads = turned_low[:, head_count:]
    value_heads = projected[:, 2 * columns :].reshape(length, head_count, HEAD).astype(jnp.bfloat16)
    scores = (
        jnp.einsum("qhd,khd->hqk", queries, key_heads, preferred_element_type=jnp.float32)
        * score_scale
    )
    masked = jnp.where(allowed[None], scores, floor_score)
    row_max = jnp.max(masked, axis=-1, keepdims=True)
    log_total = row_max + jnp.log(jnp.sum(jnp.exp(masked - row_max), axis=-1, keepdims=True))
    soft_weights = jnp.exp(masked - log_total).astype(jnp.bfloat16)
    head_mix = (
        jnp.einsum("hqk,khd->qhd", soft_weights, value_heads, preferred_element_type=jnp.float32)
        .reshape(length, columns)
        .astype(jnp.bfloat16)
    )
    return (
        matmul(head_mix, attn_out),
        (gathered, queries, key_heads, value_heads, log_total, head_mix, rope_back),
    )


def attention_backward(grad_full, kept_state, qkv_weight, attn_out, allowed):
    gathered, queries, key_heads, value_heads, log_total, head_mix, rope_back = kept_state
    length, head_count, _ = queries.shape
    score_scale = HEAD ** (-0.5)
    grad_out = contract_rows(head_mix, grad_full)
    d_mixed = (
        times_transpose(grad_full, attn_out).astype(jnp.bfloat16).reshape(length, head_count, HEAD)
    )
    scores = (
        jnp.einsum("qhd,khd->hqk", queries, key_heads, preferred_element_type=jnp.float32)
        * score_scale
    )
    soft_weights = jnp.exp(jnp.where(allowed[None], scores, floor_score) - log_total)
    d_probs = jnp.einsum("qhd,khd->hqk", d_mixed, value_heads, preferred_element_type=jnp.float32)
    d_scores = (
        soft_weights * (d_probs - jnp.sum(soft_weights * d_probs, axis=-1, keepdims=True))
    ).astype(jnp.bfloat16)
    d_queries = (
        jnp.einsum("hqk,khd->qhd", d_scores, key_heads, preferred_element_type=jnp.float32)
        * score_scale
    )
    d_keys = (
        jnp.einsum("hqk,qhd->khd", d_scores, queries, preferred_element_type=jnp.float32)
        * score_scale
    )
    d_values = jnp.einsum(
        "hqk,qhd->khd",
        soft_weights.astype(jnp.bfloat16),
        d_mixed,
        preferred_element_type=jnp.float32,
    )
    (d_turned,) = rope_back(jnp.concatenate([d_queries, d_keys], axis=1))
    d_projected = jnp.concatenate(
        [d_turned.reshape(length, -1), d_values.reshape(length, -1)], axis=1
    ).astype(jnp.bfloat16)
    grad_qkv = contract_rows(gathered, d_projected).reshape(qkv_weight.shape)
    d_normed = times_transpose(d_projected, qkv_weight.reshape(gathered.shape[1], -1))
    return (d_normed, (grad_qkv, grad_out))


def micro_batch(block_in, block_cot, seg_ids, current):
    (
        gain_table,
        mixer_in,
        mixer_x,
        mixer_dt,
        mixer_table,
        mixer_out,
        ffn_a_in,
        ffn_a_out,
        qkv_weight,
        attn_out,
        ffn_b_in,
        ffn_b_out,
    ) = current
    gain_rows = gain_table.astype(jnp.float32)
    tap_masks = reset_taps(seg_ids, CONV)
    allowed = doc_mask(seg_ids)
    residual = block_in.astype(jnp.float32)
    normed, norm_back_a = jax.vjp(rms_piece, residual, gain_rows[0])
    partial_value, kept_mixer = mixer_forward(
        gather_rows(normed.astype(jnp.bfloat16)),
        mixer_in,
        mixer_x,
        mixer_dt,
        mixer_table,
        mixer_out,
        tap_masks,
    )
    residual = residual + scatter_rows(partial_value)
    normed, norm_back_b = jax.vjp(rms_piece, residual, gain_rows[1])
    partial_value, kept_ffn_a = ffn_forward(
        gather_rows(normed.astype(jnp.bfloat16)), ffn_a_in, ffn_a_out
    )
    residual = residual + scatter_rows(partial_value)
    normed, norm_back_c = jax.vjp(rms_piece, residual, gain_rows[2])
    partial_value, kept_attn = attention_forward(
        gather_rows(normed.astype(jnp.bfloat16)), qkv_weight, attn_out, allowed
    )
    residual = residual + scatter_rows(partial_value)
    normed, norm_back_d = jax.vjp(rms_piece, residual, gain_rows[3])
    partial_value, kept_ffn_b = ffn_forward(
        gather_rows(normed.astype(jnp.bfloat16)), ffn_b_in, ffn_b_out
    )
    residual = residual + scatter_rows(partial_value)
    block_rows = residual.astype(jnp.bfloat16)
    gradient = block_cot.astype(jnp.float32)
    d_normed, grads_ffn_b = ffn_backward(
        gather_grads(gradient.astype(jnp.bfloat16)), kept_ffn_b, ffn_b_in, ffn_b_out
    )
    d_rows, gain_d = norm_back_d(scatter_grads(d_normed))
    gradient = gradient + d_rows
    d_normed, grads_attn = attention_backward(
        gather_grads(gradient.astype(jnp.bfloat16)), kept_attn, qkv_weight, attn_out, allowed
    )
    d_rows, gain_c = norm_back_c(scatter_grads(d_normed))
    gradient = gradient + d_rows
    d_normed, grads_ffn_a = ffn_backward(
        gather_grads(gradient.astype(jnp.bfloat16)), kept_ffn_a, ffn_a_in, ffn_a_out
    )
    d_rows, gain_b = norm_back_b(scatter_grads(d_normed))
    gradient = gradient + d_rows
    d_normed, grads_mixer = mixer_backward(
        gather_grads(gradient.astype(jnp.bfloat16)),
        kept_mixer,
        mixer_in,
        mixer_x,
        mixer_dt,
        mixer_out,
    )
    d_rows, gain_a = norm_back_a(scatter_grads(d_normed))
    gradient = gradient + d_rows
    grad_terms = (
        (jnp.stack([gain_a, gain_b, gain_c, gain_d]),)
        + grads_mixer
        + grads_ffn_a
        + grads_attn
        + grads_ffn_b
    )
    return (block_rows, gradient.astype(jnp.bfloat16), grad_terms)


def per_device(
    hidden_in,
    out_grad,
    segment_ids,
    norm_gains,
    w_mixer_in,
    w_xproj,
    w_dtproj,
    mixer_params,
    w_mixer_out,
    w_ffn_a_in,
    w_ffn_a_out,
    w_qkv,
    w_attn_out,
    w_ffn_b_in,
    w_ffn_b_out,
):
    outputs = []
    entries = []
    totals = None
    for micro_index in range(MICRO):
        current = gather_weights(
            norm_gains,
            w_mixer_in,
            w_xproj,
            w_dtproj,
            mixer_params,
            w_mixer_out,
            w_ffn_a_in,
            w_ffn_a_out,
            w_qkv,
            w_attn_out,
            w_ffn_b_in,
            w_ffn_b_out,
        )
        block_rows, entry_grad, grad_terms = micro_batch(
            hidden_in[micro_index], out_grad[micro_index], segment_ids[micro_index], current
        )
        outputs.append(block_rows)
        entries.append(entry_grad)
        if totals is None:
            totals = grad_terms
        else:
            totals = jax.tree.map(jnp.add, totals, grad_terms)
    summed = (
        lax.psum_scatter(totals[0], "dp", scatter_dimension=1, tiled=True),
        lax.psum_scatter(totals[1], "dp", scatter_dimension=0, tiled=True),
        lax.psum_scatter(totals[2], "dp", scatter_dimension=0, tiled=True),
        lax.psum_scatter(totals[3], "dp", scatter_dimension=1, tiled=True),
        lax.psum_scatter(totals[4], "dp", scatter_dimension=1, tiled=True),
        lax.psum_scatter(totals[5], "dp", scatter_dimension=0, tiled=True),
        lax.psum_scatter(totals[6], "dp", scatter_dimension=0, tiled=True),
        lax.psum_scatter(totals[7], "dp", scatter_dimension=0, tiled=True),
        lax.psum_scatter(totals[8], "dp", scatter_dimension=0, tiled=True),
        lax.psum_scatter(totals[9], "dp", scatter_dimension=0, tiled=True),
        lax.psum_scatter(totals[10], "dp", scatter_dimension=0, tiled=True),
        lax.psum_scatter(totals[11], "dp", scatter_dimension=0, tiled=True),
    )
    gain_total = lax.psum(summed[0], "tensor")
    return (
        jnp.stack(outputs),
        jnp.stack(entries),
        gain_total,
        summed[1],
        summed[2],
        summed[3],
        summed[4],
        summed[5],
        summed[6],
        summed[7],
        summed[8],
        summed[9],
        summed[10],
        summed[11],
    )


def solution(mesh):
    placed = (
        P(None, ("dp", "tensor"), None),
        P(None, ("dp", "tensor"), None),
        P(None, "dp"),
        P(None, "dp"),
        P("dp", None, "tensor"),
        P(("tensor", "dp"), None),
        P(None, ("tensor", "dp")),
        P(None, ("tensor", "dp")),
        P(("tensor", "dp"), None),
        P("dp", None, "tensor"),
        P(("tensor", "dp"), None),
        P("dp", None, "tensor"),
        P(("tensor", "dp"), None),
        P("dp", None, "tensor"),
        P(("tensor", "dp"), None),
    )
    return jax.shard_map(
        per_device,
        mesh=mesh,
        in_specs=placed,
        out_specs=(
            P(None, ("dp", "tensor"), None),
            P(None, ("dp", "tensor"), None),
            P(None, "dp"),
            P("dp", None, "tensor"),
            P(("tensor", "dp"), None),
            P(None, ("tensor", "dp")),
            P(None, ("tensor", "dp")),
            P(("tensor", "dp"), None),
            P("dp", None, "tensor"),
            P(("tensor", "dp"), None),
            P("dp", None, "tensor"),
            P(("tensor", "dp"), None),
            P("dp", None, "tensor"),
            P(("tensor", "dp"), None),
        ),
        check_vma=False,
    )
```

profile of v0, /device:TPU:9, one launch (start us, length us, event | category | flops | bytes accessed | tf_op | source)
XLA Modules:
  0.0 3595.2 jit_solution(11513204328490386075)
XLA Ops:
  8.0 22.8 all-gather.2
  30.9 22.7 all-gather.3
  53.7 25.4 all_gather.100
  83.3 24.9 all_gather.98
  108.2 8.7 all_gather.112
  130.6 25.4 all_gather.101
  187.4 82.0 %while.160 = (s32[]{:T(128)}, f32[4,16,768]{2,1,0:T(8,128)S(1)}, f32[4,16,768]{2,1,0:T(8,128)S(1)}, f32[8,8,4,768]{3,2,1,0:T(4,128)}, f32[8,8,4,16,768]{4,3,2,1,...) while((s32[]{:T(128)}, f32[4,16,768]{2,1,0:T(8,128)S(1)}, ...), condition=%wide.region_11.12_spmd.clone, body=%wide.region_2.11_spmd.clone.sunk | while | flops 8011783 | bytes 21866636 | solution.py:113
  292.5 65.0 %while.162 = (s32[]{:T(128)}, f32[4,16,768]{2,1,0:T(8,128)S(1)}, f32[4,16,768]{2,1,0:T(8,128)S(1)}, f32[8,8,4,768]{3,2,1,0:T(4,128)}, f32[8,8,4,16,768]{4,3,2,1,...) while((s32[]{:T(128)}, f32[4,16,768]{2,1,0:T(8,128)S(1)}, ...), condition=%wide.region_35.36_spmd.clone, body=%wide.region_26.35_spmd.clone.sunk | while | flops 8011783 | bytes 21864720 | solution.py:113
  358.6 8.1 multiply_reduce_fusion.115
  368.2 8.1 multiply_reduce_fusion.114
  388.5 23.8 reduce-scatter.32.cloned.1.call-done
  412.4 25.7 reduce-scatter.40.cloned.1.call-done
  440.6 8.9 all_gather.103
  449.5 87.6 %all-gather.17.cloned.1.call-done = bf16[1536,2,1024]{2,1,0:T(2,128)(2,1)} async-done(((bf16[192,2,1024]{2,1,0:T(2,128)(2,1)}), bf16[1536,2,1024]{2,1,0:T(2,128)(2,1)}) %all-gather.17.cloned.1.call-update) | async-done | bytes 6291472 | tf_op jit(solution)/shard_map/all_gather | solution.py:188
  546.9 52.4 %all-gather.19.cloned.1.call-done = bf16[1024,1536]{1,0:T(8,128)(2,1)} async-done(((bf16[128,1536]{1,0:T(8,128)(2,1)}), bf16[1024,1536]{1,0:T(8,128)(2,1)}) %all-gather.19.cloned.1.call-update) | async-done | bytes 3145744 | tf_op jit(solution)/shard_map/all_gather | solution.py:189
  603.1 10.3 all_gather.113
  625.6 39.6 %all-gather.21.cloned.1.call-done = bf16[1536,3,384]{2,0,1:T(8,128)(2,1)} async-done(((bf16[192,3,384]{2,0,1:T(8,128)(2,1)}), bf16[1536,3,384]{2,0,1:T(8,128)(2,1)}) %all-gather.21.cloned.1.call-update) | async-done | bytes 3538960 | tf_op jit(solution)/shard_map/all_gather | solution.py:190
  671.4 19.8 reduce-scatter.34.cloned.1.call-done
  691.2 25.7 reduce-scatter.42.cloned.1.call-done
  719.2 9.1 all_gather.106
  738.9 20.1 all-gather.23.cloned.1.call-done
  764.3 10.4 all-gather
  774.7 83.6 %all-gather.25.cloned.1.call-done = bf16[1536,2,1024]{2,1,0:T(2,128)(2,1)} async-done(((bf16[192,2,1024]{2,1,0:T(2,128)(2,1)}), bf16[1536,2,1024]{2,1,0:T(2,128)(2,1)}) %all-gather.25.cloned.1.call-update) | async-done | bytes 6291472 | tf_op jit(solution)/shard_map/all_gather | solution.py:192
  858.3 8.1 copy.362
  866.3 18.4 reduce-scatter.36.cloned.1.call-done
  886.9 8.7 all_gather.109
  902.4 43.6 %all-gather.27.cloned.1.call-done = bf16[1024,1536]{1,0:T(8,128)(2,1)} async-done(((bf16[128,1536]{1,0:T(8,128)(2,1)}), bf16[1024,1536]{1,0:T(8,128)(2,1)}) %all-gather.27.cloned.1.call-update) | async-done | bytes 3145744 | tf_op jit(solution)/shard_map/all_gather | solution.py:193
  958.1 10.7 all_gather.114
  987.5 8.7 all_gather.117
  1008.4 9.8 all-gather.1
  1031.9 9.1 all_gather.115
  1058.2 23.0 reduce-scatter.56.cloned.1.call-done
  1083.5 23.5 reduce-scatter.38.cloned.1.call-done
  1109.5 8.7 all_gather.121
  1132.9 9.0 all_gather.118
  1153.8 24.2 reduce-scatter.46.cloned.1.call-done
  1180.1 8.7 all_gather.122
  1196.6 7.4 reduce-scatter.52.cloned.1.call-done
  1204.0 25.8 reduce-scatter.60.cloned.1.call-done
  1233.9 9.2 all_gather.119
  1247.8 11.7 broadcast_multiply_fusion.1
  1262.3 200.2 %while.165 = (s32[]{:T(128)}, f32[16,768]{1,0:T(8,128)}, f32[4,16,768]{2,1,0:T(8,128)S(1)}, f32[4,16,768]{2,1,0:T(8,128)S(1)}, f32[8,8,4,768]{3,2,1,0:T(4,128)S(...) while((s32[]{:T(128)}, f32[16,768]{1,0:T(8,128)}, ...), condition=%wide.region_107.108_spmd.clone, body=%wide.region_58.107_spmd.clone.sunk | while | flops 13036552 | bytes 34720992 | solution.py:113
  1464.1 9.1 all_gather.123
  1479.5 11.7 broadcast_multiply_fusion
  1496.9 132.0 %while.167 = (s32[]{:T(128)}, f32[16,768]{1,0:T(8,128)S(1)}, f32[4,16,768]{2,1,0:T(8,128)S(1)}, f32[4,16,768]{2,1,0:T(8,128)S(1)}, f32[8,8,4,768]{3,2,1,0:T(4,12...) while((s32[]{:T(128)}, f32[16,768]{1,0:T(8,128)S(1)}, ...), condition=%wide.region_170.171_spmd.clone, body=%wide.region_121.170_spmd.clone.sunk | while | flops 13036552 | bytes 34229852 | solution.py:113
  1640.3 28.0 all-reduce.45.cloned.1.call-done
  1684.0 7.5 fusion.274
  1691.7 7.4 reduce-scatter.62.cloned.1.call-done
  1699.1 26.4 reduce-scatter.54.cloned.1.call-done
  1728.9 10.9 convolution_add_fusion.2
  1739.8 16.9 add.772
  1767.2 17.0 add.766
  1790.9 14.9 copy.326
  1834.6 8.1 copy.327
  1855.3 62.5 %reduce-scatter.76.cloned.1.call-done = f32[192,4]{1,0:T(8,128)} async-done(((f32[1536,4]{1,0:T(8,128)}), f32[192,4]{1,0:T(8,128)}) %reduce-scatter.76.cloned.1.call-update) | async-done | bytes 3088
  1918.8 8.1 psum.39
  1926.9 392.3 %all-reduce.41.cloned.1.call-done = f32[1536,2,1024]{2,1,0:T(2,128)} async-done(((f32[1536,2,1024]{2,1,0:T(2,128)}), f32[1536,2,1024]{2,1,0:T(2,128)}) %all-reduce.41.cloned.1.call-update) | async-done | bytes 12582928
  2322.3 654.8 %all-reduce.43.cloned.1.call-done = (f32[1536,2,768]{2,1,0:T(2,128)}, f32[1536,2,1024]{2,1,0:T(2,128)}) async-done(((f32[1536,2,768]{2,1,0:T(2,128)}, f32[1536,2,1024]{2,1,0:T(2,128)}), (f32[1536,2,768]{2,1,0:T(2,128)}, f32[1536,2,1024]{2,1,0:T(2,128)})) %all-reduce.43.cloned.1.call-update) | async-done | bytes 22020112
  2982.8 58.3 %reduce-scatter.64.cloned.1.call-done = f32[96,128]{1,0:T(8,128)} async-done(((f32[768,128]{1,0:T(8,128)}), f32[96,128]{1,0:T(8,128)}) %reduce-scatter.64.cloned.1.call-update) | async-done | bytes 49168 | tf_op jit(solution)/shard_map/reduce_scatter | solution.py:476
  3041.1 72.3 %reduce-scatter.72.cloned.1.call-done = f32[48,1536]{1,0:T(8,128)} async-done(((f32[384,1536]{1,0:T(8,128)}), f32[48,1536]{1,0:T(8,128)}) %reduce-scatter.72.cloned.1.call-update) | async-done | bytes 294928 | tf_op jit(solution)/shard_map/reduce_scatter | solution.py:483
  3113.4 122.2 %reduce-scatter.74.cloned.1.call-done = f32[128,1536]{1,0:T(8,128)} async-done(((f32[1024,1536]{1,0:T(8,128)}), f32[128,1536]{1,0:T(8,128)}) %reduce-scatter.74.cloned.1.call-update) | async-done | bytes 786448 | tf_op jit(solution)/shard_map/reduce_scatter | solution.py:485
  3235.6 99.7 %reduce-scatter.66.cloned.1.call-done = f32[96,1536]{1,0:T(8,128)} async-done(((f32[768,1536]{1,0:T(8,128)}), f32[96,1536]{1,0:T(8,128)}) %reduce-scatter.66.cloned.1.call-update) | async-done | bytes 589840 | tf_op jit(solution)/shard_map/reduce_scatter | solution.py:479
  3335.3 120.8 %reduce-scatter.68.cloned.1.call-done = f32[128,1536]{1,0:T(8,128)} async-done(((f32[1024,1536]{1,0:T(8,128)}), f32[128,1536]{1,0:T(8,128)}) %reduce-scatter.68.cloned.1.call-update) | async-done | bytes 786448 | tf_op jit(solution)/shard_map/reduce_scatter | solution.py:481
  3456.1 132.1 %reduce-scatter.70.cloned.1.call-done = f32[192,3,384]{2,0,1:T(8,128)} async-done(((f32[1536,3,384]{2,0,1:T(8,128)}), f32[192,3,384]{2,0,1:T(8,128)}) %reduce-scatter.70.cloned.1.call-update) | async-done | bytes 884752 | tf_op jit(solution)/shard_map/reduce_scatter | solution.py:482
  (3094 shorter events, 858.3 us)
Async XLA Ops:
  7.2 75.9 %copy-start.2 = (bf16[2,64,1536]{2,1,0:T(8,128)(2,1)S(1)}, bf16[2,64,1536]{2,1,0:T(8,128)(2,1)}, u32[]{:S(2)}) copy-start(bf16[2,64,1536]{2,1,0:T(8,128)(2,1)} %param.31) | copy-start | bytes 1179652
  7.2 109.7 %all-gather.13.cloned.1.call-start = ((), (), s32[]{:S(2)}) async-start(), calls=%async_computation.25 | async-start | bytes 5308416 | tf_op jit(solution)/shard_map/all_gather | solution.py:183
  7.9 153.8 %all-reduce.47.cloned.1.call-start = ((), (), s32[]{:S(2)}) async-start(), calls=%async_computation.61 | async-start | bytes 262144 | tf_op jit(solution)/shard_map/psum | solution.py:209
  30.9 98.8 %copy-start.166 = (f32[768,23]{0,1:T(8,128)}, f32[768,23]{0,1:T(8,128)S(1)}, u32[]{:S(2)}) copy-start(f32[768,23]{0,1:T(8,128)S(1)} %reshape.2194) | copy-start | bytes 211972
  79.1 48.9 %copy-start.114 = (bf16[768,128]{1,0:T(8,128)(2,1)}, bf16[768,128]{1,0:T(8,128)(2,1)S(1)}, u32[]{:S(2)}) copy-start(bf16[768,128]{1,0:T(8,128)(2,1)S(1)} %all_gather.100) | copy-start | bytes 589828
  80.4 43.9 %copy-start.232 = (f32[768]{0:T(1024)}, f32[768]{0:T(1024)S(1)}, u32[]{:S(2)}) copy-start(f32[768]{0:T(1024)S(1)} %get-tuple-element.2358) | copy-start | bytes 9220
  80.4 43.9 %copy-start.234 = (f32[768]{0:T(1024)}, f32[768]{0:T(1024)S(1)}, u32[]{:S(2)}) copy-start(f32[768]{0:T(1024)S(1)} %get-tuple-element.2359) | copy-start | bytes 9220
  80.4 43.9 %copy-start.236 = (f32[768]{0:T(1024)}, f32[768]{0:T(1024)S(1)}, u32[]{:S(2)}) copy-start(f32[768]{0:T(1024)S(1)} %get-tuple-element.2360) | copy-start | bytes 9220
  80.4 43.9 %copy-start.238 = (f32[768]{0:T(1024)}, f32[768]{0:T(1024)S(1)}, u32[]{:S(2)}) copy-start(f32[768]{0:T(1024)S(1)} %get-tuple-element.2361) | copy-start | bytes 9220
  82.9 47.5 %copy-start.229 = (s32[1,256]{1,0:T(1,128)}, s32[1,256]{1,0:T(1,128)S(1)}, u32[]{:S(2)}) copy-start(s32[1,256]{1,0:T(1,128)S(1)} %get-tuple-element.3061) | copy-start | bytes 3076
  82.9 47.5 %copy-start.227 = (s32[1,256]{1,0:T(1,128)}, s32[1,256]{1,0:T(1,128)S(1)}, u32[]{:S(2)}) copy-start(s32[1,256]{1,0:T(1,128)S(1)} %get-tuple-element.3060) | copy-start | bytes 3076
  83.0 41.3 %copy-start.254 = (f32[256]{0:T(256)}, f32[256]{0:T(256)S(1)}, u32[]{:S(2)}) copy-start(f32[256]{0:T(256)S(1)} %get-tuple-element.3064) | copy-start | bytes 3076
  127.1 249.8 %copy-start.14 = (bf16[256,768]{1,0:T(8,128)(2,1)}, bf16[256,768]{1,0:T(8,128)(2,1)S(1)}, u32[]{:S(2)}) copy-start(bf16[256,768]{1,0:T(8,128)(2,1)S(1)} %get-tuple-element.3053) | copy-start | bytes 1179652
  127.1 249.8 %copy-start.16 = (bf16[256,768]{1,0:T(8,128)(2,1)}, bf16[256,768]{1,0:T(8,128)(2,1)S(1)}, u32[]{:S(2)}) copy-start(bf16[256,768]{1,0:T(8,128)(2,1)S(1)} %get-tuple-element.2588) | copy-start | bytes 1179652
  128.9 250.5 %all-gather.15.cloned.1.call-start = ((), (), s32[]{:S(2)}) async-start(), calls=%async_computation.26 | async-start | bytes 2654208 | tf_op jit(solution)/shard_map/all_gather | solution.py:187
  129.6 282.7 %reduce-scatter.32.cloned.1.call-start = ((), (), s32[]{:S(2)}) async-start(), calls=%async_computation.27 | async-start | bytes 983040 | tf_op jit(solution)/shard_map/reduce_scatter | solution.py:152
  383.0 55.1 %reduce-scatter.40.cloned.1.call-start = ((), (), s32[]{:S(2)}) async-start(), calls=%async_computation.37 | async-start | bytes 983040 | tf_op jit(solution)/shard_map/reduce_scatter | solution.py:152
  386.4 53.0 %copy-start.174 = (f32[1536]{0:T(1024)S(1)}, f32[1536]{0:T(1024)}, u32[]{:S(2)}) copy-start(f32[1536]{0:T(1024)} %get-tuple-element.2365) | copy-start | bytes 18436
  386.4 150.7 %all-gather.17.cloned.1.call-start = ((), (), s32[]{:S(2)}) async-start(), calls=%async_computation.28 | async-start | bytes 7077888 | tf_op jit(solution)/shard_map/all_gather | solution.py:188
  387.0 212.2 %all-gather.19.cloned.1.call-start = ((), (), s32[]{:S(2)}) async-start(), calls=%async_computation.29 | async-start | bytes 3538944 | tf_op jit(solution)/shard_map/all_gather | solution.py:189
  387.8 277.5 %all-gather.21.cloned.1.call-start = ((), (), s32[]{:S(2)}) async-start(), calls=%async_computation.31 | async-start | bytes 3981312 | tf_op jit(solution)/shard_map/all_gather | solution.py:190
  388.5 302.7 %reduce-scatter.34.cloned.1.call-start = ((), (), s32[]{:S(2)}) async-start(), calls=%async_computation.30 | async-start | bytes 983040 | tf_op jit(solution)/shard_map/reduce_scatter | solution.py:152
  439.4 792.6 %copy-start.240 = (f32[64]{0:T(128)}, f32[64]{0:T(128)S(1)}, u32[]{:S(2)}) copy-start(f32[64]{0:T(128)S(1)} %fusion.360) | copy-start | bytes 772
  439.4 792.6 %copy-start.242 = (f32[64]{0:T(128)}, f32[64]{0:T(128)S(1)}, u32[]{:S(2)}) copy-start(f32[64]{0:T(128)S(1)} %fusion.364) | copy-start | bytes 772
  449.5 93.0 %copy-start.45 = (bf16[256,1536]{1,0:T(8,128)(2,1)}, bf16[256,1536]{1,0:T(8,128)(2,1)S(1)}, u32[]{:S(2)}) copy-start(bf16[256,1536]{1,0:T(8,128)(2,1)S(1)} %all_gather.103) | copy-start | bytes 2359300
  546.9 56.1 %copy-start.96 = (bf16[256,1024]{1,0:T(8,128)(2,1)}, bf16[256,1024]{1,0:T(8,128)(2,1)S(1)}, u32[]{:S(2)}) copy-start(bf16[256,1024]{1,0:T(8,128)(2,1)S(1)} %multiply_convert_fusion.7) | copy-start | bytes 1572868
  603.0 113.9 %reduce-scatter.42.cloned.1.call-start = ((), (), s32[]{:S(2)}) async-start(), calls=%async_computation.38 | async-start | bytes 983040 | tf_op jit(solution)/shard_map/reduce_scatter | solution.py:152
  622.4 136.7 %all-gather.23.cloned.1.call-start = ((), (), s32[]{:S(2)}) async-start(), calls=%async_computation.32 | async-start | bytes 1327104 | tf_op jit(solution)/shard_map/all_gather | solution.py:191
  623.1 235.2 %all-gather.25.cloned.1.call-start = ((), (), s32[]{:S(2)}) async-start(), calls=%async_computation.34 | async-start | bytes 7077888 | tf_op jit(solution)/shard_map/all_gather | solution.py:192
  623.7 261.1 %reduce-scatter.36.cloned.1.call-start = ((), (), s32[]{:S(2)}) async-start(), calls=%async_computation.33 | async-start | bytes 983040 | tf_op jit(solution)/shard_map/reduce_scatter | solution.py:152
  625.6 91.3 %copy-start.7 = (bf16[64,1536]{1,0:T(8,128)(2,1)S(1)}, bf16[64,1536]{1,0:T(8,128)(2,1)}, u32[]{:S(2)}) copy-start(bf16[64,1536]{1,0:T(8,128)(2,1)} %reduce-scatter.32.cloned.1.call-done) | copy-start | bytes 589828
  625.6 91.3 %copy-start.9 = (bf16[64,1536]{1,0:T(8,128)(2,1)S(1)}, bf16[64,1536]{1,0:T(8,128)(2,1)}, u32[]{:S(2)}) copy-start(bf16[64,1536]{1,0:T(8,128)(2,1)} %reduce-scatter.40.cloned.1.call-done) | copy-start | bytes 589828
  625.6 92.8 %copy-start.176 = (f32[1536]{0:T(1024)S(1)}, f32[1536]{0:T(1024)}, u32[]{:S(2)}) copy-start(f32[1536]{0:T(1024)} %get-tuple-element.2364) | copy-start | bytes 18436
  761.9 184.1 %all-gather.27.cloned.1.call-start = ((), (), s32[]{:S(2)}) async-start(), calls=%async_computation.35 | async-start | bytes 3538944 | tf_op jit(solution)/shard_map/all_gather | solution.py:193
  762.5 221.8 %reduce-scatter.48.cloned.1.call-start = ((), (), s32[]{:S(2)}) async-start(), calls=%async_computation.41 | async-start | bytes 983040 | tf_op jit(solution)/shard_map/reduce_scatter | solution.py:162
  957.3 72.3 %reduce-scatter.44.cloned.1.call-start = ((), (), s32[]{:S(2)}) async-start(), calls=%async_computation.39 | async-start | bytes 983040 | tf_op jit(solution)/shard_map/reduce_scatter | solution.py:152
  1008.3 47.6 %reduce-scatter.50.cloned.1.call-start = ((), (), s32[]{:S(2)}) async-start(), calls=%async_computation.42 | async-start | bytes 983040 | tf_op jit(solution)/shard_map/reduce_scatter | solution.py:162
  1028.7 52.5 %reduce-scatter.56.cloned.1.call-start = ((), (), s32[]{:S(2)}) async-start(), calls=%async_computation.45 | async-start | bytes 983040 | tf_op jit(solution)/shard_map/reduce_scatter | solution.py:162
  1051.9 55.2 %reduce-scatter.38.cloned.1.call-start = ((), (), s32[]{:S(2)}) async-start(), calls=%async_computation.36 | async-start | bytes 983040 | tf_op jit(solution)/shard_map/reduce_scatter | solution.py:152
  1055.8 51.2 %copy-start.27 = (bf16[64,1536]{1,0:T(8,128)(2,1)S(1)}, bf16[64,1536]{1,0:T(8,128)(2,1)}, u32[]{:S(2)}) copy-start(bf16[64,1536]{1,0:T(8,128)(2,1)} %reduce-scatter.36.cloned.1.call-done) | copy-start | bytes 589828
  1055.8 51.2 %copy-start.41 = (bf16[2,64,1536]{2,1,0:T(8,128)(2,1)S(1)}, bf16[2,64,1536]{2,1,0:T(8,128)(2,1)}, u32[]{:S(2)}) copy-start(bf16[2,64,1536]{2,1,0:T(8,128)(2,1)} %param.32) | copy-start | bytes 1179652
  1055.9 96.3 %reduce-scatter.58.cloned.1.call-start = ((), (), s32[]{:S(2)}) async-start(), calls=%async_computation.46 | async-start | bytes 983040 | tf_op jit(solution)/shard_map/reduce_scatter | solution.py:162
  1128.8 49.1 %reduce-scatter.46.cloned.1.call-start = ((), (), s32[]{:S(2)}) async-start(), calls=%async_computation.40 | async-start | bytes 983040 | tf_op jit(solution)/shard_map/reduce_scatter | solution.py:152
  1132.8 71.2 %reduce-scatter.52.cloned.1.call-start = ((), (), s32[]{:S(2)}) async-start(), calls=%async_computation.43 | async-start | bytes 983040 | tf_op jit(solution)/shard_map/reduce_scatter | solution.py:162
  1151.9 77.9 %reduce-scatter.60.cloned.1.call-start = ((), (), s32[]{:S(2)}) async-start(), calls=%async_computation.47 | async-start | bytes 983040 | tf_op jit(solution)/shard_map/reduce_scatter | solution.py:162
  1180.1 51.9 %copy-start.39 = (f32[64,1536]{1,0:T(8,128)}, f32[64,1536]{1,0:T(8,128)S(1)}, u32[]{:S(2)}) copy-start(f32[64,1536]{1,0:T(8,128)S(1)} %get-tuple-element.2580) | copy-start | bytes 1179652
  1196.5 471.8 %all-reduce.45.cloned.1.call-start = ((), (), s32[]{:S(2)}) async-start(), calls=%async_computation.60 | async-start | bytes 262144 | tf_op jit(solution)/shard_map/psum | solution.py:241
  1196.6 46.4 %copy-start.17 = (bf16[256,768]{1,0:T(8,128)(2,1)S(1)}, bf16[256,768]{1,0:T(8,128)(2,1)}, u32[]{:S(2)}) copy-start(bf16[256,768]{1,0:T(8,128)(2,1)} %copy-done.16) | copy-start | bytes 1179652
  1637.7 61.4 %reduce-scatter.62.cloned.1.call-start = ((), (), s32[]{:S(2)}) async-start(), calls=%async_computation.48 | async-start | bytes 983040 | tf_op jit(solution)/shard_map/reduce_scatter | solution.py:162
  1674.7 50.8 %reduce-scatter.54.cloned.1.call-start = ((), (), s32[]{:S(2)}) async-start(), calls=%async_computation.44 | async-start | bytes 983040 | tf_op jit(solution)/shard_map/reduce_scatter | solution.py:162
  1681.0 164.4 %reduce-scatter.80.cloned.1.call-start = ((), (), s32[]{:S(2)}) async-start(), calls=%async_computation.57 | async-start | bytes 442368
  1682.6 169.6 %reduce-scatter.78.cloned.1.call-start = ((), (), s32[]{:S(2)}) async-start(), calls=%async_computation.56 | async-start | bytes 442368
  1683.9 41.6 %copy-start.181 = (f32[1536]{0:T(1024)S(1)}, f32[1536]{0:T(1024)}, u32[]{:S(2)}) copy-start(f32[1536]{0:T(1024)} %copy-done.180) | copy-start | bytes 18436
  1683.9 41.6 %copy-start.245 = (f32[64]{0:T(128)S(1)}, f32[64]{0:T(128)}, u32[]{:S(2)}) copy-start(f32[64]{0:T(128)} %copy-done.244) | copy-start | bytes 772
  1683.9 41.6 %copy-start.248 = (f32[64]{0:T(128)S(1)}, f32[64]{0:T(128)}, u32[]{:S(2)}) copy-start(f32[64]{0:T(128)} %copy-done.247) | copy-start | bytes 772
  1683.9 233.9 %reduce-scatter.76.cloned.1.call-start = ((), (), s32[]{:S(2)}) async-start(), calls=%async_computation.55 | async-start | bytes 884736
  1728.8 590.4 %all-reduce.41.cloned.1.call-start = ((), (), s32[]{:S(2)}) async-start(), calls=%async_computation.58 | async-start | bytes 25165824
  1756.7 1220.3 %all-reduce.43.cloned.1.call-start = ((), (), s32[]{:S(2)}) async-start(), calls=%async_computation.59 | async-start | bytes 44040192
  1805.8 1235.3 %reduce-scatter.64.cloned.1.call-start = ((), (), s32[]{:S(2)}) async-start(), calls=%async_computation.49 | async-start | bytes 442368 | tf_op jit(solution)/shard_map/reduce_scatter | solution.py:476
  1808.2 1305.2 %reduce-scatter.72.cloned.1.call-start = ((), (), s32[]{:S(2)}) async-start(), calls=%async_computation.53 | async-start | bytes 2654208 | tf_op jit(solution)/shard_map/reduce_scatter | solution.py:483
  1811.2 1424.4 %reduce-scatter.74.cloned.1.call-start = ((), (), s32[]{:S(2)}) async-start(), calls=%async_computation.54 | async-start | bytes 7077888 | tf_op jit(solution)/shard_map/reduce_scatter | solution.py:485
  1817.3 1518.0 %reduce-scatter.66.cloned.1.call-start = ((), (), s32[]{:S(2)}) async-start(), calls=%async_computation.50 | async-start | bytes 5308416 | tf_op jit(solution)/shard_map/reduce_scatter | solution.py:479
  1822.3 1633.8 %reduce-scatter.68.cloned.1.call-start = ((), (), s32[]{:S(2)}) async-start(), calls=%async_computation.51 | async-start | bytes 7077888 | tf_op jit(solution)/shard_map/reduce_scatter | solution.py:481
  1828.3 1759.9 %reduce-scatter.70.cloned.1.call-start = ((), (), s32[]{:S(2)}) async-start(), calls=%async_computation.52 | async-start | bytes 7962624 | tf_op jit(solution)/shard_map/reduce_scatter | solution.py:482
  (584 other events, 3936.5 us)
Sparse Core Ops, SparseCore 0:
  10.2 82.3 all-gather.12
  129.0 30.9 all-reduce.46
  162.4 52.0 all-gather.14
  383.1 29.2 reduce-scatter.31
  414.8 23.2 reduce-scatter.39
  440.4 96.7 all-gather.16
  539.5 59.6 all-gather.18
  601.7 63.5 all-gather.20
  667.9 23.2 reduce-scatter.33
  693.6 23.2 reduce-scatter.41
  719.4 39.6 all-gather.22
  761.3 96.9 all-gather.24
  861.0 23.7 reduce-scatter.35
  886.8 59.1 all-gather.26
  957.4 23.1 reduce-scatter.47
  1008.4 21.1 reduce-scatter.43
  1032.0 23.2 reduce-scatter.49
  1057.9 23.2 reduce-scatter.55
  1083.7 23.2 reduce-scatter.37
  1129.0 23.1 reduce-scatter.57
  1154.7 23.2 reduce-scatter.45
  1180.7 23.2 reduce-scatter.51
  1206.5 23.2 reduce-scatter.59
  1637.9 30.3 all-reduce.44
  1674.8 24.2 reduce-scatter.61
  1702.2 23.2 reduce-scatter.53
  1728.6 59.2 reduce-scatter.79
  1791.8 60.4 reduce-scatter.77
  1856.1 61.6 reduce-scatter.75
  1922.3 396.8 all-reduce.40
  2323.4 653.5 all-reduce.42
  2980.9 60.2 reduce-scatter.63
  3045.1 68.3 reduce-scatter.71
  3117.6 117.9 reduce-scatter.73
  3239.8 95.4 reduce-scatter.65
  3339.3 116.7 reduce-scatter.67
  3460.2 127.9 reduce-scatter.69
where the time goes:
time: 3620 us; the launch traced here: 3600 us
  waiting for transfers between devices  2330 us (64%)
  local copies, waits for them, and re-layouts  440 us (12%)
  other arithmetic  340 us (9%)
  blocking collectives  268 us (7%)
  matrix products  183 us (5%)
    unnamed x42, waiting for transfers between devices  1120 us
    reduce_scatter x8, waiting for transfers between devices, scatter_rows(): lax.psum_scatter(partial_value.astype(jnp.bfloat16), 'tensor', scatter_di...  162 us
    reduce_scatter x1, waiting for transfers between devices, per_device(): lax.psum_scatter(totals[8], 'dp', scatter_dimension=0, tiled=True)  132 us
    reduce_scatter x1, waiting for transfers between devices, per_device(): lax.psum_scatter(totals[11], 'dp', scatter_dimension=0, tiled=True)  122 us
    reduce_scatter x1, waiting for transfers between devices, per_device(): lax.psum_scatter(totals[7], 'dp', scatter_dimension=0, tiled=True)  121 us
    reduce_sum x128, other arithmetic, advance(): output_t[:, :, None] * state  103 us
    squeeze x96, local copies, waits for them, and re-layouts, mix_piece(): lax.scan(jax.checkpoint(advance), initial, inputs_all, unroll=min(8, block))  102 us
    reduce_scatter x1, waiting for transfers between devices, per_device(): lax.psum_scatter(totals[5], 'dp', scatter_dimension=0, tiled=True)  99.7 us
  transfers between devices with their start and end apart: 37, of which 31 were waited for; matrix products, arithmetic and copies ran while one was open for 14% of the time, Pallas kernels for 0%

commit v1 on v0

v1 whole, which is shorter than its diff:
```python
import math

import jax
import jax.numpy as jnp
from jax import lax
from jax.experimental import pallas as pl
from jax.experimental.pallas import tpu as pltpu
from jax.sharding import PartitionSpec as P

STATE = 16
CONV = 4
RANK = 96
HEAD = 128
MICRO = 2
PIECES = 4
ORDER = (0, 2, 1, 3)

f32 = jnp.float32
bf16 = jnp.bfloat16
epsilon = 1e-05
floor_score = -1e30


def dot(a, b, dims=((1,), (0,)), out=f32):
    return lax.dot_general(a, b, (dims, ((), ())), preferred_element_type=out)


def dot_tn(a, b, out=f32):
    return dot(a, b, ((0,), (0,)), out)


def dot_nt(a, b, out=f32):
    return dot(a, b, ((1,), (1,)), out)


def sigmoid(v):
    return 1.0 / (1.0 + jnp.exp(-v))


def dsilu(v):
    s = jax.nn.sigmoid(v)
    return s * (1.0 + v * (1.0 - s))


def soft_plus(v):
    return jnp.maximum(v, 0.0) + jnp.log1p(jnp.exp(-jnp.abs(v)))


def conv_fwd_kernel(slot, x_ref, mask_ref, par_ref, wx_ref, val_ref, ext_ref, prev):
    @pl.when((pl.program_id(0) == 0) & (pl.program_id(1) == 0))
    def _():
        prev[...] = jnp.zeros_like(prev)

    x = x_ref[0, 0]
    rows = x.shape[0]
    xe = jnp.concatenate([prev[...], x], axis=0)
    mask = mask_ref[0, 0]
    conv = jnp.broadcast_to(par_ref[4:5, :], x.shape)
    for k in range(CONV):
        conv = conv + par_ref[k : k + 1, :] * xe[8 - k : 8 - k + rows] * mask[:, k : k + 1]
    prev[...] = x[rows - 8 :]
    val = (conv * sigmoid(conv)).astype(bf16)
    val_ref[0, 0] = val
    ext_ref[0, 0] = dot(val, wx_ref[...]).astype(bf16)


def conv_bwd_kernel(
    slot, dext_ref, dval_ref, x_ref, xp_ref, mask_ref, par_ref, wx_ref, dx_ref, sum_ref, after
):
    @pl.when((pl.program_id(0) == 0) & (pl.program_id(1) == 0))
    def _():
        after[...] = jnp.zeros_like(after)
        sum_ref[...] = jnp.zeros_like(sum_ref)

    x = x_ref[0, 0]
    rows = x.shape[0]
    xe = jnp.concatenate([xp_ref[0, 0], x], axis=0)
    mask = mask_ref[0, 0]
    conv = jnp.broadcast_to(par_ref[4:5, :], x.shape)
    for k in range(CONV):
        conv = conv + par_ref[k : k + 1, :] * xe[8 - k : 8 - k + rows] * mask[:, k : k + 1]
    sig = sigmoid(conv)
    d_conv = (dval_ref[0, 0] + dot_nt(dext_ref[0, 0], wx_ref[...])) * (
        sig * (1.0 + conv * (1.0 - sig))
    )
    d_x = jnp.zeros_like(x)
    sums = []
    for k in range(CONV):
        held = d_conv * mask[:, k : k + 1]
        sums.append(jnp.sum(held * xe[8 - k : 8 - k + rows], axis=0, keepdims=True))
        if k == 0:
            d_x = d_x + par_ref[0:1, :] * held
        else:
            he = jnp.concatenate([held, after[k - 1]], axis=0)
            d_x = d_x + par_ref[k : k + 1, :] * he[k : k + rows]
            after[k - 1] = held[:8]
    sums.append(jnp.sum(d_conv, axis=0, keepdims=True))
    for k in range(CONV + 1):
        sum_ref[k : k + 1, :] += sums[k]
    dx_ref[0, 0] = d_x.astype(bf16)


def coefficient_rows(ext):
    both = jnp.concatenate([ext, ext], axis=0)
    return both.T[RANK:]


def scan_fwd_kernel(
    slot, ext_ref, wdt_ref, val_ref, z_ref, par_ref, rate_ref, keep_ref,
    gated_ref, scan_ref, h_ref, state, se, sv, sc,
):
    @pl.when((pl.program_id(0) == 0) & (pl.program_id(1) == 0))
    def _():
        state[...] = jnp.zeros_like(state)

    ext_low = ext_ref[0, 0]
    step = soft_plus(dot(ext_low[:, :RANK], wdt_ref[...]) + par_ref[5:6, :])
    val = val_ref[0, 0].astype(f32)
    se[...] = jnp.where(keep_ref[0, 0] > 0.0, step, 1e30)
    sv[...] = step * val
    rate = rate_ref[...]
    coef = coefficient_rows(ext_low.astype(f32))
    shape = rate.shape

    def body(g, h):
        base = pl.multiple_of(8 * g, 8)
        turned = pltpu.roll(coef, (128 - base) % 128, 1)
        se_t = se[pl.ds(base, 8), :]
        sv_t = sv[pl.ds(base, 8), :]
        for j in range(8):
            a = jnp.exp(jnp.broadcast_to(se_t[j : j + 1], shape) * rate)
            h = a * h + jnp.broadcast_to(sv_t[j : j + 1], shape) * turned[:STATE, j : j + 1]
            h_ref[0, base + j] = h.astype(bf16)
            sc[pl.ds(base + j, 1), :] = jnp.sum(
                h * turned[STATE:, j : j + 1], axis=0, keepdims=True
            )
        return h

    state[...] = lax.fori_loop(0, se.shape[0] // 8, body, state[...])
    scanned = sc[...]
    z = z_ref[0, 0]
    scan_ref[0, 0] = scanned
    gated_ref[0, 0] = ((scanned + par_ref[6:7, :] * val) * (z * sigmoid(z))).astype(bf16)


def scan_bwd_kernel(
    slot, ext_ref, wdt_ref, val_ref, z_ref, par_ref, rate_ref, keep_ref, dg_ref, scan_ref,
    h_ref, hp_ref, ddt_ref, dval_ref, dz_ref, dbc_ref, drate_ref, sum_ref,
    carry, se, st, sv, ds, r1, r2, pb, pc,
):
    @pl.when((pl.program_id(0) == 0) & (pl.program_id(1) == 0))
    def _():
        carry[...] = jnp.zeros_like(carry)
        drate_ref[...] = jnp.zeros_like(drate_ref)
        sum_ref[...] = jnp.zeros_like(sum_ref)

    ext_low = ext_ref[0, 0]
    pre = dot(ext_low[:, :RANK], wdt_ref[...]) + par_ref[5:6, :]
    step = soft_plus(pre)
    val = val_ref[0, 0].astype(f32)
    z = z_ref[0, 0]
    sig_z = sigmoid(z)
    d_gated = dg_ref[0, 0].astype(f32)
    skip = par_ref[6:7, :]
    d_scan = d_gated * (z * sig_z)
    dz_ref[0, 0] = (
        d_gated * (scan_ref[0, 0] + skip * val) * (sig_z * (1.0 + z * (1.0 - sig_z)))
    ).astype(bf16)
    se[...] = jnp.where(keep_ref[0, 0] > 0.0, step, 1e30)
    st[...] = step
    sv[...] = step * val
    ds[...] = d_scan
    rate = rate_ref[...]
    shape = rate.shape
    coef = coefficient_rows(ext_low.astype(f32))
    count = se.shape[0] // 8
    lanes = shape[1] // 128

    def fold(v):
        total = v[:, :128]
        for i in range(1, lanes):
            total = total + v[:, 128 * i : 128 * (i + 1)]
        return total

    def body(i, held):
        back, d_rate = held
        base = pl.multiple_of(8 * (count - 1 - i), 8)
        turned = pltpu.roll(coef, (128 - base) % 128, 1)
        se_t = se[pl.ds(base, 8), :]
        st_t = st[pl.ds(base, 8), :]
        sv_t = sv[pl.ds(base, 8), :]
        ds_t = ds[pl.ds(base, 8), :]
        for j in range(7, -1, -1):
            row = base + j
            h_now = h_ref[0, row].astype(f32)
            if j > 0:
                h_before = h_ref[0, row - 1].astype(f32)
            else:
                h_before = jnp.where(
                    base == 0,
                    hp_ref[0, 0].astype(f32),
                    h_ref[0, jnp.maximum(row - 1, 0)].astype(f32),
                )
            a = jnp.exp(jnp.broadcast_to(se_t[j : j + 1], shape) * rate)
            d_row = jnp.broadcast_to(ds_t[j : j + 1], shape)
            lam = d_row * turned[STATE:, j : j + 1] + back
            back = a * lam
            w = back * h_before
            d_rate = d_rate + w * jnp.broadcast_to(st_t[j : j + 1], shape)
            r1[pl.ds(row, 1), :] = jnp.sum(w * rate, axis=0, keepdims=True)
            r2[pl.ds(row, 1), :] = jnp.sum(lam * turned[:STATE, j : j + 1], axis=0, keepdims=True)
            at = pl.ds(pl.multiple_of(row * STATE, STATE), STATE)
            pb[at, :] = fold(lam * jnp.broadcast_to(sv_t[j : j + 1], shape)).astype(bf16)
            pc[at, :] = fold(d_row * h_now).astype(bf16)
        return back, d_rate

    back, d_rate = lax.fori_loop(0, count, body, (carry[...], jnp.zeros(shape, f32)))
    carry[...] = back
    drate_ref[...] += d_rate
    ones = jnp.ones((8, 128), bf16)
    dbc_ref[0, 0, 0] = dot_nt(ones, pb[...])
    dbc_ref[0, 0, 1] = dot_nt(ones, pc[...])
    d_step = r1[...] + val * r2[...]
    d_dt = d_step * sigmoid(pre)
    dval_ref[0, 0] = step * r2[...] + skip * d_scan
    ddt_ref[0, 0] = d_dt.astype(bf16)
    sum_ref[0:1, :] += jnp.sum(d_dt, axis=0, keepdims=True)
    sum_ref[1:2, :] += jnp.sum(d_scan * val, axis=0, keepdims=True)


def turn(v, cos, sin):
    return v * cos + pltpu.roll(v, HEAD // 2, 1) * sin


def attention_parts(seg_c, seg_r, pos_c, pos_r):
    return (seg_c == seg_r) & (pos_r <= pos_c)


def attn_fwd_kernel(qkv_ref, cos_ref, sin_ref, segc, segr, posc, posr, mix_ref, low_ref):
    heads = qkv_ref.shape[3] // (3 * HEAD)
    length = PIECES * qkv_ref.shape[2]
    cos = cos_ref[...].reshape(length, HEAD)
    sin = sin_ref[...].reshape(length, HEAD)
    allowed = attention_parts(segc[...].reshape(length, 1), segr[0], posc[...], posr[...])

    def take(i):
        return qkv_ref[:, 0, :, i * HEAD : (i + 1) * HEAD].reshape(length, HEAD)

    def put(ref, i, v):
        ref[:, 0, :, i * HEAD : (i + 1) * HEAD] = v.reshape(PIECES, -1, HEAD)

    for h in range(heads):
        q = turn(take(h), cos, sin).astype(bf16)
        k = turn(take(heads + h), cos, sin).astype(bf16)
        v = take(2 * heads + h).astype(bf16)
        scores = jnp.where(allowed, dot_nt(q, k) * HEAD ** (-0.5), floor_score)
        e = jnp.exp(scores - jnp.max(scores, axis=1, keepdims=True))
        probs = (e / jnp.sum(e, axis=1, keepdims=True)).astype(bf16)
        put(mix_ref, h, dot(probs, v).astype(bf16))
        put(low_ref, h, q)
        put(low_ref, heads + h, k)
        put(low_ref, 2 * heads + h, v)


def attn_bwd_kernel(low_ref, dmix_ref, cos_ref, sin_ref, segc, segr, posc, posr, dqkv_ref):
    heads = low_ref.shape[3] // (3 * HEAD)
    length = PIECES * low_ref.shape[2]
    cos = cos_ref[...].reshape(length, HEAD)
    sin = -sin_ref[...].reshape(length, HEAD)
    allowed = attention_parts(segc[...].reshape(length, 1), segr[0], posc[...], posr[...])
    scale = HEAD ** (-0.5)

    def take(ref, i):
        return ref[:, 0, :, i * HEAD : (i + 1) * HEAD].reshape(length, HEAD)

    def put(i, v):
        dqkv_ref[:, 0, :, i * HEAD : (i + 1) * HEAD] = v.astype(bf16).reshape(PIECES, -1, HEAD)

    for h in range(heads):
        q, k, v = take(low_ref, h), take(low_ref, heads + h), take(low_ref, 2 * heads + h)
        d_mix = take(dmix_ref, h)
        scores = jnp.where(allowed, dot_nt(q, k) * scale, floor_score)
        e = jnp.exp(scores - jnp.max(scores, axis=1, keepdims=True))
        probs = e / jnp.sum(e, axis=1, keepdims=True)
        d_probs = dot_nt(d_mix, v)
        d_scores = (
            probs * (d_probs - jnp.sum(probs * d_probs, axis=1, keepdims=True))
        ).astype(bf16)
        put(h, turn(dot(d_scores, k) * scale, cos, sin))
        put(heads + h, turn(dot_tn(d_scores, q) * scale, cos, sin))
        put(2 * heads + h, dot_tn(probs.astype(bf16), d_mix))


BIG = 48 * 1024 * 1024


def params(dims):
    return pltpu.CompilerParams(
        dimension_semantics=("arbitrary",) * dims, vmem_limit_bytes=BIG
    )


def rel(rows, cols, col=0):
    return pl.BlockSpec((1, 1, rows, cols), lambda m, j, s: (s[j], m, 0, col))


def rel_back(rows, cols, col=0):
    return pl.BlockSpec((1, 1, rows, cols), lambda m, j, s: (s[PIECES - 1 - j], m, 0, col))


def ordered(rows, cols):
    return pl.BlockSpec((1, 1, rows, cols), lambda m, j, s: (m, j, 0, 0))


def ordered_back(rows, cols):
    return pl.BlockSpec((1, 1, rows, cols), lambda m, j, s: (m, PIECES - 1 - j, 0, 0))


def fixed(*shape):
    return pl.BlockSpec(shape, lambda m, j, s: (0,) * len(shape))


def conv_forward(slots, pre, masks, par, wx):
    rows, width = pre.shape[2], pre.shape[3] // 2
    grid = pltpu.PrefetchScalarGridSpec(
        num_scalar_prefetch=1,
        grid=(MICRO, PIECES),
        in_specs=[rel(rows, width), ordered(rows, CONV), fixed(8, width), fixed(*wx.shape)],
        out_specs=[rel(rows, width), rel(rows, wx.shape[1])],
        scratch_shapes=[pltpu.VMEM((8, width), f32)],
    )
    return pl.pallas_call(
        conv_fwd_kernel,
        grid_spec=grid,
        out_shape=[
            jax.ShapeDtypeStruct((PIECES, MICRO, rows, width), bf16),
            jax.ShapeDtypeStruct((PIECES, MICRO, rows, wx.shape[1]), bf16),
        ],
        compiler_params=params(2),
        name="conv_forward",
    )(slots, pre, masks, par, wx)


def conv_backward(slots, d_ext, d_val, pre, masks, par, wx):
    rows, width = pre.shape[2], pre.shape[3] // 2
    last = rows // 8 - 1
    grid = pltpu.PrefetchScalarGridSpec(
        num_scalar_prefetch=1,
        grid=(MICRO, PIECES),
        in_specs=[
            rel_back(rows, wx.shape[1]),
            rel_back(rows, width),
            rel_back(rows, width),
            pl.BlockSpec(
                (1, 1, 8, width),
                lambda m, j, s: (s[jnp.maximum(PIECES - 2 - j, 0)], m, last, 0),
            ),
            ordered_back(rows, CONV),
            fixed(8, width),
            fixed(*wx.shape),
        ],
        out_specs=[rel_back(rows, width), fixed(8, width)],
        scratch_shapes=[pltpu.VMEM((CONV - 1, 8, width), f32)],
    )
    return pl.pallas_call(
        conv_bwd_kernel,
        grid_spec=grid,
        out_shape=[
            jax.ShapeDtypeStruct((PIECES, MICRO, rows, width), bf16),
            jax.ShapeDtypeStruct((8, width), f32),
        ],
        compiler_params=params(2),
        name="conv_backward",
    )(slots, d_ext, d_val, pre, pre, masks, par, wx)


def scan_forward(slots, ext, wdt, val, pre, par, rate, keep):
    rows, width = val.shape[2], val.shape[3]
    grid = pltpu.PrefetchScalarGridSpec(
        num_scalar_prefetch=1,
        grid=(MICRO, PIECES),
        in_specs=[
            rel(rows, ext.shape[3]), fixed(*wdt.shape), rel(rows, width), rel(rows, width, 1),
            fixed(8, width), fixed(STATE, width), ordered(rows, 1),
        ],
        out_specs=[
            rel(rows, width), rel(rows, width),
            pl.BlockSpec((1, rows, STATE, width), lambda m, j, s: (m * PIECES + j, 0, 0, 0)),
        ],
        scratch_shapes=[pltpu.VMEM((STATE, width), f32)] + [pltpu.VMEM((rows, width), f32)] * 3,
    )
    return pl.pallas_call(
        scan_fwd_kernel,
        grid_spec=grid,
        out_shape=[
            jax.ShapeDtypeStruct((PIECES, MICRO, rows, width), bf16),
            jax.ShapeDtypeStruct((PIECES, MICRO, rows, width), f32),
            jax.ShapeDtypeStruct((MICRO * PIECES, rows, STATE, width), bf16),
        ],
        compiler_params=params(2),
        name="scan_forward",
    )(slots, ext, wdt, val, pre, par, rate, keep)


def scan_backward(slots, ext, wdt, val, pre, par, rate, keep, d_gated, scanned, states):
    rows, width = val.shape[2], val.shape[3]
    grid = pltpu.PrefetchScalarGridSpec(
        num_scalar_prefetch=1,
        grid=(MICRO, PIECES),
        in_specs=[
            rel_back(rows, ext.shape[3]), fixed(*wdt.shape), rel_back(rows, width),
            rel_back(rows, width, 1), fixed(8, width), fixed(STATE, width), ordered_back(rows, 1),
            rel_back(rows, width), rel_back(rows, width),
            pl.BlockSpec(
                (1, rows, STATE, width),
                lambda m, j, s: (m * PIECES + PIECES - 1 - j, 0, 0, 0),
            ),
            pl.BlockSpec(
                (1, 1, STATE, width),
                lambda m, j, s: (
                    jnp.maximum(m * PIECES + PIECES - 2 - j, 0), rows - 1, 0, 0,
                ),
            ),
        ],
        out_specs=[
            rel_back(rows, width), rel_back(rows, width), rel_back(rows, width),
            pl.BlockSpec(
                (1, 1, 2, 8, rows * STATE),
                lambda m, j, s: (s[PIECES - 1 - j], m, 0, 0, 0),
            ),
            fixed(STATE, width), fixed(8, width),
        ],
        scratch_shapes=[pltpu.VMEM((STATE, width), f32)]
        + [pltpu.VMEM((rows, width), f32)] * 6
        + [pltpu.VMEM((rows * STATE, 128), bf16)] * 2,
    )
    return pl.pallas_call(
        scan_bwd_kernel,
        grid_spec=grid,
        out_shape=[
            jax.ShapeDtypeStruct((PIECES, MICRO, rows, width), bf16),
            jax.ShapeDtypeStruct((PIECES, MICRO, rows, width), f32),
            jax.ShapeDtypeStruct((PIECES, MICRO, rows, width), bf16),
            jax.ShapeDtypeStruct((PIECES, MICRO, 2, 8, rows * STATE), f32),
            jax.ShapeDtypeStruct((STATE, width), f32),
            jax.ShapeDtypeStruct((8, width), f32),
        ],
        compiler_params=params(2),
        name="scan_backward",
    )(slots, ext, wdt, val, pre, par, rate, keep, d_gated, scanned, states, states)


def attention_specs(rows, length):
    return [
        pl.BlockSpec((PIECES, rows, HEAD), lambda m: (0, 0, 0)),
        pl.BlockSpec((PIECES, rows, HEAD), lambda m: (0, 0, 0)),
        pl.BlockSpec((PIECES, 1, rows, 1), lambda m: (0, m, 0, 0)),
        pl.BlockSpec((1, 1, length), lambda m: (m, 0, 0)),
        pl.BlockSpec((length, 1), lambda m: (0, 0)),
        pl.BlockSpec((1, length), lambda m: (0, 0)),
    ]


def attention_forward(qkv, tables):
    rows, width = qkv.shape[2], qkv.shape[3]

    def whole(cols):
        return pl.BlockSpec((PIECES, 1, rows, cols), lambda m: (0, m, 0, 0))

    return pl.pallas_call(
        attn_fwd_kernel,
        grid=(MICRO,),
        in_specs=[whole(width)] + attention_specs(rows, PIECES * rows),
        out_specs=[whole(width // 3), whole(width)],
        out_shape=[
            jax.ShapeDtypeStruct((PIECES, MICRO, rows, width // 3), bf16),
            jax.ShapeDtypeStruct((PIECES, MICRO, rows, width), bf16),
        ],
        compiler_params=params(1),
        name="attention_forward",
    )(qkv, *tables)


def attention_backward(low, d_mix, tables):
    rows, width = low.shape[2], low.shape[3]

    def whole(cols):
        return pl.BlockSpec((PIECES, 1, rows, cols), lambda m: (0, m, 0, 0))

    return pl.pallas_call(
        attn_bwd_kernel,
        grid=(MICRO,),
        in_specs=[whole(width), whole(width // 3)] + attention_specs(rows, PIECES * rows),
        out_specs=whole(width),
        out_shape=jax.ShapeDtypeStruct((PIECES, MICRO, rows, width), bf16),
        compiler_params=params(1),
        name="attention_backward",
    )(low, d_mix, *tables)


class Links:
    def __init__(self, mesh):
        self.dp = mesh.shape["dp"]
        self.nz = self.dp // 2
        self.y = lax.axis_index("dp") % 2
        self.z = lax.axis_index("dp") // 2
        self.t = lax.axis_index("tensor")
        self.groups = [[2 * z + y for z in range(self.nz)] for y in range(2)]

    def swap_y(self, v):
        return lax.ppermute(v, "dp", [(i, i ^ 1) for i in range(self.dp)])

    def shift_z(self, v, k):
        n = self.nz
        return lax.ppermute(
            v, "dp", [(2 * z + y, 2 * ((z + k) % n) + y) for z in range(n) for y in range(2)]
        )

    def swap_core(self, v):
        return lax.ppermute(v, "tensor", [(i, i ^ 1) for i in range(PIECES)])

    def swap_x(self, v):
        return lax.ppermute(v, "tensor", [(i, i ^ 2) for i in range(PIECES)])

    def gather_z(self, v):
        return lax.all_gather(v, "dp", axis=0, tiled=True, axis_index_groups=self.groups)

    def scatter_z(self, v):
        return lax.psum_scatter(
            v, "dp", scatter_dimension=0, tiled=True, axis_index_groups=self.groups
        )

    def gather_small(self, v):
        both = self.by_y(v[None], self.swap_y(v)[None])
        if self.nz > 4:
            return jnp.swapaxes(self.gather_z(both[None]), 0, 1)
        came = [both] + [self.shift_z(both, k) for k in range(1, self.nz)]
        ring = jnp.stack([came[k] for k in range(self.nz - 1, -1, -1)] + [
            came[k] for k in range(self.nz - 1, 0, -1)
        ])
        window = lax.dynamic_slice_in_dim(ring, self.nz - 1 - self.z, self.nz, 0)
        return jnp.swapaxes(window, 0, 1)

    def scatter_small(self, v):
        low = v.astype(bf16)
        own = lax.dynamic_index_in_dim(v, self.y, 0, False)
        other = self.swap_y(lax.dynamic_index_in_dim(low, 1 - self.y, 0, False))
        part = own + other.astype(f32)
        if self.nz > 4:
            return self.scatter_z(part.astype(bf16)).reshape(-1).astype(f32)
        total = lax.dynamic_index_in_dim(part, self.z, 0, False)
        part_low = part.astype(bf16)
        for k in range(1, self.nz):
            piece = lax.dynamic_index_in_dim(part_low, (self.z + k) % self.nz, 0, False)
            total = total + self.shift_z(piece, k).astype(f32)
        return total

    def by_y(self, own, other, axis=0):
        return jnp.where(
            self.y == 0,
            jnp.concatenate([own, other], axis),
            jnp.concatenate([other, own], axis),
        )

    def own_first(self, v):
        half = v.shape[1] // 2
        return jnp.where(
            self.y == 0, v, jnp.concatenate([v[:, half:], v[:, :half]], axis=1)
        )

    def gather_rows(self, v):
        x = self.swap_x(v)
        core = self.swap_core(v)
        return jnp.concatenate([v, x, core, self.swap_core(x)], axis=0)

    def scatter_rows(self, part):
        quarter = part.shape[0] // PIECES
        came = self.swap_core(part[2 * quarter :].astype(bf16)).astype(f32)
        x = self.swap_x((part[quarter : 2 * quarter] + came[quarter:]).astype(bf16))
        return part[:quarter] + came[:quarter] + x.astype(f32)

    def sum_rows(self, v):
        low = v.astype(bf16)
        q = low.shape[0] // PIECES
        turned = jnp.concatenate([low[2 * q :], low[: 2 * q]], axis=0)
        low = (low.astype(f32) + self.swap_core(turned).astype(f32)).astype(bf16)
        turned = jnp.concatenate([low[q : 2 * q], low[:q], low[3 * q :], low[2 * q : 3 * q]], axis=0)
        return (low.astype(f32) + self.swap_x(turned).astype(f32)).astype(bf16)

    def gather_weight(self, shard):
        own = self.gather_z(shard)
        return own, self.swap_y(own)

    def scatter_weight(self, own, other):
        came = self.swap_y(other)
        return self.scatter_z((own + came.astype(f32)).astype(bf16)).astype(f32)


def regroup(v, nz, axis):
    shape = v.shape
    u = shape[axis] // (2 * nz)
    v = v.reshape(shape[:axis] + (nz, 2, u) + shape[axis + 1 :])
    return jnp.swapaxes(v, axis, axis + 1).reshape(shape)


def ungroup(v, nz, axis):
    shape = v.shape
    u = shape[axis] // (2 * nz)
    v = v.reshape(shape[:axis] + (2, nz, u) + shape[axis + 1 :])
    return jnp.swapaxes(v, axis, axis + 1).reshape(shape)


def norm_forward(x, gain):
    r = lax.rsqrt(jnp.mean(x * x, axis=1, keepdims=True) + epsilon)
    return (x * r * gain).astype(bf16), r


def norm_backward(x, r, gain, d_n):
    u = x * r
    g = d_n * gain
    d_x = r * (g - u * jnp.mean(g * u, axis=1, keepdims=True))
    return d_x, jnp.sum(d_n * u, axis=0)


def times(x, own, other):
    half = x.shape[1] // 2
    return dot(x[:, :half], own) + dot(x[:, half:], other)


def back_times(d, own, other):
    return jnp.concatenate([dot_nt(d, own), dot_nt(d, other)], axis=1)


def ffn_forward(links, n, w_in, w_out):
    pair = times(n, *w_in)
    units = pair.shape[1] // 2
    gate, up = pair[:, :units], pair[:, units:]
    hid = (gate * jax.nn.sigmoid(gate) * up).astype(bf16)
    return dot(hid, w_out), (n, gate.astype(bf16), up.astype(bf16), hid)


def split_y(links, v):
    half = v.shape[1] // 2
    own = lax.dynamic_slice_in_dim(v, links.y * half, half, 1)
    other = lax.dynamic_slice_in_dim(v, (1 - links.y) * half, half, 1)
    return own, other


def ffn_backward(links, dy, kept, w_in, w_out):
    n, gate, up, hid = kept
    hid_own, hid_other = split_y(links, hid)
    grad_out = links.scatter_weight(dot_tn(hid_own, dy), dot_tn(hid_other, dy, bf16))
    d_hid = dot_nt(dy, w_out)
    gate, up = gate.astype(f32), up.astype(f32)
    sig = jax.nn.sigmoid(gate)
    d_pair = jnp.concatenate(
        [d_hid * up * (sig * (1.0 + gate * (1.0 - sig))), d_hid * (gate * sig)], axis=1
    ).astype(bf16)
    half = n.shape[1] // 2
    grad_in = links.scatter_weight(
        dot_tn(n[:, :half], d_pair), dot_tn(n[:, half:], d_pair, bf16)
    )
    return back_times(d_pair, *w_in), grad_in, grad_out


def per_device(
    mesh,
    hidden_in, out_grad, segment_ids, norm_gains, w_mixer_in, w_xproj, w_dtproj, mixer_params,
    w_mixer_out, w_ffn_a_in, w_ffn_a_out, w_qkv, w_attn_out, w_ffn_b_in, w_ffn_b_out,
):
    links = Links(mesh)
    nz, dp, t = links.nz, links.dp, links.t
    micro, rows, features = hidden_in.shape
    local = micro * rows
    length = PIECES * rows

    small = [norm_gains, w_xproj, w_dtproj, mixer_params]
    gathered = links.gather_small(jnp.concatenate([v.reshape(-1) for v in small]))
    offset = 0
    parts = []
    for v in small:
        parts.append(gathered[:, :, offset : offset + v.size].reshape((2, nz) + v.shape))
        offset += v.size
    gains = jnp.moveaxis(parts[0], 2, 0).reshape(norm_gains.shape[0], features).astype(f32)
    wx = parts[1].reshape(-1, w_xproj.shape[1])
    wdt = jnp.moveaxis(parts[2], 2, 0).reshape(w_dtproj.shape[0], -1)
    table = jnp.moveaxis(parts[3], 2, 0).reshape(mixer_params.shape[0], -1).astype(f32)
    width = table.shape[1]
    par = jnp.concatenate([table[: CONV + 3], jnp.zeros((1, width), f32)], axis=0)
    rate = -jnp.exp(table[CONV + 3 :])

    def in_weight(w, group):
        cols = w.shape[2]
        if group:
            w = regroup(w, nz, 2)
        return links.gather_weight(w.reshape(w.shape[0], w.shape[1] * cols))

    def out_weight(w):
        own, other = links.gather_weight(regroup(w, nz, 1))
        return links.by_y(own, other)

    mixer_in = in_weight(w_mixer_in, True)
    mixer_out = out_weight(w_mixer_out)
    ffn_a_in = in_weight(w_ffn_a_in, True)
    ffn_a_out = out_weight(w_ffn_a_out)
    qkv_in = in_weight(w_qkv, False)
    attn_out = ungroup(out_weight(w_attn_out), nz, 0)
    attn_out = attn_out.reshape(-1, features)
    ffn_b_in = in_weight(w_ffn_b_in, True)
    ffn_b_out = out_weight(w_ffn_b_out)

    seg = segment_ids.reshape(micro, length)
    masks = []
    for k in range(CONV):
        earlier = jnp.pad(seg, ((0, 0), (k, 0)), constant_values=-1)[:, :length]
        masks.append((earlier == seg).astype(f32))
    masks = jnp.stack(masks, axis=-1).reshape(micro, PIECES, rows, CONV)
    keep = masks[..., 1:2]
    slots = jnp.stack([sum(i * (ORDER[i] == (j ^ t)) for i in range(PIECES)) for j in range(PIECES)])
    slots = slots.astype(jnp.int32)
    seg_pieces = seg.reshape(micro, PIECES, rows)
    seg_rel = jnp.stack(
        [lax.dynamic_index_in_dim(seg_pieces, t ^ k, 1, False) for k in ORDER]
    )
    position = jnp.concatenate([(t ^ k) * rows + lax.iota(jnp.int32, rows) for k in ORDER])
    half = HEAD // 2
    frequency = jnp.exp(lax.iota(f32, half) * (-2.0 * math.log(10000.0) / HEAD))
    angles = position.astype(f32)[:, None] * frequency[None, :]
    cos, sin = jnp.cos(angles), jnp.sin(angles)
    tables = (
        jnp.concatenate([cos, cos], axis=1).reshape(PIECES, rows, HEAD),
        jnp.concatenate([-sin, sin], axis=1).reshape(PIECES, rows, HEAD),
        seg_rel[..., None],
        jnp.swapaxes(seg_rel, 0, 1).reshape(micro, 1, length),
        position[:, None],
        position[None, :],
    )

    def pieces(v):
        return v.reshape(PIECES, micro, rows, v.shape[-1])

    def flat(v):
        return v.reshape(PIECES * local, v.shape[-1])

    def enter(x, i):
        n, r = norm_forward(x, gains[i : i + 1])
        return links.gather_rows(links.own_first(n)), r

    x0 = regroup(hidden_in.reshape(local, features), nz, 1).astype(f32)
    n1, r1 = enter(x0, 0)
    pre = pieces(times(n1, *mixer_in))
    values, ext_part = conv_forward(slots, pre, masks, par, wx)
    ext = pieces(links.sum_rows(flat(ext_part)))
    gated, scanned, states = scan_forward(slots, ext, wdt, values, pre, par, rate, keep)
    x1 = x0 + links.scatter_rows(dot(flat(gated), mixer_out))

    n2, r2 = enter(x1, 1)
    y_a, kept_a = ffn_forward(links, n2, ffn_a_in, ffn_a_out)
    x2 = x1 + links.scatter_rows(y_a)

    n3, r3 = enter(x2, 2)
    mix, low = attention_forward(pieces(times(n3, *qkv_in)), tables)
    x3 = x2 + links.scatter_rows(dot(flat(mix), attn_out))

    n4, r4 = enter(x3, 3)
    y_b, kept_b = ffn_forward(links, n4, ffn_b_in, ffn_b_out)
    x4 = x3 + links.scatter_rows(y_b)
    block_out = ungroup(x4, nz, 1).astype(bf16).reshape(hidden_in.shape)

    def leave(g, x, r, i, d_normed):
        d_n = links.own_first(links.scatter_rows(d_normed))
        d_x, d_gain = norm_backward(x, r, gains[i : i + 1], d_n)
        return g + d_x, d_gain

    g4_low = regroup(out_grad.reshape(local, features), nz, 1)
    g4 = g4_low.astype(f32)
    d_n4, grad_b_in, grad_b_out = ffn_backward(
        links, links.gather_rows(g4_low), kept_b, ffn_b_in, ffn_b_out
    )
    g3, gain_d = leave(g4, x3, r4, 3, d_n4)

    dy3 = links.gather_rows(g3.astype(bf16))
    mix_rows = regroup(flat(mix), nz, 1)
    mix_own, mix_other = split_y(links, mix_rows)
    grad_attn_out = links.scatter_weight(dot_tn(mix_own, dy3), dot_tn(mix_other, dy3, bf16))
    d_mix = dot_nt(dy3, attn_out).astype(bf16)
    d_qkv = flat(attention_backward(low, pieces(d_mix), tables))
    fh = features // 2
    grad_qkv = links.scatter_weight(
        dot_tn(n3[:, :fh], d_qkv), dot_tn(n3[:, fh:], d_qkv, bf16)
    )
    g2, gain_c = leave(g3, x2, r3, 2, back_times(d_qkv, *qkv_in))

    dy2 = links.gather_rows(g2.astype(bf16))
    d_n2, grad_a_in, grad_a_out = ffn_backward(links, dy2, kept_a, ffn_a_in, ffn_a_out)
    g1, gain_b = leave(g2, x1, r2, 1, d_n2)

    dy1 = links.gather_rows(g1.astype(bf16))
    gated = flat(gated)
    gated_own, gated_other = split_y(links, gated)
    grad_mixer_out = links.scatter_weight(
        dot_tn(gated_own, dy1), dot_tn(gated_other, dy1, bf16)
    )
    d_gated = pieces(dot_nt(dy1, mixer_out))
    d_dt, d_val, d_z, d_bc, d_rate, sums = scan_backward(
        slots, ext, wdt, values, pre, par, rate, keep, d_gated, scanned, states
    )
    d_dt = flat(d_dt)
    d_bc = d_bc[:, :, :, 0, :].reshape(PIECES, micro, 2, rows, STATE)
    d_bc = jnp.swapaxes(d_bc, 2, 3).reshape(PIECES * local, 2 * STATE)
    d_ext = links.sum_rows(jnp.concatenate([dot_nt(d_dt, wdt), d_bc], axis=1))
    grad_dt = dot_tn(flat(ext)[:, :RANK], d_dt)
    grad_x = dot_tn(flat(values), d_ext)
    d_x, conv_sums = conv_backward(slots, pieces(d_ext), d_val, pre, masks, par, wx)
    d_pre = jnp.concatenate([flat(d_x), flat(d_z)], axis=1)
    grad_mixer_in = links.scatter_weight(
        dot_tn(n1[:, :fh], d_pre), dot_tn(n1[:, fh:], d_pre, bf16)
    )
    g0, gain_a = leave(g1, x0, r1, 0, back_times(d_pre, *mixer_in))
    input_grad = ungroup(g0, nz, 1).astype(bf16).reshape(hidden_in.shape)

    grad_table = jnp.concatenate([conv_sums[: CONV + 1], sums[:2], d_rate * rate], axis=0)
    grad_gains = jnp.stack([gain_a, gain_b, gain_c, gain_d])

    def by_owner(v, axis):
        u = v.shape[axis] // dp
        v = v.reshape(v.shape[:axis] + (2, nz, u) + v.shape[axis + 1 :])
        return jnp.moveaxis(v, (axis, axis + 1), (0, 1)).reshape(2, nz, -1)

    packed = jnp.concatenate(
        [by_owner(grad_gains, 1), by_owner(grad_x, 0), by_owner(grad_dt, 1), by_owner(grad_table, 1)],
        axis=2,
    )
    summed = links.scatter_small(packed)
    offset = 0
    outs = []
    for v in small:
        outs.append(summed[offset : offset + v.size].reshape(v.shape))
        offset += v.size
    gain_total = outs[0]
    gain_total = gain_total + links.swap_core(gain_total)
    gain_total = gain_total + links.swap_x(gain_total)

    def in_grad(v, like, group):
        v = v.reshape(like.shape)
        return ungroup(v, nz, 2) if group else v

    def out_grad_of(v):
        return ungroup(v, nz, 1)

    return (
        block_out,
        input_grad,
        gain_total,
        in_grad(grad_mixer_in, w_mixer_in, True),
        outs[1],
        outs[2],
        outs[3],
        out_grad_of(grad_mixer_out),
        in_grad(grad_a_in, w_ffn_a_in, True),
        out_grad_of(grad_a_out),
        in_grad(grad_qkv, w_qkv, False),
        out_grad_of(grad_attn_out),
        in_grad(grad_b_in, w_ffn_b_in, True),
        out_grad_of(grad_b_out),
    )


def solution(mesh):
    def body(*args):
        return per_device(mesh, *args)

    rows = P(None, ("dp", "tensor"), None)
    weight_in = P("dp", None, "tensor")
    weight_out = P(("tensor", "dp"), None)
    columns = P(None, ("tensor", "dp"))
    gains = P(None, "dp")
    weights = (
        gains, weight_in, weight_out, columns, columns, weight_out, weight_in, weight_out,
        weight_in, weight_out, weight_in, weight_out,
    )
    return jax.shard_map(
        body,
        mesh=mesh,
        in_specs=(rows, rows, P(None, "dp")) + weights,
        out_specs=(rows, rows) + weights,
        check_vma=False,
    )
```

time: 3620 us -> 1080 us (0.30)
  waiting for transfers between devices: 2330 us -> 560 us
  local copies, waits for them, and re-layouts: 440 us -> 120 us
  other arithmetic: 340 us -> 57.8 us
  blocking collectives: 268 us -> 16 us
  starting transfers between devices: 2.3 us -> 95.4 us
  Pallas kernels: 0 us -> 76.4 us
  matrix products: 183 us -> 127 us
    unnamed x42 -> x15, waiting for transfers between devices: 1120 us -> 0.25 us
    reduce_scatter x22 -> x8, waiting for transfers between devices: 858 us -> 16.5 us  [scatter_z(): lax.psum_scatter(v, 'dp', scatter_dimension=0, tiled=True, axis_index_gro...]
    ppermute x0 -> x70, waiting for transfers between devices: none -> 472 us  [the longest x18 363 us: swap_y(): return lax.ppermute(v, 'dp', [(i, i ^ 1) for i in range(self.dp)])]
    all_gather x8 -> x7, waiting for transfers between devices: 327 us -> 70.9 us  [gather_z(): lax.all_gather(v, 'dp', axis=0, tiled=True, axis_index_groups=self.groups)]
    all_gather x20 -> x1, blocking collectives: 260 us -> 16 us  [gather_z(): lax.all_gather(v, 'dp', axis=0, tiled=True, axis_index_groups=self.groups)]
    reduce_sum x193 -> x8, other arithmetic: 151 us -> 9.14 us  [the longest x4 5.4 us: norm_forward(): r = lax.rsqrt(jnp.mean(x * x, axis=1, keepdims=True) + epsilon)]
    squeeze x98 -> x1, local copies, waits for them, and re-layouts: 102 us -> 0.08 us  [scatter_small(): other = self.swap_y(lax.dynamic_index_in_dim(low, 1 - self.y, 0, False))]
    ppermute x0 -> x70, starting transfers between devices: none -> 93.3 us  [the longest x27 51.8 us: swap_core(): return lax.ppermute(v, 'tensor', [(i, i ^ 1) for i in range(PIECES)])]
  transfers between devices with their start and end apart: 37 -> 85, of which waited for: 31 -> 45; matrix products, arithmetic and copies ran while one was open for 14% -> 24% of each run, Pallas kernels for 0% -> 7%
where the time goes in v1:
time: 1080 us; the launch traced here: 1070 us
  waiting for transfers between devices  560 us (52%)
  matrix products  127 us (12%)
  local copies, waits for them, and re-layouts  120 us (11%)
  starting transfers between devices  95.4 us (9%)
  Pallas kernels  76.4 us (7%)
  other arithmetic  57.8 us (5%)
  between operations  17.3 us (2%)
  blocking collectives  16 us (1%)
    ppermute x18, waiting for transfers between devices, swap_y(): return lax.ppermute(v, 'dp', [(i, i ^ 1) for i in range(self.dp)])  363 us
    dot_general x43, matrix products, dot(): return lax.dot_general(a, b, (dims, ((), ())), preferred_element_type=out)  127 us
    ppermute x19, waiting for transfers between devices, swap_x(): return lax.ppermute(v, 'tensor', [(i, i ^ 2) for i in range(PIECES)])  79.9 us
    all_gather x7, waiting for transfers between devices, gather_z(): lax.all_gather(v, 'dp', axis=0, tiled=True, axis_index_groups=self.groups)  70.9 us
    ppermute x27, starting transfers between devices, swap_core(): return lax.ppermute(v, 'tensor', [(i, i ^ 1) for i in range(PIECES)])  51.8 us
    pallas_call x1, Pallas kernels, scan_backward(): pl.pallas_call(scan_bwd_kernel, grid_spec=grid, out_shape=[jax.ShapeDtype...  36.8 us
    unnamed x381, local copies, waits for them, and re-layouts  28.4 us
    reshape x19, local copies, waits for them, and re-layouts, ungroup(): return jnp.swapaxes(v, axis, axis + 1).reshape(shape)  28 us
  transfers between devices with their start and end apart: 85, of which 45 were waited for; matrix products, arithmetic and copies ran while one was open for 24% of the time, Pallas kernels for 7%

profile of v1, /device:TPU:9, one launch (start us, length us, event | category | flops | bytes accessed | tf_op | source)
XLA Modules:
  0.0 1070.3 jit_solution(3064176456929397013)
XLA Ops:
  7.2 3.5 reshape.514
  27.4 5.1 collective-permute-done.2
  32.7 8.1 collective-permute-done.3
  44.2 25.2 %all-gather.8.cloned.1.call-done = bf16[768,1536]{1,0:T(8,128)(2,1)} async-done(((bf16[192,1536]{1,0:T(8,128)(2,1)}), bf16[768,1536]{1,0:T(8,128)(2,1)}) %all-gather.8.cloned.1.call-update) | async-done | bytes 2359312 | tf_op jit(solution)/shard_map/all_gather | solution.py:526
  75.8 5.4 collective-permute-done.4
  86.2 17.2 %all-gather.10.cloned.1.call-done = bf16[384,1536]{1,0:T(8,128)(2,1)} async-done(((bf16[96,1536]{1,0:T(8,128)(2,1)}), bf16[384,1536]{1,0:T(8,128)(2,1)}) %all-gather.10.cloned.1.call-update) | async-done | bytes 1179664 | tf_op jit(solution)/shard_map/all_gather | solution.py:526
  104.6 17.5 %collective-permute-done.7 = bf16[768,1536]{1,0:T(8,128)(2,1)} collective-permute-done((bf16[768,1536]{1,0:T(8,128)(2,1)}, bf16[768,1536]{1,0:T(8,128)(2,1)}, u32[]{:S(2)}, u32[]{:S(2)}) %collective-permute-start.7) | collective-permute-done | bytes 2359328 | tf_op jit(solution)/shard_map/ppermute | solution.py:511
  127.8 3.8 conv_forward.1
  148.1 23.2 %scan_forward.1 = (bf16[4,2,64,768]{3,2,1,0:T(8,128)(2,1)S(1)}, f32[4,2,64,768]{3,2,1,0:T(8,128)S(1)}, bf16[8,64,16,768]{3,2,1,0:T(8,128)(2,1)}) custom-call(s32[4]{0:T(128)S(1)} %copy-done.30, bf16[4,2,64,128]{3,2,1,0:T(8,128)(2,1)S(1)} %bitcast.184, bf16[96,768]{1,0:T(8,128)(2,1)S(1)} %reshape.519.wdt_ref, bf16[4,2,64,768]{3,2,1,0:T(8,128)(2,1)S(1)} %copy-done.3, ...), custom_call_target="tpu_custom_call" | custom-call | tf_op jit(solution)/shard_map/scan_forward/pallas_call | solution.py:392
  171.4 3.9 fusion.95
  185.1 5.3 collective-permute-done.12
  195.5 6.8 collective-permute-done.13
  205.2 15.1 %all-gather.14.cloned.1.call-done = bf16[512,1536]{0,1:T(8,128)(2,1)} async-done(((bf16[128,1536]{0,1:T(8,128)(2,1)}), bf16[512,1536]{0,1:T(8,128)(2,1)}) %all-gather.14.cloned.1.call-update) | async-done | bytes 1572880 | tf_op jit(solution)/shard_map/all_gather | solution.py:526
  221.1 29.6 %collective-permute-done.16 = bf16[768,2048]{1,0:T(8,128)(2,1)} collective-permute-done((bf16[768,2048]{1,0:T(8,128)(2,1)}, bf16[768,2048]{1,0:T(8,128)(2,1)}, u32[]{:S(2)}, u32[]{:S(2)}) %collective-permute-start.16) | collective-permute-done | bytes 3145760 | tf_op jit(solution)/shard_map/ppermute | solution.py:511
  250.7 3.7 fusion.74
  258.3 26.1 %collective-permute-done.17 = bf16[512,1536]{0,1:T(8,128)(2,1)S(1)} collective-permute-done((bf16[512,1536]{0,1:T(8,128)(2,1)}, bf16[512,1536]{0,1:T(8,128)(2,1)S(1)}, u32[]{:S(2)}, u32[]{:S(2)}) %collective-permute-start.17) | collective-permute-done | bytes 1572896 | tf_op jit(solution)/shard_map/ppermute | solution.py:511
  291.2 16.0 %all_gather.29 = bf16[192,1536]{1,0:T(8,128)(2,1)} all-gather(bf16[48,1536]{1,0:T(8,128)(2,1)S(1)} %reshape.532), channel_id=1, replica_groups={{0,8,16,24},{4,12,20,28},{1,9,17,25},{5,13,21,29},{2,10,18,26},{6,14,22..., dimensions={0}, use_global_device_ids=true | all-gather | bytes 737280 | tf_op jit(solution)/shard_map/all_gather | solution.py:526
  319.5 4.7 collective-permute-done.19
  328.1 4.1 collective-permute-start.21
  333.9 4.5 collective-permute-start.22
  342.6 15.1 %collective-permute-done.23 = bf16[768,1152]{1,0:T(8,128)(2,1)} collective-permute-done((bf16[768,1152]{1,0:T(8,128)(2,1)}, bf16[768,1152]{1,0:T(8,128)(2,1)}, u32[]{:S(2)}, u32[]{:S(2)}) %collective-permute-start.23) | collective-permute-done | bytes 1769504 | tf_op jit(solution)/shard_map/ppermute | solution.py:511
  365.6 3.6 collective-permute-start.25
  378.6 5.3 collective-permute-done.26
  397.4 4.0 collective-permute-start.29
  401.5 13.4 %all-gather.20.cloned.1.call-done = bf16[512,1536]{0,1:T(8,128)(2,1)} async-done(((bf16[128,1536]{0,1:T(8,128)(2,1)}), bf16[512,1536]{0,1:T(8,128)(2,1)}) %all-gather.20.cloned.1.call-update) | async-done | bytes 1572880 | tf_op jit(solution)/shard_map/all_gather | solution.py:526
  418.2 25.1 %collective-permute-done.30 = bf16[768,2048]{1,0:T(8,128)(2,1)} collective-permute-done((bf16[768,2048]{1,0:T(8,128)(2,1)}, bf16[768,2048]{1,0:T(8,128)(2,1)}, u32[]{:S(2)}, u32[]{:S(2)}) %collective-permute-start.30) | collective-permute-done | bytes 3145760 | tf_op jit(solution)/shard_map/ppermute | solution.py:511
  443.3 3.7 fusion.62
  449.1 27.9 %collective-permute-done.31 = bf16[512,1536]{0,1:T(8,128)(2,1)S(1)} collective-permute-done((bf16[512,1536]{0,1:T(8,128)(2,1)}, bf16[512,1536]{0,1:T(8,128)(2,1)S(1)}, u32[]{:S(2)}, u32[]{:S(2)}) %collective-permute-start.31) | collective-permute-done | bytes 1572896 | tf_op jit(solution)/shard_map/ppermute | solution.py:511
  476.9 5.4 fusion.11
  484.2 4.3 fusion.129
  496.2 8.0 collective-permute-done.38
  510.0 7.6 collective-permute-done.39
  531.0 3.5 fusion.88
  537.6 4.0 attention_backward.1
  553.4 22.1 %collective-permute-done.69 = bf16[512,1536]{1,0:T(8,128)(2,1)} collective-permute-done((bf16[512,1536]{1,0:T(8,128)(2,1)}, bf16[512,1536]{1,0:T(8,128)(2,1)}, u32[]{:S(2)}, u32[]{:S(2)}) %collective-permute-start.69) | collective-permute-done | bytes 1572896 | tf_op jit(solution)/shard_map/ppermute | solution.py:511
  575.5 3.8 fusion.2
  588.2 6.2 collective-permute-done.43
  596.8 25.0 %collective-permute-done.66 = bf16[768,1152]{1,0:T(8,128)(2,1)S(1)} collective-permute-done((bf16[768,1152]{1,0:T(8,128)(2,1)S(1)}, bf16[768,1152]{1,0:T(8,128)(2,1)S(1)}, u32[]{:S(2)}, u32[]{:S(2)}) %collective-permute-start.66) | collective-permute-done | bytes 1769504 | tf_op jit(solution)/shard_map/ppermute | solution.py:511
  625.5 3.5 fusion.134
  631.8 6.4 collective-permute-done.44
  643.8 3.5 fusion.60
  648.0 30.7 %collective-permute-done.65 = bf16[512,1536]{1,0:T(8,128)(2,1)S(1)} collective-permute-done((bf16[512,1536]{1,0:T(8,128)(2,1)S(1)}, bf16[512,1536]{1,0:T(8,128)(2,1)S(1)}, u32[]{:S(2)}, u32[]{:S(2)}) %collective-permute-start.65) | collective-permute-done | bytes 1572896 | tf_op jit(solution)/shard_map/ppermute | solution.py:511
  681.2 6.8 fusion.20
  689.9 3.8 fusion.127
  697.8 48.4 %collective-permute-done.68 = bf16[768,2048]{1,0:T(8,128)(2,1)} collective-permute-done((bf16[768,2048]{1,0:T(8,128)(2,1)}, bf16[768,2048]{1,0:T(8,128)(2,1)}, u32[]{:S(2)}, u32[]{:S(2)}) %collective-permute-start.68) | collective-permute-done | bytes 3145760 | tf_op jit(solution)/shard_map/ppermute | solution.py:511
  746.2 5.4 add_convert_fusion
  754.2 8.8 collective-permute-done.48
  768.5 5.7 collective-permute-done.49
  778.5 4.4 fusion.94
  782.9 36.8 %scan_backward.1 = (bf16[4,2,64,768]{3,2,1,0:T(8,128)(2,1)S(1)}, f32[4,2,64,768]{3,2,1,0:T(8,128)S(1)}, bf16[4,2,64,768]{3,2,1,0:T(8,128)(2,1)S(1)}, f32[4,2,2,8...) custom-call(s32[4]{0:T(128)S(1)} %copy-done.31, bf16[4,2,64,128]{3,2,1,0:T(8,128)(2,1)S(1)} %bitcast.185, ...), custom_call_target="tpu_custom_call" | custom-call | tf_op jit(solution)/shard_map/scan_backward/pallas_call | solution.py:437
  823.8 3.4 fusion.96
  829.3 3.6 collective-permute-done.53
  838.5 5.7 conv_backward.1
  847.9 7.1 collective-permute-done.63
  855.1 3.3 fusion.3
  858.5 47.1 %collective-permute-done.62 = bf16[768,1536]{1,0:T(8,128)(2,1)} collective-permute-done((bf16[768,1536]{1,0:T(8,128)(2,1)}, bf16[768,1536]{1,0:T(8,128)(2,1)}, u32[]{:S(2)}, u32[]{:S(2)}) %collective-permute-start.62) | collective-permute-done | bytes 2359328 | tf_op jit(solution)/shard_map/ppermute | solution.py:511
  905.6 4.8 add_convert_fusion.2
  911.8 5.2 fusion.72
  948.9 37.2 %collective-permute-done.64 = bf16[768,2048]{1,0:T(8,128)(2,1)} collective-permute-done((bf16[768,2048]{1,0:T(8,128)(2,1)}, bf16[768,2048]{1,0:T(8,128)(2,1)}, u32[]{:S(2)}, u32[]{:S(2)}) %collective-permute-start.64) | collective-permute-done | bytes 3145760 | tf_op jit(solution)/shard_map/ppermute | solution.py:511
  986.1 5.5 add_convert_fusion.1
  997.2 4.2 collective-permute-done.56
  1006.9 3.5 collective-permute-done.58
  1010.4 3.4 collective-permute-done.57
  1040.8 16.4 %reduce-scatter.13.cloned.1.call-done = bf16[192,2048]{1,0:T(8,128)(2,1)} async-done(((bf16[768,2048]{1,0:T(8,128)(2,1)}), bf16[192,2048]{1,0:T(8,128)(2,1)}) %reduce-scatter.13.cloned.1.call-update) | async-done | bytes 786448 | tf_op jit(solution)/shard_map/reduce_scatter | solution.py:529
  (793 shorter events, 321.5 us)
Async XLA Ops:
  7.2 62.2 %all-gather.8.cloned.1.call-start = ((), (), s32[]{:S(2)}) async-start(), calls=%async_computation.8 | async-start | bytes 2949120 | tf_op jit(solution)/shard_map/all_gather | solution.py:526
  12.8 90.6 %all-gather.10.cloned.1.call-start = ((), (), s32[]{:S(2)}) async-start(), calls=%async_computation.9 | async-start | bytes 1474560 | tf_op jit(solution)/shard_map/all_gather | solution.py:526
  14.5 166.9 %all-gather.12.cloned.1.call-start = ((), (), s32[]{:S(2)}) async-start(), calls=%async_computation.10 | async-start | bytes 3932160 | tf_op jit(solution)/shard_map/all_gather | solution.py:526
  18.5 201.8 %all-gather.14.cloned.1.call-start = ((), (), s32[]{:S(2)}) async-start(), calls=%async_computation.11 | async-start | bytes 1966080 | tf_op jit(solution)/shard_map/all_gather | solution.py:526
  21.6 10.9 %collective-permute-start.2 = (bf16[2,24480]{1,0:T(2,128)(2,1)S(1)}, bf16[2,24480]{1,0:T(2,128)(2,1)S(1)}, u32[]{:S(2)}, u32[]{:S(2)}) collective-permute-start(bf16[2,24480]{1,0:T(2,128)(2,1)S(1)} %broadcast_select_fusion.1), channel_id=1, source_target_pairs={{0,16},{4,20},{8,24},{12,28},{16,0},{20,4},{24,8},{28,12},{1,17},{... | collective-permute-start | bytes 293768 | tf_op jit(solution)/shard_map/ppermute | solution.py:515
  23.9 16.8 %collective-permute-start.3 = (bf16[2,24480]{1,0:T(2,128)(2,1)S(1)}, bf16[2,24480]{1,0:T(2,128)(2,1)S(1)}, u32[]{:S(2)}, u32[]{:S(2)}) collective-permute-start(bf16[2,24480]{1,0:T(2,128)(2,1)S(1)} %broadcast_select_fusion.1), channel_id=1, source_target_pairs={{0,8},{4,12},{8,16},{12,20},{16,24},{20,28},{24,0},{28,4},{1,9},{5... | collective-permute-start | bytes 293768 | tf_op jit(solution)/shard_map/ppermute | solution.py:515
  69.4 52.7 %collective-permute-start.7 = (bf16[768,1536]{1,0:T(8,128)(2,1)}, bf16[768,1536]{1,0:T(8,128)(2,1)}, u32[]{:S(2)}, u32[]{:S(2)}) collective-permute-start(bf16[768,1536]{1,0:T(8,128)(2,1)} %all-gather.8.cloned.1.call-done), channel_id=1, source_target_pairs={{0,4},{4,0},{8,12},{12,8},{16,20},{20,16},{24,28},{28,24},{1,5},{5... | collective-permute-start | bytes 7077896 | tf_op jit(solution)/shard_map/ppermute | solution.py:511
  71.1 10.1 collective-permute-start.4
  74.8 10.3 collective-permute-start.5
  103.4 68.0 %collective-permute-start.10 = (bf16[384,1536]{1,0:T(8,128)(2,1)}, bf16[384,1536]{1,0:T(8,128)(2,1)}, u32[]{:S(2)}, u32[]{:S(2)}) collective-permute-start(bf16[384,1536]{1,0:T(8,128)(2,1)} %all-gather.10.cloned.1.call-done), channel_id=1, source_target_pairs={{0,4},{4,0},{8,12},{12,8},{16,20},{20,16},{24,28},{28,24},{1,5},{5... | collective-permute-start | bytes 3538952 | tf_op jit(solution)/shard_map/ppermute | solution.py:511
  179.9 10.5 collective-permute-start.12
  181.4 69.3 %collective-permute-start.16 = (bf16[768,2048]{1,0:T(8,128)(2,1)}, bf16[768,2048]{1,0:T(8,128)(2,1)}, u32[]{:S(2)}, u32[]{:S(2)}) collective-permute-start(bf16[768,2048]{1,0:T(8,128)(2,1)} %all-gather.12.cloned.1.call-done), channel_id=1, source_target_pairs={{0,4},{4,0},{8,12},{12,8},{16,20},{20,16},{24,28},{28,24},{1,5},{5... | collective-permute-start | bytes 9437192 | tf_op jit(solution)/shard_map/ppermute | solution.py:511
  183.7 135.8 %all-gather.16.cloned.1.call-start = ((), (), s32[]{:S(2)}) async-start(), calls=%async_computation.12 | async-start | bytes 2211840 | tf_op jit(solution)/shard_map/all_gather | solution.py:526
  192.5 9.7 collective-permute-start.13
  194.1 26.9 %collective-permute-start.14 = (bf16[128,1536]{1,0:T(8,128)(2,1)S(1)}, bf16[128,1536]{1,0:T(8,128)(2,1)S(1)}, u32[]{:S(2)}, u32[]{:S(2)}) collective-permute-start(bf16[128,1536]{1,0:T(8,128)(2,1)S(1)} %maximum_select_fusion.15), channel_id=1, source_target_pairs={{0,1},{1,0},{2,3},{3,2},{4,5},{5,4},{6,7},{7,6},{8,9},{9,8},{10,11... | collective-permute-start | bytes 1179656 | tf_op jit(solution)/shard_map/ppermute | solution.py:520
  202.2 18.8 %collective-permute-start.15 = (bf16[128,1536]{1,0:T(8,128)(2,1)S(1)}, bf16[128,1536]{1,0:T(8,128)(2,1)S(1)}, u32[]{:S(2)}, u32[]{:S(2)}) collective-permute-start(bf16[128,1536]{1,0:T(8,128)(2,1)S(1)} %collective-permute-done.13), channel_id=1, source_target_pairs={{0,1},{1,0},{2,3},{3,2},{4,5},{5,4},{6,7},{7,6},{8,9},{9,8},{10,11... | collective-permute-start | bytes 1179656 | tf_op jit(solution)/shard_map/ppermute | solution.py:520
  205.0 169.1 %all-gather.18.cloned.1.call-start = ((), (), s32[]{:S(2)}) async-start(), calls=%async_computation.13 | async-start | bytes 3932160 | tf_op jit(solution)/shard_map/all_gather | solution.py:526
  220.3 64.0 %collective-permute-start.17 = (bf16[512,1536]{0,1:T(8,128)(2,1)}, bf16[512,1536]{0,1:T(8,128)(2,1)S(1)}, u32[]{:S(2)}, u32[]{:S(2)}) collective-permute-start(bf16[512,1536]{0,1:T(8,128)(2,1)} %all-gather.14.cloned.1.call-done), channel_id=1, source_target_pairs={{0,4},{4,0},{8,12},{12,8},{16,20},{20,16},{24,28},{28,24},{1,5},{5... | collective-permute-start | bytes 4718600 | tf_op jit(solution)/shard_map/ppermute | solution.py:511
  289.1 23.7 %collective-permute-start.18 = (bf16[256,1536]{1,0:T(8,128)(2,1)}, bf16[256,1536]{1,0:T(8,128)(2,1)}, u32[]{:S(2)}, u32[]{:S(2)}) collective-permute-start(bf16[256,1536]{1,0:T(8,128)(2,1)} %slice.783), channel_id=1, source_target_pairs={{0,1},{1,0},{2,3},{3,2},{4,5},{5,4},{6,7},{7,6},{8,9},{9,8},{10,11... | collective-permute-start | bytes 2359304 | tf_op jit(solution)/shard_map/ppermute | solution.py:520
  307.2 31.8 %collective-permute-start.24 = (bf16[192,1536]{1,0:T(8,128)(2,1)}, bf16[192,1536]{1,0:T(8,128)(2,1)}, u32[]{:S(2)}, u32[]{:S(2)}) collective-permute-start(bf16[192,1536]{1,0:T(8,128)(2,1)} %all_gather.29), channel_id=1, source_target_pairs={{0,4},{4,0},{8,12},{12,8},{16,20},{20,16},{24,28},{28,24},{1,5},{5... | collective-permute-start | bytes 1769480 | tf_op jit(solution)/shard_map/ppermute | solution.py:511
  310.8 104.1 %all-gather.20.cloned.1.call-start = ((), (), s32[]{:S(2)}) async-start(), calls=%async_computation.14 | async-start | bytes 1966080 | tf_op jit(solution)/shard_map/all_gather | solution.py:526
  319.5 38.2 %collective-permute-start.23 = (bf16[768,1152]{1,0:T(8,128)(2,1)}, bf16[768,1152]{1,0:T(8,128)(2,1)}, u32[]{:S(2)}, u32[]{:S(2)}) collective-permute-start(bf16[768,1152]{1,0:T(8,128)(2,1)} %all-gather.16.cloned.1.call-done), channel_id=1, source_target_pairs={{0,4},{4,0},{8,12},{12,8},{16,20},{20,16},{24,28},{28,24},{1,5},{5... | collective-permute-start | bytes 5308424 | tf_op jit(solution)/shard_map/ppermute | solution.py:511
  328.1 13.1 %collective-permute-start.21 = (bf16[128,1536]{1,0:T(8,128)(2,1)S(1)}, bf16[128,1536]{1,0:T(8,128)(2,1)S(1)}, u32[]{:S(2)}, u32[]{:S(2)}) collective-permute-start(bf16[128,1536]{1,0:T(8,128)(2,1)S(1)} %maximum_select_fusion.16), channel_id=1, source_target_pairs={{0,1},{1,0},{2,3},{3,2},{4,5},{5,4},{6,7},{7,6},{8,9},{9,8},{10,11... | collective-permute-start | bytes 1179656 | tf_op jit(solution)/shard_map/ppermute | solution.py:520
  373.2 10.6 collective-permute-start.26
  374.0 69.3 %collective-permute-start.30 = (bf16[768,2048]{1,0:T(8,128)(2,1)}, bf16[768,2048]{1,0:T(8,128)(2,1)}, u32[]{:S(2)}, u32[]{:S(2)}) collective-permute-start(bf16[768,2048]{1,0:T(8,128)(2,1)} %all-gather.18.cloned.1.call-done), channel_id=1, source_target_pairs={{0,4},{4,0},{8,12},{12,8},{16,20},{20,16},{24,28},{28,24},{1,5},{5... | collective-permute-start | bytes 9437192 | tf_op jit(solution)/shard_map/ppermute | solution.py:511
  378.4 550.3 %reduce-scatter.19.cloned.1.call-start = ((), (), s32[]{:S(2)}) async-start(), calls=%async_computation.20 | async-start | bytes 737280 | tf_op jit(solution)/shard_map/reduce_scatter | solution.py:529
  387.8 9.6 collective-permute-start.27
  393.1 22.4 %collective-permute-start.34 = (bf16[128,1536]{0,1:T(8,128)(2,1)}, bf16[128,1536]{0,1:T(8,128)(2,1)}, u32[]{:S(2)}, u32[]{:S(2)}) collective-permute-start(bf16[128,1536]{0,1:T(8,128)(2,1)} %bitcast.228), channel_id=1, source_target_pairs={{0,2},{1,3},{2,0},{3,1},{4,6},{5,7},{6,4},{7,5},{8,10},{9,11},{10,... | collective-permute-start | bytes 1179656 | tf_op jit(solution)/shard_map/ppermute | solution.py:523
  393.8 22.9 %collective-permute-start.28 = (bf16[128,1536]{1,0:T(8,128)(2,1)}, bf16[128,1536]{1,0:T(8,128)(2,1)}, u32[]{:S(2)}, u32[]{:S(2)}) collective-permute-start(bf16[128,1536]{1,0:T(8,128)(2,1)} %maximum_select_fusion.17), channel_id=1, source_target_pairs={{0,1},{1,0},{2,3},{3,2},{4,5},{5,4},{6,7},{7,6},{8,9},{9,8},{10,11... | collective-permute-start | bytes 1179656 | tf_op jit(solution)/shard_map/ppermute | solution.py:520
  397.4 19.3 %collective-permute-start.29 = (bf16[128,1536]{1,0:T(8,128)(2,1)}, bf16[128,1536]{1,0:T(8,128)(2,1)}, u32[]{:S(2)}, u32[]{:S(2)}) collective-permute-start(bf16[128,1536]{1,0:T(8,128)(2,1)} %collective-permute-done.27), channel_id=1, source_target_pairs={{0,1},{1,0},{2,3},{3,2},{4,5},{5,4},{6,7},{7,6},{8,9},{9,8},{10,11... | collective-permute-start | bytes 1179656 | tf_op jit(solution)/shard_map/ppermute | solution.py:520
  414.8 62.1 %collective-permute-start.31 = (bf16[512,1536]{0,1:T(8,128)(2,1)}, bf16[512,1536]{0,1:T(8,128)(2,1)S(1)}, u32[]{:S(2)}, u32[]{:S(2)}) collective-permute-start(bf16[512,1536]{0,1:T(8,128)(2,1)} %all-gather.20.cloned.1.call-done), channel_id=1, source_target_pairs={{0,4},{4,0},{8,12},{12,8},{16,20},{20,16},{24,28},{28,24},{1,5},{5... | collective-permute-start | bytes 4718600 | tf_op jit(solution)/shard_map/ppermute | solution.py:511
  415.5 33.5 %collective-permute-start.35 = (bf16[128,1536]{0,1:T(8,128)(2,1)}, bf16[128,1536]{0,1:T(8,128)(2,1)S(1)}, u32[]{:S(2)}, u32[]{:S(2)}) collective-permute-start(bf16[128,1536]{0,1:T(8,128)(2,1)} %bitcast.229), channel_id=1, source_target_pairs={{0,1},{1,0},{2,3},{3,2},{4,5},{5,4},{6,7},{7,6},{8,9},{9,8},{10,11... | collective-permute-start | bytes 1179656 | tf_op jit(solution)/shard_map/ppermute | solution.py:520
  416.6 32.4 %collective-permute-start.36 = (bf16[128,1536]{0,1:T(8,128)(2,1)}, bf16[128,1536]{0,1:T(8,128)(2,1)S(1)}, u32[]{:S(2)}, u32[]{:S(2)}) collective-permute-start(bf16[128,1536]{0,1:T(8,128)(2,1)} %collective-permute-done.34), channel_id=1, source_target_pairs={{0,1},{1,0},{2,3},{3,2},{4,5},{5,4},{6,7},{7,6},{8,9},{9,8},{10,11... | collective-permute-start | bytes 1179656 | tf_op jit(solution)/shard_map/ppermute | solution.py:520
  493.6 10.6 collective-permute-start.38
  507.8 9.7 collective-permute-start.39
  508.5 16.2 %collective-permute-start.40 = (bf16[128,1536]{1,0:T(8,128)(2,1)}, bf16[128,1536]{1,0:T(8,128)(2,1)}, u32[]{:S(2)}, u32[]{:S(2)}) collective-permute-start(bf16[128,1536]{1,0:T(8,128)(2,1)} %fusion.131), channel_id=1, source_target_pairs={{0,1},{1,0},{2,3},{3,2},{4,5},{5,4},{6,7},{7,6},{8,9},{9,8},{10,11... | collective-permute-start | bytes 1179656 | tf_op jit(solution)/shard_map/ppermute | solution.py:520
  526.7 15.9 %collective-permute-start.67 = (bf16[192,1536]{1,0:T(8,128)(2,1)S(1)}, bf16[192,1536]{1,0:T(8,128)(2,1)S(1)}, u32[]{:S(2)}, u32[]{:S(2)}) collective-permute-start(bf16[192,1536]{1,0:T(8,128)(2,1)S(1)} %fusion.100), channel_id=1, source_target_pairs={{0,4},{4,0},{8,12},{12,8},{16,20},{20,16},{24,28},{28,24},{1,5},{5... | collective-permute-start | bytes 1769480 | tf_op jit(solution)/shard_map/ppermute | solution.py:511
  530.7 48.9 %collective-permute-start.32 = (bf16[256,1536]{1,0:T(8,128)(2,1)}, bf16[256,1536]{1,0:T(8,128)(2,1)}, u32[]{:S(2)}, u32[]{:S(2)}) collective-permute-start(bf16[256,1536]{1,0:T(8,128)(2,1)} %slice.781), channel_id=1, source_target_pairs={{0,1},{1,0},{2,3},{3,2},{4,5},{5,4},{6,7},{7,6},{8,9},{9,8},{10,11... | collective-permute-start | bytes 2359304 | tf_op jit(solution)/shard_map/ppermute | solution.py:520
  534.5 41.0 %collective-permute-start.69 = (bf16[512,1536]{1,0:T(8,128)(2,1)}, bf16[512,1536]{1,0:T(8,128)(2,1)}, u32[]{:S(2)}, u32[]{:S(2)}) collective-permute-start(bf16[512,1536]{1,0:T(8,128)(2,1)} %fusion.88), channel_id=1, source_target_pairs={{0,4},{4,0},{8,12},{12,8},{16,20},{20,16},{24,28},{28,24},{1,5},{5... | collective-permute-start | bytes 4718600 | tf_op jit(solution)/shard_map/ppermute | solution.py:511
  545.4 385.9 %reduce-scatter.23.cloned.1.call-start = ((), (), s32[]{:S(2)}) async-start(), calls=%async_computation.22 | async-start | bytes 1966080 | tf_op jit(solution)/shard_map/reduce_scatter | solution.py:529
  552.9 30.3 %collective-permute-start.42 = (bf16[256,1536]{1,0:T(8,128)(2,1)}, bf16[256,1536]{1,0:T(8,128)(2,1)}, u32[]{:S(2)}, u32[]{:S(2)}) collective-permute-start(bf16[256,1536]{1,0:T(8,128)(2,1)} %fusion.28), channel_id=1, source_target_pairs={{0,1},{1,0},{2,3},{3,2},{4,5},{5,4},{6,7},{7,6},{8,9},{9,8},{10,11... | collective-permute-start | bytes 2359304 | tf_op jit(solution)/shard_map/ppermute | solution.py:520
  579.3 412.3 %reduce-scatter.17.cloned.1.call-start = ((), (), s32[]{:S(2)}) async-start(), calls=%async_computation.19 | async-start | bytes 2211840 | tf_op jit(solution)/shard_map/reduce_scatter | solution.py:529
  582.4 39.4 %collective-permute-start.66 = (bf16[768,1152]{1,0:T(8,128)(2,1)S(1)}, bf16[768,1152]{1,0:T(8,128)(2,1)S(1)}, u32[]{:S(2)}, u32[]{:S(2)}) collective-permute-start(bf16[768,1152]{1,0:T(8,128)(2,1)S(1)} %fusion.66), channel_id=1, source_target_pairs={{0,4},{4,0},{8,12},{12,8},{16,20},{20,16},{24,28},{28,24},{1,5},{5... | collective-permute-start | bytes 5308424 | tf_op jit(solution)/shard_map/ppermute | solution.py:511
  584.6 9.7 collective-permute-start.43
  588.0 36.5 %collective-permute-start.33 = (bf16[128,1536]{1,0:T(8,128)(2,1)}, bf16[128,1536]{1,0:T(8,128)(2,1)}, u32[]{:S(2)}, u32[]{:S(2)}) collective-permute-start(bf16[128,1536]{1,0:T(8,128)(2,1)} %fusion.47), channel_id=1, source_target_pairs={{0,2},{1,3},{2,0},{3,1},{4,6},{5,7},{6,4},{7,5},{8,10},{9,11},{10,... | collective-permute-start | bytes 1179656 | tf_op jit(solution)/shard_map/ppermute | solution.py:523
  624.4 398.2 %reduce-scatter.15.cloned.1.call-start = ((), (), s32[]{:S(2)}) async-start(), calls=%async_computation.18 | async-start | bytes 1966080 | tf_op jit(solution)/shard_map/reduce_scatter | solution.py:529
  629.1 9.1 collective-permute-start.44
  629.8 10.9 %collective-permute-start.45 = (bf16[128,1536]{1,0:T(8,128)(2,1)S(1)}, bf16[128,1536]{1,0:T(8,128)(2,1)S(1)}, u32[]{:S(2)}, u32[]{:S(2)}) collective-permute-start(bf16[128,1536]{1,0:T(8,128)(2,1)S(1)} %get-tuple-element.173), channel_id=1, source_target_pairs={{0,1},{1,0},{2,3},{3,2},{4,5},{5,4},{6,7},{7,6},{8,9},{9,8},{10,11... | collective-permute-start | bytes 1179656 | tf_op jit(solution)/shard_map/ppermute | solution.py:520
  643.0 35.7 %collective-permute-start.65 = (bf16[512,1536]{1,0:T(8,128)(2,1)S(1)}, bf16[512,1536]{1,0:T(8,128)(2,1)S(1)}, u32[]{:S(2)}, u32[]{:S(2)}) collective-permute-start(bf16[512,1536]{1,0:T(8,128)(2,1)S(1)} %fusion.91), channel_id=1, source_target_pairs={{0,4},{4,0},{8,12},{12,8},{16,20},{20,16},{24,28},{28,24},{1,5},{5... | collective-permute-start | bytes 4718600 | tf_op jit(solution)/shard_map/ppermute | solution.py:511
  647.2 99.0 %collective-permute-start.68 = (bf16[768,2048]{1,0:T(8,128)(2,1)}, bf16[768,2048]{1,0:T(8,128)(2,1)}, u32[]{:S(2)}, u32[]{:S(2)}) collective-permute-start(bf16[768,2048]{1,0:T(8,128)(2,1)} %fusion.60), channel_id=1, source_target_pairs={{0,4},{4,0},{8,12},{12,8},{16,20},{20,16},{24,28},{28,24},{1,5},{5... | collective-permute-start | bytes 9437192 | tf_op jit(solution)/shard_map/ppermute | solution.py:511
  680.9 344.1 %reduce-scatter.21.cloned.1.call-start = ((), (), s32[]{:S(2)}) async-start(), calls=%async_computation.21 | async-start | bytes 3932160 | tf_op jit(solution)/shard_map/reduce_scatter | solution.py:529
  695.8 56.1 %collective-permute-start.47 = (bf16[256,1536]{1,0:T(8,128)(2,1)}, bf16[256,1536]{1,0:T(8,128)(2,1)S(1)}, u32[]{:S(2)}, u32[]{:S(2)}) collective-permute-start(bf16[256,1536]{1,0:T(8,128)(2,1)} %fusion.26), channel_id=1, source_target_pairs={{0,1},{1,0},{2,3},{3,2},{4,5},{5,4},{6,7},{7,6},{8,9},{9,8},{10,11... | collective-permute-start | bytes 2359304 | tf_op jit(solution)/shard_map/ppermute | solution.py:520
  751.6 279.4 %reduce-scatter.11.cloned.1.call-start = ((), (), s32[]{:S(2)}) async-start(), calls=%async_computation.16 | async-start | bytes 1474560 | tf_op jit(solution)/shard_map/reduce_scatter | solution.py:529
  753.5 9.6 collective-permute-start.48
  765.5 8.7 collective-permute-start.49
  766.2 10.9 %collective-permute-start.50 = (bf16[128,1536]{1,0:T(8,128)(2,1)S(1)}, bf16[128,1536]{1,0:T(8,128)(2,1)S(1)}, u32[]{:S(2)}, u32[]{:S(2)}) collective-permute-start(bf16[128,1536]{1,0:T(8,128)(2,1)S(1)} %get-tuple-element.170), channel_id=1, source_target_pairs={{0,1},{1,0},{2,3},{3,2},{4,5},{5,4},{6,7},{7,6},{8,9},{9,8},{10,11... | collective-permute-start | bytes 1179656 | tf_op jit(solution)/shard_map/ppermute | solution.py:520
  827.2 27.9 %collective-permute-start.63 = (bf16[384,1536]{1,0:T(8,128)(2,1)}, bf16[384,1536]{1,0:T(8,128)(2,1)}, u32[]{:S(2)}, u32[]{:S(2)}) collective-permute-start(bf16[384,1536]{1,0:T(8,128)(2,1)} %fusion.96), channel_id=1, source_target_pairs={{0,4},{4,0},{8,12},{12,8},{16,20},{20,16},{24,28},{28,24},{1,5},{5... | collective-permute-start | bytes 3538952 | tf_op jit(solution)/shard_map/ppermute | solution.py:511
  847.2 58.4 %collective-permute-start.62 = (bf16[768,1536]{1,0:T(8,128)(2,1)}, bf16[768,1536]{1,0:T(8,128)(2,1)}, u32[]{:S(2)}, u32[]{:S(2)}) collective-permute-start(bf16[768,1536]{1,0:T(8,128)(2,1)} %fusion.78), channel_id=1, source_target_pairs={{0,4},{4,0},{8,12},{12,8},{16,20},{20,16},{24,28},{28,24},{1,5},{5... | collective-permute-start | bytes 7077896 | tf_op jit(solution)/shard_map/ppermute | solution.py:511
  858.4 176.2 %reduce-scatter.9.cloned.1.call-start = ((), (), s32[]{:S(2)}) async-start(), calls=%async_computation.15 | async-start | bytes 2949120 | tf_op jit(solution)/shard_map/reduce_scatter | solution.py:529
  910.4 146.9 %reduce-scatter.13.cloned.1.call-start = ((), (), s32[]{:S(2)}) async-start(), calls=%async_computation.17 | async-start | bytes 3932160 | tf_op jit(solution)/shard_map/reduce_scatter | solution.py:529
  917.0 69.1 %collective-permute-start.64 = (bf16[768,2048]{1,0:T(8,128)(2,1)}, bf16[768,2048]{1,0:T(8,128)(2,1)}, u32[]{:S(2)}, u32[]{:S(2)}) collective-permute-start(bf16[768,2048]{1,0:T(8,128)(2,1)} %fusion.72), channel_id=1, source_target_pairs={{0,4},{4,0},{8,12},{12,8},{16,20},{20,16},{24,28},{28,24},{1,5},{5... | collective-permute-start | bytes 9437192 | tf_op jit(solution)/shard_map/ppermute | solution.py:511
  924.3 20.8 %collective-permute-start.54 = (bf16[256,1536]{1,0:T(8,128)(2,1)}, bf16[256,1536]{1,0:T(8,128)(2,1)}, u32[]{:S(2)}, u32[]{:S(2)}) collective-permute-start(bf16[256,1536]{1,0:T(8,128)(2,1)} %fusion.24), channel_id=1, source_target_pairs={{0,1},{1,0},{2,3},{3,2},{4,5},{5,4},{6,7},{7,6},{8,9},{9,8},{10,11... | collective-permute-start | bytes 2359304 | tf_op jit(solution)/shard_map/ppermute | solution.py:520
  947.7 46.1 %collective-permute-start.55 = (bf16[128,1536]{1,0:T(8,128)(2,1)}, bf16[128,1536]{1,0:T(8,128)(2,1)S(1)}, u32[]{:S(2)}, u32[]{:S(2)}) collective-permute-start(bf16[128,1536]{1,0:T(8,128)(2,1)} %fusion.43), channel_id=1, source_target_pairs={{0,2},{1,3},{2,0},{3,1},{4,6},{5,7},{6,4},{7,5},{8,10},{9,11},{10,... | collective-permute-start | bytes 1179656 | tf_op jit(solution)/shard_map/ppermute | solution.py:523
  1005.0 8.8 collective-permute-start.57
  (208 other events, 2744.5 us)
Sparse Core Ops, SparseCore 0:
  12.9 56.3 all-gather.7
  71.5 31.8 all-gather.9
  105.6 60.8 all-gather.11
  183.8 36.5 all-gather.13
  222.3 38.9 all-gather.15
  310.9 62.4 all-gather.17
  378.6 36.2 all-gather.19
  545.5 18.8 reduce-scatter.18
  579.4 34.0 reduce-scatter.22
  624.5 38.1 reduce-scatter.16
  681.0 35.2 reduce-scatter.14
  751.7 60.9 reduce-scatter.20
  858.5 28.4 reduce-scatter.10
  910.5 46.3 reduce-scatter.8
  991.7 65.5 reduce-scatter.12

commit v2 on v1

--- a/solution.py
+++ b/solution.py
@@ -531,15 +531,16 @@
         )
 
     def gather_small(self, v):
-        both = self.by_y(v[None], self.swap_y(v)[None])
-        if self.nz > 4:
+        if self.dp > 8:
+            both = self.by_y(v[None], self.swap_y(v)[None])
             return jnp.swapaxes(self.gather_z(both[None]), 0, 1)
-        came = [both] + [self.shift_z(both, k) for k in range(1, self.nz)]
-        ring = jnp.stack([came[k] for k in range(self.nz - 1, -1, -1)] + [
-            came[k] for k in range(self.nz - 1, 0, -1)
-        ])
-        window = lax.dynamic_slice_in_dim(ring, self.nz - 1 - self.z, self.nz, 0)
-        return jnp.swapaxes(window, 0, 1)
+        n = self.dp
+        came = [v] + [
+            lax.ppermute(v, "dp", [(i, (i + k) % n) for i in range(n)]) for k in range(1, n)
+        ]
+        ring = jnp.stack(came[:0:-1] + came[:1] + came[:0:-1])
+        window = lax.dynamic_slice_in_dim(ring, n - 1 - lax.axis_index("dp"), n, 0)
+        return jnp.swapaxes(window.reshape(self.nz, 2, -1), 0, 1)
 
     def scatter_small(self, v):
         low = v.astype(bf16)
@@ -573,10 +574,11 @@
         core = self.swap_core(v)
         return jnp.concatenate([v, x, core, self.swap_core(x)], axis=0)
 
-    def scatter_rows(self, part):
+    def scatter_rows(self, part, *order):
         quarter = part.shape[0] // PIECES
         came = self.swap_core(part[2 * quarter :].astype(bf16)).astype(f32)
-        x = self.swap_x((part[quarter : 2 * quarter] + came[quarter:]).astype(bf16))
+        x = (part[quarter : 2 * quarter] + came[quarter:]).astype(bf16)
+        x = self.swap_x(after(x, *order))
         return part[:quarter] + came[:quarter] + x.astype(f32)
 
     def sum_rows(self, v):
@@ -587,13 +589,47 @@
         turned = jnp.concatenate([low[q : 2 * q], low[:q], low[3 * q :], low[2 * q : 3 * q]], axis=0)
         return (low.astype(f32) + self.swap_x(turned).astype(f32)).astype(bf16)
 
-    def gather_weight(self, shard):
-        own = self.gather_z(shard)
-        return own, self.swap_y(own)
-
-    def scatter_weight(self, own, other):
-        came = self.swap_y(other)
-        return self.scatter_z((own + came.astype(f32)).astype(bf16)).astype(f32)
+    def gather_z_direct(self, shard):
+        if self.nz > 4:
+            return self.gather_z(shard)
+        came = [shard] + [self.shift_z(shard, k) for k in range(1, self.nz)]
+        ring = jnp.concatenate(came[:0:-1] + came[:1] + came[:0:-1], axis=0)
+        rows = shard.shape[0]
+        return lax.dynamic_slice_in_dim(
+            ring, (self.nz - 1 - self.z) * rows, self.nz * rows, 0
+        )
+
+    def scatter_z_direct(self, v):
+        if self.nz > 4:
+            return self.scatter_z(v.astype(bf16)).astype(f32)
+        rows = v.shape[0] // self.nz
+        total = lax.dynamic_slice_in_dim(v, self.z * rows, rows, 0).astype(f32)
+        for k in range(1, self.nz):
+            piece = lax.dynamic_slice_in_dim(v, ((self.z + k) % self.nz) * rows, rows, 0)
+            total = total + self.shift_z(piece, k).astype(f32)
+        return total
+
+
+class Sent:
+    def __init__(self, links, left_own, left_other, right, *order):
+        self.links, self.left, self.right = links, left_own, right
+        self.product = dot_tn(left_other, right, bf16)
+        self.came = links.swap_y(after(self.product, *order))
+
+    def finish(self, *order, direct=False):
+        came = after(self.came, *order)
+        self.total = (dot_tn(self.left, self.right) + came.astype(f32)).astype(bf16)
+        if direct:
+            self.out = self.links.scatter_z_direct(self.total)
+        else:
+            self.out = self.links.scatter_z(self.total).astype(f32)
+        return self.total
+
+
+def after(v, *order):
+    if not order:
+        return v
+    return lax.optimization_barrier((v,) + order)[0]
 
 
 def regroup(v, nz, axis):
@@ -631,12 +667,12 @@
     return jnp.concatenate([dot_nt(d, own), dot_nt(d, other)], axis=1)
 
 
-def ffn_forward(links, n, w_in, w_out):
+def ffn_forward(links, n, w_in, w_out, *order):
     pair = times(n, *w_in)
     units = pair.shape[1] // 2
     gate, up = pair[:, :units], pair[:, units:]
     hid = (gate * jax.nn.sigmoid(gate) * up).astype(bf16)
-    return dot(hid, w_out), (n, gate.astype(bf16), up.astype(bf16), hid)
+    return dot(after(hid, *order), w_out), (n, gate.astype(bf16), up.astype(bf16), hid)
 
 
 def split_y(links, v):
@@ -646,21 +682,20 @@
     return own, other
 
 
-def ffn_backward(links, dy, kept, w_in, w_out):
+def ffn_backward(links, dy, kept, w_in, w_out, *order):
     n, gate, up, hid = kept
     hid_own, hid_other = split_y(links, hid)
-    grad_out = links.scatter_weight(dot_tn(hid_own, dy), dot_tn(hid_other, dy, bf16))
-    d_hid = dot_nt(dy, w_out)
+    sent_out = Sent(links, hid_own, hid_other, dy, *order)
+    d_hid = dot_nt(after(dy, sent_out.product), w_out)
     gate, up = gate.astype(f32), up.astype(f32)
     sig = jax.nn.sigmoid(gate)
     d_pair = jnp.concatenate(
         [d_hid * up * (sig * (1.0 + gate * (1.0 - sig))), d_hid * (gate * sig)], axis=1
     ).astype(bf16)
     half = n.shape[1] // 2
-    grad_in = links.scatter_weight(
-        dot_tn(n[:, :half], d_pair), dot_tn(n[:, half:], d_pair, bf16)
-    )
-    return back_times(d_pair, *w_in), grad_in, grad_out
+    sent_in = Sent(links, n[:, :half], n[:, half:], d_pair, sent_out.came)
+    d_normed = back_times(after(d_pair, sent_in.product), *w_in)
+    return d_normed, sent_in, sent_out
 
 
 def per_device(
@@ -689,25 +724,35 @@
     par = jnp.concatenate([table[: CONV + 3], jnp.zeros((1, width), f32)], axis=0)
     rate = -jnp.exp(table[CONV + 3 :])
 
-    def in_weight(w, group):
-        cols = w.shape[2]
+    def in_shard(w, group):
         if group:
             w = regroup(w, nz, 2)
-        return links.gather_weight(w.reshape(w.shape[0], w.shape[1] * cols))
-
-    def out_weight(w):
-        own, other = links.gather_weight(regroup(w, nz, 1))
-        return links.by_y(own, other)
-
-    mixer_in = in_weight(w_mixer_in, True)
-    mixer_out = out_weight(w_mixer_out)
-    ffn_a_in = in_weight(w_ffn_a_in, True)
-    ffn_a_out = out_weight(w_ffn_a_out)
-    qkv_in = in_weight(w_qkv, False)
-    attn_out = ungroup(out_weight(w_attn_out), nz, 0)
-    attn_out = attn_out.reshape(-1, features)
-    ffn_b_in = in_weight(w_ffn_b_in, True)
-    ffn_b_out = out_weight(w_ffn_b_out)
+        return w.reshape(w.shape[0], -1)
+
+    shards = [
+        in_shard(w_mixer_in, True),
+        jnp.concatenate([regroup(w_mixer_out, nz, 1), regroup(w_attn_out, nz, 1)], axis=0),
+        in_shard(w_ffn_a_in, True),
+        regroup(w_ffn_a_out, nz, 1),
+        in_shard(w_qkv, False),
+        in_shard(w_ffn_b_in, True),
+        regroup(w_ffn_b_out, nz, 1),
+    ]
+    shards = lax.optimization_barrier(shards)
+    own = [links.gather_z(v) for v in shards]
+    other = []
+    for v in own:
+        other.append(links.swap_y(after(v, *other[-1:])))
+    mixer_in, outs, ffn_a_in, ffn_a_out, qkv_in, ffn_b_in, ffn_b_out = zip(own, other)
+
+    def rows_of(v, lo, hi):
+        return v.reshape(nz, -1, features)[:, lo:hi].reshape(-1, features)
+
+    cut, end = w_mixer_out.shape[0], w_mixer_out.shape[0] + w_attn_out.shape[0]
+    mixer_out = links.by_y(*[rows_of(v, 0, cut) for v in outs])
+    attn_out = ungroup(links.by_y(*[rows_of(v, cut, end) for v in outs]), nz, 0)
+    ffn_a_out = links.by_y(*ffn_a_out)
+    ffn_b_out = links.by_y(*ffn_b_out)
 
     seg = segment_ids.reshape(micro, length)
     masks = []
@@ -746,7 +791,7 @@
         n, r = norm_forward(x, gains[i : i + 1])
         return links.gather_rows(links.own_first(n)), r
 
-    x0 = regroup(hidden_in.reshape(local, features), nz, 1).astype(f32)
+    x0 = regroup(after(hidden_in, *shards).reshape(local, features), nz, 1).astype(f32)
     n1, r1 = enter(x0, 0)
     pre = pieces(times(n1, *mixer_in))
     values, ext_part = conv_forward(slots, pre, masks, par, wx)
@@ -760,64 +805,69 @@
 
     n3, r3 = enter(x2, 2)
     mix, low = attention_forward(pieces(times(n3, *qkv_in)), tables)
-    x3 = x2 + links.scatter_rows(dot(flat(mix), attn_out))
+    x3 = x2 + links.scatter_rows(dot(after(flat(mix), own[5]), attn_out))
 
     n4, r4 = enter(x3, 3)
     y_b, kept_b = ffn_forward(links, n4, ffn_b_in, ffn_b_out)
     x4 = x3 + links.scatter_rows(y_b)
     block_out = ungroup(x4, nz, 1).astype(bf16).reshape(hidden_in.shape)
 
-    def leave(g, x, r, i, d_normed):
-        d_n = links.own_first(links.scatter_rows(d_normed))
+    def leave(g, x, r, i, d_normed, *order):
+        d_n = links.own_first(links.scatter_rows(d_normed, *order))
         d_x, d_gain = norm_backward(x, r, gains[i : i + 1], d_n)
         return g + d_x, d_gain
 
     g4_low = regroup(out_grad.reshape(local, features), nz, 1)
     g4 = g4_low.astype(f32)
-    d_n4, grad_b_in, grad_b_out = ffn_backward(
-        links, links.gather_rows(g4_low), kept_b, ffn_b_in, ffn_b_out
-    )
-    g3, gain_d = leave(g4, x3, r4, 3, d_n4)
+    fh = features // 2
+    dy4 = links.gather_rows(g4_low)
+    d_n4, b_in, b_out = ffn_backward(links, dy4, kept_b, ffn_b_in, ffn_b_out)
+    g3, gain_d = leave(g4, x3, r4, 3, d_n4, b_out.finish(d_n4))
 
     dy3 = links.gather_rows(g3.astype(bf16))
-    mix_rows = regroup(flat(mix), nz, 1)
-    mix_own, mix_other = split_y(links, mix_rows)
-    grad_attn_out = links.scatter_weight(dot_tn(mix_own, dy3), dot_tn(mix_other, dy3, bf16))
-    d_mix = dot_nt(dy3, attn_out).astype(bf16)
+    mix_own, mix_other = split_y(links, regroup(flat(mix), nz, 1))
+    a_out = Sent(links, mix_own, mix_other, dy3, b_in.came)
+    d_mix = dot_nt(after(dy3, a_out.product), attn_out).astype(bf16)
     d_qkv = flat(attention_backward(low, pieces(d_mix), tables))
-    fh = features // 2
-    grad_qkv = links.scatter_weight(
-        dot_tn(n3[:, :fh], d_qkv), dot_tn(n3[:, fh:], d_qkv, bf16)
-    )
-    g2, gain_c = leave(g3, x2, r3, 2, back_times(d_qkv, *qkv_in))
+    q_in = Sent(links, n3[:, :fh], n3[:, fh:], d_qkv, a_out.came)
+    d_qkv = after(d_qkv, q_in.product, b_in.finish(b_out.out, q_in.product))
+    d_n3 = back_times(d_qkv, *qkv_in)
+    g2, gain_c = leave(g3, x2, r3, 2, d_n3, a_out.finish(d_n3))
 
     dy2 = links.gather_rows(g2.astype(bf16))
-    d_n2, grad_a_in, grad_a_out = ffn_backward(links, dy2, kept_a, ffn_a_in, ffn_a_out)
+    d_n2, f_in, f_out = ffn_backward(
+        links, after(dy2, q_in.finish(dy2)), kept_a, ffn_a_in, ffn_a_out, q_in.came
+    )
+    d_n2 = after(d_n2, f_out.finish(b_in.out, d_n2))
     g1, gain_b = leave(g2, x1, r2, 1, d_n2)
 
     dy1 = links.gather_rows(g1.astype(bf16))
     gated = flat(gated)
-    gated_own, gated_other = split_y(links, gated)
-    grad_mixer_out = links.scatter_weight(
-        dot_tn(gated_own, dy1), dot_tn(gated_other, dy1, bf16)
-    )
-    d_gated = pieces(dot_nt(dy1, mixer_out))
+    m_out = Sent(links, *split_y(links, gated), dy1, f_in.came)
+    d_gated = pieces(dot_nt(after(dy1, m_out.product), mixer_out))
     d_dt, d_val, d_z, d_bc, d_rate, sums = scan_backward(
         slots, ext, wdt, values, pre, par, rate, keep, d_gated, scanned, states
     )
-    d_dt = flat(d_dt)
+    d_dt, d_z = flat(d_dt), flat(d_z)
+    m_z = Sent(links, n1[:, :fh], n1[:, fh:], d_z, m_out.came)
+    d_dt = after(d_dt, m_z.product, f_in.finish(m_z.product, a_out.out, q_in.out, f_out.out))
     d_bc = d_bc[:, :, :, 0, :].reshape(PIECES, micro, 2, rows, STATE)
     d_bc = jnp.swapaxes(d_bc, 2, 3).reshape(PIECES * local, 2 * STATE)
     d_ext = links.sum_rows(jnp.concatenate([dot_nt(d_dt, wdt), d_bc], axis=1))
     grad_dt = dot_tn(flat(ext)[:, :RANK], d_dt)
     grad_x = dot_tn(flat(values), d_ext)
-    d_x, conv_sums = conv_backward(slots, pieces(d_ext), d_val, pre, masks, par, wx)
-    d_pre = jnp.concatenate([flat(d_x), flat(d_z)], axis=1)
-    grad_mixer_in = links.scatter_weight(
-        dot_tn(n1[:, :fh], d_pre), dot_tn(n1[:, fh:], d_pre, bf16)
-    )
-    g0, gain_a = leave(g1, x0, r1, 0, back_times(d_pre, *mixer_in))
+    d_x, conv_sums = conv_backward(
+        slots, pieces(after(d_ext, m_out.finish(d_ext, direct=True))), d_val, pre, masks, par, wx
+    )
+    d_x = flat(d_x)
+    m_x = Sent(links, n1[:, :fh], n1[:, fh:], d_x, m_z.came)
+    d_x = after(d_x, m_x.product)
+    d_n1 = back_times(d_x, *[w[:, :width] for w in mixer_in])
+    d_n1 = d_n1 + back_times(d_z, *[w[:, width:] for w in mixer_in])
+    d_n1 = after(d_n1, m_z.finish(d_n1, f_in.out))
+    g0, gain_a = leave(g1, x0, r1, 0, d_n1)
     input_grad = ungroup(g0, nz, 1).astype(bf16).reshape(hidden_in.shape)
+    m_x.finish(direct=True)
 
     grad_table = jnp.concatenate([conv_sums[: CONV + 1], sums[:2], d_rate * rate], axis=0)
     grad_gains = jnp.stack([gain_a, gain_b, gain_c, gain_d])
@@ -833,11 +883,11 @@
     )
     summed = links.scatter_small(packed)
     offset = 0
-    outs = []
+    grads = []
     for v in small:
-        outs.append(summed[offset : offset + v.size].reshape(v.shape))
+        grads.append(summed[offset : offset + v.size].reshape(v.shape))
         offset += v.size
-    gain_total = outs[0]
+    gain_total = grads[0]
     gain_total = gain_total + links.swap_core(gain_total)
     gain_total = gain_total + links.swap_x(gain_total)
 
@@ -846,23 +896,23 @@
         return ungroup(v, nz, 2) if group else v
 
     def out_grad_of(v):
-        return ungroup(v, nz, 1)
+        return ungroup(v.out, nz, 1)
 
     return (
         block_out,
         input_grad,
         gain_total,
-        in_grad(grad_mixer_in, w_mixer_in, True),
-        outs[1],
-        outs[2],
-        outs[3],
-        out_grad_of(grad_mixer_out),
-        in_grad(grad_a_in, w_ffn_a_in, True),
-        out_grad_of(grad_a_out),
-        in_grad(grad_qkv, w_qkv, False),
-        out_grad_of(grad_attn_out),
-        in_grad(grad_b_in, w_ffn_b_in, True),
-        out_grad_of(grad_b_out),
+        jnp.stack([ungroup(m_x.out, nz, 1), ungroup(m_z.out, nz, 1)], axis=1),
+        grads[1],
+        grads[2],
+        grads[3],
+        out_grad_of(m_out),
+        in_grad(f_in.out, w_ffn_a_in, True),
+        out_grad_of(f_out),
+        in_grad(q_in.out, w_qkv, False),
+        out_grad_of(a_out),
+        in_grad(b_in.out, w_ffn_b_in, True),
+        out_grad_of(b_out),
     )
 
 

time: 1080 us -> 993 us (0.919)
  waiting for transfers between devices: 560 us -> 452 us
  blocking collectives: 16 us -> 0 us
  matrix products: 127 us -> 138 us
    ppermute x18 -> x17, waiting for transfers between devices: 363 us -> 227 us  [swap_y(): return lax.ppermute(v, 'dp', [(i, i ^ 1) for i in range(self.dp)])]
    reshape x19 -> x4, local copies, waits for them, and re-layouts: 28 us -> 10.6 us  [ungroup(): return jnp.swapaxes(v, axis, axis + 1).reshape(shape)]
    reduce_scatter x8 -> x7, waiting for transfers between devices: 16.5 us -> 0.01 us  [scatter_z(): lax.psum_scatter(v, 'dp', scatter_dimension=0, tiled=True, axis_index_gro...]
    all_gather x1 -> x0, blocking collectives: 16 us -> none  [gather_z(): lax.all_gather(v, 'dp', axis=0, tiled=True, axis_index_groups=self.groups)]
    ppermute x19, waiting for transfers between devices: 79.9 us -> 94.3 us  [swap_x(): return lax.ppermute(v, 'tensor', [(i, i ^ 2) for i in range(PIECES)])]
    ppermute x6 -> x9, waiting for transfers between devices: 20.6 us -> 32.1 us  [shift_z(): lax.ppermute(v, 'dp', [(2 * z + y, 2 * ((z + k) % n) + y) for z in range(...]
    dot_general x43 -> x47, matrix products: 127 us -> 138 us  [dot(): return lax.dot_general(a, b, (dims, ((), ())), preferred_element_type=out)]
    unnamed x381 -> x286, local copies, waits for them, and re-layouts: 28.4 us -> 30.1 us
  transfers between devices with their start and end apart: 85 -> 93, of which waited for: 45 -> 49; matrix products, arithmetic and copies ran while one was open for 24% -> 28% of each run, Pallas kernels for 7% -> 8%
where the time goes in v2:
time: 993 us; the launch traced here: 981 us
  waiting for transfers between devices  452 us (46%)
  matrix products  138 us (14%)
  local copies, waits for them, and re-layouts  127 us (13%)
  starting transfers between devices  102 us (10%)
  Pallas kernels  77.1 us (8%)
  other arithmetic  68.2 us (7%)
  between operations  16.9 us (2%)
    ppermute x17, waiting for transfers between devices, swap_y(): return lax.ppermute(v, 'dp', [(i, i ^ 1) for i in range(self.dp)])  227 us
    dot_general x47, matrix products, dot(): return lax.dot_general(a, b, (dims, ((), ())), preferred_element_type=out)  138 us
    ppermute x19, waiting for transfers between devices, swap_x(): return lax.ppermute(v, 'tensor', [(i, i ^ 2) for i in range(PIECES)])  94.3 us
    all_gather x7, waiting for transfers between devices, gather_z(): lax.all_gather(v, 'dp', axis=0, tiled=True, axis_index_groups=self.groups)  80.8 us
    ppermute x27, starting transfers between devices, swap_core(): return lax.ppermute(v, 'tensor', [(i, i ^ 1) for i in range(PIECES)])  47.1 us
    pallas_call x1, Pallas kernels, scan_backward(): pl.pallas_call(scan_bwd_kernel, grid_spec=grid, out_shape=[jax.ShapeDtype...  37.2 us
    ppermute x9, waiting for transfers between devices, shift_z(): lax.ppermute(v, 'dp', [(2 * z + y, 2 * ((z + k) % n) + y) for z in range(...  32.1 us
    unnamed x286, local copies, waits for them, and re-layouts  30.1 us
  transfers between devices with their start and end apart: 93, of which 49 were waited for; matrix products, arithmetic and copies ran while one was open for 28% of the time, Pallas kernels for 8%

profile of v2, /device:TPU:9, one launch (start us, length us, event | category | flops | bytes accessed | tf_op | source)
XLA Modules:
  0.0 980.7 jit_solution(7886081204161899524)
XLA Ops:
  7.2 3.5 reshape.451
  38.7 3.6 collective-permute-done.4
  49.6 26.5 %all-gather.8.cloned.1.call-done = bf16[768,1536]{1,0:T(8,128)(2,1)} async-done(((bf16[192,1536]{1,0:T(8,128)(2,1)}), bf16[768,1536]{1,0:T(8,128)(2,1)}) %all-gather.8.cloned.1.call-update) | async-done | bytes 2359312 | tf_op jit(solution)/shard_map/all_gather | solution.py:526
  81.9 5.8 collective-permute-done.7
  90.8 28.2 %all-gather.10.cloned.1.call-done = bf16[576,1536]{1,0:T(8,128)(2,1)} async-done(((bf16[144,1536]{1,0:T(8,128)(2,1)}), bf16[576,1536]{1,0:T(8,128)(2,1)}) %all-gather.10.cloned.1.call-update) | async-done | bytes 1769488 | tf_op jit(solution)/shard_map/all_gather | solution.py:526
  119.0 9.7 collective-permute-done.10
  136.0 3.8 conv_forward.1
  151.6 4.0 collective-permute-done.12
  155.6 23.2 %scan_forward.1 = (bf16[4,2,64,768]{3,2,1,0:T(8,128)(2,1)S(1)}, f32[4,2,64,768]{3,2,1,0:T(8,128)S(1)}, bf16[8,64,16,768]{3,2,1,0:T(8,128)(2,1)}) custom-call(s32[4]{0:T(128)S(1)} %pad_add_fusion.2.slot, bf16[4,2,64,128]{3,2,1,0:T(8,128)(2,1)S(1)} %bitcast.202, bf16[96,768]{1,0:T(8,128)(2,1)S(1)} %reshape.472.wdt_ref, bf16[4,2,64,768]{3,2,1,0:T(8,128)(2,1)S(1)} %copy-done.3, ...), custom_call_target="tpu_custom_call" | custom-call | tf_op jit(solution)/shard_map/scan_forward/pallas_call | solution.py:392
  191.1 9.1 collective-permute-done.15
  205.0 7.0 collective-permute-done.16
  214.2 13.0 %all-gather.14.cloned.1.call-done = bf16[512,1536]{0,1:T(8,128)(2,1)} async-done(((bf16[128,1536]{0,1:T(8,128)(2,1)}), bf16[512,1536]{0,1:T(8,128)(2,1)}) %all-gather.14.cloned.1.call-update) | async-done | bytes 1572880 | tf_op jit(solution)/shard_map/all_gather | solution.py:526
  227.1 28.0 %collective-permute-done.19 = bf16[768,2048]{1,0:T(8,128)(2,1)} collective-permute-done((bf16[768,2048]{1,0:T(8,128)(2,1)}, bf16[768,2048]{1,0:T(8,128)(2,1)}, u32[]{:S(2)}, u32[]{:S(2)}) %collective-permute-start.19) | collective-permute-done | bytes 3145760 | tf_op jit(solution)/shard_map/ppermute | solution.py:511
  255.5 4.4 fusion.77
  264.3 26.1 %collective-permute-done.20 = bf16[512,1536]{0,1:T(8,128)(2,1)S(1)} collective-permute-done((bf16[512,1536]{0,1:T(8,128)(2,1)}, bf16[512,1536]{0,1:T(8,128)(2,1)S(1)}, u32[]{:S(2)}, u32[]{:S(2)}) %collective-permute-start.20) | collective-permute-done | bytes 1572896 | tf_op jit(solution)/shard_map/ppermute | solution.py:511
  302.3 8.8 collective-permute-done.22
  316.9 6.1 collective-permute-done.23
  330.3 11.5 %collective-permute-done.26 = bf16[768,1152]{1,0:T(8,128)(2,1)} collective-permute-done((bf16[768,1152]{1,0:T(8,128)(2,1)}, bf16[768,1152]{1,0:T(8,128)(2,1)}, u32[]{:S(2)}, u32[]{:S(2)}) %collective-permute-start.26) | collective-permute-done | bytes 1769504 | tf_op jit(solution)/shard_map/ppermute | solution.py:511
  348.7 9.2 all-gather.18.cloned.1.call-done
  385.2 6.4 collective-permute-done.29
  398.1 3.9 all-gather.20.cloned.1.call-done
  402.0 32.6 %collective-permute-done.32 = bf16[768,2048]{1,0:T(8,128)(2,1)} collective-permute-done((bf16[768,2048]{1,0:T(8,128)(2,1)}, bf16[768,2048]{1,0:T(8,128)(2,1)}, u32[]{:S(2)}, u32[]{:S(2)}) %collective-permute-start.32) | collective-permute-done | bytes 3145760 | tf_op jit(solution)/shard_map/ppermute | solution.py:511
  435.8 3.9 fusion.65
  439.8 3.8 convolution_add_fusion.5
  444.2 4.0 fusion.101
  448.5 20.7 %collective-permute-done.33 = bf16[512,1536]{0,1:T(8,128)(2,1)S(1)} collective-permute-done((bf16[512,1536]{0,1:T(8,128)(2,1)}, bf16[512,1536]{0,1:T(8,128)(2,1)S(1)}, u32[]{:S(2)}, u32[]{:S(2)}) %collective-permute-start.33) | collective-permute-done | bytes 1572896 | tf_op jit(solution)/shard_map/ppermute | solution.py:511
  469.2 4.1 fusion.10
  474.6 3.4 fusion.63
  478.0 3.7 fusion.157
  481.8 4.3 fusion.158
  487.5 4.5 collective-permute-start.39
  492.0 11.0 %collective-permute-done.40 = bf16[512,1536]{1,0:T(8,128)(2,1)} collective-permute-done((bf16[512,1536]{1,0:T(8,128)(2,1)}, bf16[512,1536]{1,0:T(8,128)(2,1)}, u32[]{:S(2)}, u32[]{:S(2)}) %collective-permute-start.40) | collective-permute-done | bytes 1572896 | tf_op jit(solution)/shard_map/ppermute | solution.py:511
  503.0 4.2 fusion.1
  514.8 4.7 collective-permute-done.41
  530.4 3.8 collective-permute-start.43
  534.9 5.1 fusion.91
  545.0 4.0 attention_backward.1
  551.5 29.4 %collective-permute-done.45 = bf16[768,2048]{1,0:T(8,128)(2,1)} collective-permute-done((bf16[768,2048]{1,0:T(8,128)(2,1)}, bf16[768,2048]{1,0:T(8,128)(2,1)}, u32[]{:S(2)}, u32[]{:S(2)}) %collective-permute-start.45) | collective-permute-done | bytes 3145760 | tf_op jit(solution)/shard_map/ppermute | solution.py:511
  581.0 6.0 add_convert_fusion.1
  596.6 4.0 collective-permute-start.46
  611.5 7.0 collective-permute-done.48
  619.0 7.8 collective-permute-done.35
  631.9 6.5 collective-permute-done.49
  643.3 6.7 collective-permute-done.52
  652.5 3.7 fusion.98
  656.5 7.1 fusion.19
  663.6 3.5 fusion.75
  667.3 4.0 fusion.162
  675.2 14.9 %collective-permute-done.53 = bf16[512,1536]{1,0:T(8,128)(2,1)} collective-permute-done((bf16[512,1536]{1,0:T(8,128)(2,1)}, bf16[512,1536]{1,0:T(8,128)(2,1)}, u32[]{:S(2)}, u32[]{:S(2)}) %collective-permute-start.53) | collective-permute-done | bytes 1572896 | tf_op jit(solution)/shard_map/ppermute | solution.py:511
  690.1 3.8 add_convert_fusion.2
  704.4 9.2 collective-permute-done.55
  719.4 7.4 collective-permute-done.56
  738.3 37.2 %scan_backward.1 = (bf16[4,2,64,768]{3,2,1,0:T(8,128)(2,1)S(1)}, f32[4,2,64,768]{3,2,1,0:T(8,128)S(1)}, bf16[4,2,64,768]{3,2,1,0:T(8,128)(2,1)S(1)}, f32[4,2,2,8...) custom-call(s32[4]{0:T(128)S(1)} %pad_add_fusion.2.slot, ...), custom_call_target="tpu_custom_call" | custom-call | tf_op jit(solution)/shard_map/scan_backward/pallas_call | solution.py:437
  779.4 6.0 add_convert_fusion
  805.2 3.9 reshape.513
  816.1 20.9 %collective-permute-done.62 = bf16[384,1536]{1,0:T(8,128)(2,1)} collective-permute-done((bf16[384,1536]{1,0:T(8,128)(2,1)}, bf16[384,1536]{1,0:T(8,128)(2,1)}, u32[]{:S(2)}, u32[]{:S(2)}) %collective-permute-start.62) | collective-permute-done | bytes 1179680 | tf_op jit(solution)/shard_map/ppermute | solution.py:511
  842.3 3.8 fusion.2
  851.0 5.9 conv_backward.1
  880.1 9.6 collective-permute-done.72
  902.3 14.7 %collective-permute-done.76 = bf16[96,1536]{1,0:T(8,128)(2,1)S(1)} collective-permute-done((bf16[96,1536]{1,0:T(8,128)(2,1)S(1)}, bf16[96,1536]{1,0:T(8,128)(2,1)S(1)}, u32[]{:S(2)}, u32[]{:S(2)}) %collective-permute-start.76) | collective-permute-done | bytes 294944 | tf_op jit(solution)/shard_map/ppermute | solution.py:515
  923.9 5.8 collective-permute-done.73
  942.8 5.5 collective-permute-done.66
  953.1 3.6 collective-permute-done.69
  957.9 3.7 collective-permute-done.67
  (735 shorter events, 362.2 us)
Async XLA Ops:
  7.2 68.9 %all-gather.8.cloned.1.call-start = ((), (), s32[]{:S(2)}) async-start(), calls=%async_computation.7 | async-start | bytes 2949120 | tf_op jit(solution)/shard_map/all_gather | solution.py:526
  23.5 95.6 %all-gather.10.cloned.1.call-start = ((), (), s32[]{:S(2)}) async-start(), calls=%async_computation.8 | async-start | bytes 2211840 | tf_op jit(solution)/shard_map/all_gather | solution.py:526
  24.2 160.9 %all-gather.12.cloned.1.call-start = ((), (), s32[]{:S(2)}) async-start(), calls=%async_computation.9 | async-start | bytes 3932160 | tf_op jit(solution)/shard_map/all_gather | solution.py:526
  29.1 13.2 %collective-permute-start.4 = (bf16[24480]{0:T(1024)(128)(2,1)S(1)}, bf16[24480]{0:T(1024)(128)(2,1)S(1)}, u32[]{:S(2)}, u32[]{:S(2)}) collective-permute-start(bf16[24480]{0:T(1024)(128)(2,1)S(1)} %pad_maximum_fusion.24), channel_id=1, source_target_pairs={{0,12},{4,16},{8,20},{12,24},{16,28},{20,0},{24,4},{28,8},{1,13},{... | collective-permute-start | bytes 146888 | tf_op jit(solution)/shard_map/ppermute | solution.py:539
  31.6 195.6 %all-gather.14.cloned.1.call-start = ((), (), s32[]{:S(2)}) async-start(), calls=%async_computation.10 | async-start | bytes 1966080 | tf_op jit(solution)/shard_map/all_gather | solution.py:526
  31.8 13.7 %collective-permute-start.5 = (bf16[24480]{0:T(1024)(128)(2,1)S(1)}, bf16[24480]{0:T(1024)(128)(2,1)S(1)}, u32[]{:S(2)}, u32[]{:S(2)}) collective-permute-start(bf16[24480]{0:T(1024)(128)(2,1)S(1)} %pad_maximum_fusion.24), channel_id=1, source_target_pairs={{0,8},{4,12},{8,16},{12,20},{16,24},{20,28},{24,0},{28,4},{1,9},{5... | collective-permute-start | bytes 146888 | tf_op jit(solution)/shard_map/ppermute | solution.py:539
  33.1 12.4 %collective-permute-start.6 = (bf16[24480]{0:T(1024)(128)(2,1)S(1)}, bf16[24480]{0:T(1024)(128)(2,1)S(1)}, u32[]{:S(2)}, u32[]{:S(2)}) collective-permute-start(bf16[24480]{0:T(1024)(128)(2,1)S(1)} %pad_maximum_fusion.24), channel_id=1, source_target_pairs={{0,4},{4,8},{8,12},{12,16},{16,20},{20,24},{24,28},{28,0},{1,5},{5... | collective-permute-start | bytes 146888 | tf_op jit(solution)/shard_map/ppermute | solution.py:539
  76.1 52.7 %collective-permute-start.10 = (bf16[768,1536]{1,0:T(8,128)(2,1)}, bf16[768,1536]{1,0:T(8,128)(2,1)}, u32[]{:S(2)}, u32[]{:S(2)}) collective-permute-start(bf16[768,1536]{1,0:T(8,128)(2,1)} %all-gather.8.cloned.1.call-done), channel_id=1, source_target_pairs={{0,4},{4,0},{8,12},{12,8},{16,20},{20,16},{24,28},{28,24},{1,5},{5... | collective-permute-start | bytes 7077896 | tf_op jit(solution)/shard_map/ppermute | solution.py:511
  77.7 10.0 %collective-permute-start.7 = (bf16[128,1536]{1,0:T(8,128)(2,1)S(1)}, bf16[128,1536]{1,0:T(8,128)(2,1)S(1)}, u32[]{:S(2)}, u32[]{:S(2)}) collective-permute-start(bf16[128,1536]{1,0:T(8,128)(2,1)S(1)} %maximum_select_fusion.14), channel_id=1, source_target_pairs={{0,2},{1,3},{2,0},{3,1},{4,6},{5,7},{6,4},{7,5},{8,10},{9,11},{10,... | collective-permute-start | bytes 1179656 | tf_op jit(solution)/shard_map/ppermute | solution.py:523
  80.9 9.8 collective-permute-start.8
  128.8 50.1 %collective-permute-start.13 = (bf16[576,1536]{1,0:T(8,128)(2,1)}, bf16[576,1536]{1,0:T(8,128)(2,1)}, u32[]{:S(2)}, u32[]{:S(2)}) collective-permute-start(bf16[576,1536]{1,0:T(8,128)(2,1)} %all-gather.10.cloned.1.call-done), channel_id=1, source_target_pairs={{0,4},{4,0},{8,12},{12,8},{16,20},{20,16},{24,28},{28,24},{1,5},{5... | collective-permute-start | bytes 5308424 | tf_op jit(solution)/shard_map/ppermute | solution.py:511
  185.1 70.0 %collective-permute-start.19 = (bf16[768,2048]{1,0:T(8,128)(2,1)}, bf16[768,2048]{1,0:T(8,128)(2,1)}, u32[]{:S(2)}, u32[]{:S(2)}) collective-permute-start(bf16[768,2048]{1,0:T(8,128)(2,1)} %all-gather.12.cloned.1.call-done), channel_id=1, source_target_pairs={{0,4},{4,0},{8,12},{12,8},{16,20},{20,16},{24,28},{28,24},{1,5},{5... | collective-permute-start | bytes 9437192 | tf_op jit(solution)/shard_map/ppermute | solution.py:511
  189.7 10.5 %collective-permute-start.15 = (bf16[128,1536]{1,0:T(8,128)(2,1)S(1)}, bf16[128,1536]{1,0:T(8,128)(2,1)S(1)}, u32[]{:S(2)}, u32[]{:S(2)}) collective-permute-start(bf16[128,1536]{1,0:T(8,128)(2,1)S(1)} %fusion.60), channel_id=1, source_target_pairs={{0,2},{1,3},{2,0},{3,1},{4,6},{5,7},{6,4},{7,5},{8,10},{9,11},{10,... | collective-permute-start | bytes 1179656 | tf_op jit(solution)/shard_map/ppermute | solution.py:523
  190.9 111.1 %all-gather.16.cloned.1.call-start = ((), (), s32[]{:S(2)}) async-start(), calls=%async_computation.11 | async-start | bytes 2211840 | tf_op jit(solution)/shard_map/all_gather | solution.py:526
  203.6 51.7 %collective-permute-start.17 = (bf16[128,1536]{1,0:T(8,128)(2,1)S(1)}, bf16[128,1536]{1,0:T(8,128)(2,1)S(1)}, u32[]{:S(2)}, u32[]{:S(2)}) collective-permute-start(bf16[128,1536]{1,0:T(8,128)(2,1)S(1)} %maximum_select_fusion.15), channel_id=1, source_target_pairs={{0,1},{1,0},{2,3},{3,2},{4,5},{5,4},{6,7},{7,6},{8,9},{9,8},{10,11... | collective-permute-start | bytes 1179656 | tf_op jit(solution)/shard_map/ppermute | solution.py:520
  212.0 43.3 %collective-permute-start.18 = (bf16[128,1536]{1,0:T(8,128)(2,1)S(1)}, bf16[128,1536]{1,0:T(8,128)(2,1)S(1)}, u32[]{:S(2)}, u32[]{:S(2)}) collective-permute-start(bf16[128,1536]{1,0:T(8,128)(2,1)S(1)} %collective-permute-done.16), channel_id=1, source_target_pairs={{0,1},{1,0},{2,3},{3,2},{4,5},{5,4},{6,7},{7,6},{8,9},{9,8},{10,11... | collective-permute-start | bytes 1179656 | tf_op jit(solution)/shard_map/ppermute | solution.py:520
  213.9 143.9 %all-gather.18.cloned.1.call-start = ((), (), s32[]{:S(2)}) async-start(), calls=%async_computation.12 | async-start | bytes 3932160 | tf_op jit(solution)/shard_map/all_gather | solution.py:526
  255.1 35.3 %collective-permute-start.20 = (bf16[512,1536]{0,1:T(8,128)(2,1)}, bf16[512,1536]{0,1:T(8,128)(2,1)S(1)}, u32[]{:S(2)}, u32[]{:S(2)}) collective-permute-start(bf16[512,1536]{0,1:T(8,128)(2,1)} %all-gather.14.cloned.1.call-done), channel_id=1, source_target_pairs={{0,4},{4,0},{8,12},{12,8},{16,20},{20,16},{24,28},{28,24},{1,5},{5... | collective-permute-start | bytes 4718600 | tf_op jit(solution)/shard_map/ppermute | solution.py:511
  296.1 105.9 %all-gather.20.cloned.1.call-start = ((), (), s32[]{:S(2)}) async-start(), calls=%async_computation.13 | async-start | bytes 1966080 | tf_op jit(solution)/shard_map/all_gather | solution.py:526
  300.6 10.5 %collective-permute-start.22 = (bf16[128,1536]{1,0:T(8,128)(2,1)S(1)}, bf16[128,1536]{1,0:T(8,128)(2,1)S(1)}, u32[]{:S(2)}, u32[]{:S(2)}) collective-permute-start(bf16[128,1536]{1,0:T(8,128)(2,1)S(1)} %fusion.57), channel_id=1, source_target_pairs={{0,2},{1,3},{2,0},{3,1},{4,6},{5,7},{6,4},{7,5},{8,10},{9,11},{10,... | collective-permute-start | bytes 1179656 | tf_op jit(solution)/shard_map/ppermute | solution.py:523
  302.0 39.8 %collective-permute-start.26 = (bf16[768,1152]{1,0:T(8,128)(2,1)}, bf16[768,1152]{1,0:T(8,128)(2,1)}, u32[]{:S(2)}, u32[]{:S(2)}) collective-permute-start(bf16[768,1152]{1,0:T(8,128)(2,1)} %all-gather.16.cloned.1.call-done), channel_id=1, source_target_pairs={{0,4},{4,0},{8,12},{12,8},{16,20},{20,16},{24,28},{28,24},{1,5},{5... | collective-permute-start | bytes 5308424 | tf_op jit(solution)/shard_map/ppermute | solution.py:511
  315.4 13.8 %collective-permute-start.24 = (bf16[128,1536]{1,0:T(8,128)(2,1)S(1)}, bf16[128,1536]{1,0:T(8,128)(2,1)S(1)}, u32[]{:S(2)}, u32[]{:S(2)}) collective-permute-start(bf16[128,1536]{1,0:T(8,128)(2,1)S(1)} %maximum_select_fusion.16), channel_id=1, source_target_pairs={{0,1},{1,0},{2,3},{3,2},{4,5},{5,4},{6,7},{7,6},{8,9},{9,8},{10,11... | collective-permute-start | bytes 1179656 | tf_op jit(solution)/shard_map/ppermute | solution.py:520
  364.1 10.6 %collective-permute-start.28 = (bf16[128,1536]{1,0:T(8,128)(2,1)}, bf16[128,1536]{1,0:T(8,128)(2,1)}, u32[]{:S(2)}, u32[]{:S(2)}) collective-permute-start(bf16[128,1536]{1,0:T(8,128)(2,1)} %fusion.54), channel_id=1, source_target_pairs={{0,2},{1,3},{2,0},{3,1},{4,6},{5,7},{6,4},{7,5},{8,10},{9,11},{10,... | collective-permute-start | bytes 1179656 | tf_op jit(solution)/shard_map/ppermute | solution.py:523
  365.3 69.3 %collective-permute-start.32 = (bf16[768,2048]{1,0:T(8,128)(2,1)}, bf16[768,2048]{1,0:T(8,128)(2,1)}, u32[]{:S(2)}, u32[]{:S(2)}) collective-permute-start(bf16[768,2048]{1,0:T(8,128)(2,1)} %all-gather.18.cloned.1.call-done), channel_id=1, source_target_pairs={{0,4},{4,0},{8,12},{12,8},{16,20},{20,16},{24,28},{28,24},{1,5},{5... | collective-permute-start | bytes 9437192 | tf_op jit(solution)/shard_map/ppermute | solution.py:511
  366.5 214.4 %reduce-scatter.8.cloned.1.call-start = ((), (), s32[]{:S(2)}) async-start(), calls=%async_computation.14 | async-start | bytes 1966080 | tf_op jit(solution)/shard_map/reduce_scatter | solution.py:529
  371.1 12.1 %collective-permute-start.36 = (bf16[128,1536]{0,1:T(8,128)(2,1)}, bf16[128,1536]{0,1:T(8,128)(2,1)}, u32[]{:S(2)}, u32[]{:S(2)}) collective-permute-start(bf16[128,1536]{0,1:T(8,128)(2,1)} %bitcast.50), channel_id=1, source_target_pairs={{0,2},{1,3},{2,0},{3,1},{4,6},{5,7},{6,4},{7,5},{8,10},{9,11},{10,... | collective-permute-start | bytes 1179656 | tf_op jit(solution)/shard_map/ppermute | solution.py:523
  378.7 12.9 %collective-permute-start.29 = (bf16[128,1536]{1,0:T(8,128)(2,1)}, bf16[128,1536]{1,0:T(8,128)(2,1)}, u32[]{:S(2)}, u32[]{:S(2)}) collective-permute-start(bf16[128,1536]{1,0:T(8,128)(2,1)} %maximum_select_fusion.17), channel_id=1, source_target_pairs={{0,2},{1,3},{2,0},{3,1},{4,6},{5,7},{6,4},{7,5},{8,10},{9,11},{10,... | collective-permute-start | bytes 1179656 | tf_op jit(solution)/shard_map/ppermute | solution.py:523
  379.9 12.9 %collective-permute-start.37 = (bf16[128,1536]{0,1:T(8,128)(2,1)}, bf16[128,1536]{0,1:T(8,128)(2,1)}, u32[]{:S(2)}, u32[]{:S(2)}) collective-permute-start(bf16[128,1536]{0,1:T(8,128)(2,1)} %bitcast.50), channel_id=1, source_target_pairs={{0,1},{1,0},{2,3},{3,2},{4,5},{5,4},{6,7},{7,6},{8,9},{9,8},{10,11... | collective-permute-start | bytes 1179656 | tf_op jit(solution)/shard_map/ppermute | solution.py:520
  385.2 10.3 %collective-permute-start.30 = (bf16[128,1536]{1,0:T(8,128)(2,1)}, bf16[128,1536]{1,0:T(8,128)(2,1)}, u32[]{:S(2)}, u32[]{:S(2)}) collective-permute-start(bf16[128,1536]{1,0:T(8,128)(2,1)} %maximum_select_fusion.17), channel_id=1, source_target_pairs={{0,1},{1,0},{2,3},{3,2},{4,5},{5,4},{6,7},{7,6},{8,9},{9,8},{10,11... | collective-permute-start | bytes 1179656 | tf_op jit(solution)/shard_map/ppermute | solution.py:520
  434.6 34.6 %collective-permute-start.33 = (bf16[512,1536]{0,1:T(8,128)(2,1)}, bf16[512,1536]{0,1:T(8,128)(2,1)S(1)}, u32[]{:S(2)}, u32[]{:S(2)}) collective-permute-start(bf16[512,1536]{0,1:T(8,128)(2,1)} %all-gather.20.cloned.1.call-done), channel_id=1, source_target_pairs={{0,4},{4,0},{8,12},{12,8},{16,20},{20,16},{24,28},{28,24},{1,5},{5... | collective-permute-start | bytes 4718600 | tf_op jit(solution)/shard_map/ppermute | solution.py:511
  448.2 54.8 %collective-permute-start.40 = (bf16[512,1536]{1,0:T(8,128)(2,1)}, bf16[512,1536]{1,0:T(8,128)(2,1)}, u32[]{:S(2)}, u32[]{:S(2)}) collective-permute-start(bf16[512,1536]{1,0:T(8,128)(2,1)} %fusion.101), channel_id=1, source_target_pairs={{0,4},{4,0},{8,12},{12,8},{16,20},{20,16},{24,28},{28,24},{1,5},{5... | collective-permute-start | bytes 4718600 | tf_op jit(solution)/shard_map/ppermute | solution.py:511
  487.5 19.7 %collective-permute-start.39 = (bf16[256,1536]{1,0:T(8,128)(2,1)}, bf16[256,1536]{1,0:T(8,128)(2,1)}, u32[]{:S(2)}, u32[]{:S(2)}) collective-permute-start(bf16[256,1536]{1,0:T(8,128)(2,1)} %fusion.25), channel_id=1, source_target_pairs={{0,1},{1,0},{2,3},{3,2},{4,5},{5,4},{6,7},{7,6},{8,9},{9,8},{10,11... | collective-permute-start | bytes 2359304 | tf_op jit(solution)/shard_map/ppermute | solution.py:520
  513.5 176.6 %reduce-scatter.10.cloned.1.call-start = ((), (), s32[]{:S(2)}) async-start(), calls=%async_computation.15 | async-start | bytes 3932160 | tf_op jit(solution)/shard_map/reduce_scatter | solution.py:529
  513.6 67.4 %collective-permute-start.45 = (bf16[768,2048]{1,0:T(8,128)(2,1)}, bf16[768,2048]{1,0:T(8,128)(2,1)}, u32[]{:S(2)}, u32[]{:S(2)}) collective-permute-start(bf16[768,2048]{1,0:T(8,128)(2,1)} %fusion.63), channel_id=1, source_target_pairs={{0,4},{4,0},{8,12},{12,8},{16,20},{20,16},{24,28},{28,24},{1,5},{5... | collective-permute-start | bytes 9437192 | tf_op jit(solution)/shard_map/ppermute | solution.py:511
  523.1 11.1 %collective-permute-start.42 = (bf16[128,1536]{1,0:T(8,128)(2,1)}, bf16[128,1536]{1,0:T(8,128)(2,1)}, u32[]{:S(2)}, u32[]{:S(2)}) collective-permute-start(bf16[128,1536]{1,0:T(8,128)(2,1)} %fusion.137), channel_id=1, source_target_pairs={{0,2},{1,3},{2,0},{3,1},{4,6},{5,7},{6,4},{7,5},{8,10},{9,11},{10,... | collective-permute-start | bytes 1179656 | tf_op jit(solution)/shard_map/ppermute | solution.py:523
  530.4 10.8 %collective-permute-start.43 = (bf16[128,1536]{1,0:T(8,128)(2,1)}, bf16[128,1536]{1,0:T(8,128)(2,1)S(1)}, u32[]{:S(2)}, u32[]{:S(2)}) collective-permute-start(bf16[128,1536]{1,0:T(8,128)(2,1)} %fusion.137), channel_id=1, source_target_pairs={{0,1},{1,0},{2,3},{3,2},{4,5},{5,4},{6,7},{7,6},{8,9},{9,8},{10,11... | collective-permute-start | bytes 1179656 | tf_op jit(solution)/shard_map/ppermute | solution.py:520
  541.1 59.4 %collective-permute-start.34 = (bf16[256,1536]{1,0:T(8,128)(2,1)}, bf16[256,1536]{1,0:T(8,128)(2,1)}, u32[]{:S(2)}, u32[]{:S(2)}) collective-permute-start(bf16[256,1536]{1,0:T(8,128)(2,1)} %slice.825), channel_id=1, source_target_pairs={{0,1},{1,0},{2,3},{3,2},{4,5},{5,4},{6,7},{7,6},{8,9},{9,8},{10,11... | collective-permute-start | bytes 2359304 | tf_op jit(solution)/shard_map/ppermute | solution.py:520
  587.0 141.7 %reduce-scatter.14.cloned.1.call-start = ((), (), s32[]{:S(2)}) async-start(), calls=%async_computation.17 | async-start | bytes 2211840 | tf_op jit(solution)/shard_map/reduce_scatter | solution.py:529
  588.1 15.1 %collective-permute-start.47 = (bf16[192,1536]{1,0:T(8,128)(2,1)S(1)}, bf16[192,1536]{1,0:T(8,128)(2,1)}, u32[]{:S(2)}, u32[]{:S(2)}) collective-permute-start(bf16[192,1536]{1,0:T(8,128)(2,1)S(1)} %copy-done.113), channel_id=1, source_target_pairs={{0,4},{4,0},{8,12},{12,8},{16,20},{20,16},{24,28},{28,24},{1,5},{5... | collective-permute-start | bytes 1769480 | tf_op jit(solution)/shard_map/ppermute | solution.py:511
  608.4 10.0 %collective-permute-start.48 = (bf16[128,1536]{1,0:T(8,128)(2,1)S(1)}, bf16[128,1536]{1,0:T(8,128)(2,1)S(1)}, u32[]{:S(2)}, u32[]{:S(2)}) collective-permute-start(bf16[128,1536]{1,0:T(8,128)(2,1)S(1)} %fusion.39), channel_id=1, source_target_pairs={{0,2},{1,3},{2,0},{3,1},{4,6},{5,7},{6,4},{7,5},{8,10},{9,11},{10,... | collective-permute-start | bytes 1179656 | tf_op jit(solution)/shard_map/ppermute | solution.py:523
  610.5 16.3 %collective-permute-start.35 = (bf16[128,1536]{1,0:T(8,128)(2,1)S(1)}, bf16[128,1536]{1,0:T(8,128)(2,1)S(1)}, u32[]{:S(2)}, u32[]{:S(2)}) collective-permute-start(bf16[128,1536]{1,0:T(8,128)(2,1)S(1)} %fusion.50), channel_id=1, source_target_pairs={{0,2},{1,3},{2,0},{3,1},{4,6},{5,7},{6,4},{7,5},{8,10},{9,11},{10,... | collective-permute-start | bytes 1179656 | tf_op jit(solution)/shard_map/ppermute | solution.py:523
  611.3 38.8 %collective-permute-start.52 = (bf16[768,1152]{1,0:T(8,128)(2,1)S(1)}, bf16[768,1152]{1,0:T(8,128)(2,1)S(1)}, u32[]{:S(2)}, u32[]{:S(2)}) collective-permute-start(bf16[768,1152]{1,0:T(8,128)(2,1)S(1)} %copy-done.134), channel_id=1, source_target_pairs={{0,4},{4,0},{8,12},{12,8},{16,20},{20,16},{24,28},{28,24},{1,5},{5... | collective-permute-start | bytes 5308424 | tf_op jit(solution)/shard_map/ppermute | solution.py:511
  630.1 10.7 %collective-permute-start.50 = (bf16[128,1536]{1,0:T(8,128)(2,1)S(1)}, bf16[128,1536]{1,0:T(8,128)(2,1)S(1)}, u32[]{:S(2)}, u32[]{:S(2)}) collective-permute-start(bf16[128,1536]{1,0:T(8,128)(2,1)S(1)} %get-tuple-element.237), channel_id=1, source_target_pairs={{0,1},{1,0},{2,3},{3,2},{4,5},{5,4},{6,7},{7,6},{8,9},{9,8},{10,11... | collective-permute-start | bytes 1179656 | tf_op jit(solution)/shard_map/ppermute | solution.py:520
  656.2 33.9 %collective-permute-start.53 = (bf16[512,1536]{1,0:T(8,128)(2,1)}, bf16[512,1536]{1,0:T(8,128)(2,1)}, u32[]{:S(2)}, u32[]{:S(2)}) collective-permute-start(bf16[512,1536]{1,0:T(8,128)(2,1)} %fusion.98), channel_id=1, source_target_pairs={{0,4},{4,0},{8,12},{12,8},{16,20},{20,16},{24,28},{28,24},{1,5},{5... | collective-permute-start | bytes 4718600 | tf_op jit(solution)/shard_map/ppermute | solution.py:511
  656.2 123.2 %reduce-scatter.12.cloned.1.call-start = ((), (), s32[]{:S(2)}) async-start(), calls=%async_computation.16 | async-start | bytes 737280 | tf_op jit(solution)/shard_map/reduce_scatter | solution.py:529
  698.7 80.7 %reduce-scatter.16.cloned.1.call-start = ((), (), s32[]{:S(2)}) async-start(), calls=%async_computation.18 | async-start | bytes 1966080 | tf_op jit(solution)/shard_map/reduce_scatter | solution.py:529
  703.1 10.5 %collective-permute-start.55 = (bf16[128,1536]{1,0:T(8,128)(2,1)S(1)}, bf16[128,1536]{1,0:T(8,128)(2,1)}, u32[]{:S(2)}, u32[]{:S(2)}) collective-permute-start(bf16[128,1536]{1,0:T(8,128)(2,1)S(1)} %fusion.48), channel_id=1, source_target_pairs={{0,2},{1,3},{2,0},{3,1},{4,6},{5,7},{6,4},{7,5},{8,10},{9,11},{10,... | collective-permute-start | bytes 1179656 | tf_op jit(solution)/shard_map/ppermute | solution.py:523
  704.1 75.3 %collective-permute-start.59 = (bf16[768,2048]{1,0:T(8,128)(2,1)}, bf16[768,2048]{1,0:T(8,128)(2,1)}, u32[]{:S(2)}, u32[]{:S(2)}) collective-permute-start(bf16[768,2048]{1,0:T(8,128)(2,1)} %fusion.75), channel_id=1, source_target_pairs={{0,4},{4,0},{8,12},{12,8},{16,20},{20,16},{24,28},{28,24},{1,5},{5... | collective-permute-start | bytes 9437192 | tf_op jit(solution)/shard_map/ppermute | solution.py:511
  704.1 163.6 %reduce-scatter.18.cloned.1.call-start = ((), (), s32[]{:S(2)}) async-start(), calls=%async_computation.19 | async-start | bytes 3932160 | tf_op jit(solution)/shard_map/reduce_scatter | solution.py:529
  717.0 9.7 collective-permute-start.56
  717.9 12.9 %collective-permute-start.57 = (bf16[128,1536]{1,0:T(8,128)(2,1)}, bf16[128,1536]{1,0:T(8,128)(2,1)S(1)}, u32[]{:S(2)}, u32[]{:S(2)}) collective-permute-start(bf16[128,1536]{1,0:T(8,128)(2,1)} %get-tuple-element.234), channel_id=1, source_target_pairs={{0,1},{1,0},{2,3},{3,2},{4,5},{5,4},{6,7},{7,6},{8,9},{9,8},{10,11... | collective-permute-start | bytes 1179656 | tf_op jit(solution)/shard_map/ppermute | solution.py:520
  785.4 183.5 %reduce-scatter.20.cloned.1.call-start = ((), (), s32[]{:S(2)}) async-start(), calls=%async_computation.20 | async-start | bytes 1474560 | tf_op jit(solution)/shard_map/reduce_scatter | solution.py:529
  809.2 27.8 %collective-permute-start.62 = (bf16[384,1536]{1,0:T(8,128)(2,1)}, bf16[384,1536]{1,0:T(8,128)(2,1)}, u32[]{:S(2)}, u32[]{:S(2)}) collective-permute-start(bf16[384,1536]{1,0:T(8,128)(2,1)} %fusion.106), channel_id=1, source_target_pairs={{0,4},{4,0},{8,12},{12,8},{16,20},{20,16},{24,28},{28,24},{1,5},{5... | collective-permute-start | bytes 3538952 | tf_op jit(solution)/shard_map/ppermute | solution.py:511
  813.8 23.4 %collective-permute-start.60 = (bf16[512,128]{0,1:T(8,128)(2,1)S(1)}, bf16[512,128]{0,1:T(8,128)(2,1)S(1)}, u32[]{:S(2)}, u32[]{:S(2)}) collective-permute-start(bf16[512,128]{0,1:T(8,128)(2,1)S(1)} %pad_maximum_fusion.21), channel_id=1, source_target_pairs={{0,1},{1,0},{2,3},{3,2},{4,5},{5,4},{6,7},{7,6},{8,9},{9,8},{10,11... | collective-permute-start | bytes 393224 | tf_op jit(solution)/shard_map/ppermute | solution.py:520
  837.0 26.8 %collective-permute-start.63 = (bf16[768,768]{1,0:T(8,128)(2,1)}, bf16[768,768]{1,0:T(8,128)(2,1)}, u32[]{:S(2)}, u32[]{:S(2)}) collective-permute-start(bf16[768,768]{1,0:T(8,128)(2,1)} %fusion.83), channel_id=1, source_target_pairs={{0,4},{4,0},{8,12},{12,8},{16,20},{20,16},{24,28},{28,24},{1,5},{5... | collective-permute-start | bytes 3538952 | tf_op jit(solution)/shard_map/ppermute | solution.py:511
  863.8 25.9 %collective-permute-start.72 = (bf16[768,768]{1,0:T(8,128)(2,1)}, bf16[768,768]{1,0:T(8,128)(2,1)}, u32[]{:S(2)}, u32[]{:S(2)}) collective-permute-start(bf16[768,768]{1,0:T(8,128)(2,1)} %fusion.81), channel_id=1, source_target_pairs={{0,4},{4,0},{8,12},{12,8},{16,20},{20,16},{24,28},{28,24},{1,5},{5... | collective-permute-start | bytes 3538952 | tf_op jit(solution)/shard_map/ppermute | solution.py:511
  872.3 21.9 %collective-permute-start.64 = (bf16[256,1536]{1,0:T(8,128)(2,1)S(1)}, bf16[256,1536]{1,0:T(8,128)(2,1)}, u32[]{:S(2)}, u32[]{:S(2)}) collective-permute-start(bf16[256,1536]{1,0:T(8,128)(2,1)S(1)} %slice.823), channel_id=1, source_target_pairs={{0,1},{1,0},{2,3},{3,2},{4,5},{5,4},{6,7},{7,6},{8,9},{9,8},{10,11... | collective-permute-start | bytes 2359304 | tf_op jit(solution)/shard_map/ppermute | solution.py:520
  876.2 23.7 %collective-permute-start.78 = (bf16[96,1536]{1,0:T(8,128)(2,1)S(1)}, bf16[96,1536]{1,0:T(8,128)(2,1)S(1)}, u32[]{:S(2)}, u32[]{:S(2)}) collective-permute-start(bf16[96,1536]{1,0:T(8,128)(2,1)S(1)} %get-tuple-element.252), channel_id=1, source_target_pairs={{0,24},{4,28},{8,0},{12,4},{16,8},{20,12},{24,16},{28,20},{1,25},{... | collective-permute-start | bytes 884744 | tf_op jit(solution)/shard_map/ppermute | solution.py:515
  878.5 22.1 %collective-permute-start.77 = (bf16[96,1536]{1,0:T(8,128)(2,1)S(1)}, bf16[96,1536]{1,0:T(8,128)(2,1)S(1)}, u32[]{:S(2)}, u32[]{:S(2)}) collective-permute-start(bf16[96,1536]{1,0:T(8,128)(2,1)S(1)} %get-tuple-element.253), channel_id=1, source_target_pairs={{0,16},{4,20},{8,24},{12,28},{16,0},{20,4},{24,8},{28,12},{1,17},{... | collective-permute-start | bytes 884744 | tf_op jit(solution)/shard_map/ppermute | solution.py:515
  879.7 37.3 %collective-permute-start.76 = (bf16[96,1536]{1,0:T(8,128)(2,1)S(1)}, bf16[96,1536]{1,0:T(8,128)(2,1)S(1)}, u32[]{:S(2)}, u32[]{:S(2)}) collective-permute-start(bf16[96,1536]{1,0:T(8,128)(2,1)S(1)} %get-tuple-element.251), channel_id=1, source_target_pairs={{0,8},{4,12},{8,16},{12,20},{16,24},{20,28},{24,0},{28,4},{1,9},{5... | collective-permute-start | bytes 884744 | tf_op jit(solution)/shard_map/ppermute | solution.py:515
  891.9 32.0 %collective-permute-start.75 = (bf16[192,768]{1,0:T(8,128)(2,1)S(1)}, bf16[192,768]{1,0:T(8,128)(2,1)S(1)}, u32[]{:S(2)}, u32[]{:S(2)}) collective-permute-start(bf16[192,768]{1,0:T(8,128)(2,1)S(1)} %get-tuple-element.255), channel_id=1, source_target_pairs={{0,24},{4,28},{8,0},{12,4},{16,8},{20,12},{24,16},{28,20},{1,25},{... | collective-permute-start | bytes 884744 | tf_op jit(solution)/shard_map/ppermute | solution.py:515
  894.2 29.7 %collective-permute-start.74 = (bf16[192,768]{1,0:T(8,128)(2,1)S(1)}, bf16[192,768]{1,0:T(8,128)(2,1)S(1)}, u32[]{:S(2)}, u32[]{:S(2)}) collective-permute-start(bf16[192,768]{1,0:T(8,128)(2,1)S(1)} %get-tuple-element.256), channel_id=1, source_target_pairs={{0,16},{4,20},{8,24},{12,28},{16,0},{20,4},{24,8},{28,12},{1,17},{... | collective-permute-start | bytes 884744 | tf_op jit(solution)/shard_map/ppermute | solution.py:515
  899.9 29.8 %collective-permute-start.73 = (bf16[192,768]{1,0:T(8,128)(2,1)S(1)}, bf16[192,768]{1,0:T(8,128)(2,1)}, u32[]{:S(2)}, u32[]{:S(2)}) collective-permute-start(bf16[192,768]{1,0:T(8,128)(2,1)S(1)} %get-tuple-element.254), channel_id=1, source_target_pairs={{0,8},{4,12},{8,16},{12,20},{16,24},{20,28},{24,0},{28,4},{1,9},{5... | collective-permute-start | bytes 884744 | tf_op jit(solution)/shard_map/ppermute | solution.py:515
  900.6 38.4 %collective-permute-start.65 = (bf16[128,1536]{1,0:T(8,128)(2,1)}, bf16[128,1536]{1,0:T(8,128)(2,1)}, u32[]{:S(2)}, u32[]{:S(2)}) collective-permute-start(bf16[128,1536]{1,0:T(8,128)(2,1)} %fusion.46), channel_id=1, source_target_pairs={{0,2},{1,3},{2,0},{3,1},{4,6},{5,7},{6,4},{7,5},{8,10},{9,11},{10,... | collective-permute-start | bytes 1179656 | tf_op jit(solution)/shard_map/ppermute | solution.py:523
  (168 other events, 2043.6 us)
Sparse Core Ops, SparseCore 0:
  23.6 52.4 all-gather.7
  78.2 40.7 all-gather.9
  121.2 61.2 all-gather.11
  191.1 36.0 all-gather.13
  229.1 38.9 all-gather.15
  296.3 61.5 all-gather.17
  366.7 35.3 all-gather.19
  513.7 36.0 reduce-scatter.7
  587.1 63.2 reduce-scatter.9
  656.3 39.5 reduce-scatter.13
  698.9 19.3 reduce-scatter.11
  720.6 35.2 reduce-scatter.15
  785.5 59.5 reduce-scatter.17
  934.1 32.7 reduce-scatter.19

commit v3 on v2

--- a/solution.py
+++ b/solution.py
@@ -292,6 +292,7 @@
 
 
 BIG = 48 * 1024 * 1024
+BRIEF = pl.CostEstimate(flops=1, bytes_accessed=1, transcendentals=0)
 
 
 def params(dims):
@@ -337,6 +338,7 @@
             jax.ShapeDtypeStruct((PIECES, MICRO, rows, wx.shape[1]), bf16),
         ],
         compiler_params=params(2),
+        cost_estimate=BRIEF,
         name="conv_forward",
     )(slots, pre, masks, par, wx)
 
@@ -370,6 +372,7 @@
             jax.ShapeDtypeStruct((8, width), f32),
         ],
         compiler_params=params(2),
+        cost_estimate=BRIEF,
         name="conv_backward",
     )(slots, d_ext, d_val, pre, pre, masks, par, wx)
 
@@ -398,6 +401,7 @@
             jax.ShapeDtypeStruct((MICRO * PIECES, rows, STATE, width), bf16),
         ],
         compiler_params=params(2),
+        cost_estimate=BRIEF,
         name="scan_forward",
     )(slots, ext, wdt, val, pre, par, rate, keep)
 
@@ -446,6 +450,7 @@
             jax.ShapeDtypeStruct((8, width), f32),
         ],
         compiler_params=params(2),
+        cost_estimate=BRIEF,
         name="scan_backward",
     )(slots, ext, wdt, val, pre, par, rate, keep, d_gated, scanned, states, states)
 
@@ -477,6 +482,7 @@
             jax.ShapeDtypeStruct((PIECES, MICRO, rows, width), bf16),
         ],
         compiler_params=params(1),
+        cost_estimate=BRIEF,
         name="attention_forward",
     )(qkv, *tables)
 
@@ -494,8 +500,146 @@
         out_specs=whole(width),
         out_shape=jax.ShapeDtypeStruct((PIECES, MICRO, rows, width), bf16),
         compiler_params=params(1),
+        cost_estimate=BRIEF,
         name="attention_backward",
     )(low, d_mix, *tables)
+
+
+def tile_of(n):
+    return 256 if n % 256 == 0 else n
+
+
+def tn_kernel(count, added, *refs):
+    left, rights, adds, out = refs[0], refs[1 : 1 + count], refs[1 + count : -1], refs[-1]
+    col = 0
+    for i in range(count):
+        width = rights[i].shape[1]
+        part = dot_tn(left[...], rights[i][...])
+        if added:
+            part = part + adds[0][:, col : col + width].astype(f32)
+        out[:, col : col + width] = part.astype(bf16)
+        col += width
+
+
+def product_tn(left, rights, adds=()):
+    rows, m = left.shape
+    tile = tile_of(m)
+    width = sum(v.shape[1] for v in rights)
+    whole = [pl.BlockSpec(v.shape, lambda i: (0, 0)) for v in rights]
+    return pl.pallas_call(
+        lambda *refs: tn_kernel(len(rights), bool(adds), *refs),
+        grid=(m // tile,),
+        in_specs=[pl.BlockSpec((rows, tile), lambda i: (0, i))]
+        + whole
+        + [pl.BlockSpec((tile, v.shape[1]), lambda i: (i, 0)) for v in adds],
+        out_specs=pl.BlockSpec((tile, width), lambda i: (i, 0)),
+        out_shape=jax.ShapeDtypeStruct((m, width), bf16),
+        compiler_params=params(1),
+        cost_estimate=BRIEF,
+        name="product_tn",
+    )(left, *rights, *adds)
+
+
+def nt_kernel(count, steps, *refs):
+    ds, ws, out = refs[:count], refs[count:-1], refs[-1]
+
+    def part(w):
+        total, col = None, 0
+        for d in ds:
+            width = d.shape[1]
+            term = dot_nt(d[...], w[:, col : col + width])
+            total = term if total is None else total + term
+            col += width
+        out[...] = total.astype(bf16)
+
+    if len(ws) == 1:
+        part(ws[0])
+    else:
+        pl.when(pl.program_id(0) < steps)(lambda: part(ws[0]))
+        pl.when(pl.program_id(0) >= steps)(lambda: part(ws[1]))
+
+
+def product_nt(ds, ws):
+    rows = ds[0].shape[0]
+    m, width = ws[0].shape
+    tile = tile_of(m)
+    steps = m // tile
+    maps = [lambda i: (jnp.minimum(i, steps - 1), 0), lambda i: (jnp.maximum(i - steps, 0), 0)]
+    return pl.pallas_call(
+        lambda *refs: nt_kernel(len(ds), steps, *refs),
+        grid=(steps * len(ws),),
+        in_specs=[pl.BlockSpec(v.shape, lambda i: (0, 0)) for v in ds]
+        + [pl.BlockSpec((tile, width), maps[j]) for j in range(len(ws))],
+        out_specs=pl.BlockSpec((rows, tile), lambda i: (0, i)),
+        out_shape=jax.ShapeDtypeStruct((rows, m * len(ws)), bf16),
+        compiler_params=params(1),
+        cost_estimate=BRIEF,
+        name="product_nt",
+    )(*ds, *ws)
+
+
+def gate_bwd_kernel(dy, w, gate, up, d_gate, d_up):
+    d_hid = dot_nt(dy[...], w[...])
+    g = gate[...].astype(f32)
+    sig = sigmoid(g)
+    d_gate[...] = (d_hid * up[...].astype(f32) * (sig * (1.0 + g * (1.0 - sig)))).astype(bf16)
+    d_up[...] = (d_hid * (g * sig)).astype(bf16)
+
+
+def gate_backward(dy, w, gate, up):
+    rows, units = gate.shape
+    tile = tile_of(units)
+    column = pl.BlockSpec((rows, tile), lambda i: (0, i))
+    return pl.pallas_call(
+        gate_bwd_kernel,
+        grid=(units // tile,),
+        in_specs=[
+            pl.BlockSpec(dy.shape, lambda i: (0, 0)),
+            pl.BlockSpec((tile, w.shape[1]), lambda i: (i, 0)),
+            column,
+            column,
+        ],
+        out_specs=[column, column],
+        out_shape=[jax.ShapeDtypeStruct((rows, units), bf16)] * 2,
+        compiler_params=params(1),
+        cost_estimate=BRIEF,
+        name="gate_backward",
+    )(dy, w, gate, up)
+
+
+def spread_kernel(nz, count, *refs):
+    terms, out = refs[:-1], refs[-1]
+    total = sum(v[...].astype(f32) for v in terms)
+    cols = total.shape[1] // count
+    u = cols // (2 * nz)
+    for i in range(count):
+        blocks = []
+        for z in range(nz):
+            for y in range(2):
+                at = i * cols + (y * nz + z) * u
+                blocks.append(total[:, at : at + u])
+        if count == 1:
+            out[...] = jnp.concatenate(blocks, axis=1)
+        else:
+            for j, block in enumerate(blocks):
+                out[:, i, j * u : (j + 1) * u] = block
+
+
+def spread(terms, nz, shape):
+    rows, cols = terms[0].shape
+    count = shape[1] if len(shape) == 3 else 1
+    tile = rows // 2 if rows % 32 == 0 else rows
+    block = (tile, cols) if count == 1 else (tile, count, cols // count)
+    return pl.pallas_call(
+        lambda *refs: spread_kernel(nz, count, *refs),
+        grid=(rows // tile,),
+        in_specs=[pl.BlockSpec((tile, cols), lambda i: (i, 0))] * len(terms),
+        out_specs=pl.BlockSpec(block, lambda i: (i,) + (0,) * (len(block) - 1)),
+        out_shape=jax.ShapeDtypeStruct(shape, f32),
+        compiler_params=params(1),
+        cost_estimate=BRIEF,
+        name="spread",
+    )(*terms)
 
 
 class Links:
@@ -542,13 +686,13 @@
         window = lax.dynamic_slice_in_dim(ring, n - 1 - lax.axis_index("dp"), n, 0)
         return jnp.swapaxes(window.reshape(self.nz, 2, -1), 0, 1)
 
-    def scatter_small(self, v):
+    def scatter_small(self, v, order=()):
         low = v.astype(bf16)
         own = lax.dynamic_index_in_dim(v, self.y, 0, False)
         other = self.swap_y(lax.dynamic_index_in_dim(low, 1 - self.y, 0, False))
-        part = own + other.astype(f32)
+        part = after(own + other.astype(f32), *order)
         if self.nz > 4:
-            return self.scatter_z(part.astype(bf16)).reshape(-1).astype(f32)
+            return self.scatter_z(part.astype(bf16))[0].astype(f32)
         total = lax.dynamic_index_in_dim(part, self.z, 0, False)
         part_low = part.astype(bf16)
         for k in range(1, self.nz):
@@ -577,9 +721,9 @@
     def scatter_rows(self, part, *order):
         quarter = part.shape[0] // PIECES
         came = self.swap_core(part[2 * quarter :].astype(bf16)).astype(f32)
-        x = (part[quarter : 2 * quarter] + came[quarter:]).astype(bf16)
+        x = (part[quarter : 2 * quarter].astype(f32) + came[quarter:]).astype(bf16)
         x = self.swap_x(after(x, *order))
-        return part[:quarter] + came[:quarter] + x.astype(f32)
+        return part[:quarter].astype(f32) + came[:quarter] + x.astype(f32)
 
     def sum_rows(self, v):
         low = v.astype(bf16)
@@ -601,29 +745,31 @@
 
     def scatter_z_direct(self, v):
         if self.nz > 4:
-            return self.scatter_z(v.astype(bf16)).astype(f32)
+            return [self.scatter_z(v)]
         rows = v.shape[0] // self.nz
-        total = lax.dynamic_slice_in_dim(v, self.z * rows, rows, 0).astype(f32)
+        terms = [lax.dynamic_slice_in_dim(v, self.z * rows, rows, 0)]
         for k in range(1, self.nz):
             piece = lax.dynamic_slice_in_dim(v, ((self.z + k) % self.nz) * rows, rows, 0)
-            total = total + self.shift_z(piece, k).astype(f32)
-        return total
+            terms.append(self.shift_z(piece, k))
+        return terms
 
 
 class Sent:
-    def __init__(self, links, left_own, left_other, right, *order):
-        self.links, self.left, self.right = links, left_own, right
-        self.product = dot_tn(left_other, right, bf16)
+    def __init__(self, links, left_own, left_other, rights, *order):
+        self.links, self.left, self.rights = links, left_own, rights
+        self.product = product_tn(left_other, rights)
         self.came = links.swap_y(after(self.product, *order))
 
     def finish(self, *order, direct=False):
-        came = after(self.came, *order)
-        self.total = (dot_tn(self.left, self.right) + came.astype(f32)).astype(bf16)
+        self.total = product_tn(self.left, self.rights, [after(self.came, *order)])
         if direct:
-            self.out = self.links.scatter_z_direct(self.total)
+            self.terms = self.links.scatter_z_direct(self.total)
         else:
-            self.out = self.links.scatter_z(self.total).astype(f32)
+            self.terms = [self.links.scatter_z(self.total)]
         return self.total
+
+    def land(self, *order):
+        return [after(v, *order) for v in self.terms]
 
 
 def after(v, *order):
@@ -658,21 +804,21 @@
     return d_x, jnp.sum(d_n * u, axis=0)
 
 
-def times(x, own, other):
+def times(x, own, other, *order):
     half = x.shape[1] // 2
-    return dot(x[:, :half], own) + dot(x[:, half:], other)
+    return after(dot(x[:, :half], own), *order) + dot(x[:, half:], other)
 
 
 def back_times(d, own, other):
     return jnp.concatenate([dot_nt(d, own), dot_nt(d, other)], axis=1)
 
 
-def ffn_forward(links, n, w_in, w_out, *order):
-    pair = times(n, *w_in)
+def ffn_forward(n, w_in, *order):
+    pair = times(n, *w_in, *order)
     units = pair.shape[1] // 2
     gate, up = pair[:, :units], pair[:, units:]
     hid = (gate * jax.nn.sigmoid(gate) * up).astype(bf16)
-    return dot(after(hid, *order), w_out), (n, gate.astype(bf16), up.astype(bf16), hid)
+    return hid, (n, gate.astype(bf16), up.astype(bf16), hid)
 
 
 def split_y(links, v):
@@ -682,20 +828,17 @@
     return own, other
 
 
-def ffn_backward(links, dy, kept, w_in, w_out, *order):
+def ffn_backward(links, dy, kept, w_out, *order, finish=None):
     n, gate, up, hid = kept
     hid_own, hid_other = split_y(links, hid)
-    sent_out = Sent(links, hid_own, hid_other, dy, *order)
-    d_hid = dot_nt(after(dy, sent_out.product), w_out)
-    gate, up = gate.astype(f32), up.astype(f32)
-    sig = jax.nn.sigmoid(gate)
-    d_pair = jnp.concatenate(
-        [d_hid * up * (sig * (1.0 + gate * (1.0 - sig))), d_hid * (gate * sig)], axis=1
-    ).astype(bf16)
+    sent_out = Sent(links, hid_own, hid_other, [dy], *order)
+    dy = after(dy, sent_out.product)
+    if finish is not None:
+        dy = after(dy, finish.finish(sent_out.product))
+    d_pair = gate_backward(dy, w_out, gate, up)
     half = n.shape[1] // 2
     sent_in = Sent(links, n[:, :half], n[:, half:], d_pair, sent_out.came)
-    d_normed = back_times(after(d_pair, sent_in.product), *w_in)
-    return d_normed, sent_in, sent_out
+    return sent_in, sent_out, [after(d_pair[0], sent_in.product), d_pair[1]]
 
 
 def per_device(
@@ -738,7 +881,7 @@
         in_shard(w_ffn_b_in, True),
         regroup(w_ffn_b_out, nz, 1),
     ]
-    shards = lax.optimization_barrier(shards)
+    shards[1:] = lax.optimization_barrier(shards[1:])
     own = [links.gather_z(v) for v in shards]
     other = []
     for v in own:
@@ -791,7 +934,7 @@
         n, r = norm_forward(x, gains[i : i + 1])
         return links.gather_rows(links.own_first(n)), r
 
-    x0 = regroup(after(hidden_in, *shards).reshape(local, features), nz, 1).astype(f32)
+    x0 = regroup(after(hidden_in, *shards[1:]).reshape(local, features), nz, 1).astype(f32)
     n1, r1 = enter(x0, 0)
     pre = pieces(times(n1, *mixer_in))
     values, ext_part = conv_forward(slots, pre, masks, par, wx)
@@ -800,120 +943,110 @@
     x1 = x0 + links.scatter_rows(dot(flat(gated), mixer_out))
 
     n2, r2 = enter(x1, 1)
-    y_a, kept_a = ffn_forward(links, n2, ffn_a_in, ffn_a_out)
-    x2 = x1 + links.scatter_rows(y_a)
+    g4_low = regroup(out_grad.reshape(local, features), nz, 1)
+    dy4 = links.gather_rows(g4_low)
+    hid_a, kept_a = ffn_forward(after(n2, dy4), ffn_a_in, own[4])
+    x2 = x1 + links.scatter_rows(dot(hid_a, ffn_a_out), other[4])
 
     n3, r3 = enter(x2, 2)
     mix, low = attention_forward(pieces(times(n3, *qkv_in)), tables)
-    x3 = x2 + links.scatter_rows(dot(after(flat(mix), own[5]), attn_out))
+    mix = after(flat(mix), other[5])
+    mix_own, mix_other = split_y(links, regroup(mix, nz, 1))
+    x3 = x2 + links.scatter_rows(dot(mix, attn_out), own[6])
 
     n4, r4 = enter(x3, 3)
-    y_b, kept_b = ffn_forward(links, n4, ffn_b_in, ffn_b_out)
-    x4 = x3 + links.scatter_rows(y_b)
-    block_out = ungroup(x4, nz, 1).astype(bf16).reshape(hidden_in.shape)
-
-    def leave(g, x, r, i, d_normed, *order):
-        d_n = links.own_first(links.scatter_rows(d_normed, *order))
+    n4 = after(n4, mix_own, mix_other, other[6])
+    hid_b, kept_b = ffn_forward(n4, ffn_b_in)
+
+    def leave(g, x, r, i, d_normed, *order, late=()):
+        d_n = links.own_first(after(links.scatter_rows(d_normed, *order), *late))
         d_x, d_gain = norm_backward(x, r, gains[i : i + 1], d_n)
         return g + d_x, d_gain
 
-    g4_low = regroup(out_grad.reshape(local, features), nz, 1)
     g4 = g4_low.astype(f32)
     fh = features // 2
-    dy4 = links.gather_rows(g4_low)
-    d_n4, b_in, b_out = ffn_backward(links, dy4, kept_b, ffn_b_in, ffn_b_out)
-    g3, gain_d = leave(g4, x3, r4, 3, d_n4, b_out.finish(d_n4))
+    b_in, b_out, d_pair = ffn_backward(links, dy4, kept_b, ffn_b_out)
+    x4 = x3 + links.scatter_rows(dot(after(hid_b, b_in.product), ffn_b_out))
+    block_out = ungroup(x4, nz, 1).astype(bf16).reshape(hidden_in.shape)
+    d_n4 = product_nt(d_pair, ffn_b_in)
+    g3, gain_d = leave(g4, x3, r4, 3, d_n4, b_out.came)
 
     dy3 = links.gather_rows(g3.astype(bf16))
-    mix_own, mix_other = split_y(links, regroup(flat(mix), nz, 1))
-    a_out = Sent(links, mix_own, mix_other, dy3, b_in.came)
-    d_mix = dot_nt(after(dy3, a_out.product), attn_out).astype(bf16)
+    dy3 = after(dy3, b_out.finish(g3))
+    a_out = Sent(links, mix_own, mix_other, [dy3], b_in.came)
+    d_mix = product_nt([after(dy3, a_out.product)], [attn_out])
     d_qkv = flat(attention_backward(low, pieces(d_mix), tables))
-    q_in = Sent(links, n3[:, :fh], n3[:, fh:], d_qkv, a_out.came)
-    d_qkv = after(d_qkv, q_in.product, b_in.finish(b_out.out, q_in.product))
-    d_n3 = back_times(d_qkv, *qkv_in)
+    q_in = Sent(links, n3[:, :fh], n3[:, fh:], [d_qkv], a_out.came)
+    done = b_in.finish(b_out.terms[0], q_in.product, block_out)
+    d_n3 = product_nt([after(d_qkv, done, a_out.came)], qkv_in)
     g2, gain_c = leave(g3, x2, r3, 2, d_n3, a_out.finish(d_n3))
 
     dy2 = links.gather_rows(g2.astype(bf16))
-    d_n2, f_in, f_out = ffn_backward(
-        links, after(dy2, q_in.finish(dy2)), kept_a, ffn_a_in, ffn_a_out, q_in.came
-    )
-    d_n2 = after(d_n2, f_out.finish(b_in.out, d_n2))
-    g1, gain_b = leave(g2, x1, r2, 1, d_n2)
+    dy2 = after(dy2, q_in.came)
+    f_in, f_out, d_pair = ffn_backward(
+        links, dy2, kept_a, ffn_a_out, q_in.came, finish=q_in
+    )
+    d_n2 = product_nt(d_pair, ffn_a_in)
+    g1, gain_b = leave(g2, x1, r2, 1, d_n2, f_out.came)
 
     dy1 = links.gather_rows(g1.astype(bf16))
+    dy1 = after(dy1, f_out.finish(b_in.terms[0], g1))
     gated = flat(gated)
-    m_out = Sent(links, *split_y(links, gated), dy1, f_in.came)
-    d_gated = pieces(dot_nt(after(dy1, m_out.product), mixer_out))
+    m_out = Sent(links, *split_y(links, gated), [dy1], f_in.came)
+    d_gated = pieces(product_nt([after(dy1, m_out.product)], [mixer_out]))
     d_dt, d_val, d_z, d_bc, d_rate, sums = scan_backward(
         slots, ext, wdt, values, pre, par, rate, keep, d_gated, scanned, states
     )
     d_dt, d_z = flat(d_dt), flat(d_z)
-    m_z = Sent(links, n1[:, :fh], n1[:, fh:], d_z, m_out.came)
-    d_dt = after(d_dt, m_z.product, f_in.finish(m_z.product, a_out.out, q_in.out, f_out.out))
+    m_z = Sent(links, n1[:, :fh], n1[:, fh:], [d_z], m_out.came)
+    d_dt = after(d_dt, f_in.finish(m_z.product, a_out.terms[0], q_in.terms[0], f_out.terms[0]))
     d_bc = d_bc[:, :, :, 0, :].reshape(PIECES, micro, 2, rows, STATE)
     d_bc = jnp.swapaxes(d_bc, 2, 3).reshape(PIECES * local, 2 * STATE)
     d_ext = links.sum_rows(jnp.concatenate([dot_nt(d_dt, wdt), d_bc], axis=1))
-    grad_dt = dot_tn(flat(ext)[:, :RANK], d_dt)
+    d_x, conv_sums = conv_backward(slots, pieces(d_ext), d_val, pre, masks, par, wx)
+    d_x = flat(d_x)
+    m_x = Sent(links, n1[:, :fh], n1[:, fh:], [d_x], m_z.came)
+    d_x = after(d_x, m_x.product, m_out.finish(m_x.product))
+
+    grad_dt = dot_tn(d_dt, flat(ext)[:, :RANK])
     grad_x = dot_tn(flat(values), d_ext)
-    d_x, conv_sums = conv_backward(
-        slots, pieces(after(d_ext, m_out.finish(d_ext, direct=True))), d_val, pre, masks, par, wx
-    )
-    d_x = flat(d_x)
-    m_x = Sent(links, n1[:, :fh], n1[:, fh:], d_x, m_z.came)
-    d_x = after(d_x, m_x.product)
-    d_n1 = back_times(d_x, *[w[:, :width] for w in mixer_in])
-    d_n1 = d_n1 + back_times(d_z, *[w[:, width:] for w in mixer_in])
-    d_n1 = after(d_n1, m_z.finish(d_n1, f_in.out))
-    g0, gain_a = leave(g1, x0, r1, 0, d_n1)
+    grad_table = jnp.concatenate([conv_sums[: CONV + 1], sums[:2], d_rate * rate], axis=0)
+    packed = jnp.concatenate([grad_x, grad_dt, grad_table.T], axis=1)
+    summed = links.scatter_small(after(packed, m_x.product).reshape(2, nz, -1, packed.shape[1]))
+    states = w_xproj.shape[1]
+    grads = [
+        summed[:, :states],
+        summed[:, states : states + RANK].T,
+        summed[:, states + RANK :].T,
+    ]
+
+    d_n1 = product_nt([d_x, d_z], mixer_in)
+    done = m_z.finish(d_n1, *f_in.terms, direct=True)
+    last = m_x.finish(done, direct=True)
+    g0, gain_a = leave(g1, x0, r1, 0, d_n1, done, summed, late=(last, *m_z.terms))
     input_grad = ungroup(g0, nz, 1).astype(bf16).reshape(hidden_in.shape)
-    m_x.finish(direct=True)
-
-    grad_table = jnp.concatenate([conv_sums[: CONV + 1], sums[:2], d_rate * rate], axis=0)
+
+    def grad_of(sent, like):
+        return spread(sent.land(done), nz, like.shape)
+
+    outs = [
+        grad_of(f_in, w_ffn_a_in),
+        grad_of(f_out, w_ffn_a_out),
+        q_in.land(done)[0].astype(f32).reshape(w_qkv.shape),
+        grad_of(a_out, w_attn_out),
+        grad_of(b_in, w_ffn_b_in),
+        grad_of(b_out, w_ffn_b_out),
+    ]
     grad_gains = jnp.stack([gain_a, gain_b, gain_c, gain_d])
-
-    def by_owner(v, axis):
-        u = v.shape[axis] // dp
-        v = v.reshape(v.shape[:axis] + (2, nz, u) + v.shape[axis + 1 :])
-        return jnp.moveaxis(v, (axis, axis + 1), (0, 1)).reshape(2, nz, -1)
-
-    packed = jnp.concatenate(
-        [by_owner(grad_gains, 1), by_owner(grad_x, 0), by_owner(grad_dt, 1), by_owner(grad_table, 1)],
-        axis=2,
-    )
-    summed = links.scatter_small(packed)
-    offset = 0
-    grads = []
-    for v in small:
-        grads.append(summed[offset : offset + v.size].reshape(v.shape))
-        offset += v.size
-    gain_total = grads[0]
+    grad_gains = jnp.moveaxis(grad_gains.reshape(4, 2, nz, -1), 0, 2)
+    gain_total = links.scatter_small(after(grad_gains, *outs, *m_x.terms))
     gain_total = gain_total + links.swap_core(gain_total)
     gain_total = gain_total + links.swap_x(gain_total)
-
-    def in_grad(v, like, group):
-        v = v.reshape(like.shape)
-        return ungroup(v, nz, 2) if group else v
-
-    def out_grad_of(v):
-        return ungroup(v.out, nz, 1)
-
-    return (
-        block_out,
-        input_grad,
-        gain_total,
-        jnp.stack([ungroup(m_x.out, nz, 1), ungroup(m_z.out, nz, 1)], axis=1),
-        grads[1],
-        grads[2],
-        grads[3],
-        out_grad_of(m_out),
-        in_grad(f_in.out, w_ffn_a_in, True),
-        out_grad_of(f_out),
-        in_grad(q_in.out, w_qkv, False),
-        out_grad_of(a_out),
-        in_grad(b_in.out, w_ffn_b_in, True),
-        out_grad_of(b_out),
-    )
+    grad_out = spread(m_out.land(last), nz, w_mixer_out.shape)
+    grad_z = ungroup(sum(v.astype(f32) for v in m_z.land(last)), nz, 1)
+    grad_x_in = ungroup(sum(v.astype(f32) for v in m_x.land()), nz, 1)
+    grad_in = jnp.stack([grad_x_in, grad_z], axis=1)
+    return (block_out, input_grad, gain_total, grad_in, *grads, grad_out, *outs)
 
 
 def solution(mesh):

time: 993 us -> 941 us (0.948)
  matrix products: 138 us -> 34.7 us
  Pallas kernels: 77.1 us -> 167 us
  waiting for transfers between devices: 452 us -> 383 us
  starting transfers between devices: 102 us -> 137 us
    dot_general x47 -> x15, matrix products: 138 us -> 34.7 us  [dot(): return lax.dot_general(a, b, (dims, ((), ())), preferred_element_type=out)]
    pallas_call x0 -> x32, Pallas kernels: none -> 90.1 us  [the longest x18 44.8 us: product_tn(): pl.pallas_call(lambda *refs: tn_kernel(len(rights), bool(adds), *refs), g...]
    ppermute x17 -> x18, waiting for transfers between devices: 227 us -> 194 us  [swap_y(): return lax.ppermute(v, 'dp', [(i, i ^ 1) for i in range(self.dp)])]
    all_gather x7, waiting for transfers between devices: 80.8 us -> 60 us  [gather_z(): lax.all_gather(v, 'dp', axis=0, tiled=True, axis_index_groups=self.groups)]
    ppermute x27, starting transfers between devices: 47.1 us -> 66.1 us  [swap_core(): return lax.ppermute(v, 'tensor', [(i, i ^ 1) for i in range(PIECES)])]
    unnamed x286 -> x385, local copies, waits for them, and re-layouts: 30.1 us -> 48.7 us
    ppermute x19, waiting for transfers between devices: 94.3 us -> 77.4 us  [swap_x(): return lax.ppermute(v, 'tensor', [(i, i ^ 2) for i in range(PIECES)])]
    reshape x13 -> x1, local copies, waits for them, and re-layouts: 14 us -> 0.97 us  [per_device(): q_in.land(done)[0].astype(f32).reshape(w_qkv.shape)]
  transfers between devices with their start and end apart: 93 -> 97, of which waited for: 49 -> 47; matrix products, arithmetic and copies ran while one was open for 28% -> 18% of each run, Pallas kernels for 8% -> 17%
where the time goes in v3:
time: 941 us; the launch traced here: 928 us
  waiting for transfers between devices  383 us (41%)
  Pallas kernels  167 us (18%)
  starting transfers between devices  137 us (15%)
  local copies, waits for them, and re-layouts  123 us (13%)
  other arithmetic  66.5 us (7%)
  matrix products  34.7 us (4%)
  between operations  17.2 us (2%)
    ppermute x18, waiting for transfers between devices, swap_y(): return lax.ppermute(v, 'dp', [(i, i ^ 1) for i in range(self.dp)])  194 us
    ppermute x19, waiting for transfers between devices, swap_x(): return lax.ppermute(v, 'tensor', [(i, i ^ 2) for i in range(PIECES)])  77.4 us
    ppermute x27, starting transfers between devices, swap_core(): return lax.ppermute(v, 'tensor', [(i, i ^ 1) for i in range(PIECES)])  66.1 us
    all_gather x7, waiting for transfers between devices, gather_z(): lax.all_gather(v, 'dp', axis=0, tiled=True, axis_index_groups=self.groups)  60 us
    unnamed x385, local copies, waits for them, and re-layouts  48.7 us
    pallas_call x18, Pallas kernels, product_tn(): pl.pallas_call(lambda *refs: tn_kernel(len(rights), bool(adds), *refs), g...  44.8 us
    pallas_call x1, Pallas kernels, scan_backward(): pl.pallas_call(scan_bwd_kernel, grid_spec=grid, out_shape=[jax.ShapeDtype...  36.7 us
    dot_general x15, matrix products, dot(): return lax.dot_general(a, b, (dims, ((), ())), preferred_element_type=out)  34.7 us
  transfers between devices with their start and end apart: 97, of which 47 were waited for; matrix products, arithmetic and copies ran while one was open for 18% of the time, Pallas kernels for 17%

profile of v3, /device:TPU:9, one launch (start us, length us, event | category | flops | bytes accessed | tf_op | source)
XLA Modules:
  0.0 927.9 jit_solution(3960781432792445622)
XLA Ops:
  7.2 3.5 reshape.406
  37.2 3.3 collective-permute-done.3
  40.6 4.0 collective-permute-done.2
  48.8 20.6 %all-gather.8.cloned.1.call-done.refs_2_ = bf16[768,1536]{1,0:T(8,128)(2,1)} async-done(((bf16[192,1536]{1,0:T(8,128)(2,1)}), bf16[768,1536]{1,0:T(8,128)(2,1)}) %all-gather.8.cloned.1.call-update) | async-done | bytes 2359312 | tf_op jit(solution)/shard_map/all_gather | solution.py:670
  75.2 6.0 collective-permute-done.7
  84.2 28.5 %all-gather.10.cloned.1.call-done = bf16[576,1536]{1,0:T(8,128)(2,1)} async-done(((bf16[144,1536]{1,0:T(8,128)(2,1)}), bf16[576,1536]{1,0:T(8,128)(2,1)}) %all-gather.10.cloned.1.call-update) | async-done | bytes 1769488 | tf_op jit(solution)/shard_map/all_gather | solution.py:670
  112.7 9.4 %collective-permute-done.10.refs_3_ = bf16[768,1536]{1,0:T(8,128)(2,1)} collective-permute-done((bf16[768,1536]{1,0:T(8,128)(2,1)}, bf16[768,1536]{1,0:T(8,128)(2,1)}, u32[]{:S(2)}, u32[]{:S(2)}) %collective-permute-start.10) | collective-permute-done | bytes 2359328 | tf_op jit(solution)/shard_map/ppermute | solution.py:655
  129.4 3.8 conv_forward.1
  144.3 23.2 %scan_forward.1 = (bf16[4,2,64,768]{3,2,1,0:T(8,128)(2,1)S(1)}, f32[4,2,64,768]{3,2,1,0:T(8,128)S(1)}, bf16[8,64,16,768]{3,2,1,0:T(8,128)(2,1)}) custom-call(s32[4]{0:T(128)S(1)} %pad_add_fusion.2.slot, bf16[4,2,64,128]{3,2,1,0:T(8,128)(2,1)S(1)} %bitcast.204, bf16[96,768]{1,0:T(8,128)(2,1)S(1)} %reshape.411.wdt_ref, bf16[4,2,64,768]{3,2,1,0:T(8,128)(2,1)S(1)} %copy-done.23, ...), custom_call_target="tpu_custom_call" | custom-call | flops 1 | bytes 1 | tf_op jit(solution)/shard_map/scan_forward/pallas_call | solution.py:395
  184.1 5.4 collective-permute-done.15
  192.7 3.8 collective-permute-start.20
  197.9 3.5 collective-permute-start.21
  201.4 4.9 collective-permute-done.16
  209.3 5.8 all-gather.16.cloned.1.call-done
  215.2 30.2 %collective-permute-done.22.refs_3_ = bf16[768,2048]{1,0:T(8,128)(2,1)} collective-permute-done((bf16[768,2048]{1,0:T(8,128)(2,1)}, bf16[768,2048]{1,0:T(8,128)(2,1)}, u32[]{:S(2)}, u32[]{:S(2)}) %collective-permute-start.22) | collective-permute-done | bytes 3145760 | tf_op jit(solution)/shard_map/ppermute | solution.py:655
  248.9 3.8 fusion.53
  252.7 3.5 all-gather.14.cloned.1.call-done.refs_1_
  256.2 4.9 convolution_add_fusion.3
  263.3 16.5 %collective-permute-done.23 = bf16[512,1536]{1,0:T(8,128)(2,1)} collective-permute-done((bf16[512,1536]{1,0:T(8,128)(2,1)}, bf16[512,1536]{1,0:T(8,128)(2,1)}, u32[]{:S(2)}, u32[]{:S(2)}) %collective-permute-start.23) | collective-permute-done | bytes 1572896 | tf_op jit(solution)/shard_map/ppermute | solution.py:655
  297.5 19.9 %collective-permute-done.25.refs_2_ = bf16[768,1152]{1,0:T(8,128)(2,1)} collective-permute-done((bf16[768,1152]{1,0:T(8,128)(2,1)S(1)}, bf16[768,1152]{1,0:T(8,128)(2,1)}, u32[]{:S(2)}, u32[]{:S(2)}) %collective-permute-start.25) | collective-permute-done | bytes 1769504 | tf_op jit(solution)/shard_map/ppermute | solution.py:655
  331.7 4.9 collective-permute-start.28
  336.6 4.7 collective-permute-start.29
  350.3 3.2 fusion.43
  357.7 29.2 %collective-permute-done.30.refs_3_ = bf16[768,2048]{1,0:T(8,128)(2,1)} collective-permute-done((bf16[768,2048]{1,0:T(8,128)(2,1)}, bf16[768,2048]{1,0:T(8,128)(2,1)}, u32[]{:S(2)}, u32[]{:S(2)}) %collective-permute-start.30) | collective-permute-done | bytes 3145760 | tf_op jit(solution)/shard_map/ppermute | solution.py:655
  388.0 4.7 collective-permute-start.31
  399.0 7.6 collective-permute-done.32
  412.3 6.0 collective-permute-done.33
  420.4 12.8 %collective-permute-done.36 = bf16[512,1536]{1,0:T(8,128)(2,1)} collective-permute-done((bf16[512,1536]{1,0:T(8,128)(2,1)}, bf16[512,1536]{1,0:T(8,128)(2,1)}, u32[]{:S(2)}, u32[]{:S(2)}) %collective-permute-start.36) | collective-permute-done | bytes 1572896 | tf_op jit(solution)/shard_map/ppermute | solution.py:655
  433.2 4.6 maximum_select_fusion.1.w
  439.0 3.9 fusion.49
  448.6 4.7 gate_backward.2
  453.3 3.5 product_tn.19
  456.8 7.6 product_nt.6
  471.4 10.2 %collective-permute-done.40.refs_2_ = bf16[512,1536]{1,0:T(8,128)(2,1)S(1)} collective-permute-done((bf16[512,1536]{1,0:T(8,128)(2,1)S(1)}, bf16[512,1536]{1,0:T(8,128)(2,1)S(1)}, u32[]{:S(2)}, u32[]{:S(2)}) %collective-permute-start.40) | collective-permute-done | bytes 1572896 | tf_op jit(solution)/shard_map/ppermute | solution.py:655
  484.6 5.3 collective-permute-done.41
  490.9 7.4 collective-permute-done.38
  503.5 3.5 collective-permute-start.43
  509.6 4.1 collective-permute-start.44
  520.6 4.0 attention_backward.1
  527.3 22.9 %collective-permute-done.45.refs_3_ = bf16[768,2048]{1,0:T(8,128)(2,1)} collective-permute-done((bf16[768,2048]{1,0:T(8,128)(2,1)}, bf16[768,2048]{1,0:T(8,128)(2,1)}, u32[]{:S(2)}, u32[]{:S(2)}) %collective-permute-start.45) | collective-permute-done | bytes 3145760 | tf_op jit(solution)/shard_map/ppermute | solution.py:655
  552.6 4.0 product_tn.23
  559.8 9.8 %collective-permute-done.46.refs_2_ = bf16[192,1536]{1,0:T(8,128)(2,1)S(1)} collective-permute-done((bf16[192,1536]{1,0:T(8,128)(2,1)}, bf16[192,1536]{1,0:T(8,128)(2,1)S(1)}, u32[]{:S(2)}, u32[]{:S(2)}) %collective-permute-start.46) | collective-permute-done | bytes 589856 | tf_op jit(solution)/shard_map/ppermute | solution.py:655
  571.3 5.1 product_nt.8
  578.5 4.6 collective-permute-start.47
  589.4 7.9 collective-permute-done.48
  602.7 6.9 collective-permute-done.49
  615.0 13.1 %collective-permute-done.52.refs_2_ = bf16[768,1152]{1,0:T(8,128)(2,1)} collective-permute-done((bf16[768,1152]{1,0:T(8,128)(2,1)}, bf16[768,1152]{1,0:T(8,128)(2,1)}, u32[]{:S(2)}, u32[]{:S(2)}) %collective-permute-start.52) | collective-permute-done | bytes 1769504 | tf_op jit(solution)/shard_map/ppermute | solution.py:655
  633.4 3.3 product_tn.26
  640.4 4.8 gate_backward.3
  649.1 7.2 product_nt.9
  666.8 6.8 collective-permute-done.55
  681.0 3.5 collective-permute-start.57
  684.5 4.0 collective-permute-done.56
  688.5 4.1 collective-permute-start.58
  700.7 36.7 %scan_backward.1 = (bf16[4,2,64,768]{3,2,1,0:T(8,128)(2,1)S(1)}, f32[4,2,64,768]{3,2,1,0:T(8,128)S(1)}, bf16[4,2,64,768]{3,2,1,0:T(8,128)(2,1)S(1)}, f32[4,2,2,8...) custom-call(s32[4]{0:T(128)S(1)} %pad_add_fusion.2.slot, ...), custom_call_target="tpu_custom_call" | custom-call | flops 1 | bytes 1 | tf_op jit(solution)/shard_map/scan_backward/pallas_call | solution.py:441
  744.0 5.3 product_tn.31
  758.8 18.6 %collective-permute-done.62.refs_2_ = bf16[384,1536]{1,0:T(8,128)(2,1)} collective-permute-done((bf16[384,1536]{1,0:T(8,128)(2,1)}, bf16[384,1536]{1,0:T(8,128)(2,1)}, u32[]{:S(2)}, u32[]{:S(2)}) %collective-permute-start.62) | collective-permute-done | bytes 1179680 | tf_op jit(solution)/shard_map/ppermute | solution.py:655
  789.6 5.9 conv_backward.1
  797.9 3.2 product_tn.33
  809.0 5.7 product_nt.11
  824.8 3.4 collective-permute-done.68
  835.2 3.3 collective-permute-start.72
  848.5 12.8 %collective-permute-done.72 = bf16[192,768]{1,0:T(8,128)(2,1)} collective-permute-done((bf16[192,768]{1,0:T(8,128)(2,1)}, bf16[192,768]{1,0:T(8,128)(2,1)}, u32[]{:S(2)}, u32[]{:S(2)}) %collective-permute-start.72) | collective-permute-done | bytes 294944 | tf_op jit(solution)/shard_map/ppermute | solution.py:659
  865.1 15.0 %collective-permute-done.71 = bf16[192,768]{1,0:T(8,128)(2,1)} collective-permute-done((bf16[192,768]{1,0:T(8,128)(2,1)}, bf16[192,768]{1,0:T(8,128)(2,1)}, u32[]{:S(2)}, u32[]{:S(2)}) %collective-permute-start.71) | collective-permute-done | bytes 294944 | tf_op jit(solution)/shard_map/ppermute | solution.py:659
  (828 shorter events, 356.5 us)
Async XLA Ops:
  7.2 62.2 %all-gather.8.cloned.1.call-start = ((), (), s32[]{:S(2)}) async-start(), calls=%async_computation.7 | async-start | bytes 2949120 | tf_op jit(solution)/shard_map/all_gather | solution.py:670
  12.8 99.9 %all-gather.10.cloned.1.call-start = ((), (), s32[]{:S(2)}) async-start(), calls=%async_computation.8 | async-start | bytes 2211840 | tf_op jit(solution)/shard_map/all_gather | solution.py:670
  22.8 153.4 %all-gather.12.cloned.1.call-start = ((), (), s32[]{:S(2)}) async-start(), calls=%async_computation.9 | async-start | bytes 3932160 | tf_op jit(solution)/shard_map/all_gather | solution.py:670
  23.6 191.6 %all-gather.16.cloned.1.call-start = ((), (), s32[]{:S(2)}) async-start(), calls=%async_computation.11 | async-start | bytes 1966080 | tf_op jit(solution)/shard_map/all_gather | solution.py:670
  26.5 10.7 %collective-permute-start.4 = (bf16[24480]{0:T(1024)(128)(2,1)S(1)}, bf16[24480]{0:T(1024)(128)(2,1)S(1)}, u32[]{:S(2)}, u32[]{:S(2)}) collective-permute-start(bf16[24480]{0:T(1024)(128)(2,1)S(1)} %pad_maximum_fusion.19), channel_id=1, source_target_pairs={{0,12},{4,16},{8,20},{12,24},{16,28},{20,0},{24,4},{28,8},{1,13},{... | collective-permute-start | bytes 146888 | tf_op jit(solution)/shard_map/ppermute | solution.py:683
  27.6 13.0 %collective-permute-start.3 = (bf16[24480]{0:T(1024)(128)(2,1)S(1)}, bf16[24480]{0:T(1024)(128)(2,1)S(1)}, u32[]{:S(2)}, u32[]{:S(2)}) collective-permute-start(bf16[24480]{0:T(1024)(128)(2,1)S(1)} %pad_maximum_fusion.19), channel_id=1, source_target_pairs={{0,16},{4,20},{8,24},{12,28},{16,0},{20,4},{24,8},{28,12},{1,17},{... | collective-permute-start | bytes 146888 | tf_op jit(solution)/shard_map/ppermute | solution.py:683
  29.7 14.9 %collective-permute-start.2 = (bf16[24480]{0:T(1024)(128)(2,1)S(1)}, bf16[24480]{0:T(1024)(128)(2,1)S(1)}, u32[]{:S(2)}, u32[]{:S(2)}) collective-permute-start(bf16[24480]{0:T(1024)(128)(2,1)S(1)} %pad_maximum_fusion.19), channel_id=1, source_target_pairs={{0,20},{4,24},{8,28},{12,0},{16,4},{20,8},{24,12},{28,16},{1,21},{... | collective-permute-start | bytes 146888 | tf_op jit(solution)/shard_map/ppermute | solution.py:683
  31.8 224.5 %all-gather.14.cloned.1.call-start = ((), (), s32[]{:S(2)}) async-start(), calls=%async_computation.10 | async-start | bytes 2211840 | tf_op jit(solution)/shard_map/all_gather | solution.py:670
  32.0 12.7 %collective-permute-start.1 = (bf16[24480]{0:T(1024)(128)(2,1)S(1)}, bf16[24480]{0:T(1024)(128)(2,1)S(1)}, u32[]{:S(2)}, u32[]{:S(2)}) collective-permute-start(bf16[24480]{0:T(1024)(128)(2,1)S(1)} %pad_maximum_fusion.19), channel_id=1, source_target_pairs={{0,24},{4,28},{8,0},{12,4},{16,8},{20,12},{24,16},{28,20},{1,25},{... | collective-permute-start | bytes 146888 | tf_op jit(solution)/shard_map/ppermute | solution.py:683
  33.5 11.3 %collective-permute-start = (bf16[24480]{0:T(1024)(128)(2,1)S(1)}, bf16[24480]{0:T(1024)(128)(2,1)S(1)}, u32[]{:S(2)}, u32[]{:S(2)}) collective-permute-start(bf16[24480]{0:T(1024)(128)(2,1)S(1)} %pad_maximum_fusion.19), channel_id=1, source_target_pairs={{0,28},{4,0},{8,4},{12,8},{16,12},{20,16},{24,20},{28,24},{1,29},{... | collective-permute-start | bytes 146888 | tf_op jit(solution)/shard_map/ppermute | solution.py:683
  69.4 52.7 %collective-permute-start.10 = (bf16[768,1536]{1,0:T(8,128)(2,1)}, bf16[768,1536]{1,0:T(8,128)(2,1)}, u32[]{:S(2)}, u32[]{:S(2)}) collective-permute-start(bf16[768,1536]{1,0:T(8,128)(2,1)} %all-gather.8.cloned.1.call-done.refs_2_), channel_id=1, source_target_pairs={{0,4},{4,0},{8,12},{12,8},{16,20},{20,16},{24,28},{28,24},{1,5},{5... | collective-permute-start | bytes 7077896 | tf_op jit(solution)/shard_map/ppermute | solution.py:655
  71.1 10.1 %collective-permute-start.7 = (bf16[128,1536]{1,0:T(8,128)(2,1)S(1)}, bf16[128,1536]{1,0:T(8,128)(2,1)S(1)}, u32[]{:S(2)}, u32[]{:S(2)}) collective-permute-start(bf16[128,1536]{1,0:T(8,128)(2,1)S(1)} %maximum_select_fusion.8), channel_id=1, source_target_pairs={{0,2},{1,3},{2,0},{3,1},{4,6},{5,7},{6,4},{7,5},{8,10},{9,11},{10,... | collective-permute-start | bytes 1179656 | tf_op jit(solution)/shard_map/ppermute | solution.py:667
  122.1 45.5 %collective-permute-start.13 = (bf16[576,1536]{1,0:T(8,128)(2,1)}, bf16[576,1536]{1,0:T(8,128)(2,1)}, u32[]{:S(2)}, u32[]{:S(2)}) collective-permute-start(bf16[576,1536]{1,0:T(8,128)(2,1)} %all-gather.10.cloned.1.call-done), channel_id=1, source_target_pairs={{0,4},{4,0},{8,12},{12,8},{16,20},{20,16},{24,28},{28,24},{1,5},{5... | collective-permute-start | bytes 5308424 | tf_op jit(solution)/shard_map/ppermute | solution.py:655
  137.0 183.7 %all-gather.18.cloned.1.call-start = ((), (), s32[]{:S(2)}) async-start(), calls=%async_computation.12 | async-start | bytes 3932160 | tf_op jit(solution)/shard_map/all_gather | solution.py:670
  176.2 69.1 %collective-permute-start.22 = (bf16[768,2048]{1,0:T(8,128)(2,1)}, bf16[768,2048]{1,0:T(8,128)(2,1)}, u32[]{:S(2)}, u32[]{:S(2)}) collective-permute-start(bf16[768,2048]{1,0:T(8,128)(2,1)} %all-gather.12.cloned.1.call-done.refs_2_), channel_id=1, source_target_pairs={{0,4},{4,0},{8,12},{12,8},{16,20},{20,16},{24,28},{28,24},{1,5},{5... | collective-permute-start | bytes 9437192 | tf_op jit(solution)/shard_map/ppermute | solution.py:655
  179.6 9.9 %collective-permute-start.15 = (bf16[128,1536]{1,0:T(8,128)(2,1)}, bf16[128,1536]{1,0:T(8,128)(2,1)}, u32[]{:S(2)}, u32[]{:S(2)}) collective-permute-start(bf16[128,1536]{1,0:T(8,128)(2,1)} %fusion.18), channel_id=1, source_target_pairs={{0,2},{1,3},{2,0},{3,1},{4,6},{5,7},{6,4},{7,5},{8,10},{9,11},{10,... | collective-permute-start | bytes 1179656 | tf_op jit(solution)/shard_map/ppermute | solution.py:667
  183.6 14.3 %collective-permute-start.19 = (bf16[128,1536]{1,0:T(8,128)(2,1)S(1)}, bf16[128,1536]{1,0:T(8,128)(2,1)}, u32[]{:S(2)}, u32[]{:S(2)}) collective-permute-start(bf16[128,1536]{1,0:T(8,128)(2,1)S(1)} %copy.309), channel_id=1, source_target_pairs={{0,2},{1,3},{2,0},{3,1},{4,6},{5,7},{6,4},{7,5},{8,10},{9,11},{10,... | collective-permute-start | bytes 1179656 | tf_op jit(solution)/shard_map/ppermute | solution.py:667
  183.9 212.1 %all-gather.20.cloned.1.call-start = ((), (), s32[]{:S(2)}) async-start(), calls=%async_computation.13 | async-start | bytes 1966080 | tf_op jit(solution)/shard_map/all_gather | solution.py:670
  191.4 14.9 %collective-permute-start.16 = (bf16[128,1536]{1,0:T(8,128)(2,1)S(1)}, bf16[128,1536]{1,0:T(8,128)(2,1)S(1)}, u32[]{:S(2)}, u32[]{:S(2)}) collective-permute-start(bf16[128,1536]{1,0:T(8,128)(2,1)S(1)} %maximum_select_fusion.9), channel_id=1, source_target_pairs={{0,2},{1,3},{2,0},{3,1},{4,6},{5,7},{6,4},{7,5},{8,10},{9,11},{10,... | collective-permute-start | bytes 1179656 | tf_op jit(solution)/shard_map/ppermute | solution.py:667
  192.7 15.5 %collective-permute-start.20 = (bf16[128,1536]{1,0:T(8,128)(2,1)S(1)}, bf16[128,1536]{1,0:T(8,128)(2,1)S(1)}, u32[]{:S(2)}, u32[]{:S(2)}) collective-permute-start(bf16[128,1536]{1,0:T(8,128)(2,1)S(1)} %copy.309), channel_id=1, source_target_pairs={{0,1},{1,0},{2,3},{3,2},{4,5},{5,4},{6,7},{7,6},{8,9},{9,8},{10,11... | collective-permute-start | bytes 1179656 | tf_op jit(solution)/shard_map/ppermute | solution.py:664
  197.9 10.3 %collective-permute-start.21 = (bf16[128,1536]{1,0:T(8,128)(2,1)}, bf16[128,1536]{1,0:T(8,128)(2,1)S(1)}, u32[]{:S(2)}, u32[]{:S(2)}) collective-permute-start(bf16[128,1536]{1,0:T(8,128)(2,1)} %collective-permute-done.19), channel_id=1, source_target_pairs={{0,1},{1,0},{2,3},{3,2},{4,5},{5,4},{6,7},{7,6},{8,9},{9,8},{10,11... | collective-permute-start | bytes 1179656 | tf_op jit(solution)/shard_map/ppermute | solution.py:664
  201.4 45.2 %collective-permute-start.17 = (bf16[128,1536]{1,0:T(8,128)(2,1)S(1)}, bf16[128,1536]{1,0:T(8,128)(2,1)S(1)}, u32[]{:S(2)}, u32[]{:S(2)}) collective-permute-start(bf16[128,1536]{1,0:T(8,128)(2,1)S(1)} %maximum_select_fusion.9), channel_id=1, source_target_pairs={{0,1},{1,0},{2,3},{3,2},{4,5},{5,4},{6,7},{7,6},{8,9},{9,8},{10,11... | collective-permute-start | bytes 1179656 | tf_op jit(solution)/shard_map/ppermute | solution.py:664
  206.3 41.1 %collective-permute-start.18 = (bf16[128,1536]{1,0:T(8,128)(2,1)S(1)}, bf16[128,1536]{1,0:T(8,128)(2,1)}, u32[]{:S(2)}, u32[]{:S(2)}) collective-permute-start(bf16[128,1536]{1,0:T(8,128)(2,1)S(1)} %collective-permute-done.16), channel_id=1, source_target_pairs={{0,1},{1,0},{2,3},{3,2},{4,5},{5,4},{6,7},{7,6},{8,9},{9,8},{10,11... | collective-permute-start | bytes 1179656 | tf_op jit(solution)/shard_map/ppermute | solution.py:664
  245.3 34.5 %collective-permute-start.23 = (bf16[512,1536]{1,0:T(8,128)(2,1)}, bf16[512,1536]{1,0:T(8,128)(2,1)}, u32[]{:S(2)}, u32[]{:S(2)}) collective-permute-start(bf16[512,1536]{1,0:T(8,128)(2,1)} %all-gather.16.cloned.1.call-done), channel_id=1, source_target_pairs={{0,4},{4,0},{8,12},{12,8},{16,20},{20,16},{24,28},{28,24},{1,5},{5... | collective-permute-start | bytes 4718600 | tf_op jit(solution)/shard_map/ppermute | solution.py:655
  279.8 37.6 %collective-permute-start.25 = (bf16[768,1152]{1,0:T(8,128)(2,1)S(1)}, bf16[768,1152]{1,0:T(8,128)(2,1)}, u32[]{:S(2)}, u32[]{:S(2)}) collective-permute-start(bf16[768,1152]{1,0:T(8,128)(2,1)S(1)} %copy-done.17), channel_id=1, source_target_pairs={{0,4},{4,0},{8,12},{12,8},{16,20},{20,16},{24,28},{28,24},{1,5},{5... | collective-permute-start | bytes 5308424 | tf_op jit(solution)/shard_map/ppermute | solution.py:655
  292.0 258.2 %reduce-scatter.8.cloned.1.call-start = ((), (), s32[]{:S(2)}) async-start(), calls=%async_computation.14 | async-start | bytes 1966080 | tf_op jit(solution)/shard_map/reduce_scatter | solution.py:673
  320.7 66.2 %collective-permute-start.30 = (bf16[768,2048]{1,0:T(8,128)(2,1)}, bf16[768,2048]{1,0:T(8,128)(2,1)}, u32[]{:S(2)}, u32[]{:S(2)}) collective-permute-start(bf16[768,2048]{1,0:T(8,128)(2,1)} %all-gather.18.cloned.1.call-done.refs_2_), channel_id=1, source_target_pairs={{0,4},{4,0},{8,12},{12,8},{16,20},{20,16},{24,28},{28,24},{1,5},{5... | collective-permute-start | bytes 9437192 | tf_op jit(solution)/shard_map/ppermute | solution.py:655
  331.7 16.6 %collective-permute-start.28 = (bf16[128,1536]{1,0:T(8,128)(2,1)}, bf16[128,1536]{1,0:T(8,128)(2,1)}, u32[]{:S(2)}, u32[]{:S(2)}) collective-permute-start(bf16[128,1536]{1,0:T(8,128)(2,1)} %maximum_select_fusion.10), channel_id=1, source_target_pairs={{0,1},{1,0},{2,3},{3,2},{4,5},{5,4},{6,7},{7,6},{8,9},{9,8},{10,11... | collective-permute-start | bytes 1179656 | tf_op jit(solution)/shard_map/ppermute | solution.py:664
  336.6 11.7 %collective-permute-start.29 = (bf16[128,1536]{1,0:T(8,128)(2,1)}, bf16[128,1536]{1,0:T(8,128)(2,1)}, u32[]{:S(2)}, u32[]{:S(2)}) collective-permute-start(bf16[128,1536]{1,0:T(8,128)(2,1)} %collective-permute-done.27), channel_id=1, source_target_pairs={{0,1},{1,0},{2,3},{3,2},{4,5},{5,4},{6,7},{7,6},{8,9},{9,8},{10,11... | collective-permute-start | bytes 1179656 | tf_op jit(solution)/shard_map/ppermute | solution.py:664
  396.1 10.5 %collective-permute-start.32 = (bf16[128,1536]{1,0:T(8,128)(2,1)S(1)}, bf16[128,1536]{1,0:T(8,128)(2,1)}, u32[]{:S(2)}, u32[]{:S(2)}) collective-permute-start(bf16[128,1536]{1,0:T(8,128)(2,1)S(1)} %fusion.12), channel_id=1, source_target_pairs={{0,2},{1,3},{2,0},{3,1},{4,6},{5,7},{6,4},{7,5},{8,10},{9,11},{10,... | collective-permute-start | bytes 1179656 | tf_op jit(solution)/shard_map/ppermute | solution.py:667
  397.6 35.6 %collective-permute-start.36 = (bf16[512,1536]{1,0:T(8,128)(2,1)}, bf16[512,1536]{1,0:T(8,128)(2,1)}, u32[]{:S(2)}, u32[]{:S(2)}) collective-permute-start(bf16[512,1536]{1,0:T(8,128)(2,1)} %all-gather.20.cloned.1.call-done), channel_id=1, source_target_pairs={{0,4},{4,0},{8,12},{12,8},{16,20},{20,16},{24,28},{28,24},{1,5},{5... | collective-permute-start | bytes 4718600 | tf_op jit(solution)/shard_map/ppermute | solution.py:655
  411.0 26.8 %collective-permute-start.34 = (bf16[128,1536]{1,0:T(8,128)(2,1)S(1)}, bf16[128,1536]{1,0:T(8,128)(2,1)S(1)}, u32[]{:S(2)}, u32[]{:S(2)}) collective-permute-start(bf16[128,1536]{1,0:T(8,128)(2,1)S(1)} %maximum_select_fusion.11), channel_id=1, source_target_pairs={{0,1},{1,0},{2,3},{3,2},{4,5},{5,4},{6,7},{7,6},{8,9},{9,8},{10,11... | collective-permute-start | bytes 1179656 | tf_op jit(solution)/shard_map/ppermute | solution.py:664
  418.3 19.5 %collective-permute-start.35 = (bf16[128,1536]{1,0:T(8,128)(2,1)}, bf16[128,1536]{1,0:T(8,128)(2,1)S(1)}, u32[]{:S(2)}, u32[]{:S(2)}) collective-permute-start(bf16[128,1536]{1,0:T(8,128)(2,1)} %collective-permute-done.33), channel_id=1, source_target_pairs={{0,1},{1,0},{2,3},{3,2},{4,5},{5,4},{6,7},{7,6},{8,9},{9,8},{10,11... | collective-permute-start | bytes 1179656 | tf_op jit(solution)/shard_map/ppermute | solution.py:664
  447.2 34.4 %collective-permute-start.40 = (bf16[512,1536]{1,0:T(8,128)(2,1)S(1)}, bf16[512,1536]{1,0:T(8,128)(2,1)S(1)}, u32[]{:S(2)}, u32[]{:S(2)}) collective-permute-start(bf16[512,1536]{1,0:T(8,128)(2,1)S(1)} %product_tn.18), channel_id=1, source_target_pairs={{0,4},{4,0},{8,12},{12,8},{16,20},{20,16},{24,28},{28,24},{1,5},{5... | collective-permute-start | bytes 4718600 | tf_op jit(solution)/shard_map/ppermute | solution.py:655
  483.1 15.2 %collective-permute-start.38 = (bf16[128,1536]{1,0:T(8,128)(2,1)S(1)}, bf16[128,1536]{1,0:T(8,128)(2,1)S(1)}, u32[]{:S(2)}, u32[]{:S(2)}) collective-permute-start(bf16[128,1536]{1,0:T(8,128)(2,1)S(1)} %fusion.8), channel_id=1, source_target_pairs={{0,2},{1,3},{2,0},{3,1},{4,6},{5,7},{6,4},{7,5},{8,10},{9,11},{10,... | collective-permute-start | bytes 1179656 | tf_op jit(solution)/shard_map/ppermute | solution.py:667
  483.3 66.9 %collective-permute-start.45 = (bf16[768,2048]{1,0:T(8,128)(2,1)}, bf16[768,2048]{1,0:T(8,128)(2,1)}, u32[]{:S(2)}, u32[]{:S(2)}) collective-permute-start(bf16[768,2048]{1,0:T(8,128)(2,1)} %product_tn.19), channel_id=1, source_target_pairs={{0,4},{4,0},{8,12},{12,8},{16,20},{20,16},{24,28},{28,24},{1,5},{5... | collective-permute-start | bytes 9437192 | tf_op jit(solution)/shard_map/ppermute | solution.py:655
  502.0 174.1 %reduce-scatter.10.cloned.1.call-start = ((), (), s32[]{:S(2)}) async-start(), calls=%async_computation.15 | async-start | bytes 3932160 | tf_op jit(solution)/shard_map/reduce_scatter | solution.py:673
  503.5 13.3 %collective-permute-start.43 = (bf16[128,1536]{1,0:T(8,128)(2,1)S(1)}, bf16[128,1536]{1,0:T(8,128)(2,1)}, u32[]{:S(2)}, u32[]{:S(2)}) collective-permute-start(bf16[128,1536]{1,0:T(8,128)(2,1)S(1)} %copy-done.133), channel_id=1, source_target_pairs={{0,1},{1,0},{2,3},{3,2},{4,5},{5,4},{6,7},{7,6},{8,9},{9,8},{10,11... | collective-permute-start | bytes 1179656 | tf_op jit(solution)/shard_map/ppermute | solution.py:664
  558.4 185.6 %reduce-scatter.12.cloned.1.call-start = ((), (), s32[]{:S(2)}) async-start(), calls=%async_computation.16 | async-start | bytes 737280 | tf_op jit(solution)/shard_map/reduce_scatter | solution.py:673
  558.4 11.2 %collective-permute-start.46 = (bf16[192,1536]{1,0:T(8,128)(2,1)}, bf16[192,1536]{1,0:T(8,128)(2,1)S(1)}, u32[]{:S(2)}, u32[]{:S(2)}) collective-permute-start(bf16[192,1536]{1,0:T(8,128)(2,1)} %copy-done.86), channel_id=1, source_target_pairs={{0,4},{4,0},{8,12},{12,8},{16,20},{20,16},{24,28},{28,24},{1,5},{5... | collective-permute-start | bytes 1769480 | tf_op jit(solution)/shard_map/ppermute | solution.py:655
  586.8 10.5 %collective-permute-start.48 = (bf16[128,1536]{1,0:T(8,128)(2,1)S(1)}, bf16[128,1536]{1,0:T(8,128)(2,1)S(1)}, u32[]{:S(2)}, u32[]{:S(2)}) collective-permute-start(bf16[128,1536]{1,0:T(8,128)(2,1)S(1)} %fusion.4), channel_id=1, source_target_pairs={{0,2},{1,3},{2,0},{3,1},{4,6},{5,7},{6,4},{7,5},{8,10},{9,11},{10,... | collective-permute-start | bytes 1179656 | tf_op jit(solution)/shard_map/ppermute | solution.py:667
  588.2 39.8 %collective-permute-start.52 = (bf16[768,1152]{1,0:T(8,128)(2,1)}, bf16[768,1152]{1,0:T(8,128)(2,1)}, u32[]{:S(2)}, u32[]{:S(2)}) collective-permute-start(bf16[768,1152]{1,0:T(8,128)(2,1)} %product_tn.22), channel_id=1, source_target_pairs={{0,4},{4,0},{8,12},{12,8},{16,20},{20,16},{24,28},{28,24},{1,5},{5... | collective-permute-start | bytes 5308424 | tf_op jit(solution)/shard_map/ppermute | solution.py:655
  599.8 9.8 %collective-permute-start.49 = (bf16[128,1536]{1,0:T(8,128)(2,1)}, bf16[128,1536]{1,0:T(8,128)(2,1)}, u32[]{:S(2)}, u32[]{:S(2)}) collective-permute-start(bf16[128,1536]{1,0:T(8,128)(2,1)} %get-tuple-element.290), channel_id=1, source_target_pairs={{0,2},{1,3},{2,0},{3,1},{4,6},{5,7},{6,4},{7,5},{8,10},{9,11},{10,... | collective-permute-start | bytes 1179656 | tf_op jit(solution)/shard_map/ppermute | solution.py:667
  601.2 142.8 %reduce-scatter.14.cloned.1.call-start = ((), (), s32[]{:S(2)}) async-start(), calls=%async_computation.17 | async-start | bytes 2211840 | tf_op jit(solution)/shard_map/reduce_scatter | solution.py:673
  601.3 12.3 %collective-permute-start.50 = (bf16[128,1536]{1,0:T(8,128)(2,1)}, bf16[128,1536]{1,0:T(8,128)(2,1)S(1)}, u32[]{:S(2)}, u32[]{:S(2)}) collective-permute-start(bf16[128,1536]{1,0:T(8,128)(2,1)} %get-tuple-element.290), channel_id=1, source_target_pairs={{0,1},{1,0},{2,3},{3,2},{4,5},{5,4},{6,7},{7,6},{8,9},{9,8},{10,11... | collective-permute-start | bytes 1179656 | tf_op jit(solution)/shard_map/ppermute | solution.py:664
  630.6 34.7 %collective-permute-start.54 = (bf16[512,1536]{1,0:T(8,128)(2,1)}, bf16[512,1536]{1,0:T(8,128)(2,1)}, u32[]{:S(2)}, u32[]{:S(2)}) collective-permute-start(bf16[512,1536]{1,0:T(8,128)(2,1)} %product_tn.25), channel_id=1, source_target_pairs={{0,4},{4,0},{8,12},{12,8},{16,20},{20,16},{24,28},{28,24},{1,5},{5... | collective-permute-start | bytes 4718600 | tf_op jit(solution)/shard_map/ppermute | solution.py:655
  660.2 83.8 %reduce-scatter.16.cloned.1.call-start = ((), (), s32[]{:S(2)}) async-start(), calls=%async_computation.18 | async-start | bytes 1966080 | tf_op jit(solution)/shard_map/reduce_scatter | solution.py:673
  665.4 78.6 %collective-permute-start.59 = (bf16[768,2048]{1,0:T(8,128)(2,1)}, bf16[768,2048]{1,0:T(8,128)(2,1)}, u32[]{:S(2)}, u32[]{:S(2)}) collective-permute-start(bf16[768,2048]{1,0:T(8,128)(2,1)} %copy-done.44), channel_id=1, source_target_pairs={{0,4},{4,0},{8,12},{12,8},{16,20},{20,16},{24,28},{28,24},{1,5},{5... | collective-permute-start | bytes 9437192 | tf_op jit(solution)/shard_map/ppermute | solution.py:655
  680.7 150.6 %reduce-scatter.18.cloned.1.call-start = ((), (), s32[]{:S(2)}) async-start(), calls=%async_computation.19 | async-start | bytes 3932160 | tf_op jit(solution)/shard_map/reduce_scatter | solution.py:673
  681.0 14.9 %collective-permute-start.57 = (bf16[128,1536]{1,0:T(8,128)(2,1)}, bf16[128,1536]{1,0:T(8,128)(2,1)S(1)}, u32[]{:S(2)}, u32[]{:S(2)}) collective-permute-start(bf16[128,1536]{1,0:T(8,128)(2,1)} %get-tuple-element.287), channel_id=1, source_target_pairs={{0,1},{1,0},{2,3},{3,2},{4,5},{5,4},{6,7},{7,6},{8,9},{9,8},{10,11... | collective-permute-start | bytes 1179656 | tf_op jit(solution)/shard_map/ppermute | solution.py:664
  749.3 140.3 %reduce-scatter.20.cloned.1.call-start = ((), (), s32[]{:S(2)}) async-start(), calls=%async_computation.20 | async-start | bytes 1474560 | tf_op jit(solution)/shard_map/reduce_scatter | solution.py:673
  749.4 28.0 %collective-permute-start.62 = (bf16[384,1536]{1,0:T(8,128)(2,1)}, bf16[384,1536]{1,0:T(8,128)(2,1)}, u32[]{:S(2)}, u32[]{:S(2)}) collective-permute-start(bf16[384,1536]{1,0:T(8,128)(2,1)} %product_tn.29), channel_id=1, source_target_pairs={{0,4},{4,0},{8,12},{12,8},{16,20},{20,16},{24,28},{28,24},{1,5},{5... | collective-permute-start | bytes 3538952 | tf_op jit(solution)/shard_map/ppermute | solution.py:655
  755.7 22.9 %collective-permute-start.60 = (bf16[512,128]{0,1:T(8,128)(2,1)}, bf16[512,128]{0,1:T(8,128)(2,1)}, u32[]{:S(2)}, u32[]{:S(2)}) collective-permute-start(bf16[512,128]{0,1:T(8,128)(2,1)} %pad_maximum_fusion.17), channel_id=1, source_target_pairs={{0,1},{1,0},{2,3},{3,2},{4,5},{5,4},{6,7},{7,6},{8,9},{9,8},{10,11... | collective-permute-start | bytes 393224 | tf_op jit(solution)/shard_map/ppermute | solution.py:664
  777.4 29.3 %collective-permute-start.64 = (bf16[768,768]{1,0:T(8,128)(2,1)}, bf16[768,768]{1,0:T(8,128)(2,1)}, u32[]{:S(2)}, u32[]{:S(2)}) collective-permute-start(bf16[768,768]{1,0:T(8,128)(2,1)} %copy-done.74), channel_id=1, source_target_pairs={{0,4},{4,0},{8,12},{12,8},{16,20},{20,16},{24,28},{28,24},{1,5},{5... | collective-permute-start | bytes 3538952 | tf_op jit(solution)/shard_map/ppermute | solution.py:655
  806.3 12.0 %collective-permute-start.65 = (bf16[4,96,247]{2,1,0:T(8,128)(2,1)S(1)}, bf16[4,96,247]{2,1,0:T(8,128)(2,1)S(1)}, u32[]{:S(2)}, u32[]{:S(2)}) collective-permute-start(bf16[4,96,247]{2,1,0:T(8,128)(2,1)S(1)} %fusion.22), channel_id=1, source_target_pairs={{0,4},{4,0},{8,12},{12,8},{16,20},{20,16},{24,28},{28,24},{1,5},{5... | collective-permute-start | bytes 569096 | tf_op jit(solution)/shard_map/ppermute | solution.py:655
  806.7 35.5 %collective-permute-start.70 = (bf16[768,768]{1,0:T(8,128)(2,1)}, bf16[768,768]{1,0:T(8,128)(2,1)}, u32[]{:S(2)}, u32[]{:S(2)}) collective-permute-start(bf16[768,768]{1,0:T(8,128)(2,1)} %copy-done.73), channel_id=1, source_target_pairs={{0,4},{4,0},{8,12},{12,8},{16,20},{20,16},{24,28},{28,24},{1,5},{5... | collective-permute-start | bytes 3538952 | tf_op jit(solution)/shard_map/ppermute | solution.py:655
  815.9 23.4 %collective-permute-start.63 = (bf16[256,1536]{1,0:T(8,128)(2,1)S(1)}, bf16[256,1536]{1,0:T(8,128)(2,1)}, u32[]{:S(2)}, u32[]{:S(2)}) collective-permute-start(bf16[256,1536]{1,0:T(8,128)(2,1)S(1)} %slice.536), channel_id=1, source_target_pairs={{0,1},{1,0},{2,3},{3,2},{4,5},{5,4},{6,7},{7,6},{8,9},{9,8},{10,11... | collective-permute-start | bytes 2359304 | tf_op jit(solution)/shard_map/ppermute | solution.py:664
  835.2 26.0 %collective-permute-start.72 = (bf16[192,768]{1,0:T(8,128)(2,1)}, bf16[192,768]{1,0:T(8,128)(2,1)}, u32[]{:S(2)}, u32[]{:S(2)}) collective-permute-start(bf16[192,768]{1,0:T(8,128)(2,1)} %get-tuple-element.318), channel_id=1, source_target_pairs={{0,16},{4,20},{8,24},{12,28},{16,0},{20,4},{24,8},{28,12},{1,17},{... | collective-permute-start | bytes 884744 | tf_op jit(solution)/shard_map/ppermute | solution.py:659
  840.6 52.0 %collective-permute-start.73 = (bf16[192,768]{1,0:T(8,128)(2,1)}, bf16[192,768]{1,0:T(8,128)(2,1)}, u32[]{:S(2)}, u32[]{:S(2)}) collective-permute-start(bf16[192,768]{1,0:T(8,128)(2,1)} %get-tuple-element.317), channel_id=1, source_target_pairs={{0,24},{4,28},{8,0},{12,4},{16,8},{20,12},{24,16},{28,20},{1,25},{... | collective-permute-start | bytes 884744 | tf_op jit(solution)/shard_map/ppermute | solution.py:659
  840.8 39.4 %collective-permute-start.71 = (bf16[192,768]{1,0:T(8,128)(2,1)}, bf16[192,768]{1,0:T(8,128)(2,1)}, u32[]{:S(2)}, u32[]{:S(2)}) collective-permute-start(bf16[192,768]{1,0:T(8,128)(2,1)} %get-tuple-element.319), channel_id=1, source_target_pairs={{0,8},{4,12},{8,16},{12,20},{16,24},{20,28},{24,0},{28,4},{1,9},{5... | collective-permute-start | bytes 884744 | tf_op jit(solution)/shard_map/ppermute | solution.py:659
  847.0 45.6 %collective-permute-start.74 = (bf16[192,768]{1,0:T(8,128)(2,1)}, bf16[192,768]{1,0:T(8,128)(2,1)}, u32[]{:S(2)}, u32[]{:S(2)}) collective-permute-start(bf16[192,768]{1,0:T(8,128)(2,1)} %get-tuple-element.314), channel_id=1, source_target_pairs={{0,8},{4,12},{8,16},{12,20},{16,24},{20,28},{24,0},{28,4},{1,9},{5... | collective-permute-start | bytes 884744 | tf_op jit(solution)/shard_map/ppermute | solution.py:659
  848.4 44.2 %collective-permute-start.76 = (bf16[192,768]{1,0:T(8,128)(2,1)}, bf16[192,768]{1,0:T(8,128)(2,1)}, u32[]{:S(2)}, u32[]{:S(2)}) collective-permute-start(bf16[192,768]{1,0:T(8,128)(2,1)} %get-tuple-element.315), channel_id=1, source_target_pairs={{0,24},{4,28},{8,0},{12,4},{16,8},{20,12},{24,16},{28,20},{1,25},{... | collective-permute-start | bytes 884744 | tf_op jit(solution)/shard_map/ppermute | solution.py:659
  861.2 31.6 %collective-permute-start.75 = (bf16[192,768]{1,0:T(8,128)(2,1)}, bf16[192,768]{1,0:T(8,128)(2,1)}, u32[]{:S(2)}, u32[]{:S(2)}) collective-permute-start(bf16[192,768]{1,0:T(8,128)(2,1)} %get-tuple-element.316), channel_id=1, source_target_pairs={{0,16},{4,20},{8,24},{12,28},{16,0},{20,4},{24,8},{28,12},{1,17},{... | collective-permute-start | bytes 884744 | tf_op jit(solution)/shard_map/ppermute | solution.py:659
  880.2 14.8 %collective-permute-start.69 = (bf16[128,1536]{1,0:T(8,128)(2,1)}, bf16[128,1536]{1,0:T(8,128)(2,1)}, u32[]{:S(2)}, u32[]{:S(2)}) collective-permute-start(bf16[128,1536]{1,0:T(8,128)(2,1)} %fusion), channel_id=1, source_target_pairs={{0,2},{1,3},{2,0},{3,1},{4,6},{5,7},{6,4},{7,5},{8,10},{9,11},{10,... | collective-permute-start | bytes 1179656 | tf_op jit(solution)/shard_map/ppermute | solution.py:667
  (222 other events, 2620.0 us)
Sparse Core Ops, SparseCore 0:
  12.9 56.4 all-gather.7
  71.5 41.1 all-gather.9
  114.8 61.2 all-gather.11
  178.2 36.9 all-gather.15
  217.1 39.0 all-gather.13
  258.2 61.2 all-gather.17
  321.7 36.9 all-gather.19
  502.1 38.2 reduce-scatter.7
  558.5 65.3 reduce-scatter.9
  626.6 19.0 reduce-scatter.11
  660.3 36.3 reduce-scatter.13
  699.0 34.4 reduce-scatter.15
  749.5 60.5 reduce-scatter.17
  812.3 44.9 reduce-scatter.19

commit v4 on v3

--- a/solution.py
+++ b/solution.py
@@ -620,6 +620,8 @@
                 blocks.append(total[:, at : at + u])
         if count == 1:
             out[...] = jnp.concatenate(blocks, axis=1)
+        elif u % 128 != 0:
+            out[:, i, :] = jnp.concatenate(blocks, axis=1)
         else:
             for j, block in enumerate(blocks):
                 out[:, i, j * u : (j + 1) * u] = block
@@ -642,6 +644,35 @@
     )(*terms)
 
 
+def gate_fwd_kernel(n, own_g, own_u, other_g, other_u, gate, up, hid):
+    half = n.shape[1] // 2
+    g = dot(n[:, :half], own_g[...]) + dot(n[:, half:], other_g[...])
+    u = dot(n[:, :half], own_u[...]) + dot(n[:, half:], other_u[...])
+    gate[...] = g.astype(bf16)
+    up[...] = u.astype(bf16)
+    hid[...] = (g * sigmoid(g) * u).astype(bf16)
+
+
+def gate_forward(n, own, other):
+    rows, features = n.shape
+    units = own.shape[1] // 2
+    tile = tile_of(units)
+    steps = units // tile
+    column = pl.BlockSpec((rows, tile), lambda i: (0, i))
+    w_gate = pl.BlockSpec((own.shape[0], tile), lambda i: (0, i))
+    w_up = pl.BlockSpec((own.shape[0], tile), lambda i: (0, i + steps))
+    return pl.pallas_call(
+        gate_fwd_kernel,
+        grid=(steps,),
+        in_specs=[pl.BlockSpec((rows, features), lambda i: (0, 0)), w_gate, w_up, w_gate, w_up],
+        out_specs=[column] * 3,
+        out_shape=[jax.ShapeDtypeStruct((rows, units), bf16)] * 3,
+        compiler_params=params(1),
+        cost_estimate=BRIEF,
+        name="gate_forward",
+    )(n, own, own, other, other)
+
+
 class Links:
     def __init__(self, mesh):
         self.dp = mesh.shape["dp"]
@@ -760,10 +791,10 @@
         self.product = product_tn(left_other, rights)
         self.came = links.swap_y(after(self.product, *order))
 
-    def finish(self, *order, direct=False):
+    def finish(self, *order, direct=False, last=()):
         self.total = product_tn(self.left, self.rights, [after(self.came, *order)])
         if direct:
-            self.terms = self.links.scatter_z_direct(self.total)
+            self.terms = self.links.scatter_z_direct(after(self.total, *last))
         else:
             self.terms = [self.links.scatter_z(self.total)]
         return self.total
@@ -804,21 +835,18 @@
     return d_x, jnp.sum(d_n * u, axis=0)
 
 
-def times(x, own, other, *order):
+def times(x, own, other):
     half = x.shape[1] // 2
-    return after(dot(x[:, :half], own), *order) + dot(x[:, half:], other)
+    return dot(x[:, :half], own) + dot(x[:, half:], other)
 
 
 def back_times(d, own, other):
     return jnp.concatenate([dot_nt(d, own), dot_nt(d, other)], axis=1)
 
 
-def ffn_forward(n, w_in, *order):
-    pair = times(n, *w_in, *order)
-    units = pair.shape[1] // 2
-    gate, up = pair[:, :units], pair[:, units:]
-    hid = (gate * jax.nn.sigmoid(gate) * up).astype(bf16)
-    return hid, (n, gate.astype(bf16), up.astype(bf16), hid)
+def ffn_forward(n, w_in):
+    gate, up, hid = gate_forward(n, *w_in)
+    return hid, (n, gate, up, hid)
 
 
 def split_y(links, v):
@@ -895,7 +923,6 @@
     mixer_out = links.by_y(*[rows_of(v, 0, cut) for v in outs])
     attn_out = ungroup(links.by_y(*[rows_of(v, cut, end) for v in outs]), nz, 0)
     ffn_a_out = links.by_y(*ffn_a_out)
-    ffn_b_out = links.by_y(*ffn_b_out)
 
     seg = segment_ids.reshape(micro, length)
     masks = []
@@ -945,7 +972,8 @@
     n2, r2 = enter(x1, 1)
     g4_low = regroup(out_grad.reshape(local, features), nz, 1)
     dy4 = links.gather_rows(g4_low)
-    hid_a, kept_a = ffn_forward(after(n2, dy4), ffn_a_in, own[4])
+    hid_a, kept_a = ffn_forward(after(n2, dy4), ffn_a_in)
+    hid_a = after(hid_a, own[4])
     x2 = x1 + links.scatter_rows(dot(hid_a, ffn_a_out), other[4])
 
     n3, r3 = enter(x2, 2)
@@ -955,8 +983,10 @@
     x3 = x2 + links.scatter_rows(dot(mix, attn_out), own[6])
 
     n4, r4 = enter(x3, 3)
-    n4 = after(n4, mix_own, mix_other, other[6])
+    n4 = after(n4, mix_own, mix_other)
     hid_b, kept_b = ffn_forward(n4, ffn_b_in)
+    hid_b = after(hid_b, other[6])
+    kept_b = kept_b[:3] + (hid_b,)
 
     def leave(g, x, r, i, d_normed, *order, late=()):
         d_n = links.own_first(after(links.scatter_rows(d_normed, *order), *late))
@@ -965,6 +995,7 @@
 
     g4 = g4_low.astype(f32)
     fh = features // 2
+    ffn_b_out = links.by_y(own[6], after(other[6], hid_b))
     b_in, b_out, d_pair = ffn_backward(links, dy4, kept_b, ffn_b_out)
     x4 = x3 + links.scatter_rows(dot(after(hid_b, b_in.product), ffn_b_out))
     block_out = ungroup(x4, nz, 1).astype(bf16).reshape(hidden_in.shape)
@@ -998,38 +1029,47 @@
         slots, ext, wdt, values, pre, par, rate, keep, d_gated, scanned, states
     )
     d_dt, d_z = flat(d_dt), flat(d_z)
-    m_z = Sent(links, n1[:, :fh], n1[:, fh:], [d_z], m_out.came)
-    d_dt = after(d_dt, f_in.finish(m_z.product, a_out.terms[0], q_in.terms[0], f_out.terms[0]))
+    d_dt = after(d_dt, f_in.finish(d_z, a_out.terms[0], q_in.terms[0], f_out.terms[0]))
     d_bc = d_bc[:, :, :, 0, :].reshape(PIECES, micro, 2, rows, STATE)
     d_bc = jnp.swapaxes(d_bc, 2, 3).reshape(PIECES * local, 2 * STATE)
     d_ext = links.sum_rows(jnp.concatenate([dot_nt(d_dt, wdt), d_bc], axis=1))
     d_x, conv_sums = conv_backward(slots, pieces(d_ext), d_val, pre, masks, par, wx)
     d_x = flat(d_x)
-    m_x = Sent(links, n1[:, :fh], n1[:, fh:], [d_x], m_z.came)
-    d_x = after(d_x, m_x.product, m_out.finish(m_x.product))
+    m_in = Sent(links, n1[:, :fh], n1[:, fh:], [d_x, d_z], m_out.came)
+    done = m_out.finish(m_in.product)
+    d_n1 = product_nt([after(d_x, m_in.product, done), d_z], mixer_in)
+
+    done = m_in.finish(d_n1, *f_in.terms, direct=True, last=m_out.terms)
+    g0, gain_a = leave(g1, x0, r1, 0, d_n1, late=(done,))
+    input_grad = ungroup(g0, nz, 1).astype(bf16).reshape(hidden_in.shape)
 
     grad_dt = dot_tn(d_dt, flat(ext)[:, :RANK])
     grad_x = dot_tn(flat(values), d_ext)
     grad_table = jnp.concatenate([conv_sums[: CONV + 1], sums[:2], d_rate * rate], axis=0)
     packed = jnp.concatenate([grad_x, grad_dt, grad_table.T], axis=1)
-    summed = links.scatter_small(after(packed, m_x.product).reshape(2, nz, -1, packed.shape[1]))
+    grad_gains = jnp.stack([gain_a, gain_b, gain_c, gain_d])
+    grad_gains = jnp.moveaxis(grad_gains.reshape(4, 2, nz, -1), 0, 2)
+    packed = jnp.concatenate(
+        [after(packed, d_n1).reshape(2, nz, -1, packed.shape[1]), grad_gains.reshape(2, nz, width // dp, -1)],
+        axis=3,
+    )
+    summed = links.scatter_small(packed)
     states = w_xproj.shape[1]
+    tail = states + RANK + mixer_params.shape[0]
     grads = [
         summed[:, :states],
         summed[:, states : states + RANK].T,
-        summed[:, states + RANK :].T,
+        summed[:, states + RANK : tail].T,
     ]
-
-    d_n1 = product_nt([d_x, d_z], mixer_in)
-    done = m_z.finish(d_n1, *f_in.terms, direct=True)
-    last = m_x.finish(done, direct=True)
-    g0, gain_a = leave(g1, x0, r1, 0, d_n1, done, summed, late=(last, *m_z.terms))
-    input_grad = ungroup(g0, nz, 1).astype(bf16).reshape(hidden_in.shape)
+    gain_total = summed[:, tail:].reshape(norm_gains.shape)
+    gain_total = gain_total + links.swap_core(gain_total)
+    gain_total = gain_total + links.swap_x(gain_total)
 
     def grad_of(sent, like):
         return spread(sent.land(done), nz, like.shape)
 
     outs = [
+        grad_of(m_out, w_mixer_out),
         grad_of(f_in, w_ffn_a_in),
         grad_of(f_out, w_ffn_a_out),
         q_in.land(done)[0].astype(f32).reshape(w_qkv.shape),
@@ -1037,16 +1077,8 @@
         grad_of(b_in, w_ffn_b_in),
         grad_of(b_out, w_ffn_b_out),
     ]
-    grad_gains = jnp.stack([gain_a, gain_b, gain_c, gain_d])
-    grad_gains = jnp.moveaxis(grad_gains.reshape(4, 2, nz, -1), 0, 2)
-    gain_total = links.scatter_small(after(grad_gains, *outs, *m_x.terms))
-    gain_total = gain_total + links.swap_core(gain_total)
-    gain_total = gain_total + links.swap_x(gain_total)
-    grad_out = spread(m_out.land(last), nz, w_mixer_out.shape)
-    grad_z = ungroup(sum(v.astype(f32) for v in m_z.land(last)), nz, 1)
-    grad_x_in = ungroup(sum(v.astype(f32) for v in m_x.land()), nz, 1)
-    grad_in = jnp.stack([grad_x_in, grad_z], axis=1)
-    return (block_out, input_grad, gain_total, grad_in, *grads, grad_out, *outs)
+    grad_in = grad_of(m_in, w_mixer_in)
+    return (block_out, input_grad, gain_total, grad_in, *grads, *outs)
 
 
 def solution(mesh):

time: 941 us -> 917 us (0.974)
  starting transfers between devices: 137 us -> 120 us
  matrix products: 34.7 us -> 19.1 us
    dot_general x15 -> x11, matrix products: 34.7 us -> 19.1 us  [dot(): return lax.dot_general(a, b, (dims, ((), ())), preferred_element_type=out)]
    pallas_call x0 -> x2, Pallas kernels: none -> 12.5 us  [gate_forward(): pl.pallas_call(gate_fwd_kernel, grid=(steps,), in_specs=[pl.BlockSpec((ro...]
    ppermute x18 -> x16, waiting for transfers between devices: 194 us -> 182 us  [swap_y(): return lax.ppermute(v, 'dp', [(i, i ^ 1) for i in range(self.dp)])]
    ppermute x12 -> x6, starting transfers between devices: 19.5 us -> 8.04 us  [shift_z(): lax.ppermute(v, 'dp', [(2 * z + y, 2 * ((z + k) % n) + y) for z in range(...]
    ppermute x19, waiting for transfers between devices: 77.4 us -> 86.8 us  [swap_x(): return lax.ppermute(v, 'tensor', [(i, i ^ 2) for i in range(PIECES)])]
    pallas_call x18 -> x16, Pallas kernels: 44.8 us -> 39.6 us  [product_tn(): pl.pallas_call(lambda *refs: tn_kernel(len(rights), bool(adds), *refs), g...]
    unnamed x385 -> x370, local copies, waits for them, and re-layouts: 48.7 us -> 52 us
    ppermute x18 -> x16, starting transfers between devices: 22.6 us -> 21.2 us  [swap_y(): return lax.ppermute(v, 'dp', [(i, i ^ 1) for i in range(self.dp)])]
  transfers between devices with their start and end apart: 97 -> 89, of which waited for: 47 -> 50; matrix products, arithmetic and copies ran while one was open for 18% -> 17% of each run, Pallas kernels for 17% -> 18%
where the time goes in v4:
time: 917 us; the launch traced here: 907 us
  waiting for transfers between devices  386 us (42%)
  Pallas kernels  175 us (19%)
  local copies, waits for them, and re-layouts  124 us (14%)
  starting transfers between devices  120 us (13%)
  other arithmetic  65.4 us (7%)
  matrix products  19.1 us (2%)
  between operations  17 us (2%)
    ppermute x16, waiting for transfers between devices, swap_y(): return lax.ppermute(v, 'dp', [(i, i ^ 1) for i in range(self.dp)])  182 us
    ppermute x19, waiting for transfers between devices, swap_x(): return lax.ppermute(v, 'tensor', [(i, i ^ 2) for i in range(PIECES)])  86.8 us
    ppermute x27, starting transfers between devices, swap_core(): return lax.ppermute(v, 'tensor', [(i, i ^ 1) for i in range(PIECES)])  65.3 us
    all_gather x7, waiting for transfers between devices, gather_z(): lax.all_gather(v, 'dp', axis=0, tiled=True, axis_index_groups=self.groups)  62.6 us
    unnamed x370, local copies, waits for them, and re-layouts  52 us
    pallas_call x16, Pallas kernels, product_tn(): pl.pallas_call(lambda *refs: tn_kernel(len(rights), bool(adds), *refs), g...  39.6 us
    pallas_call x1, Pallas kernels, scan_backward(): pl.pallas_call(scan_bwd_kernel, grid_spec=grid, out_shape=[jax.ShapeDtype...  36.7 us
    ppermute x6, waiting for transfers between devices, shift_z(): lax.ppermute(v, 'dp', [(2 * z + y, 2 * ((z + k) % n) + y) for z in range(...  32.8 us
  transfers between devices with their start and end apart: 89, of which 50 were waited for; matrix products, arithmetic and copies ran while one was open for 17% of the time, Pallas kernels for 18%

profile of v4, /device:TPU:9, one launch (start us, length us, event | category | flops | bytes accessed | tf_op | source)
XLA Modules:
  0.0 906.8 jit_solution(4120089838694899502)
XLA Ops:
  7.2 3.5 reshape.406
  24.2 3.3 collective-permute-start.1
  37.9 3.5 collective-permute-done.4
  41.4 3.8 collective-permute-done.5
  49.4 20.0 %all-gather.8.cloned.1.call-done.refs_2_ = bf16[768,1536]{1,0:T(8,128)(2,1)} async-done(((bf16[192,1536]{1,0:T(8,128)(2,1)}), bf16[768,1536]{1,0:T(8,128)(2,1)}) %all-gather.8.cloned.1.call-update) | async-done | bytes 2359312 | tf_op jit(solution)/shard_map/all_gather | solution.py:701
  75.1 6.0 collective-permute-done.7
  84.1 28.5 %all-gather.10.cloned.1.call-done = bf16[576,1536]{1,0:T(8,128)(2,1)} async-done(((bf16[144,1536]{1,0:T(8,128)(2,1)}), bf16[576,1536]{1,0:T(8,128)(2,1)}) %all-gather.10.cloned.1.call-update) | async-done | bytes 1769488 | tf_op jit(solution)/shard_map/all_gather | solution.py:701
  112.6 9.4 %collective-permute-done.10.refs_3_ = bf16[768,1536]{1,0:T(8,128)(2,1)} collective-permute-done((bf16[768,1536]{1,0:T(8,128)(2,1)}, bf16[768,1536]{1,0:T(8,128)(2,1)}, u32[]{:S(2)}, u32[]{:S(2)}) %collective-permute-start.10) | collective-permute-done | bytes 2359328 | tf_op jit(solution)/shard_map/ppermute | solution.py:686
  123.5 3.2 fusion.43
  129.3 3.8 conv_forward.1
  148.1 23.2 %scan_forward.1 = (bf16[4,2,64,768]{3,2,1,0:T(8,128)(2,1)S(1)}, f32[4,2,64,768]{3,2,1,0:T(8,128)S(1)}, bf16[8,64,16,768]{3,2,1,0:T(8,128)(2,1)}) custom-call(s32[4]{0:T(128)S(1)} %pad_add_fusion.2.slot, bf16[4,2,64,128]{3,2,1,0:T(8,128)(2,1)S(1)} %bitcast.177, bf16[96,768]{1,0:T(8,128)(2,1)S(1)} %reshape.411.wdt_ref, bf16[4,2,64,768]{3,2,1,0:T(8,128)(2,1)S(1)} %copy-done.29, ...), custom_call_target="tpu_custom_call" | custom-call | flops 1 | bytes 1 | tf_op jit(solution)/shard_map/scan_forward/pallas_call | solution.py:395
  196.1 3.9 collective-permute-done.15
  202.0 13.1 %all-gather.16.cloned.1.call-done = bf16[512,1536]{1,0:T(8,128)(2,1)} async-done(((bf16[128,1536]{1,0:T(8,128)(2,1)}), bf16[512,1536]{1,0:T(8,128)(2,1)}) %all-gather.16.cloned.1.call-update) | async-done | bytes 1572880 | tf_op jit(solution)/shard_map/all_gather | solution.py:701
  215.1 30.2 %collective-permute-done.22.other_g.other_u.refs_3_ = bf16[768,2048]{1,0:T(8,128)(2,1)} collective-permute-done((bf16[768,2048]{1,0:T(8,128)(2,1)}, bf16[768,2048]{1,0:T(8,128)(2,1)}, u32[]{:S(2)}, u32[]{:S(2)}) %collective-permute-start.22) | collective-permute-done | bytes 3145760 | tf_op jit(solution)/shard_map/ppermute | solution.py:686
  250.8 4.9 collective-permute-done.16
  259.8 6.3 gate_forward.2
  269.3 10.4 %collective-permute-done.23 = bf16[512,1536]{1,0:T(8,128)(2,1)} collective-permute-done((bf16[512,1536]{1,0:T(8,128)(2,1)}, bf16[512,1536]{1,0:T(8,128)(2,1)}, u32[]{:S(2)}, u32[]{:S(2)}) %collective-permute-start.23) | collective-permute-done | bytes 1572896 | tf_op jit(solution)/shard_map/ppermute | solution.py:686
  281.1 3.3 maximum_select_fusion.w
  298.7 18.8 %collective-permute-done.25.refs_2_ = bf16[768,1152]{1,0:T(8,128)(2,1)} collective-permute-done((bf16[768,1152]{1,0:T(8,128)(2,1)}, bf16[768,1152]{1,0:T(8,128)(2,1)}, u32[]{:S(2)}, u32[]{:S(2)}) %collective-permute-start.25) | collective-permute-done | bytes 1769504 | tf_op jit(solution)/shard_map/ppermute | solution.py:686
  330.0 4.8 collective-permute-start.28
  334.8 5.3 collective-permute-start.29
  346.6 3.3 fusion.40
  354.3 33.3 %collective-permute-done.30.other_g.other_u.refs_3_ = bf16[768,2048]{1,0:T(8,128)(2,1)} collective-permute-done((bf16[768,2048]{1,0:T(8,128)(2,1)}, bf16[768,2048]{1,0:T(8,128)(2,1)}, u32[]{:S(2)}, u32[]{:S(2)}) %collective-permute-start.30) | collective-permute-done | bytes 3145760 | tf_op jit(solution)/shard_map/ppermute | solution.py:686
  388.7 4.8 collective-permute-start.31
  400.4 7.8 collective-permute-done.32
  412.6 8.0 collective-permute-done.33
  426.0 6.2 gate_forward.3
  437.5 3.7 maximum_select_fusion.1.w
  441.2 4.7 gate_backward.2
  445.9 3.5 product_tn.17
  449.4 7.4 product_nt.6
  463.2 7.2 collective-permute-done.40.refs_2_
  473.5 5.2 collective-permute-done.41
  479.7 7.4 collective-permute-done.38
  492.6 3.5 collective-permute-start.43
  498.6 4.2 collective-permute-start.44
  510.4 4.0 attention_backward.1
  517.1 21.9 %collective-permute-done.45.refs_3_ = bf16[768,2048]{1,0:T(8,128)(2,1)} collective-permute-done((bf16[768,2048]{1,0:T(8,128)(2,1)}, bf16[768,2048]{1,0:T(8,128)(2,1)}, u32[]{:S(2)}, u32[]{:S(2)}) %collective-permute-start.45) | collective-permute-done | bytes 3145760 | tf_op jit(solution)/shard_map/ppermute | solution.py:686
  542.6 4.0 product_tn.21
  549.8 9.7 %collective-permute-done.46.refs_2_ = bf16[192,1536]{1,0:T(8,128)(2,1)S(1)} collective-permute-done((bf16[192,1536]{1,0:T(8,128)(2,1)}, bf16[192,1536]{1,0:T(8,128)(2,1)S(1)}, u32[]{:S(2)}, u32[]{:S(2)}) %collective-permute-start.46) | collective-permute-done | bytes 589856 | tf_op jit(solution)/shard_map/ppermute | solution.py:686
  561.2 5.1 product_nt.8
  568.5 4.6 collective-permute-start.47
  579.3 7.9 collective-permute-done.48
  592.5 6.7 collective-permute-done.49
  604.1 13.9 %collective-permute-done.52.refs_2_ = bf16[768,1152]{1,0:T(8,128)(2,1)} collective-permute-done((bf16[768,1152]{1,0:T(8,128)(2,1)}, bf16[768,1152]{1,0:T(8,128)(2,1)}, u32[]{:S(2)}, u32[]{:S(2)}) %collective-permute-start.52) | collective-permute-done | bytes 1769504 | tf_op jit(solution)/shard_map/ppermute | solution.py:686
  622.6 3.3 product_tn.24
  629.5 4.8 gate_backward.3
  638.3 7.2 product_nt.9
  656.3 6.8 collective-permute-done.55
  670.6 3.5 collective-permute-start.57
  674.1 4.1 collective-permute-done.56
  678.1 4.1 collective-permute-start.58
  688.6 36.7 %scan_backward.1 = (bf16[4,2,64,768]{3,2,1,0:T(8,128)(2,1)S(1)}, f32[4,2,64,768]{3,2,1,0:T(8,128)S(1)}, bf16[4,2,64,768]{3,2,1,0:T(8,128)(2,1)S(1)}, f32[4,2,2,8...) custom-call(s32[4]{0:T(128)S(1)} %pad_add_fusion.2.slot, ...), custom_call_target="tpu_custom_call" | custom-call | flops 1 | bytes 1 | tf_op jit(solution)/shard_map/scan_backward/pallas_call | solution.py:441
  730.3 5.3 product_tn.28
  751.3 5.7 conv_backward.1
  757.6 3.1 product_tn.29
  760.7 5.0 collective-permute-done.62.refs_2_
  771.1 5.7 product_nt.11
  788.1 9.1 %collective-permute-done.64 = bf16[128,1536]{1,0:T(8,128)(2,1)} collective-permute-done((bf16[128,1536]{1,0:T(8,128)(2,1)}, bf16[128,1536]{1,0:T(8,128)(2,1)}, u32[]{:S(2)}, u32[]{:S(2)}) %collective-permute-start.64) | collective-permute-done | bytes 393248 | tf_op jit(solution)/shard_map/ppermute | solution.py:698
  799.4 18.0 %collective-permute-done.65.refs_3_ = bf16[768,1536]{1,0:T(8,128)(2,1)} collective-permute-done((bf16[768,1536]{1,0:T(8,128)(2,1)}, bf16[768,1536]{1,0:T(8,128)(2,1)}, u32[]{:S(2)}, u32[]{:S(2)}) %collective-permute-start.65) | collective-permute-done | bytes 2359328 | tf_op jit(solution)/shard_map/ppermute | solution.py:686
  819.8 3.7 product_tn.31
  856.8 4.8 collective-permute-start.70
  865.7 26.8 %collective-permute-done.73.refs_2_ = bf16[192,1536]{1,0:T(8,128)(2,1)S(1)} collective-permute-done((bf16[192,1536]{1,0:T(8,128)(2,1)}, bf16[192,1536]{1,0:T(8,128)(2,1)S(1)}, u32[]{:S(2)}, u32[]{:S(2)}) %collective-permute-start.73) | collective-permute-done | bytes 589856 | tf_op jit(solution)/shard_map/ppermute | solution.py:690
  892.5 6.0 collective-permute-done.74.refs_3_
  (779 shorter events, 329.0 us)
Async XLA Ops:
  7.2 62.2 %all-gather.8.cloned.1.call-start = ((), (), s32[]{:S(2)}) async-start(), calls=%async_computation.7 | async-start | bytes 2949120 | tf_op jit(solution)/shard_map/all_gather | solution.py:701
  12.8 99.8 %all-gather.10.cloned.1.call-start = ((), (), s32[]{:S(2)}) async-start(), calls=%async_computation.8 | async-start | bytes 2211840 | tf_op jit(solution)/shard_map/all_gather | solution.py:701
  21.9 154.2 %all-gather.12.cloned.1.call-start = ((), (), s32[]{:S(2)}) async-start(), calls=%async_computation.9 | async-start | bytes 3932160 | tf_op jit(solution)/shard_map/all_gather | solution.py:701
  22.7 192.4 %all-gather.16.cloned.1.call-start = ((), (), s32[]{:S(2)}) async-start(), calls=%async_computation.11 | async-start | bytes 1966080 | tf_op jit(solution)/shard_map/all_gather | solution.py:701
  23.0 8.1 collective-permute-start
  24.2 9.4 %collective-permute-start.1 = (bf16[24480]{0:T(1024)(128)(2,1)S(1)}, bf16[24480]{0:T(1024)(128)(2,1)S(1)}, u32[]{:S(2)}, u32[]{:S(2)}) collective-permute-start(bf16[24480]{0:T(1024)(128)(2,1)S(1)} %pad_maximum_fusion.18), channel_id=1, source_target_pairs={{0,24},{4,28},{8,0},{12,4},{16,8},{20,12},{24,16},{28,20},{1,25},{... | collective-permute-start | bytes 146888 | tf_op jit(solution)/shard_map/ppermute | solution.py:714
  27.5 8.6 collective-permute-start.2
  27.5 10.3 %collective-permute-start.3 = (bf16[24480]{0:T(1024)(128)(2,1)S(1)}, bf16[24480]{0:T(1024)(128)(2,1)S(1)}, u32[]{:S(2)}, u32[]{:S(2)}) collective-permute-start(bf16[24480]{0:T(1024)(128)(2,1)S(1)} %pad_maximum_fusion.18), channel_id=1, source_target_pairs={{0,16},{4,20},{8,24},{12,28},{16,0},{20,4},{24,8},{28,12},{1,17},{... | collective-permute-start | bytes 146888 | tf_op jit(solution)/shard_map/ppermute | solution.py:714
  27.5 13.8 %collective-permute-start.4 = (bf16[24480]{0:T(1024)(128)(2,1)S(1)}, bf16[24480]{0:T(1024)(128)(2,1)S(1)}, u32[]{:S(2)}, u32[]{:S(2)}) collective-permute-start(bf16[24480]{0:T(1024)(128)(2,1)S(1)} %pad_maximum_fusion.18), channel_id=1, source_target_pairs={{0,12},{4,16},{8,20},{12,24},{16,28},{20,0},{24,4},{28,8},{1,13},{... | collective-permute-start | bytes 146888 | tf_op jit(solution)/shard_map/ppermute | solution.py:714
  30.9 238.4 %all-gather.14.cloned.1.call-start = ((), (), s32[]{:S(2)}) async-start(), calls=%async_computation.10 | async-start | bytes 2211840 | tf_op jit(solution)/shard_map/all_gather | solution.py:701
  31.1 14.1 %collective-permute-start.5 = (bf16[24480]{0:T(1024)(128)(2,1)S(1)}, bf16[24480]{0:T(1024)(128)(2,1)S(1)}, u32[]{:S(2)}, u32[]{:S(2)}) collective-permute-start(bf16[24480]{0:T(1024)(128)(2,1)S(1)} %pad_maximum_fusion.18), channel_id=1, source_target_pairs={{0,8},{4,12},{8,16},{12,20},{16,24},{20,28},{24,0},{28,4},{1,9},{5... | collective-permute-start | bytes 146888 | tf_op jit(solution)/shard_map/ppermute | solution.py:714
  33.6 11.7 %collective-permute-start.6 = (bf16[24480]{0:T(1024)(128)(2,1)S(1)}, bf16[24480]{0:T(1024)(128)(2,1)S(1)}, u32[]{:S(2)}, u32[]{:S(2)}) collective-permute-start(bf16[24480]{0:T(1024)(128)(2,1)S(1)} %pad_maximum_fusion.18), channel_id=1, source_target_pairs={{0,4},{4,8},{8,12},{12,16},{16,20},{20,24},{24,28},{28,0},{1,5},{5... | collective-permute-start | bytes 146888 | tf_op jit(solution)/shard_map/ppermute | solution.py:714
  69.4 52.6 %collective-permute-start.10 = (bf16[768,1536]{1,0:T(8,128)(2,1)}, bf16[768,1536]{1,0:T(8,128)(2,1)}, u32[]{:S(2)}, u32[]{:S(2)}) collective-permute-start(bf16[768,1536]{1,0:T(8,128)(2,1)} %all-gather.8.cloned.1.call-done.refs_2_), channel_id=1, source_target_pairs={{0,4},{4,0},{8,12},{12,8},{16,20},{20,16},{24,28},{28,24},{1,5},{5... | collective-permute-start | bytes 7077896 | tf_op jit(solution)/shard_map/ppermute | solution.py:686
  71.0 10.1 %collective-permute-start.7 = (bf16[128,1536]{1,0:T(8,128)(2,1)S(1)}, bf16[128,1536]{1,0:T(8,128)(2,1)S(1)}, u32[]{:S(2)}, u32[]{:S(2)}) collective-permute-start(bf16[128,1536]{1,0:T(8,128)(2,1)S(1)} %maximum_select_fusion.8), channel_id=1, source_target_pairs={{0,2},{1,3},{2,0},{3,1},{4,6},{5,7},{6,4},{7,5},{8,10},{9,11},{10,... | collective-permute-start | bytes 1179656 | tf_op jit(solution)/shard_map/ppermute | solution.py:698
  74.1 9.8 %collective-permute-start.8 = (bf16[128,1536]{1,0:T(8,128)(2,1)S(1)}, bf16[128,1536]{1,0:T(8,128)(2,1)S(1)}, u32[]{:S(2)}, u32[]{:S(2)}) collective-permute-start(bf16[128,1536]{1,0:T(8,128)(2,1)S(1)} %maximum_select_fusion.8), channel_id=1, source_target_pairs={{0,1},{1,0},{2,3},{3,2},{4,5},{5,4},{6,7},{7,6},{8,9},{9,8},{10,11... | collective-permute-start | bytes 1179656 | tf_op jit(solution)/shard_map/ppermute | solution.py:695
  122.0 50.5 %collective-permute-start.13 = (bf16[576,1536]{1,0:T(8,128)(2,1)}, bf16[576,1536]{1,0:T(8,128)(2,1)}, u32[]{:S(2)}, u32[]{:S(2)}) collective-permute-start(bf16[576,1536]{1,0:T(8,128)(2,1)} %all-gather.10.cloned.1.call-done), channel_id=1, source_target_pairs={{0,4},{4,0},{8,12},{12,8},{16,20},{20,16},{24,28},{28,24},{1,5},{5... | collective-permute-start | bytes 5308424 | tf_op jit(solution)/shard_map/ppermute | solution.py:686
  136.9 184.5 %all-gather.18.cloned.1.call-start = ((), (), s32[]{:S(2)}) async-start(), calls=%async_computation.12 | async-start | bytes 3932160 | tf_op jit(solution)/shard_map/all_gather | solution.py:701
  176.1 69.1 %collective-permute-start.22 = (bf16[768,2048]{1,0:T(8,128)(2,1)}, bf16[768,2048]{1,0:T(8,128)(2,1)}, u32[]{:S(2)}, u32[]{:S(2)}) collective-permute-start(bf16[768,2048]{1,0:T(8,128)(2,1)} %all-gather.12.cloned.1.call-done.own_g.own_u.refs_2_), channel_id=1, source_target_pairs={{0,4},{4,0},{8,12},{12,8},{16,20},{20,16},{24,28},{28,24},{1,5},{5... | collective-permute-start | bytes 9437192 | tf_op jit(solution)/shard_map/ppermute | solution.py:686
  183.4 214.1 %all-gather.20.cloned.1.call-start = ((), (), s32[]{:S(2)}) async-start(), calls=%async_computation.13 | async-start | bytes 1966080 | tf_op jit(solution)/shard_map/all_gather | solution.py:701
  189.4 10.6 %collective-permute-start.15 = (bf16[128,1536]{1,0:T(8,128)(2,1)}, bf16[128,1536]{1,0:T(8,128)(2,1)}, u32[]{:S(2)}, u32[]{:S(2)}) collective-permute-start(bf16[128,1536]{1,0:T(8,128)(2,1)} %fusion.18), channel_id=1, source_target_pairs={{0,2},{1,3},{2,0},{3,1},{4,6},{5,7},{6,4},{7,5},{8,10},{9,11},{10,... | collective-permute-start | bytes 1179656 | tf_op jit(solution)/shard_map/ppermute | solution.py:698
  195.0 55.3 %collective-permute-start.19 = (bf16[128,1536]{1,0:T(8,128)(2,1)S(1)}, bf16[128,1536]{1,0:T(8,128)(2,1)}, u32[]{:S(2)}, u32[]{:S(2)}) collective-permute-start(bf16[128,1536]{1,0:T(8,128)(2,1)S(1)} %copy.296), channel_id=1, source_target_pairs={{0,2},{1,3},{2,0},{3,1},{4,6},{5,7},{6,4},{7,5},{8,10},{9,11},{10,... | collective-permute-start | bytes 1179656 | tf_op jit(solution)/shard_map/ppermute | solution.py:698
  245.2 34.5 %collective-permute-start.23 = (bf16[512,1536]{1,0:T(8,128)(2,1)}, bf16[512,1536]{1,0:T(8,128)(2,1)}, u32[]{:S(2)}, u32[]{:S(2)}) collective-permute-start(bf16[512,1536]{1,0:T(8,128)(2,1)} %all-gather.16.cloned.1.call-done), channel_id=1, source_target_pairs={{0,4},{4,0},{8,12},{12,8},{16,20},{20,16},{24,28},{28,24},{1,5},{5... | collective-permute-start | bytes 4718600 | tf_op jit(solution)/shard_map/ppermute | solution.py:686
  246.8 8.9 collective-permute-start.16
  248.0 10.4 %collective-permute-start.20 = (bf16[128,1536]{1,0:T(8,128)(2,1)S(1)}, bf16[128,1536]{1,0:T(8,128)(2,1)S(1)}, u32[]{:S(2)}, u32[]{:S(2)}) collective-permute-start(bf16[128,1536]{1,0:T(8,128)(2,1)S(1)} %copy.296), channel_id=1, source_target_pairs={{0,1},{1,0},{2,3},{3,2},{4,5},{5,4},{6,7},{7,6},{8,9},{9,8},{10,11... | collective-permute-start | bytes 1179656 | tf_op jit(solution)/shard_map/ppermute | solution.py:695
  250.2 8.1 collective-permute-start.21
  250.2 9.3 %collective-permute-start.17 = (bf16[128,1536]{1,0:T(8,128)(2,1)S(1)}, bf16[128,1536]{1,0:T(8,128)(2,1)S(1)}, u32[]{:S(2)}, u32[]{:S(2)}) collective-permute-start(bf16[128,1536]{1,0:T(8,128)(2,1)S(1)} %maximum_select_fusion.9), channel_id=1, source_target_pairs={{0,1},{1,0},{2,3},{3,2},{4,5},{5,4},{6,7},{7,6},{8,9},{9,8},{10,11... | collective-permute-start | bytes 1179656 | tf_op jit(solution)/shard_map/ppermute | solution.py:695
  279.7 37.8 %collective-permute-start.25 = (bf16[768,1152]{1,0:T(8,128)(2,1)}, bf16[768,1152]{1,0:T(8,128)(2,1)}, u32[]{:S(2)}, u32[]{:S(2)}) collective-permute-start(bf16[768,1152]{1,0:T(8,128)(2,1)} %all-gather.14.cloned.1.call-done.refs_1_), channel_id=1, source_target_pairs={{0,4},{4,0},{8,12},{12,8},{16,20},{20,16},{24,28},{28,24},{1,5},{5... | collective-permute-start | bytes 5308424 | tf_op jit(solution)/shard_map/ppermute | solution.py:686
  293.0 246.0 %reduce-scatter.8.cloned.1.call-start = ((), (), s32[]{:S(2)}) async-start(), calls=%async_computation.14 | async-start | bytes 1966080 | tf_op jit(solution)/shard_map/reduce_scatter | solution.py:704
  321.4 66.2 %collective-permute-start.30 = (bf16[768,2048]{1,0:T(8,128)(2,1)}, bf16[768,2048]{1,0:T(8,128)(2,1)}, u32[]{:S(2)}, u32[]{:S(2)}) collective-permute-start(bf16[768,2048]{1,0:T(8,128)(2,1)} %all-gather.18.cloned.1.call-done.own_g.own_u.refs_2_), channel_id=1, source_target_pairs={{0,4},{4,0},{8,12},{12,8},{16,20},{20,16},{24,28},{28,24},{1,5},{5... | collective-permute-start | bytes 9437192 | tf_op jit(solution)/shard_map/ppermute | solution.py:686
  330.0 14.9 %collective-permute-start.28 = (bf16[128,1536]{1,0:T(8,128)(2,1)S(1)}, bf16[128,1536]{1,0:T(8,128)(2,1)}, u32[]{:S(2)}, u32[]{:S(2)}) collective-permute-start(bf16[128,1536]{1,0:T(8,128)(2,1)S(1)} %maximum_select_fusion.10), channel_id=1, source_target_pairs={{0,1},{1,0},{2,3},{3,2},{4,5},{5,4},{6,7},{7,6},{8,9},{9,8},{10,11... | collective-permute-start | bytes 1179656 | tf_op jit(solution)/shard_map/ppermute | solution.py:695
  334.8 10.0 %collective-permute-start.29 = (bf16[128,1536]{1,0:T(8,128)(2,1)}, bf16[128,1536]{1,0:T(8,128)(2,1)}, u32[]{:S(2)}, u32[]{:S(2)}) collective-permute-start(bf16[128,1536]{1,0:T(8,128)(2,1)} %collective-permute-done.27), channel_id=1, source_target_pairs={{0,1},{1,0},{2,3},{3,2},{4,5},{5,4},{6,7},{7,6},{8,9},{9,8},{10,11... | collective-permute-start | bytes 1179656 | tf_op jit(solution)/shard_map/ppermute | solution.py:695
  397.5 10.6 %collective-permute-start.32 = (bf16[128,1536]{1,0:T(8,128)(2,1)}, bf16[128,1536]{1,0:T(8,128)(2,1)}, u32[]{:S(2)}, u32[]{:S(2)}) collective-permute-start(bf16[128,1536]{1,0:T(8,128)(2,1)} %fusion.12), channel_id=1, source_target_pairs={{0,2},{1,3},{2,0},{3,1},{4,6},{5,7},{6,4},{7,5},{8,10},{9,11},{10,... | collective-permute-start | bytes 1179656 | tf_op jit(solution)/shard_map/ppermute | solution.py:698
  399.0 35.6 %collective-permute-start.36 = (bf16[512,1536]{1,0:T(8,128)(2,1)}, bf16[512,1536]{1,0:T(8,128)(2,1)}, u32[]{:S(2)}, u32[]{:S(2)}) collective-permute-start(bf16[512,1536]{1,0:T(8,128)(2,1)} %all-gather.20.cloned.1.call-done), channel_id=1, source_target_pairs={{0,4},{4,0},{8,12},{12,8},{16,20},{20,16},{24,28},{28,24},{1,5},{5... | collective-permute-start | bytes 4718600 | tf_op jit(solution)/shard_map/ppermute | solution.py:686
  411.0 9.6 %collective-permute-start.33 = (bf16[128,1536]{1,0:T(8,128)(2,1)S(1)}, bf16[128,1536]{1,0:T(8,128)(2,1)}, u32[]{:S(2)}, u32[]{:S(2)}) collective-permute-start(bf16[128,1536]{1,0:T(8,128)(2,1)S(1)} %maximum_select_fusion.11), channel_id=1, source_target_pairs={{0,2},{1,3},{2,0},{3,1},{4,6},{5,7},{6,4},{7,5},{8,10},{9,11},{10,... | collective-permute-start | bytes 1179656 | tf_op jit(solution)/shard_map/ppermute | solution.py:698
  411.2 13.5 %collective-permute-start.34 = (bf16[128,1536]{1,0:T(8,128)(2,1)S(1)}, bf16[128,1536]{1,0:T(8,128)(2,1)}, u32[]{:S(2)}, u32[]{:S(2)}) collective-permute-start(bf16[128,1536]{1,0:T(8,128)(2,1)S(1)} %maximum_select_fusion.11), channel_id=1, source_target_pairs={{0,1},{1,0},{2,3},{3,2},{4,5},{5,4},{6,7},{7,6},{8,9},{9,8},{10,11... | collective-permute-start | bytes 1179656 | tf_op jit(solution)/shard_map/ppermute | solution.py:695
  436.0 34.4 %collective-permute-start.40 = (bf16[512,1536]{1,0:T(8,128)(2,1)S(1)}, bf16[512,1536]{1,0:T(8,128)(2,1)S(1)}, u32[]{:S(2)}, u32[]{:S(2)}) collective-permute-start(bf16[512,1536]{1,0:T(8,128)(2,1)S(1)} %product_tn.16), channel_id=1, source_target_pairs={{0,4},{4,0},{8,12},{12,8},{16,20},{20,16},{24,28},{28,24},{1,5},{5... | collective-permute-start | bytes 4718600 | tf_op jit(solution)/shard_map/ppermute | solution.py:686
  470.4 8.3 collective-permute-start.41
  471.9 15.2 %collective-permute-start.38 = (bf16[128,1536]{1,0:T(8,128)(2,1)S(1)}, bf16[128,1536]{1,0:T(8,128)(2,1)S(1)}, u32[]{:S(2)}, u32[]{:S(2)}) collective-permute-start(bf16[128,1536]{1,0:T(8,128)(2,1)S(1)} %fusion.8), channel_id=1, source_target_pairs={{0,2},{1,3},{2,0},{3,1},{4,6},{5,7},{6,4},{7,5},{8,10},{9,11},{10,... | collective-permute-start | bytes 1179656 | tf_op jit(solution)/shard_map/ppermute | solution.py:698
  472.1 66.9 %collective-permute-start.45 = (bf16[768,2048]{1,0:T(8,128)(2,1)}, bf16[768,2048]{1,0:T(8,128)(2,1)}, u32[]{:S(2)}, u32[]{:S(2)}) collective-permute-start(bf16[768,2048]{1,0:T(8,128)(2,1)} %product_tn.17), channel_id=1, source_target_pairs={{0,4},{4,0},{8,12},{12,8},{16,20},{20,16},{24,28},{28,24},{1,5},{5... | collective-permute-start | bytes 9437192 | tf_op jit(solution)/shard_map/ppermute | solution.py:686
  491.1 174.6 %reduce-scatter.10.cloned.1.call-start = ((), (), s32[]{:S(2)}) async-start(), calls=%async_computation.15 | async-start | bytes 3932160 | tf_op jit(solution)/shard_map/reduce_scatter | solution.py:704
  492.6 13.6 %collective-permute-start.43 = (bf16[128,1536]{1,0:T(8,128)(2,1)S(1)}, bf16[128,1536]{1,0:T(8,128)(2,1)}, u32[]{:S(2)}, u32[]{:S(2)}) collective-permute-start(bf16[128,1536]{1,0:T(8,128)(2,1)S(1)} %copy-done.135), channel_id=1, source_target_pairs={{0,1},{1,0},{2,3},{3,2},{4,5},{5,4},{6,7},{7,6},{8,9},{9,8},{10,11... | collective-permute-start | bytes 1179656 | tf_op jit(solution)/shard_map/ppermute | solution.py:695
  548.2 180.9 %reduce-scatter.12.cloned.1.call-start = ((), (), s32[]{:S(2)}) async-start(), calls=%async_computation.16 | async-start | bytes 737280 | tf_op jit(solution)/shard_map/reduce_scatter | solution.py:704
  548.3 11.2 %collective-permute-start.46 = (bf16[192,1536]{1,0:T(8,128)(2,1)}, bf16[192,1536]{1,0:T(8,128)(2,1)S(1)}, u32[]{:S(2)}, u32[]{:S(2)}) collective-permute-start(bf16[192,1536]{1,0:T(8,128)(2,1)} %copy-done.93), channel_id=1, source_target_pairs={{0,4},{4,0},{8,12},{12,8},{16,20},{20,16},{24,28},{28,24},{1,5},{5... | collective-permute-start | bytes 1769480 | tf_op jit(solution)/shard_map/ppermute | solution.py:686
  576.7 10.5 %collective-permute-start.48 = (bf16[128,1536]{1,0:T(8,128)(2,1)S(1)}, bf16[128,1536]{1,0:T(8,128)(2,1)S(1)}, u32[]{:S(2)}, u32[]{:S(2)}) collective-permute-start(bf16[128,1536]{1,0:T(8,128)(2,1)S(1)} %fusion.4), channel_id=1, source_target_pairs={{0,2},{1,3},{2,0},{3,1},{4,6},{5,7},{6,4},{7,5},{8,10},{9,11},{10,... | collective-permute-start | bytes 1179656 | tf_op jit(solution)/shard_map/ppermute | solution.py:698
  578.1 39.8 %collective-permute-start.52 = (bf16[768,1152]{1,0:T(8,128)(2,1)}, bf16[768,1152]{1,0:T(8,128)(2,1)}, u32[]{:S(2)}, u32[]{:S(2)}) collective-permute-start(bf16[768,1152]{1,0:T(8,128)(2,1)} %product_tn.20), channel_id=1, source_target_pairs={{0,4},{4,0},{8,12},{12,8},{16,20},{20,16},{24,28},{28,24},{1,5},{5... | collective-permute-start | bytes 5308424 | tf_op jit(solution)/shard_map/ppermute | solution.py:686
  589.6 9.6 %collective-permute-start.49 = (bf16[128,1536]{1,0:T(8,128)(2,1)S(1)}, bf16[128,1536]{1,0:T(8,128)(2,1)}, u32[]{:S(2)}, u32[]{:S(2)}) collective-permute-start(bf16[128,1536]{1,0:T(8,128)(2,1)S(1)} %get-tuple-element.296), channel_id=1, source_target_pairs={{0,2},{1,3},{2,0},{3,1},{4,6},{5,7},{6,4},{7,5},{8,10},{9,11},{10,... | collective-permute-start | bytes 1179656 | tf_op jit(solution)/shard_map/ppermute | solution.py:698
  591.0 138.1 %reduce-scatter.14.cloned.1.call-start = ((), (), s32[]{:S(2)}) async-start(), calls=%async_computation.17 | async-start | bytes 2211840 | tf_op jit(solution)/shard_map/reduce_scatter | solution.py:704
  591.1 11.1 %collective-permute-start.50 = (bf16[128,1536]{1,0:T(8,128)(2,1)S(1)}, bf16[128,1536]{1,0:T(8,128)(2,1)S(1)}, u32[]{:S(2)}, u32[]{:S(2)}) collective-permute-start(bf16[128,1536]{1,0:T(8,128)(2,1)S(1)} %get-tuple-element.296), channel_id=1, source_target_pairs={{0,1},{1,0},{2,3},{3,2},{4,5},{5,4},{6,7},{7,6},{8,9},{9,8},{10,11... | collective-permute-start | bytes 1179656 | tf_op jit(solution)/shard_map/ppermute | solution.py:695
  620.1 34.7 %collective-permute-start.54 = (bf16[512,1536]{1,0:T(8,128)(2,1)}, bf16[512,1536]{1,0:T(8,128)(2,1)}, u32[]{:S(2)}, u32[]{:S(2)}) collective-permute-start(bf16[512,1536]{1,0:T(8,128)(2,1)} %product_tn.23), channel_id=1, source_target_pairs={{0,4},{4,0},{8,12},{12,8},{16,20},{20,16},{24,28},{28,24},{1,5},{5... | collective-permute-start | bytes 4718600 | tf_op jit(solution)/shard_map/ppermute | solution.py:686
  649.4 79.8 %reduce-scatter.16.cloned.1.call-start = ((), (), s32[]{:S(2)}) async-start(), calls=%async_computation.18 | async-start | bytes 1966080 | tf_op jit(solution)/shard_map/reduce_scatter | solution.py:704
  654.8 8.3 collective-permute-start.55
  654.9 74.2 %collective-permute-start.59 = (bf16[768,2048]{1,0:T(8,128)(2,1)}, bf16[768,2048]{1,0:T(8,128)(2,1)}, u32[]{:S(2)}, u32[]{:S(2)}) collective-permute-start(bf16[768,2048]{1,0:T(8,128)(2,1)} %copy-done.42), channel_id=1, source_target_pairs={{0,4},{4,0},{8,12},{12,8},{16,20},{20,16},{24,28},{28,24},{1,5},{5... | collective-permute-start | bytes 9437192 | tf_op jit(solution)/shard_map/ppermute | solution.py:686
  670.4 147.1 %reduce-scatter.18.cloned.1.call-start = ((), (), s32[]{:S(2)}) async-start(), calls=%async_computation.19 | async-start | bytes 3932160 | tf_op jit(solution)/shard_map/reduce_scatter | solution.py:704
  670.6 13.6 %collective-permute-start.57 = (bf16[128,1536]{1,0:T(8,128)(2,1)}, bf16[128,1536]{1,0:T(8,128)(2,1)S(1)}, u32[]{:S(2)}, u32[]{:S(2)}) collective-permute-start(bf16[128,1536]{1,0:T(8,128)(2,1)} %get-tuple-element.293), channel_id=1, source_target_pairs={{0,1},{1,0},{2,3},{3,2},{4,5},{5,4},{6,7},{7,6},{8,9},{9,8},{10,11... | collective-permute-start | bytes 1179656 | tf_op jit(solution)/shard_map/ppermute | solution.py:695
  735.6 96.0 %reduce-scatter.20.cloned.1.call-start = ((), (), s32[]{:S(2)}) async-start(), calls=%async_computation.20 | async-start | bytes 1474560 | tf_op jit(solution)/shard_map/reduce_scatter | solution.py:704
  738.2 27.5 %collective-permute-start.62 = (bf16[384,1536]{1,0:T(8,128)(2,1)}, bf16[384,1536]{1,0:T(8,128)(2,1)}, u32[]{:S(2)}, u32[]{:S(2)}) collective-permute-start(bf16[384,1536]{1,0:T(8,128)(2,1)} %copy-done.67), channel_id=1, source_target_pairs={{0,4},{4,0},{8,12},{12,8},{16,20},{20,16},{24,28},{28,24},{1,5},{5... | collective-permute-start | bytes 3538952 | tf_op jit(solution)/shard_map/ppermute | solution.py:686
  765.7 51.8 %collective-permute-start.65 = (bf16[768,1536]{1,0:T(8,128)(2,1)}, bf16[768,1536]{1,0:T(8,128)(2,1)}, u32[]{:S(2)}, u32[]{:S(2)}) collective-permute-start(bf16[768,1536]{1,0:T(8,128)(2,1)} %product_tn.29), channel_id=1, source_target_pairs={{0,4},{4,0},{8,12},{12,8},{16,20},{20,16},{24,28},{28,24},{1,5},{5... | collective-permute-start | bytes 7077896 | tf_op jit(solution)/shard_map/ppermute | solution.py:686
  786.2 11.0 %collective-permute-start.64 = (bf16[128,1536]{1,0:T(8,128)(2,1)}, bf16[128,1536]{1,0:T(8,128)(2,1)}, u32[]{:S(2)}, u32[]{:S(2)}) collective-permute-start(bf16[128,1536]{1,0:T(8,128)(2,1)} %fusion), channel_id=1, source_target_pairs={{0,2},{1,3},{2,0},{3,1},{4,6},{5,7},{6,4},{7,5},{8,10},{9,11},{10,... | collective-permute-start | bytes 1179656 | tf_op jit(solution)/shard_map/ppermute | solution.py:698
  834.9 20.1 %collective-permute-start.69 = (bf16[96,255]{1,0:T(8,128)(2,1)S(1)}, bf16[96,255]{1,0:T(8,128)(2,1)S(1)}, u32[]{:S(2)}, u32[]{:S(2)}) collective-permute-start(bf16[96,255]{1,0:T(8,128)(2,1)S(1)} %get-tuple-element.346), channel_id=1, source_target_pairs={{0,24},{4,28},{8,0},{12,4},{16,8},{20,12},{24,16},{28,20},{1,25},{... | collective-permute-start | bytes 146888 | tf_op jit(solution)/shard_map/ppermute | solution.py:690
  837.8 18.0 %collective-permute-start.68 = (bf16[96,255]{1,0:T(8,128)(2,1)S(1)}, bf16[96,255]{1,0:T(8,128)(2,1)S(1)}, u32[]{:S(2)}, u32[]{:S(2)}) collective-permute-start(bf16[96,255]{1,0:T(8,128)(2,1)S(1)} %get-tuple-element.347), channel_id=1, source_target_pairs={{0,16},{4,20},{8,24},{12,28},{16,0},{20,4},{24,8},{28,12},{1,17},{... | collective-permute-start | bytes 146888 | tf_op jit(solution)/shard_map/ppermute | solution.py:690
  838.7 17.0 %collective-permute-start.67 = (bf16[96,255]{1,0:T(8,128)(2,1)S(1)}, bf16[96,255]{1,0:T(8,128)(2,1)S(1)}, u32[]{:S(2)}, u32[]{:S(2)}) collective-permute-start(bf16[96,255]{1,0:T(8,128)(2,1)S(1)} %get-tuple-element.345), channel_id=1, source_target_pairs={{0,8},{4,12},{8,16},{12,20},{16,24},{20,28},{24,0},{28,4},{1,9},{5... | collective-permute-start | bytes 146888 | tf_op jit(solution)/shard_map/ppermute | solution.py:690
  844.8 20.8 %collective-permute-start.72 = (bf16[192,1536]{1,0:T(8,128)(2,1)}, bf16[192,1536]{1,0:T(8,128)(2,1)S(1)}, u32[]{:S(2)}, u32[]{:S(2)}) collective-permute-start(bf16[192,1536]{1,0:T(8,128)(2,1)} %get-tuple-element.310), channel_id=1, source_target_pairs={{0,8},{4,12},{8,16},{12,20},{16,24},{20,28},{24,0},{28,4},{1,9},{5... | collective-permute-start | bytes 1769480 | tf_op jit(solution)/shard_map/ppermute | solution.py:690
  844.8 47.7 %collective-permute-start.73 = (bf16[192,1536]{1,0:T(8,128)(2,1)}, bf16[192,1536]{1,0:T(8,128)(2,1)S(1)}, u32[]{:S(2)}, u32[]{:S(2)}) collective-permute-start(bf16[192,1536]{1,0:T(8,128)(2,1)} %get-tuple-element.309), channel_id=1, source_target_pairs={{0,16},{4,20},{8,24},{12,28},{16,0},{20,4},{24,8},{28,12},{1,17},{... | collective-permute-start | bytes 1769480 | tf_op jit(solution)/shard_map/ppermute | solution.py:690
  855.1 43.4 %collective-permute-start.74 = (bf16[192,1536]{1,0:T(8,128)(2,1)S(1)}, bf16[192,1536]{1,0:T(8,128)(2,1)S(1)}, u32[]{:S(2)}, u32[]{:S(2)}) collective-permute-start(bf16[192,1536]{1,0:T(8,128)(2,1)S(1)} %copy-done.146), channel_id=1, source_target_pairs={{0,24},{4,28},{8,0},{12,4},{16,8},{20,12},{24,16},{28,20},{1,25},{... | collective-permute-start | bytes 1769480 | tf_op jit(solution)/shard_map/ppermute | solution.py:690
  (207 other events, 1679.3 us)
Sparse Core Ops, SparseCore 0:
  12.9 56.3 all-gather.7
  71.5 41.0 all-gather.9
  114.8 61.2 all-gather.11
  178.1 36.9 all-gather.15
  216.5 39.0 all-gather.13
  257.0 61.2 all-gather.17
  320.5 36.9 all-gather.19
  491.2 38.3 reduce-scatter.7
  548.4 65.4 reduce-scatter.9
  616.5 18.9 reduce-scatter.11
  649.5 36.4 reduce-scatter.13
  688.2 34.3 reduce-scatter.15
  735.7 60.4 reduce-scatter.17
  799.1 27.6 reduce-scatter.19

commit v5 on v4

--- a/solution.py
+++ b/solution.py
@@ -717,19 +717,18 @@
         window = lax.dynamic_slice_in_dim(ring, n - 1 - lax.axis_index("dp"), n, 0)
         return jnp.swapaxes(window.reshape(self.nz, 2, -1), 0, 1)
 
-    def scatter_small(self, v, order=()):
+    def scatter_small(self, v):
         low = v.astype(bf16)
-        own = lax.dynamic_index_in_dim(v, self.y, 0, False)
-        other = self.swap_y(lax.dynamic_index_in_dim(low, 1 - self.y, 0, False))
-        part = after(own + other.astype(f32), *order)
         if self.nz > 4:
-            return self.scatter_z(part.astype(bf16))[0].astype(f32)
-        total = lax.dynamic_index_in_dim(part, self.z, 0, False)
-        part_low = part.astype(bf16)
-        for k in range(1, self.nz):
-            piece = lax.dynamic_index_in_dim(part_low, (self.z + k) % self.nz, 0, False)
-            total = total + self.shift_z(piece, k).astype(f32)
-        return total
+            total = self.scatter_z(jnp.swapaxes(low, 0, 1))[0].astype(f32)
+        else:
+            total = lax.dynamic_index_in_dim(v, self.z, 1, False)
+            for k in range(1, self.nz):
+                piece = lax.dynamic_index_in_dim(low, (self.z + k) % self.nz, 1, False)
+                total = total + self.shift_z(piece, k).astype(f32)
+        other = lax.dynamic_index_in_dim(total.astype(bf16), 1 - self.y, 0, False)
+        own = lax.dynamic_index_in_dim(total, self.y, 0, False)
+        return own + self.swap_y(other).astype(f32)
 
     def by_y(self, own, other, axis=0):
         return jnp.where(
@@ -1008,12 +1007,13 @@
     d_mix = product_nt([after(dy3, a_out.product)], [attn_out])
     d_qkv = flat(attention_backward(low, pieces(d_mix), tables))
     q_in = Sent(links, n3[:, :fh], n3[:, fh:], [d_qkv], a_out.came)
-    done = b_in.finish(b_out.terms[0], q_in.product, block_out)
-    d_n3 = product_nt([after(d_qkv, done, a_out.came)], qkv_in)
-    g2, gain_c = leave(g3, x2, r3, 2, d_n3, a_out.finish(d_n3))
+    seen = after(b_in.came, q_in.product)[:8, :128]
+    d_n3 = product_nt([after(d_qkv, q_in.product, seen + seen)], qkv_in)
+    done = b_in.finish(b_out.terms[0], d_n3, block_out)
+    g2, gain_c = leave(g3, x2, r3, 2, d_n3, done, a_out.came)
 
     dy2 = links.gather_rows(g2.astype(bf16))
-    dy2 = after(dy2, q_in.came)
+    dy2 = after(dy2, a_out.finish(g2), q_in.came)
     f_in, f_out, d_pair = ffn_backward(
         links, dy2, kept_a, ffn_a_out, q_in.came, finish=q_in
     )
@@ -1039,9 +1039,7 @@
     done = m_out.finish(m_in.product)
     d_n1 = product_nt([after(d_x, m_in.product, done), d_z], mixer_in)
 
-    done = m_in.finish(d_n1, *f_in.terms, direct=True, last=m_out.terms)
-    g0, gain_a = leave(g1, x0, r1, 0, d_n1, late=(done,))
-    input_grad = ungroup(g0, nz, 1).astype(bf16).reshape(hidden_in.shape)
+    g0, gain_a = leave(g1, x0, r1, 0, d_n1, late=(m_in.came,))
 
     grad_dt = dot_tn(d_dt, flat(ext)[:, :RANK])
     grad_x = dot_tn(flat(values), d_ext)
@@ -1061,6 +1059,8 @@
         summed[:, states : states + RANK].T,
         summed[:, states + RANK : tail].T,
     ]
+    done = m_in.finish(packed, *f_in.terms, direct=True, last=m_out.terms)
+    input_grad = ungroup(after(g0, done), nz, 1).astype(bf16).reshape(hidden_in.shape)
     gain_total = summed[:, tail:].reshape(norm_gains.shape)
     gain_total = gain_total + links.swap_core(gain_total)
     gain_total = gain_total + links.swap_x(gain_total)

time: 917 us -> 907 us (0.989)
    unnamed x370 -> x372, local copies, waits for them, and re-layouts: 52 us -> 51.9 us
where the time goes in v5:
time: 907 us; the launch traced here: 896 us
  waiting for transfers between devices  378 us (42%)
  Pallas kernels  175 us (19%)
  local copies, waits for them, and re-layouts  127 us (14%)
  starting transfers between devices  122 us (13%)
  other arithmetic  59 us (7%)
  matrix products  18.3 us (2%)
  between operations  17.1 us (2%)
    ppermute x16, waiting for transfers between devices, swap_y(): return lax.ppermute(v, 'dp', [(i, i ^ 1) for i in range(self.dp)])  177 us
    ppermute x19, waiting for transfers between devices, swap_x(): return lax.ppermute(v, 'tensor', [(i, i ^ 2) for i in range(PIECES)])  82.8 us
    ppermute x27, starting transfers between devices, swap_core(): return lax.ppermute(v, 'tensor', [(i, i ^ 1) for i in range(PIECES)])  63.9 us
    all_gather x7, waiting for transfers between devices, gather_z(): lax.all_gather(v, 'dp', axis=0, tiled=True, axis_index_groups=self.groups)  62.6 us
    unnamed x372, local copies, waits for them, and re-layouts  51.9 us
    pallas_call x16, Pallas kernels, product_tn(): pl.pallas_call(lambda *refs: tn_kernel(len(rights), bool(adds), *refs), g...  39.7 us
    pallas_call x1, Pallas kernels, scan_backward(): pl.pallas_call(scan_bwd_kernel, grid_spec=grid, out_shape=[jax.ShapeDtype...  36.7 us
    ppermute x6, waiting for transfers between devices, shift_z(): lax.ppermute(v, 'dp', [(2 * z + y, 2 * ((z + k) % n) + y) for z in range(...  35.5 us
  transfers between devices with their start and end apart: 89, of which 50 were waited for; matrix products, arithmetic and copies ran while one was open for 17% of the time, Pallas kernels for 18%

profile of v5, /device:TPU:9, one launch (start us, length us, event | category | flops | bytes accessed | tf_op | source)
XLA Modules:
  0.0 896.4 jit_solution(3644600727681678024)
XLA Ops:
  7.2 3.5 reshape.406
  24.2 3.3 collective-permute-start.1
  37.9 3.5 collective-permute-done.4
  41.4 3.8 collective-permute-done.5
  49.4 20.0 %all-gather.8.cloned.1.call-done.refs_2_ = bf16[768,1536]{1,0:T(8,128)(2,1)} async-done(((bf16[192,1536]{1,0:T(8,128)(2,1)}), bf16[768,1536]{1,0:T(8,128)(2,1)}) %all-gather.8.cloned.1.call-update) | async-done | bytes 2359312 | tf_op jit(solution)/shard_map/all_gather | solution.py:701
  75.1 6.0 collective-permute-done.7
  84.1 28.5 %all-gather.10.cloned.1.call-done = bf16[576,1536]{1,0:T(8,128)(2,1)} async-done(((bf16[144,1536]{1,0:T(8,128)(2,1)}), bf16[576,1536]{1,0:T(8,128)(2,1)}) %all-gather.10.cloned.1.call-update) | async-done | bytes 1769488 | tf_op jit(solution)/shard_map/all_gather | solution.py:701
  112.6 9.4 %collective-permute-done.10.refs_3_ = bf16[768,1536]{1,0:T(8,128)(2,1)} collective-permute-done((bf16[768,1536]{1,0:T(8,128)(2,1)}, bf16[768,1536]{1,0:T(8,128)(2,1)}, u32[]{:S(2)}, u32[]{:S(2)}) %collective-permute-start.10) | collective-permute-done | bytes 2359328 | tf_op jit(solution)/shard_map/ppermute | solution.py:686
  123.5 3.2 fusion.41
  129.3 3.8 conv_forward.1
  148.1 23.2 %scan_forward.1 = (bf16[4,2,64,768]{3,2,1,0:T(8,128)(2,1)S(1)}, f32[4,2,64,768]{3,2,1,0:T(8,128)S(1)}, bf16[8,64,16,768]{3,2,1,0:T(8,128)(2,1)}) custom-call(s32[4]{0:T(128)S(1)} %pad_add_fusion.2.slot, bf16[4,2,64,128]{3,2,1,0:T(8,128)(2,1)S(1)} %bitcast.176, bf16[96,768]{1,0:T(8,128)(2,1)S(1)} %reshape.411.wdt_ref, bf16[4,2,64,768]{3,2,1,0:T(8,128)(2,1)S(1)} %copy-done.29, ...), custom_call_target="tpu_custom_call" | custom-call | flops 1 | bytes 1 | tf_op jit(solution)/shard_map/scan_forward/pallas_call | solution.py:395
  196.1 3.9 collective-permute-done.15
  202.0 13.1 %all-gather.16.cloned.1.call-done = bf16[512,1536]{1,0:T(8,128)(2,1)} async-done(((bf16[128,1536]{1,0:T(8,128)(2,1)}), bf16[512,1536]{1,0:T(8,128)(2,1)}) %all-gather.16.cloned.1.call-update) | async-done | bytes 1572880 | tf_op jit(solution)/shard_map/all_gather | solution.py:701
  215.1 30.2 %collective-permute-done.22.other_g.other_u.refs_3_ = bf16[768,2048]{1,0:T(8,128)(2,1)} collective-permute-done((bf16[768,2048]{1,0:T(8,128)(2,1)}, bf16[768,2048]{1,0:T(8,128)(2,1)}, u32[]{:S(2)}, u32[]{:S(2)}) %collective-permute-start.22) | collective-permute-done | bytes 3145760 | tf_op jit(solution)/shard_map/ppermute | solution.py:686
  250.8 4.9 collective-permute-done.16
  259.8 6.3 gate_forward.2
  269.3 10.4 %collective-permute-done.23 = bf16[512,1536]{1,0:T(8,128)(2,1)} collective-permute-done((bf16[512,1536]{1,0:T(8,128)(2,1)}, bf16[512,1536]{1,0:T(8,128)(2,1)}, u32[]{:S(2)}, u32[]{:S(2)}) %collective-permute-start.23) | collective-permute-done | bytes 1572896 | tf_op jit(solution)/shard_map/ppermute | solution.py:686
  281.1 3.3 maximum_select_fusion.w
  298.7 18.8 %collective-permute-done.25.refs_2_ = bf16[768,1152]{1,0:T(8,128)(2,1)} collective-permute-done((bf16[768,1152]{1,0:T(8,128)(2,1)}, bf16[768,1152]{1,0:T(8,128)(2,1)}, u32[]{:S(2)}, u32[]{:S(2)}) %collective-permute-start.25) | collective-permute-done | bytes 1769504 | tf_op jit(solution)/shard_map/ppermute | solution.py:686
  330.0 4.8 collective-permute-start.28
  334.8 5.3 collective-permute-start.29
  346.6 3.3 fusion.38
  351.2 3.1 attention_forward.1
  354.3 33.3 %collective-permute-done.30.other_g.other_u.refs_3_ = bf16[768,2048]{1,0:T(8,128)(2,1)} collective-permute-done((bf16[768,2048]{1,0:T(8,128)(2,1)}, bf16[768,2048]{1,0:T(8,128)(2,1)}, u32[]{:S(2)}, u32[]{:S(2)}) %collective-permute-start.30) | collective-permute-done | bytes 3145760 | tf_op jit(solution)/shard_map/ppermute | solution.py:686
  388.7 4.8 collective-permute-start.31
  400.4 7.8 collective-permute-done.32
  412.6 8.0 collective-permute-done.33
  426.0 6.2 gate_forward.3
  437.5 3.7 maximum_select_fusion.1.w
  441.2 4.7 gate_backward.2
  445.9 3.5 product_tn.17
  449.4 7.4 product_nt.6
  463.2 7.2 collective-permute-done.40.refs_2_
  473.5 5.2 collective-permute-done.41
  479.7 7.4 collective-permute-done.38
  492.6 3.5 collective-permute-start.43
  498.7 4.2 collective-permute-start.44
  510.3 4.0 attention_backward.1
  517.1 5.1 product_nt.8
  523.4 15.6 %collective-permute-done.46.refs_3_ = bf16[768,2048]{1,0:T(8,128)(2,1)} collective-permute-done((bf16[768,2048]{1,0:T(8,128)(2,1)}, bf16[768,2048]{1,0:T(8,128)(2,1)}, u32[]{:S(2)}, u32[]{:S(2)}) %collective-permute-start.46) | collective-permute-done | bytes 3145760 | tf_op jit(solution)/shard_map/ppermute | solution.py:686
  542.6 4.0 product_tn.21
  549.6 4.0 collective-permute-start.45
  555.8 13.0 %collective-permute-done.47.refs_2_ = bf16[192,1536]{1,0:T(8,128)(2,1)S(1)} collective-permute-done((bf16[192,1536]{1,0:T(8,128)(2,1)}, bf16[192,1536]{1,0:T(8,128)(2,1)S(1)}, u32[]{:S(2)}, u32[]{:S(2)}) %collective-permute-start.47) | collective-permute-done | bytes 589856 | tf_op jit(solution)/shard_map/ppermute | solution.py:686
  571.4 7.4 collective-permute-done.48
  586.0 4.7 collective-permute-done.49
  596.5 13.1 %collective-permute-done.52.refs_2_ = bf16[768,1152]{1,0:T(8,128)(2,1)} collective-permute-done((bf16[768,1152]{1,0:T(8,128)(2,1)}, bf16[768,1152]{1,0:T(8,128)(2,1)}, u32[]{:S(2)}, u32[]{:S(2)}) %collective-permute-start.52) | collective-permute-done | bytes 1769504 | tf_op jit(solution)/shard_map/ppermute | solution.py:686
  614.2 3.2 product_tn.24
  621.1 4.8 gate_backward.3
  629.9 7.2 product_nt.9
  647.5 6.4 collective-permute-done.55
  661.3 4.0 collective-permute-start.57
  665.2 3.2 collective-permute-done.56
  668.5 4.5 collective-permute-start.58
  679.3 36.7 %scan_backward.1 = (bf16[4,2,64,768]{3,2,1,0:T(8,128)(2,1)S(1)}, f32[4,2,64,768]{3,2,1,0:T(8,128)S(1)}, bf16[4,2,64,768]{3,2,1,0:T(8,128)(2,1)S(1)}, f32[4,2,2,8...) custom-call(s32[4]{0:T(128)S(1)} %pad_add_fusion.2.slot, ...), custom_call_target="tpu_custom_call" | custom-call | flops 1 | bytes 1 | tf_op jit(solution)/shard_map/scan_backward/pallas_call | solution.py:441
  721.0 5.3 product_tn.28
  742.0 5.7 conv_backward.1
  748.3 3.1 product_tn.29
  751.4 5.0 collective-permute-done.62.refs_2_
  757.6 3.1 product_tn.30
  761.8 5.6 product_nt.11
  779.1 9.1 %collective-permute-done.64 = bf16[128,1536]{1,0:T(8,128)(2,1)S(1)} collective-permute-done((bf16[128,1536]{1,0:T(8,128)(2,1)}, bf16[128,1536]{1,0:T(8,128)(2,1)S(1)}, u32[]{:S(2)}, u32[]{:S(2)}) %collective-permute-start.64) | collective-permute-done | bytes 393248 | tf_op jit(solution)/shard_map/ppermute | solution.py:698
  789.5 18.7 %collective-permute-done.65.refs_3_ = bf16[768,1536]{1,0:T(8,128)(2,1)} collective-permute-done((bf16[768,1536]{1,0:T(8,128)(2,1)}, bf16[768,1536]{1,0:T(8,128)(2,1)}, u32[]{:S(2)}, u32[]{:S(2)}) %collective-permute-start.65) | collective-permute-done | bytes 2359328 | tf_op jit(solution)/shard_map/ppermute | solution.py:686
  828.2 3.5 product_tn.31
  858.8 26.5 %collective-permute-done.73.refs_2_ = bf16[192,1536]{1,0:T(8,128)(2,1)S(1)} collective-permute-done((bf16[192,1536]{1,0:T(8,128)(2,1)}, bf16[192,1536]{1,0:T(8,128)(2,1)S(1)}, u32[]{:S(2)}, u32[]{:S(2)}) %collective-permute-start.73) | collective-permute-done | bytes 589856 | tf_op jit(solution)/shard_map/ppermute | solution.py:690
  (782 shorter events, 330.3 us)
Async XLA Ops:
  7.2 62.2 %all-gather.8.cloned.1.call-start = ((), (), s32[]{:S(2)}) async-start(), calls=%async_computation.7 | async-start | bytes 2949120 | tf_op jit(solution)/shard_map/all_gather | solution.py:701
  12.8 99.8 %all-gather.10.cloned.1.call-start = ((), (), s32[]{:S(2)}) async-start(), calls=%async_computation.8 | async-start | bytes 2211840 | tf_op jit(solution)/shard_map/all_gather | solution.py:701
  21.9 154.2 %all-gather.12.cloned.1.call-start = ((), (), s32[]{:S(2)}) async-start(), calls=%async_computation.9 | async-start | bytes 3932160 | tf_op jit(solution)/shard_map/all_gather | solution.py:701
  22.7 192.4 %all-gather.16.cloned.1.call-start = ((), (), s32[]{:S(2)}) async-start(), calls=%async_computation.11 | async-start | bytes 1966080 | tf_op jit(solution)/shard_map/all_gather | solution.py:701
  23.0 8.1 collective-permute-start
  24.2 9.4 %collective-permute-start.1 = (bf16[24480]{0:T(1024)(128)(2,1)S(1)}, bf16[24480]{0:T(1024)(128)(2,1)S(1)}, u32[]{:S(2)}, u32[]{:S(2)}) collective-permute-start(bf16[24480]{0:T(1024)(128)(2,1)S(1)} %pad_maximum_fusion.19), channel_id=1, source_target_pairs={{0,24},{4,28},{8,0},{12,4},{16,8},{20,12},{24,16},{28,20},{1,25},{... | collective-permute-start | bytes 146888 | tf_op jit(solution)/shard_map/ppermute | solution.py:714
  27.5 8.6 collective-permute-start.2
  27.5 10.3 %collective-permute-start.3 = (bf16[24480]{0:T(1024)(128)(2,1)S(1)}, bf16[24480]{0:T(1024)(128)(2,1)S(1)}, u32[]{:S(2)}, u32[]{:S(2)}) collective-permute-start(bf16[24480]{0:T(1024)(128)(2,1)S(1)} %pad_maximum_fusion.19), channel_id=1, source_target_pairs={{0,16},{4,20},{8,24},{12,28},{16,0},{20,4},{24,8},{28,12},{1,17},{... | collective-permute-start | bytes 146888 | tf_op jit(solution)/shard_map/ppermute | solution.py:714
  27.5 13.8 %collective-permute-start.4 = (bf16[24480]{0:T(1024)(128)(2,1)S(1)}, bf16[24480]{0:T(1024)(128)(2,1)S(1)}, u32[]{:S(2)}, u32[]{:S(2)}) collective-permute-start(bf16[24480]{0:T(1024)(128)(2,1)S(1)} %pad_maximum_fusion.19), channel_id=1, source_target_pairs={{0,12},{4,16},{8,20},{12,24},{16,28},{20,0},{24,4},{28,8},{1,13},{... | collective-permute-start | bytes 146888 | tf_op jit(solution)/shard_map/ppermute | solution.py:714
  30.9 238.4 %all-gather.14.cloned.1.call-start = ((), (), s32[]{:S(2)}) async-start(), calls=%async_computation.10 | async-start | bytes 2211840 | tf_op jit(solution)/shard_map/all_gather | solution.py:701
  31.1 14.1 %collective-permute-start.5 = (bf16[24480]{0:T(1024)(128)(2,1)S(1)}, bf16[24480]{0:T(1024)(128)(2,1)S(1)}, u32[]{:S(2)}, u32[]{:S(2)}) collective-permute-start(bf16[24480]{0:T(1024)(128)(2,1)S(1)} %pad_maximum_fusion.19), channel_id=1, source_target_pairs={{0,8},{4,12},{8,16},{12,20},{16,24},{20,28},{24,0},{28,4},{1,9},{5... | collective-permute-start | bytes 146888 | tf_op jit(solution)/shard_map/ppermute | solution.py:714
  33.6 11.7 %collective-permute-start.6 = (bf16[24480]{0:T(1024)(128)(2,1)S(1)}, bf16[24480]{0:T(1024)(128)(2,1)S(1)}, u32[]{:S(2)}, u32[]{:S(2)}) collective-permute-start(bf16[24480]{0:T(1024)(128)(2,1)S(1)} %pad_maximum_fusion.19), channel_id=1, source_target_pairs={{0,4},{4,8},{8,12},{12,16},{16,20},{20,24},{24,28},{28,0},{1,5},{5... | collective-permute-start | bytes 146888 | tf_op jit(solution)/shard_map/ppermute | solution.py:714
  69.4 52.6 %collective-permute-start.10 = (bf16[768,1536]{1,0:T(8,128)(2,1)}, bf16[768,1536]{1,0:T(8,128)(2,1)}, u32[]{:S(2)}, u32[]{:S(2)}) collective-permute-start(bf16[768,1536]{1,0:T(8,128)(2,1)} %all-gather.8.cloned.1.call-done.refs_2_), channel_id=1, source_target_pairs={{0,4},{4,0},{8,12},{12,8},{16,20},{20,16},{24,28},{28,24},{1,5},{5... | collective-permute-start | bytes 7077896 | tf_op jit(solution)/shard_map/ppermute | solution.py:686
  71.0 10.1 %collective-permute-start.7 = (bf16[128,1536]{1,0:T(8,128)(2,1)S(1)}, bf16[128,1536]{1,0:T(8,128)(2,1)S(1)}, u32[]{:S(2)}, u32[]{:S(2)}) collective-permute-start(bf16[128,1536]{1,0:T(8,128)(2,1)S(1)} %maximum_select_fusion.8), channel_id=1, source_target_pairs={{0,2},{1,3},{2,0},{3,1},{4,6},{5,7},{6,4},{7,5},{8,10},{9,11},{10,... | collective-permute-start | bytes 1179656 | tf_op jit(solution)/shard_map/ppermute | solution.py:698
  74.1 9.8 %collective-permute-start.8 = (bf16[128,1536]{1,0:T(8,128)(2,1)S(1)}, bf16[128,1536]{1,0:T(8,128)(2,1)S(1)}, u32[]{:S(2)}, u32[]{:S(2)}) collective-permute-start(bf16[128,1536]{1,0:T(8,128)(2,1)S(1)} %maximum_select_fusion.8), channel_id=1, source_target_pairs={{0,1},{1,0},{2,3},{3,2},{4,5},{5,4},{6,7},{7,6},{8,9},{9,8},{10,11... | collective-permute-start | bytes 1179656 | tf_op jit(solution)/shard_map/ppermute | solution.py:695
  122.0 50.5 %collective-permute-start.13 = (bf16[576,1536]{1,0:T(8,128)(2,1)}, bf16[576,1536]{1,0:T(8,128)(2,1)}, u32[]{:S(2)}, u32[]{:S(2)}) collective-permute-start(bf16[576,1536]{1,0:T(8,128)(2,1)} %all-gather.10.cloned.1.call-done), channel_id=1, source_target_pairs={{0,4},{4,0},{8,12},{12,8},{16,20},{20,16},{24,28},{28,24},{1,5},{5... | collective-permute-start | bytes 5308424 | tf_op jit(solution)/shard_map/ppermute | solution.py:686
  136.9 184.5 %all-gather.18.cloned.1.call-start = ((), (), s32[]{:S(2)}) async-start(), calls=%async_computation.12 | async-start | bytes 3932160 | tf_op jit(solution)/shard_map/all_gather | solution.py:701
  176.1 69.1 %collective-permute-start.22 = (bf16[768,2048]{1,0:T(8,128)(2,1)}, bf16[768,2048]{1,0:T(8,128)(2,1)}, u32[]{:S(2)}, u32[]{:S(2)}) collective-permute-start(bf16[768,2048]{1,0:T(8,128)(2,1)} %all-gather.12.cloned.1.call-done.own_g.own_u.refs_2_), channel_id=1, source_target_pairs={{0,4},{4,0},{8,12},{12,8},{16,20},{20,16},{24,28},{28,24},{1,5},{5... | collective-permute-start | bytes 9437192 | tf_op jit(solution)/shard_map/ppermute | solution.py:686
  183.4 214.1 %all-gather.20.cloned.1.call-start = ((), (), s32[]{:S(2)}) async-start(), calls=%async_computation.13 | async-start | bytes 1966080 | tf_op jit(solution)/shard_map/all_gather | solution.py:701
  189.4 10.6 %collective-permute-start.15 = (bf16[128,1536]{1,0:T(8,128)(2,1)}, bf16[128,1536]{1,0:T(8,128)(2,1)}, u32[]{:S(2)}, u32[]{:S(2)}) collective-permute-start(bf16[128,1536]{1,0:T(8,128)(2,1)} %fusion.18), channel_id=1, source_target_pairs={{0,2},{1,3},{2,0},{3,1},{4,6},{5,7},{6,4},{7,5},{8,10},{9,11},{10,... | collective-permute-start | bytes 1179656 | tf_op jit(solution)/shard_map/ppermute | solution.py:698
  195.0 55.3 %collective-permute-start.19 = (bf16[128,1536]{1,0:T(8,128)(2,1)S(1)}, bf16[128,1536]{1,0:T(8,128)(2,1)}, u32[]{:S(2)}, u32[]{:S(2)}) collective-permute-start(bf16[128,1536]{1,0:T(8,128)(2,1)S(1)} %copy.296), channel_id=1, source_target_pairs={{0,2},{1,3},{2,0},{3,1},{4,6},{5,7},{6,4},{7,5},{8,10},{9,11},{10,... | collective-permute-start | bytes 1179656 | tf_op jit(solution)/shard_map/ppermute | solution.py:698
  245.2 34.5 %collective-permute-start.23 = (bf16[512,1536]{1,0:T(8,128)(2,1)}, bf16[512,1536]{1,0:T(8,128)(2,1)}, u32[]{:S(2)}, u32[]{:S(2)}) collective-permute-start(bf16[512,1536]{1,0:T(8,128)(2,1)} %all-gather.16.cloned.1.call-done), channel_id=1, source_target_pairs={{0,4},{4,0},{8,12},{12,8},{16,20},{20,16},{24,28},{28,24},{1,5},{5... | collective-permute-start | bytes 4718600 | tf_op jit(solution)/shard_map/ppermute | solution.py:686
  246.8 8.9 collective-permute-start.16
  248.0 10.4 %collective-permute-start.20 = (bf16[128,1536]{1,0:T(8,128)(2,1)S(1)}, bf16[128,1536]{1,0:T(8,128)(2,1)S(1)}, u32[]{:S(2)}, u32[]{:S(2)}) collective-permute-start(bf16[128,1536]{1,0:T(8,128)(2,1)S(1)} %copy.296), channel_id=1, source_target_pairs={{0,1},{1,0},{2,3},{3,2},{4,5},{5,4},{6,7},{7,6},{8,9},{9,8},{10,11... | collective-permute-start | bytes 1179656 | tf_op jit(solution)/shard_map/ppermute | solution.py:695
  250.2 8.1 collective-permute-start.21
  250.2 9.3 %collective-permute-start.17 = (bf16[128,1536]{1,0:T(8,128)(2,1)S(1)}, bf16[128,1536]{1,0:T(8,128)(2,1)S(1)}, u32[]{:S(2)}, u32[]{:S(2)}) collective-permute-start(bf16[128,1536]{1,0:T(8,128)(2,1)S(1)} %maximum_select_fusion.9), channel_id=1, source_target_pairs={{0,1},{1,0},{2,3},{3,2},{4,5},{5,4},{6,7},{7,6},{8,9},{9,8},{10,11... | collective-permute-start | bytes 1179656 | tf_op jit(solution)/shard_map/ppermute | solution.py:695
  279.7 37.8 %collective-permute-start.25 = (bf16[768,1152]{1,0:T(8,128)(2,1)}, bf16[768,1152]{1,0:T(8,128)(2,1)}, u32[]{:S(2)}, u32[]{:S(2)}) collective-permute-start(bf16[768,1152]{1,0:T(8,128)(2,1)} %all-gather.14.cloned.1.call-done.refs_1_), channel_id=1, source_target_pairs={{0,4},{4,0},{8,12},{12,8},{16,20},{20,16},{24,28},{28,24},{1,5},{5... | collective-permute-start | bytes 5308424 | tf_op jit(solution)/shard_map/ppermute | solution.py:686
  293.0 246.0 %reduce-scatter.8.cloned.1.call-start = ((), (), s32[]{:S(2)}) async-start(), calls=%async_computation.14 | async-start | bytes 1966080 | tf_op jit(solution)/shard_map/reduce_scatter | solution.py:704
  321.4 66.2 %collective-permute-start.30 = (bf16[768,2048]{1,0:T(8,128)(2,1)}, bf16[768,2048]{1,0:T(8,128)(2,1)}, u32[]{:S(2)}, u32[]{:S(2)}) collective-permute-start(bf16[768,2048]{1,0:T(8,128)(2,1)} %all-gather.18.cloned.1.call-done.own_g.own_u.refs_2_), channel_id=1, source_target_pairs={{0,4},{4,0},{8,12},{12,8},{16,20},{20,16},{24,28},{28,24},{1,5},{5... | collective-permute-start | bytes 9437192 | tf_op jit(solution)/shard_map/ppermute | solution.py:686
  330.0 14.9 %collective-permute-start.28 = (bf16[128,1536]{1,0:T(8,128)(2,1)S(1)}, bf16[128,1536]{1,0:T(8,128)(2,1)}, u32[]{:S(2)}, u32[]{:S(2)}) collective-permute-start(bf16[128,1536]{1,0:T(8,128)(2,1)S(1)} %maximum_select_fusion.10), channel_id=1, source_target_pairs={{0,1},{1,0},{2,3},{3,2},{4,5},{5,4},{6,7},{7,6},{8,9},{9,8},{10,11... | collective-permute-start | bytes 1179656 | tf_op jit(solution)/shard_map/ppermute | solution.py:695
  334.8 10.0 %collective-permute-start.29 = (bf16[128,1536]{1,0:T(8,128)(2,1)}, bf16[128,1536]{1,0:T(8,128)(2,1)}, u32[]{:S(2)}, u32[]{:S(2)}) collective-permute-start(bf16[128,1536]{1,0:T(8,128)(2,1)} %collective-permute-done.27), channel_id=1, source_target_pairs={{0,1},{1,0},{2,3},{3,2},{4,5},{5,4},{6,7},{7,6},{8,9},{9,8},{10,11... | collective-permute-start | bytes 1179656 | tf_op jit(solution)/shard_map/ppermute | solution.py:695
  397.5 10.6 %collective-permute-start.32 = (bf16[128,1536]{1,0:T(8,128)(2,1)}, bf16[128,1536]{1,0:T(8,128)(2,1)}, u32[]{:S(2)}, u32[]{:S(2)}) collective-permute-start(bf16[128,1536]{1,0:T(8,128)(2,1)} %fusion.12), channel_id=1, source_target_pairs={{0,2},{1,3},{2,0},{3,1},{4,6},{5,7},{6,4},{7,5},{8,10},{9,11},{10,... | collective-permute-start | bytes 1179656 | tf_op jit(solution)/shard_map/ppermute | solution.py:698
  399.0 35.6 %collective-permute-start.36 = (bf16[512,1536]{1,0:T(8,128)(2,1)}, bf16[512,1536]{1,0:T(8,128)(2,1)}, u32[]{:S(2)}, u32[]{:S(2)}) collective-permute-start(bf16[512,1536]{1,0:T(8,128)(2,1)} %all-gather.20.cloned.1.call-done), channel_id=1, source_target_pairs={{0,4},{4,0},{8,12},{12,8},{16,20},{20,16},{24,28},{28,24},{1,5},{5... | collective-permute-start | bytes 4718600 | tf_op jit(solution)/shard_map/ppermute | solution.py:686
  411.0 9.6 %collective-permute-start.33 = (bf16[128,1536]{1,0:T(8,128)(2,1)S(1)}, bf16[128,1536]{1,0:T(8,128)(2,1)}, u32[]{:S(2)}, u32[]{:S(2)}) collective-permute-start(bf16[128,1536]{1,0:T(8,128)(2,1)S(1)} %maximum_select_fusion.11), channel_id=1, source_target_pairs={{0,2},{1,3},{2,0},{3,1},{4,6},{5,7},{6,4},{7,5},{8,10},{9,11},{10,... | collective-permute-start | bytes 1179656 | tf_op jit(solution)/shard_map/ppermute | solution.py:698
  411.2 13.5 %collective-permute-start.34 = (bf16[128,1536]{1,0:T(8,128)(2,1)S(1)}, bf16[128,1536]{1,0:T(8,128)(2,1)}, u32[]{:S(2)}, u32[]{:S(2)}) collective-permute-start(bf16[128,1536]{1,0:T(8,128)(2,1)S(1)} %maximum_select_fusion.11), channel_id=1, source_target_pairs={{0,1},{1,0},{2,3},{3,2},{4,5},{5,4},{6,7},{7,6},{8,9},{9,8},{10,11... | collective-permute-start | bytes 1179656 | tf_op jit(solution)/shard_map/ppermute | solution.py:695
  436.0 34.4 %collective-permute-start.40 = (bf16[512,1536]{1,0:T(8,128)(2,1)S(1)}, bf16[512,1536]{1,0:T(8,128)(2,1)S(1)}, u32[]{:S(2)}, u32[]{:S(2)}) collective-permute-start(bf16[512,1536]{1,0:T(8,128)(2,1)S(1)} %product_tn.16), channel_id=1, source_target_pairs={{0,4},{4,0},{8,12},{12,8},{16,20},{20,16},{24,28},{28,24},{1,5},{5... | collective-permute-start | bytes 4718600 | tf_op jit(solution)/shard_map/ppermute | solution.py:686
  470.4 8.3 collective-permute-start.41
  471.9 15.2 %collective-permute-start.38 = (bf16[128,1536]{1,0:T(8,128)(2,1)S(1)}, bf16[128,1536]{1,0:T(8,128)(2,1)S(1)}, u32[]{:S(2)}, u32[]{:S(2)}) collective-permute-start(bf16[128,1536]{1,0:T(8,128)(2,1)S(1)} %fusion.8), channel_id=1, source_target_pairs={{0,2},{1,3},{2,0},{3,1},{4,6},{5,7},{6,4},{7,5},{8,10},{9,11},{10,... | collective-permute-start | bytes 1179656 | tf_op jit(solution)/shard_map/ppermute | solution.py:698
  472.1 66.9 %collective-permute-start.46 = (bf16[768,2048]{1,0:T(8,128)(2,1)}, bf16[768,2048]{1,0:T(8,128)(2,1)}, u32[]{:S(2)}, u32[]{:S(2)}) collective-permute-start(bf16[768,2048]{1,0:T(8,128)(2,1)} %product_tn.17), channel_id=1, source_target_pairs={{0,4},{4,0},{8,12},{12,8},{16,20},{20,16},{24,28},{28,24},{1,5},{5... | collective-permute-start | bytes 9437192 | tf_op jit(solution)/shard_map/ppermute | solution.py:686
  491.1 165.3 %reduce-scatter.10.cloned.1.call-start = ((), (), s32[]{:S(2)}) async-start(), calls=%async_computation.15 | async-start | bytes 3932160 | tf_op jit(solution)/shard_map/reduce_scatter | solution.py:704
  492.6 13.6 %collective-permute-start.43 = (bf16[128,1536]{1,0:T(8,128)(2,1)S(1)}, bf16[128,1536]{1,0:T(8,128)(2,1)}, u32[]{:S(2)}, u32[]{:S(2)}) collective-permute-start(bf16[128,1536]{1,0:T(8,128)(2,1)S(1)} %copy-done.134), channel_id=1, source_target_pairs={{0,1},{1,0},{2,3},{3,2},{4,5},{5,4},{6,7},{7,6},{8,9},{9,8},{10,11... | collective-permute-start | bytes 1179656 | tf_op jit(solution)/shard_map/ppermute | solution.py:695
  548.2 171.6 %reduce-scatter.12.cloned.1.call-start = ((), (), s32[]{:S(2)}) async-start(), calls=%async_computation.16 | async-start | bytes 737280 | tf_op jit(solution)/shard_map/reduce_scatter | solution.py:704
  553.6 15.2 %collective-permute-start.47 = (bf16[192,1536]{1,0:T(8,128)(2,1)}, bf16[192,1536]{1,0:T(8,128)(2,1)S(1)}, u32[]{:S(2)}, u32[]{:S(2)}) collective-permute-start(bf16[192,1536]{1,0:T(8,128)(2,1)} %copy-done.92), channel_id=1, source_target_pairs={{0,4},{4,0},{8,12},{12,8},{16,20},{20,16},{24,28},{28,24},{1,5},{5... | collective-permute-start | bytes 1769480 | tf_op jit(solution)/shard_map/ppermute | solution.py:686
  568.8 10.0 %collective-permute-start.48 = (bf16[128,1536]{1,0:T(8,128)(2,1)S(1)}, bf16[128,1536]{1,0:T(8,128)(2,1)S(1)}, u32[]{:S(2)}, u32[]{:S(2)}) collective-permute-start(bf16[128,1536]{1,0:T(8,128)(2,1)S(1)} %fusion.4), channel_id=1, source_target_pairs={{0,2},{1,3},{2,0},{3,1},{4,6},{5,7},{6,4},{7,5},{8,10},{9,11},{10,... | collective-permute-start | bytes 1179656 | tf_op jit(solution)/shard_map/ppermute | solution.py:698
  570.2 39.4 %collective-permute-start.52 = (bf16[768,1152]{1,0:T(8,128)(2,1)}, bf16[768,1152]{1,0:T(8,128)(2,1)}, u32[]{:S(2)}, u32[]{:S(2)}) collective-permute-start(bf16[768,1152]{1,0:T(8,128)(2,1)} %product_tn.20), channel_id=1, source_target_pairs={{0,4},{4,0},{8,12},{12,8},{16,20},{20,16},{24,28},{28,24},{1,5},{5... | collective-permute-start | bytes 5308424 | tf_op jit(solution)/shard_map/ppermute | solution.py:686
  581.3 9.4 %collective-permute-start.49 = (bf16[128,1536]{1,0:T(8,128)(2,1)}, bf16[128,1536]{1,0:T(8,128)(2,1)}, u32[]{:S(2)}, u32[]{:S(2)}) collective-permute-start(bf16[128,1536]{1,0:T(8,128)(2,1)} %get-tuple-element.296), channel_id=1, source_target_pairs={{0,2},{1,3},{2,0},{3,1},{4,6},{5,7},{6,4},{7,5},{8,10},{9,11},{10,... | collective-permute-start | bytes 1179656 | tf_op jit(solution)/shard_map/ppermute | solution.py:698
  584.1 135.8 %reduce-scatter.14.cloned.1.call-start = ((), (), s32[]{:S(2)}) async-start(), calls=%async_computation.17 | async-start | bytes 2211840 | tf_op jit(solution)/shard_map/reduce_scatter | solution.py:704
  584.1 11.1 %collective-permute-start.50 = (bf16[128,1536]{1,0:T(8,128)(2,1)}, bf16[128,1536]{1,0:T(8,128)(2,1)S(1)}, u32[]{:S(2)}, u32[]{:S(2)}) collective-permute-start(bf16[128,1536]{1,0:T(8,128)(2,1)} %get-tuple-element.296), channel_id=1, source_target_pairs={{0,1},{1,0},{2,3},{3,2},{4,5},{5,4},{6,7},{7,6},{8,9},{9,8},{10,11... | collective-permute-start | bytes 1179656 | tf_op jit(solution)/shard_map/ppermute | solution.py:695
  611.8 34.3 %collective-permute-start.54 = (bf16[512,1536]{1,0:T(8,128)(2,1)}, bf16[512,1536]{1,0:T(8,128)(2,1)}, u32[]{:S(2)}, u32[]{:S(2)}) collective-permute-start(bf16[512,1536]{1,0:T(8,128)(2,1)} %product_tn.23), channel_id=1, source_target_pairs={{0,4},{4,0},{8,12},{12,8},{16,20},{20,16},{24,28},{28,24},{1,5},{5... | collective-permute-start | bytes 4718600 | tf_op jit(solution)/shard_map/ppermute | solution.py:686
  641.5 78.4 %reduce-scatter.16.cloned.1.call-start = ((), (), s32[]{:S(2)}) async-start(), calls=%async_computation.18 | async-start | bytes 1966080 | tf_op jit(solution)/shard_map/reduce_scatter | solution.py:704
  646.1 73.7 %collective-permute-start.59 = (bf16[768,2048]{1,0:T(8,128)(2,1)}, bf16[768,2048]{1,0:T(8,128)(2,1)}, u32[]{:S(2)}, u32[]{:S(2)}) collective-permute-start(bf16[768,2048]{1,0:T(8,128)(2,1)} %copy-done.41), channel_id=1, source_target_pairs={{0,4},{4,0},{8,12},{12,8},{16,20},{20,16},{24,28},{28,24},{1,5},{5... | collective-permute-start | bytes 9437192 | tf_op jit(solution)/shard_map/ppermute | solution.py:686
  661.1 164.8 %reduce-scatter.18.cloned.1.call-start = ((), (), s32[]{:S(2)}) async-start(), calls=%async_computation.19 | async-start | bytes 3932160 | tf_op jit(solution)/shard_map/reduce_scatter | solution.py:704
  661.3 13.6 %collective-permute-start.57 = (bf16[128,1536]{1,0:T(8,128)(2,1)}, bf16[128,1536]{1,0:T(8,128)(2,1)S(1)}, u32[]{:S(2)}, u32[]{:S(2)}) collective-permute-start(bf16[128,1536]{1,0:T(8,128)(2,1)} %get-tuple-element.293), channel_id=1, source_target_pairs={{0,1},{1,0},{2,3},{3,2},{4,5},{5,4},{6,7},{7,6},{8,9},{9,8},{10,11... | collective-permute-start | bytes 1179656 | tf_op jit(solution)/shard_map/ppermute | solution.py:695
  726.3 105.4 %reduce-scatter.20.cloned.1.call-start = ((), (), s32[]{:S(2)}) async-start(), calls=%async_computation.20 | async-start | bytes 1474560 | tf_op jit(solution)/shard_map/reduce_scatter | solution.py:704
  728.9 27.5 %collective-permute-start.62 = (bf16[384,1536]{1,0:T(8,128)(2,1)}, bf16[384,1536]{1,0:T(8,128)(2,1)}, u32[]{:S(2)}, u32[]{:S(2)}) collective-permute-start(bf16[384,1536]{1,0:T(8,128)(2,1)} %copy-done.67), channel_id=1, source_target_pairs={{0,4},{4,0},{8,12},{12,8},{16,20},{20,16},{24,28},{28,24},{1,5},{5... | collective-permute-start | bytes 3538952 | tf_op jit(solution)/shard_map/ppermute | solution.py:686
  756.4 51.8 %collective-permute-start.65 = (bf16[768,1536]{1,0:T(8,128)(2,1)}, bf16[768,1536]{1,0:T(8,128)(2,1)}, u32[]{:S(2)}, u32[]{:S(2)}) collective-permute-start(bf16[768,1536]{1,0:T(8,128)(2,1)} %product_tn.29), channel_id=1, source_target_pairs={{0,4},{4,0},{8,12},{12,8},{16,20},{20,16},{24,28},{28,24},{1,5},{5... | collective-permute-start | bytes 7077896 | tf_op jit(solution)/shard_map/ppermute | solution.py:686
  777.1 11.1 %collective-permute-start.64 = (bf16[128,1536]{1,0:T(8,128)(2,1)}, bf16[128,1536]{1,0:T(8,128)(2,1)S(1)}, u32[]{:S(2)}, u32[]{:S(2)}) collective-permute-start(bf16[128,1536]{1,0:T(8,128)(2,1)} %fusion), channel_id=1, source_target_pairs={{0,2},{1,3},{2,0},{3,1},{4,6},{5,7},{6,4},{7,5},{8,10},{9,11},{10,... | collective-permute-start | bytes 1179656 | tf_op jit(solution)/shard_map/ppermute | solution.py:698
  809.9 9.5 %collective-permute-start.68 = (bf16[2,96,255]{2,1,0:T(8,128)(2,1)S(1)}, bf16[2,96,255]{2,1,0:T(8,128)(2,1)S(1)}, u32[]{:S(2)}, u32[]{:S(2)}) collective-permute-start(bf16[2,96,255]{2,1,0:T(8,128)(2,1)S(1)} %get-tuple-element.337), channel_id=1, source_target_pairs={{0,24},{4,28},{8,0},{12,4},{16,8},{20,12},{24,16},{28,20},{1,25},{... | collective-permute-start | bytes 293768 | tf_op jit(solution)/shard_map/ppermute | solution.py:690
  812.7 9.2 %collective-permute-start.67 = (bf16[2,96,255]{2,1,0:T(8,128)(2,1)S(1)}, bf16[2,96,255]{2,1,0:T(8,128)(2,1)S(1)}, u32[]{:S(2)}, u32[]{:S(2)}) collective-permute-start(bf16[2,96,255]{2,1,0:T(8,128)(2,1)S(1)} %get-tuple-element.336), channel_id=1, source_target_pairs={{0,16},{4,20},{8,24},{12,28},{16,0},{20,4},{24,8},{28,12},{1,17},{... | collective-permute-start | bytes 293768 | tf_op jit(solution)/shard_map/ppermute | solution.py:690
  813.7 10.3 %collective-permute-start.66 = (bf16[2,96,255]{2,1,0:T(8,128)(2,1)S(1)}, bf16[2,96,255]{2,1,0:T(8,128)(2,1)S(1)}, u32[]{:S(2)}, u32[]{:S(2)}) collective-permute-start(bf16[2,96,255]{2,1,0:T(8,128)(2,1)S(1)} %get-tuple-element.335), channel_id=1, source_target_pairs={{0,8},{4,12},{8,16},{12,20},{16,24},{20,28},{24,0},{28,4},{1,9},{5... | collective-permute-start | bytes 293768 | tf_op jit(solution)/shard_map/ppermute | solution.py:690
  824.8 13.2 %collective-permute-start.69 = (bf16[96,255]{1,0:T(8,128)(2,1)S(1)}, bf16[96,255]{1,0:T(8,128)(2,1)S(1)}, u32[]{:S(2)}, u32[]{:S(2)}) collective-permute-start(bf16[96,255]{1,0:T(8,128)(2,1)S(1)} %fusion.33), channel_id=1, source_target_pairs={{0,4},{4,0},{8,12},{12,8},{16,20},{20,16},{24,28},{28,24},{1,5},{5... | collective-permute-start | bytes 146888 | tf_op jit(solution)/shard_map/ppermute | solution.py:686
  833.1 25.7 %collective-permute-start.72 = (bf16[192,1536]{1,0:T(8,128)(2,1)}, bf16[192,1536]{1,0:T(8,128)(2,1)S(1)}, u32[]{:S(2)}, u32[]{:S(2)}) collective-permute-start(bf16[192,1536]{1,0:T(8,128)(2,1)} %get-tuple-element.310), channel_id=1, source_target_pairs={{0,8},{4,12},{8,16},{12,20},{16,24},{20,28},{24,0},{28,4},{1,9},{5... | collective-permute-start | bytes 1769480 | tf_op jit(solution)/shard_map/ppermute | solution.py:690
  835.3 50.0 %collective-permute-start.73 = (bf16[192,1536]{1,0:T(8,128)(2,1)}, bf16[192,1536]{1,0:T(8,128)(2,1)S(1)}, u32[]{:S(2)}, u32[]{:S(2)}) collective-permute-start(bf16[192,1536]{1,0:T(8,128)(2,1)} %get-tuple-element.309), channel_id=1, source_target_pairs={{0,16},{4,20},{8,24},{12,28},{16,0},{20,4},{24,8},{28,12},{1,17},{... | collective-permute-start | bytes 1769480 | tf_op jit(solution)/shard_map/ppermute | solution.py:690
  838.0 50.1 %collective-permute-start.74 = (bf16[192,1536]{1,0:T(8,128)(2,1)}, bf16[192,1536]{1,0:T(8,128)(2,1)S(1)}, u32[]{:S(2)}, u32[]{:S(2)}) collective-permute-start(bf16[192,1536]{1,0:T(8,128)(2,1)} %get-tuple-element.308), channel_id=1, source_target_pairs={{0,24},{4,28},{8,0},{12,4},{16,8},{20,12},{24,16},{28,20},{1,25},{... | collective-permute-start | bytes 1769480 | tf_op jit(solution)/shard_map/ppermute | solution.py:690
  (208 other events, 1847.6 us)
Sparse Core Ops, SparseCore 0:
  12.9 56.3 all-gather.7
  71.5 41.0 all-gather.9
  114.8 61.2 all-gather.11
  178.1 36.9 all-gather.15
  216.5 39.0 all-gather.13
  257.0 61.2 all-gather.17
  320.5 36.9 all-gather.19
  491.2 38.3 reduce-scatter.7
  548.4 65.4 reduce-scatter.9
  616.5 18.8 reduce-scatter.11
  641.6 36.4 reduce-scatter.13
  680.3 34.3 reduce-scatter.15
  726.5 60.5 reduce-scatter.17
  789.9 28.4 reduce-scatter.19

commit v6 on v5

--- a/solution.py
+++ b/solution.py
@@ -1051,7 +1051,8 @@
         [after(packed, d_n1).reshape(2, nz, -1, packed.shape[1]), grad_gains.reshape(2, nz, width // dp, -1)],
         axis=3,
     )
-    summed = links.scatter_small(packed)
+    done = m_in.finish(g0, *f_in.terms)
+    summed = links.scatter_small(after(packed, done))
     states = w_xproj.shape[1]
     tail = states + RANK + mixer_params.shape[0]
     grads = [
@@ -1059,7 +1060,6 @@
         summed[:, states : states + RANK].T,
         summed[:, states + RANK : tail].T,
     ]
-    done = m_in.finish(packed, *f_in.terms, direct=True, last=m_out.terms)
     input_grad = ungroup(after(g0, done), nz, 1).astype(bf16).reshape(hidden_in.shape)
     gain_total = summed[:, tail:].reshape(norm_gains.shape)
     gain_total = gain_total + links.swap_core(gain_total)

time: 907 us -> 892 us (0.983)
    ppermute x6 -> x3, waiting for transfers between devices: 35.5 us -> 4.5 us  [shift_z(): lax.ppermute(v, 'dp', [(2 * z + y, 2 * ((z + k) % n) + y) for z in range(...]
    reduce_scatter x7 -> x8, waiting for transfers between devices: 0.05 us -> 16.9 us  [scatter_z(): lax.psum_scatter(v, 'dp', scatter_dimension=0, tiled=True, axis_index_gro...]
    unnamed x372 -> x362, local copies, waits for them, and re-layouts: 51.9 us -> 52 us
  transfers between devices with their start and end apart: 89 -> 87, of which waited for: 50 -> 49; matrix products, arithmetic and copies ran while one was open for 17% -> 15% of each run, Pallas kernels for 18% -> 19%
where the time goes in v6:
time: 892 us; the launch traced here: 882 us
  waiting for transfers between devices  376 us (42%)
  Pallas kernels  176 us (20%)
  starting transfers between devices  125 us (14%)
  local copies, waits for them, and re-layouts  118 us (13%)
  other arithmetic  52.8 us (6%)
  between operations  17.3 us (2%)
  matrix products  17.1 us (2%)
    ppermute x16, waiting for transfers between devices, swap_y(): return lax.ppermute(v, 'dp', [(i, i ^ 1) for i in range(self.dp)])  183 us
    ppermute x19, waiting for transfers between devices, swap_x(): return lax.ppermute(v, 'tensor', [(i, i ^ 2) for i in range(PIECES)])  83.2 us
    ppermute x27, starting transfers between devices, swap_core(): return lax.ppermute(v, 'tensor', [(i, i ^ 1) for i in range(PIECES)])  72.2 us
    all_gather x7, waiting for transfers between devices, gather_z(): lax.all_gather(v, 'dp', axis=0, tiled=True, axis_index_groups=self.groups)  68 us
    unnamed x362, local copies, waits for them, and re-layouts  52 us
    pallas_call x16, Pallas kernels, product_tn(): pl.pallas_call(lambda *refs: tn_kernel(len(rights), bool(adds), *refs), g...  40.9 us
    pallas_call x1, Pallas kernels, scan_backward(): pl.pallas_call(scan_bwd_kernel, grid_spec=grid, out_shape=[jax.ShapeDtype...  36.7 us
    pallas_call x6, Pallas kernels, product_nt(): pl.pallas_call(lambda *refs: nt_kernel(len(ds), steps, *refs), grid=(step...  28.2 us
  transfers between devices with their start and end apart: 87, of which 49 were waited for; matrix products, arithmetic and copies ran while one was open for 15% of the time, Pallas kernels for 19%

profile of v6, /device:TPU:9, one launch (start us, length us, event | category | flops | bytes accessed | tf_op | source)
XLA Modules:
  0.0 882.1 jit_solution(15757057154244409464)
XLA Ops:
  7.2 3.5 reshape.406
  37.1 3.5 collective-permute-done.3
  40.7 4.0 collective-permute-done.2
  48.9 20.6 %all-gather.8.cloned.1.call-done.refs_2_ = bf16[768,1536]{1,0:T(8,128)(2,1)} async-done(((bf16[192,1536]{1,0:T(8,128)(2,1)}), bf16[768,1536]{1,0:T(8,128)(2,1)}) %all-gather.8.cloned.1.call-update) | async-done | bytes 2359312 | tf_op jit(solution)/shard_map/all_gather | solution.py:701
  75.3 6.0 collective-permute-done.7
  84.2 28.5 %all-gather.10.cloned.1.call-done = bf16[576,1536]{1,0:T(8,128)(2,1)} async-done(((bf16[144,1536]{1,0:T(8,128)(2,1)}), bf16[576,1536]{1,0:T(8,128)(2,1)}) %all-gather.10.cloned.1.call-update) | async-done | bytes 1769488 | tf_op jit(solution)/shard_map/all_gather | solution.py:701
  112.7 9.4 %collective-permute-done.10.refs_3_ = bf16[768,1536]{1,0:T(8,128)(2,1)} collective-permute-done((bf16[768,1536]{1,0:T(8,128)(2,1)}, bf16[768,1536]{1,0:T(8,128)(2,1)}, u32[]{:S(2)}, u32[]{:S(2)}) %collective-permute-start.10) | collective-permute-done | bytes 2359328 | tf_op jit(solution)/shard_map/ppermute | solution.py:686
  123.6 3.2 fusion.38
  129.4 3.8 conv_forward.1
  145.1 23.2 %scan_forward.1 = (bf16[4,2,64,768]{3,2,1,0:T(8,128)(2,1)S(1)}, f32[4,2,64,768]{3,2,1,0:T(8,128)S(1)}, bf16[8,64,16,768]{3,2,1,0:T(8,128)(2,1)}) custom-call(s32[4]{0:T(128)S(1)} %pad_add_fusion.2.slot, bf16[4,2,64,128]{3,2,1,0:T(8,128)(2,1)S(1)} %bitcast.174, bf16[96,768]{1,0:T(8,128)(2,1)S(1)} %reshape.411.wdt_ref, bf16[4,2,64,768]{3,2,1,0:T(8,128)(2,1)S(1)} %copy-done.29, ...), custom_call_target="tpu_custom_call" | custom-call | flops 1 | bytes 1 | tf_op jit(solution)/shard_map/scan_forward/pallas_call | solution.py:395
  170.1 6.1 all-gather.12.cloned.1.call-done.own_g.own_u.refs_2_
  196.4 3.9 collective-permute-done.15
  202.3 12.9 %all-gather.16.cloned.1.call-done = bf16[512,1536]{1,0:T(8,128)(2,1)} async-done(((bf16[128,1536]{1,0:T(8,128)(2,1)}), bf16[512,1536]{1,0:T(8,128)(2,1)}) %all-gather.16.cloned.1.call-update) | async-done | bytes 1572880 | tf_op jit(solution)/shard_map/all_gather | solution.py:701
  215.2 31.6 %collective-permute-done.22.other_g.other_u.refs_3_ = bf16[768,2048]{1,0:T(8,128)(2,1)} collective-permute-done((bf16[768,2048]{1,0:T(8,128)(2,1)}, bf16[768,2048]{1,0:T(8,128)(2,1)}, u32[]{:S(2)}, u32[]{:S(2)}) %collective-permute-start.22) | collective-permute-done | bytes 3145760 | tf_op jit(solution)/shard_map/ppermute | solution.py:686
  252.3 4.9 collective-permute-done.16
  261.4 6.3 gate_forward.2
  270.8 10.5 %collective-permute-done.23 = bf16[512,1536]{1,0:T(8,128)(2,1)} collective-permute-done((bf16[512,1536]{1,0:T(8,128)(2,1)}, bf16[512,1536]{1,0:T(8,128)(2,1)}, u32[]{:S(2)}, u32[]{:S(2)}) %collective-permute-start.23) | collective-permute-done | bytes 1572896 | tf_op jit(solution)/shard_map/ppermute | solution.py:686
  282.6 3.3 maximum_select_fusion.w
  300.3 18.8 %collective-permute-done.25.refs_2_ = bf16[768,1152]{1,0:T(8,128)(2,1)} collective-permute-done((bf16[768,1152]{1,0:T(8,128)(2,1)}, bf16[768,1152]{1,0:T(8,128)(2,1)}, u32[]{:S(2)}, u32[]{:S(2)}) %collective-permute-start.25) | collective-permute-done | bytes 1769504 | tf_op jit(solution)/shard_map/ppermute | solution.py:686
  331.6 4.9 collective-permute-start.28
  336.4 5.2 collective-permute-start.29
  348.2 3.3 fusion.35
  352.7 3.1 attention_forward.1
  355.8 33.4 %collective-permute-done.30.other_g.other_u.refs_3_ = bf16[768,2048]{1,0:T(8,128)(2,1)} collective-permute-done((bf16[768,2048]{1,0:T(8,128)(2,1)}, bf16[768,2048]{1,0:T(8,128)(2,1)}, u32[]{:S(2)}, u32[]{:S(2)}) %collective-permute-start.30) | collective-permute-done | bytes 3145760 | tf_op jit(solution)/shard_map/ppermute | solution.py:686
  390.3 4.7 collective-permute-start.31
  402.0 7.8 collective-permute-done.32
  414.3 8.0 collective-permute-done.33
  427.7 6.2 gate_forward.3
  439.1 3.6 maximum_select_fusion.1.w
  442.7 4.7 gate_backward.2
  447.4 3.5 product_tn.17
  450.9 7.4 product_nt.6
  465.3 6.7 collective-permute-done.40.refs_2_
  475.1 5.2 collective-permute-done.41
  481.3 7.4 collective-permute-done.38
  494.2 3.5 collective-permute-start.43
  500.3 4.2 collective-permute-start.44
  512.0 4.0 attention_backward.1
  518.8 5.1 product_nt.8
  525.0 15.6 %collective-permute-done.46.refs_3_ = bf16[768,2048]{1,0:T(8,128)(2,1)} collective-permute-done((bf16[768,2048]{1,0:T(8,128)(2,1)}, bf16[768,2048]{1,0:T(8,128)(2,1)}, u32[]{:S(2)}, u32[]{:S(2)}) %collective-permute-start.46) | collective-permute-done | bytes 3145760 | tf_op jit(solution)/shard_map/ppermute | solution.py:686
  544.2 4.0 product_tn.21
  551.2 4.0 collective-permute-start.45
  557.4 13.0 %collective-permute-done.47.refs_2_ = bf16[192,1536]{1,0:T(8,128)(2,1)S(1)} collective-permute-done((bf16[192,1536]{1,0:T(8,128)(2,1)}, bf16[192,1536]{1,0:T(8,128)(2,1)S(1)}, u32[]{:S(2)}, u32[]{:S(2)}) %collective-permute-start.47) | collective-permute-done | bytes 589856 | tf_op jit(solution)/shard_map/ppermute | solution.py:686
  573.0 7.4 collective-permute-done.48
  587.6 4.7 collective-permute-done.49
  598.1 13.1 %collective-permute-done.52.refs_2_ = bf16[768,1152]{1,0:T(8,128)(2,1)} collective-permute-done((bf16[768,1152]{1,0:T(8,128)(2,1)}, bf16[768,1152]{1,0:T(8,128)(2,1)}, u32[]{:S(2)}, u32[]{:S(2)}) %collective-permute-start.52) | collective-permute-done | bytes 1769504 | tf_op jit(solution)/shard_map/ppermute | solution.py:686
  615.8 3.2 product_tn.24
  622.7 4.8 gate_backward.3
  631.5 7.2 product_nt.9
  649.1 6.4 collective-permute-done.55
  662.9 4.0 collective-permute-start.57
  666.9 3.2 collective-permute-done.56
  670.1 4.5 collective-permute-start.58
  681.0 36.7 %scan_backward.1 = (bf16[4,2,64,768]{3,2,1,0:T(8,128)(2,1)S(1)}, f32[4,2,64,768]{3,2,1,0:T(8,128)S(1)}, bf16[4,2,64,768]{3,2,1,0:T(8,128)(2,1)S(1)}, f32[4,2,2,8...) custom-call(s32[4]{0:T(128)S(1)} %pad_add_fusion.2.slot, ...), custom_call_target="tpu_custom_call" | custom-call | flops 1 | bytes 1 | tf_op jit(solution)/shard_map/scan_backward/pallas_call | solution.py:441
  722.7 5.3 product_tn.28
  743.7 5.7 conv_backward.1
  753.1 5.0 collective-permute-done.62.refs_2_
  759.2 3.1 product_tn.30
  763.5 5.6 product_nt.11
  775.8 10.1 %collective-permute-done.64 = bf16[128,1536]{1,0:T(8,128)(2,1)S(1)} collective-permute-done((bf16[128,1536]{1,0:T(8,128)(2,1)S(1)}, bf16[128,1536]{1,0:T(8,128)(2,1)S(1)}, u32[]{:S(2)}, u32[]{:S(2)}) %collective-permute-start.64) | collective-permute-done | bytes 393248 | tf_op jit(solution)/shard_map/ppermute | solution.py:698
  786.0 23.9 %collective-permute-done.65.refs_3_ = bf16[768,1536]{1,0:T(8,128)(2,1)} collective-permute-done((bf16[768,1536]{1,0:T(8,128)(2,1)}, bf16[768,1536]{1,0:T(8,128)(2,1)}, u32[]{:S(2)}, u32[]{:S(2)}) %collective-permute-start.65) | collective-permute-done | bytes 2359328 | tf_op jit(solution)/shard_map/ppermute | solution.py:686
  811.3 4.7 product_tn.31
  841.8 10.0 %collective-permute-start.70 = (f32[4,192]{1,0:T(4,128)S(1)}, f32[4,192]{1,0:T(4,128)S(1)}, u32[]{:S(2)}, u32[]{:S(2)}) collective-permute-start(f32[4,192]{1,0:T(4,128)S(1)} %reshape.438), channel_id=1, source_target_pairs={{0,1},{1,0},{2,3},{3,2},{4,5},{5,4},{6,7},{7,6},{8,9},{9,8},{10,11... | collective-permute-start | bytes 9224 | tf_op jit(solution)/shard_map/ppermute | solution.py:695
  856.1 16.8 %reduce-scatter.21.cloned.1.call-done.refs_0_ = bf16[192,1536]{1,0:T(8,128)(2,1)} async-done(((bf16[768,1536]{1,0:T(8,128)(2,1)}), bf16[192,1536]{1,0:T(8,128)(2,1)}) %reduce-scatter.21.cloned.1.call-update) | async-done | bytes 589840 | tf_op jit(solution)/shard_map/reduce_scatter | solution.py:704
  (769 shorter events, 307.1 us)
Async XLA Ops:
  7.2 62.2 %all-gather.8.cloned.1.call-start = ((), (), s32[]{:S(2)}) async-start(), calls=%async_computation.8 | async-start | bytes 2949120 | tf_op jit(solution)/shard_map/all_gather | solution.py:701
  12.8 99.9 %all-gather.10.cloned.1.call-start = ((), (), s32[]{:S(2)}) async-start(), calls=%async_computation.9 | async-start | bytes 2211840 | tf_op jit(solution)/shard_map/all_gather | solution.py:701
  22.9 153.3 %all-gather.12.cloned.1.call-start = ((), (), s32[]{:S(2)}) async-start(), calls=%async_computation.10 | async-start | bytes 3932160 | tf_op jit(solution)/shard_map/all_gather | solution.py:701
  23.6 191.6 %all-gather.16.cloned.1.call-start = ((), (), s32[]{:S(2)}) async-start(), calls=%async_computation.12 | async-start | bytes 1966080 | tf_op jit(solution)/shard_map/all_gather | solution.py:701
  24.0 8.0 collective-permute-start.6
  25.3 8.3 collective-permute-start.5
  26.6 10.5 %collective-permute-start.4 = (bf16[24480]{0:T(1024)(128)(2,1)S(1)}, bf16[24480]{0:T(1024)(128)(2,1)S(1)}, u32[]{:S(2)}, u32[]{:S(2)}) collective-permute-start(bf16[24480]{0:T(1024)(128)(2,1)S(1)} %pad_maximum_fusion.19), channel_id=1, source_target_pairs={{0,12},{4,16},{8,20},{12,24},{16,28},{20,0},{24,4},{28,8},{1,13},{... | collective-permute-start | bytes 146888 | tf_op jit(solution)/shard_map/ppermute | solution.py:714
  27.7 12.9 %collective-permute-start.3 = (bf16[24480]{0:T(1024)(128)(2,1)S(1)}, bf16[24480]{0:T(1024)(128)(2,1)S(1)}, u32[]{:S(2)}, u32[]{:S(2)}) collective-permute-start(bf16[24480]{0:T(1024)(128)(2,1)S(1)} %pad_maximum_fusion.19), channel_id=1, source_target_pairs={{0,16},{4,20},{8,24},{12,28},{16,0},{20,4},{24,8},{28,12},{1,17},{... | collective-permute-start | bytes 146888 | tf_op jit(solution)/shard_map/ppermute | solution.py:714
  29.8 14.9 %collective-permute-start.2 = (bf16[24480]{0:T(1024)(128)(2,1)S(1)}, bf16[24480]{0:T(1024)(128)(2,1)S(1)}, u32[]{:S(2)}, u32[]{:S(2)}) collective-permute-start(bf16[24480]{0:T(1024)(128)(2,1)S(1)} %pad_maximum_fusion.19), channel_id=1, source_target_pairs={{0,20},{4,24},{8,28},{12,0},{16,4},{20,8},{24,12},{28,16},{1,21},{... | collective-permute-start | bytes 146888 | tf_op jit(solution)/shard_map/ppermute | solution.py:714
  31.8 239.0 %all-gather.14.cloned.1.call-start = ((), (), s32[]{:S(2)}) async-start(), calls=%async_computation.11 | async-start | bytes 2211840 | tf_op jit(solution)/shard_map/all_gather | solution.py:701
  32.0 12.7 %collective-permute-start.1 = (bf16[24480]{0:T(1024)(128)(2,1)S(1)}, bf16[24480]{0:T(1024)(128)(2,1)S(1)}, u32[]{:S(2)}, u32[]{:S(2)}) collective-permute-start(bf16[24480]{0:T(1024)(128)(2,1)S(1)} %pad_maximum_fusion.19), channel_id=1, source_target_pairs={{0,24},{4,28},{8,0},{12,4},{16,8},{20,12},{24,16},{28,20},{1,25},{... | collective-permute-start | bytes 146888 | tf_op jit(solution)/shard_map/ppermute | solution.py:714
  33.5 11.3 %collective-permute-start = (bf16[24480]{0:T(1024)(128)(2,1)S(1)}, bf16[24480]{0:T(1024)(128)(2,1)S(1)}, u32[]{:S(2)}, u32[]{:S(2)}) collective-permute-start(bf16[24480]{0:T(1024)(128)(2,1)S(1)} %pad_maximum_fusion.19), channel_id=1, source_target_pairs={{0,28},{4,0},{8,4},{12,8},{16,12},{20,16},{24,20},{28,24},{1,29},{... | collective-permute-start | bytes 146888 | tf_op jit(solution)/shard_map/ppermute | solution.py:714
  69.4 52.7 %collective-permute-start.10 = (bf16[768,1536]{1,0:T(8,128)(2,1)}, bf16[768,1536]{1,0:T(8,128)(2,1)}, u32[]{:S(2)}, u32[]{:S(2)}) collective-permute-start(bf16[768,1536]{1,0:T(8,128)(2,1)} %all-gather.8.cloned.1.call-done.refs_2_), channel_id=1, source_target_pairs={{0,4},{4,0},{8,12},{12,8},{16,20},{20,16},{24,28},{28,24},{1,5},{5... | collective-permute-start | bytes 7077896 | tf_op jit(solution)/shard_map/ppermute | solution.py:686
  71.2 10.1 %collective-permute-start.7 = (bf16[128,1536]{1,0:T(8,128)(2,1)S(1)}, bf16[128,1536]{1,0:T(8,128)(2,1)S(1)}, u32[]{:S(2)}, u32[]{:S(2)}) collective-permute-start(bf16[128,1536]{1,0:T(8,128)(2,1)S(1)} %maximum_select_fusion.8), channel_id=1, source_target_pairs={{0,2},{1,3},{2,0},{3,1},{4,6},{5,7},{6,4},{7,5},{8,10},{9,11},{10,... | collective-permute-start | bytes 1179656 | tf_op jit(solution)/shard_map/ppermute | solution.py:698
  74.3 9.8 %collective-permute-start.8 = (bf16[128,1536]{1,0:T(8,128)(2,1)S(1)}, bf16[128,1536]{1,0:T(8,128)(2,1)S(1)}, u32[]{:S(2)}, u32[]{:S(2)}) collective-permute-start(bf16[128,1536]{1,0:T(8,128)(2,1)S(1)} %maximum_select_fusion.8), channel_id=1, source_target_pairs={{0,1},{1,0},{2,3},{3,2},{4,5},{5,4},{6,7},{7,6},{8,9},{9,8},{10,11... | collective-permute-start | bytes 1179656 | tf_op jit(solution)/shard_map/ppermute | solution.py:695
  122.1 54.1 %collective-permute-start.13 = (bf16[576,1536]{1,0:T(8,128)(2,1)}, bf16[576,1536]{1,0:T(8,128)(2,1)}, u32[]{:S(2)}, u32[]{:S(2)}) collective-permute-start(bf16[576,1536]{1,0:T(8,128)(2,1)} %all-gather.10.cloned.1.call-done), channel_id=1, source_target_pairs={{0,4},{4,0},{8,12},{12,8},{16,20},{20,16},{24,28},{28,24},{1,5},{5... | collective-permute-start | bytes 5308424 | tf_op jit(solution)/shard_map/ppermute | solution.py:686
  137.0 186.0 %all-gather.18.cloned.1.call-start = ((), (), s32[]{:S(2)}) async-start(), calls=%async_computation.13 | async-start | bytes 3932160 | tf_op jit(solution)/shard_map/all_gather | solution.py:701
  177.6 69.2 %collective-permute-start.22 = (bf16[768,2048]{1,0:T(8,128)(2,1)}, bf16[768,2048]{1,0:T(8,128)(2,1)}, u32[]{:S(2)}, u32[]{:S(2)}) collective-permute-start(bf16[768,2048]{1,0:T(8,128)(2,1)} %all-gather.12.cloned.1.call-done.own_g.own_u.refs_2_), channel_id=1, source_target_pairs={{0,4},{4,0},{8,12},{12,8},{16,20},{20,16},{24,28},{28,24},{1,5},{5... | collective-permute-start | bytes 9437192 | tf_op jit(solution)/shard_map/ppermute | solution.py:686
  183.7 215.4 %all-gather.20.cloned.1.call-start = ((), (), s32[]{:S(2)}) async-start(), calls=%async_computation.14 | async-start | bytes 1966080 | tf_op jit(solution)/shard_map/all_gather | solution.py:701
  189.7 10.6 %collective-permute-start.15 = (bf16[128,1536]{1,0:T(8,128)(2,1)}, bf16[128,1536]{1,0:T(8,128)(2,1)}, u32[]{:S(2)}, u32[]{:S(2)}) collective-permute-start(bf16[128,1536]{1,0:T(8,128)(2,1)} %fusion.18), channel_id=1, source_target_pairs={{0,2},{1,3},{2,0},{3,1},{4,6},{5,7},{6,4},{7,5},{8,10},{9,11},{10,... | collective-permute-start | bytes 1179656 | tf_op jit(solution)/shard_map/ppermute | solution.py:698
  195.3 56.5 %collective-permute-start.19 = (bf16[128,1536]{1,0:T(8,128)(2,1)S(1)}, bf16[128,1536]{1,0:T(8,128)(2,1)}, u32[]{:S(2)}, u32[]{:S(2)}) collective-permute-start(bf16[128,1536]{1,0:T(8,128)(2,1)S(1)} %copy.296), channel_id=1, source_target_pairs={{0,2},{1,3},{2,0},{3,1},{4,6},{5,7},{6,4},{7,5},{8,10},{9,11},{10,... | collective-permute-start | bytes 1179656 | tf_op jit(solution)/shard_map/ppermute | solution.py:698
  246.8 34.5 %collective-permute-start.23 = (bf16[512,1536]{1,0:T(8,128)(2,1)}, bf16[512,1536]{1,0:T(8,128)(2,1)}, u32[]{:S(2)}, u32[]{:S(2)}) collective-permute-start(bf16[512,1536]{1,0:T(8,128)(2,1)} %all-gather.16.cloned.1.call-done), channel_id=1, source_target_pairs={{0,4},{4,0},{8,12},{12,8},{16,20},{20,16},{24,28},{28,24},{1,5},{5... | collective-permute-start | bytes 4718600 | tf_op jit(solution)/shard_map/ppermute | solution.py:686
  248.3 8.9 %collective-permute-start.16 = (bf16[128,1536]{1,0:T(8,128)(2,1)S(1)}, bf16[128,1536]{1,0:T(8,128)(2,1)S(1)}, u32[]{:S(2)}, u32[]{:S(2)}) collective-permute-start(bf16[128,1536]{1,0:T(8,128)(2,1)S(1)} %maximum_select_fusion.9), channel_id=1, source_target_pairs={{0,2},{1,3},{2,0},{3,1},{4,6},{5,7},{6,4},{7,5},{8,10},{9,11},{10,... | collective-permute-start | bytes 1179656 | tf_op jit(solution)/shard_map/ppermute | solution.py:698
  249.6 10.3 %collective-permute-start.20 = (bf16[128,1536]{1,0:T(8,128)(2,1)S(1)}, bf16[128,1536]{1,0:T(8,128)(2,1)S(1)}, u32[]{:S(2)}, u32[]{:S(2)}) collective-permute-start(bf16[128,1536]{1,0:T(8,128)(2,1)S(1)} %copy.296), channel_id=1, source_target_pairs={{0,1},{1,0},{2,3},{3,2},{4,5},{5,4},{6,7},{7,6},{8,9},{9,8},{10,11... | collective-permute-start | bytes 1179656 | tf_op jit(solution)/shard_map/ppermute | solution.py:695
  251.8 8.1 collective-permute-start.21
  251.8 9.3 %collective-permute-start.17 = (bf16[128,1536]{1,0:T(8,128)(2,1)S(1)}, bf16[128,1536]{1,0:T(8,128)(2,1)S(1)}, u32[]{:S(2)}, u32[]{:S(2)}) collective-permute-start(bf16[128,1536]{1,0:T(8,128)(2,1)S(1)} %maximum_select_fusion.9), channel_id=1, source_target_pairs={{0,1},{1,0},{2,3},{3,2},{4,5},{5,4},{6,7},{7,6},{8,9},{9,8},{10,11... | collective-permute-start | bytes 1179656 | tf_op jit(solution)/shard_map/ppermute | solution.py:695
  281.3 37.8 %collective-permute-start.25 = (bf16[768,1152]{1,0:T(8,128)(2,1)}, bf16[768,1152]{1,0:T(8,128)(2,1)}, u32[]{:S(2)}, u32[]{:S(2)}) collective-permute-start(bf16[768,1152]{1,0:T(8,128)(2,1)} %all-gather.14.cloned.1.call-done.refs_1_), channel_id=1, source_target_pairs={{0,4},{4,0},{8,12},{12,8},{16,20},{20,16},{24,28},{28,24},{1,5},{5... | collective-permute-start | bytes 5308424 | tf_op jit(solution)/shard_map/ppermute | solution.py:686
  294.6 246.1 %reduce-scatter.9.cloned.1.call-start = ((), (), s32[]{:S(2)}) async-start(), calls=%async_computation.15 | async-start | bytes 1966080 | tf_op jit(solution)/shard_map/reduce_scatter | solution.py:704
  323.1 66.2 %collective-permute-start.30 = (bf16[768,2048]{1,0:T(8,128)(2,1)}, bf16[768,2048]{1,0:T(8,128)(2,1)}, u32[]{:S(2)}, u32[]{:S(2)}) collective-permute-start(bf16[768,2048]{1,0:T(8,128)(2,1)} %all-gather.18.cloned.1.call-done.own_g.own_u.refs_2_), channel_id=1, source_target_pairs={{0,4},{4,0},{8,12},{12,8},{16,20},{20,16},{24,28},{28,24},{1,5},{5... | collective-permute-start | bytes 9437192 | tf_op jit(solution)/shard_map/ppermute | solution.py:686
  331.6 14.8 %collective-permute-start.28 = (bf16[128,1536]{1,0:T(8,128)(2,1)S(1)}, bf16[128,1536]{1,0:T(8,128)(2,1)}, u32[]{:S(2)}, u32[]{:S(2)}) collective-permute-start(bf16[128,1536]{1,0:T(8,128)(2,1)S(1)} %maximum_select_fusion.10), channel_id=1, source_target_pairs={{0,1},{1,0},{2,3},{3,2},{4,5},{5,4},{6,7},{7,6},{8,9},{9,8},{10,11... | collective-permute-start | bytes 1179656 | tf_op jit(solution)/shard_map/ppermute | solution.py:695
  336.4 10.0 %collective-permute-start.29 = (bf16[128,1536]{1,0:T(8,128)(2,1)}, bf16[128,1536]{1,0:T(8,128)(2,1)}, u32[]{:S(2)}, u32[]{:S(2)}) collective-permute-start(bf16[128,1536]{1,0:T(8,128)(2,1)} %collective-permute-done.27), channel_id=1, source_target_pairs={{0,1},{1,0},{2,3},{3,2},{4,5},{5,4},{6,7},{7,6},{8,9},{9,8},{10,11... | collective-permute-start | bytes 1179656 | tf_op jit(solution)/shard_map/ppermute | solution.py:695
  399.2 10.6 %collective-permute-start.32 = (bf16[128,1536]{1,0:T(8,128)(2,1)}, bf16[128,1536]{1,0:T(8,128)(2,1)}, u32[]{:S(2)}, u32[]{:S(2)}) collective-permute-start(bf16[128,1536]{1,0:T(8,128)(2,1)} %fusion.12), channel_id=1, source_target_pairs={{0,2},{1,3},{2,0},{3,1},{4,6},{5,7},{6,4},{7,5},{8,10},{9,11},{10,... | collective-permute-start | bytes 1179656 | tf_op jit(solution)/shard_map/ppermute | solution.py:698
  400.6 35.6 %collective-permute-start.36 = (bf16[512,1536]{1,0:T(8,128)(2,1)}, bf16[512,1536]{1,0:T(8,128)(2,1)}, u32[]{:S(2)}, u32[]{:S(2)}) collective-permute-start(bf16[512,1536]{1,0:T(8,128)(2,1)} %all-gather.20.cloned.1.call-done), channel_id=1, source_target_pairs={{0,4},{4,0},{8,12},{12,8},{16,20},{20,16},{24,28},{28,24},{1,5},{5... | collective-permute-start | bytes 4718600 | tf_op jit(solution)/shard_map/ppermute | solution.py:686
  412.7 9.6 %collective-permute-start.33 = (bf16[128,1536]{1,0:T(8,128)(2,1)S(1)}, bf16[128,1536]{1,0:T(8,128)(2,1)}, u32[]{:S(2)}, u32[]{:S(2)}) collective-permute-start(bf16[128,1536]{1,0:T(8,128)(2,1)S(1)} %maximum_select_fusion.11), channel_id=1, source_target_pairs={{0,2},{1,3},{2,0},{3,1},{4,6},{5,7},{6,4},{7,5},{8,10},{9,11},{10,... | collective-permute-start | bytes 1179656 | tf_op jit(solution)/shard_map/ppermute | solution.py:698
  412.8 13.6 %collective-permute-start.34 = (bf16[128,1536]{1,0:T(8,128)(2,1)S(1)}, bf16[128,1536]{1,0:T(8,128)(2,1)}, u32[]{:S(2)}, u32[]{:S(2)}) collective-permute-start(bf16[128,1536]{1,0:T(8,128)(2,1)S(1)} %maximum_select_fusion.11), channel_id=1, source_target_pairs={{0,1},{1,0},{2,3},{3,2},{4,5},{5,4},{6,7},{7,6},{8,9},{9,8},{10,11... | collective-permute-start | bytes 1179656 | tf_op jit(solution)/shard_map/ppermute | solution.py:695
  437.6 34.4 %collective-permute-start.40 = (bf16[512,1536]{1,0:T(8,128)(2,1)S(1)}, bf16[512,1536]{1,0:T(8,128)(2,1)S(1)}, u32[]{:S(2)}, u32[]{:S(2)}) collective-permute-start(bf16[512,1536]{1,0:T(8,128)(2,1)S(1)} %product_tn.16), channel_id=1, source_target_pairs={{0,4},{4,0},{8,12},{12,8},{16,20},{20,16},{24,28},{28,24},{1,5},{5... | collective-permute-start | bytes 4718600 | tf_op jit(solution)/shard_map/ppermute | solution.py:686
  472.0 8.3 collective-permute-start.41
  473.6 15.2 %collective-permute-start.38 = (bf16[128,1536]{1,0:T(8,128)(2,1)S(1)}, bf16[128,1536]{1,0:T(8,128)(2,1)S(1)}, u32[]{:S(2)}, u32[]{:S(2)}) collective-permute-start(bf16[128,1536]{1,0:T(8,128)(2,1)S(1)} %fusion.8), channel_id=1, source_target_pairs={{0,2},{1,3},{2,0},{3,1},{4,6},{5,7},{6,4},{7,5},{8,10},{9,11},{10,... | collective-permute-start | bytes 1179656 | tf_op jit(solution)/shard_map/ppermute | solution.py:698
  473.7 66.9 %collective-permute-start.46 = (bf16[768,2048]{1,0:T(8,128)(2,1)}, bf16[768,2048]{1,0:T(8,128)(2,1)}, u32[]{:S(2)}, u32[]{:S(2)}) collective-permute-start(bf16[768,2048]{1,0:T(8,128)(2,1)} %product_tn.17), channel_id=1, source_target_pairs={{0,4},{4,0},{8,12},{12,8},{16,20},{20,16},{24,28},{28,24},{1,5},{5... | collective-permute-start | bytes 9437192 | tf_op jit(solution)/shard_map/ppermute | solution.py:686
  492.7 165.3 %reduce-scatter.11.cloned.1.call-start = ((), (), s32[]{:S(2)}) async-start(), calls=%async_computation.16 | async-start | bytes 3932160 | tf_op jit(solution)/shard_map/reduce_scatter | solution.py:704
  492.8 7.5 collective-permute-start.42
  494.2 13.6 %collective-permute-start.43 = (bf16[128,1536]{1,0:T(8,128)(2,1)S(1)}, bf16[128,1536]{1,0:T(8,128)(2,1)}, u32[]{:S(2)}, u32[]{:S(2)}) collective-permute-start(bf16[128,1536]{1,0:T(8,128)(2,1)S(1)} %copy-done.134), channel_id=1, source_target_pairs={{0,1},{1,0},{2,3},{3,2},{4,5},{5,4},{6,7},{7,6},{8,9},{9,8},{10,11... | collective-permute-start | bytes 1179656 | tf_op jit(solution)/shard_map/ppermute | solution.py:695
  500.3 7.5 collective-permute-start.44
  549.9 171.6 %reduce-scatter.13.cloned.1.call-start = ((), (), s32[]{:S(2)}) async-start(), calls=%async_computation.17 | async-start | bytes 737280 | tf_op jit(solution)/shard_map/reduce_scatter | solution.py:704
  555.2 15.2 %collective-permute-start.47 = (bf16[192,1536]{1,0:T(8,128)(2,1)}, bf16[192,1536]{1,0:T(8,128)(2,1)S(1)}, u32[]{:S(2)}, u32[]{:S(2)}) collective-permute-start(bf16[192,1536]{1,0:T(8,128)(2,1)} %copy-done.94), channel_id=1, source_target_pairs={{0,4},{4,0},{8,12},{12,8},{16,20},{20,16},{24,28},{28,24},{1,5},{5... | collective-permute-start | bytes 1769480 | tf_op jit(solution)/shard_map/ppermute | solution.py:686
  570.4 10.0 %collective-permute-start.48 = (bf16[128,1536]{1,0:T(8,128)(2,1)S(1)}, bf16[128,1536]{1,0:T(8,128)(2,1)S(1)}, u32[]{:S(2)}, u32[]{:S(2)}) collective-permute-start(bf16[128,1536]{1,0:T(8,128)(2,1)S(1)} %fusion.4), channel_id=1, source_target_pairs={{0,2},{1,3},{2,0},{3,1},{4,6},{5,7},{6,4},{7,5},{8,10},{9,11},{10,... | collective-permute-start | bytes 1179656 | tf_op jit(solution)/shard_map/ppermute | solution.py:698
  571.8 39.4 %collective-permute-start.52 = (bf16[768,1152]{1,0:T(8,128)(2,1)}, bf16[768,1152]{1,0:T(8,128)(2,1)}, u32[]{:S(2)}, u32[]{:S(2)}) collective-permute-start(bf16[768,1152]{1,0:T(8,128)(2,1)} %product_tn.20), channel_id=1, source_target_pairs={{0,4},{4,0},{8,12},{12,8},{16,20},{20,16},{24,28},{28,24},{1,5},{5... | collective-permute-start | bytes 5308424 | tf_op jit(solution)/shard_map/ppermute | solution.py:686
  582.9 9.4 %collective-permute-start.49 = (bf16[128,1536]{1,0:T(8,128)(2,1)}, bf16[128,1536]{1,0:T(8,128)(2,1)}, u32[]{:S(2)}, u32[]{:S(2)}) collective-permute-start(bf16[128,1536]{1,0:T(8,128)(2,1)} %get-tuple-element.290), channel_id=1, source_target_pairs={{0,2},{1,3},{2,0},{3,1},{4,6},{5,7},{6,4},{7,5},{8,10},{9,11},{10,... | collective-permute-start | bytes 1179656 | tf_op jit(solution)/shard_map/ppermute | solution.py:698
  585.7 135.8 %reduce-scatter.15.cloned.1.call-start = ((), (), s32[]{:S(2)}) async-start(), calls=%async_computation.18 | async-start | bytes 2211840 | tf_op jit(solution)/shard_map/reduce_scatter | solution.py:704
  585.7 11.1 %collective-permute-start.50 = (bf16[128,1536]{1,0:T(8,128)(2,1)}, bf16[128,1536]{1,0:T(8,128)(2,1)S(1)}, u32[]{:S(2)}, u32[]{:S(2)}) collective-permute-start(bf16[128,1536]{1,0:T(8,128)(2,1)} %get-tuple-element.290), channel_id=1, source_target_pairs={{0,1},{1,0},{2,3},{3,2},{4,5},{5,4},{6,7},{7,6},{8,9},{9,8},{10,11... | collective-permute-start | bytes 1179656 | tf_op jit(solution)/shard_map/ppermute | solution.py:695
  613.4 34.3 %collective-permute-start.54 = (bf16[512,1536]{1,0:T(8,128)(2,1)}, bf16[512,1536]{1,0:T(8,128)(2,1)}, u32[]{:S(2)}, u32[]{:S(2)}) collective-permute-start(bf16[512,1536]{1,0:T(8,128)(2,1)} %product_tn.23), channel_id=1, source_target_pairs={{0,4},{4,0},{8,12},{12,8},{16,20},{20,16},{24,28},{28,24},{1,5},{5... | collective-permute-start | bytes 4718600 | tf_op jit(solution)/shard_map/ppermute | solution.py:686
  643.1 78.4 %reduce-scatter.17.cloned.1.call-start = ((), (), s32[]{:S(2)}) async-start(), calls=%async_computation.19 | async-start | bytes 1966080 | tf_op jit(solution)/shard_map/reduce_scatter | solution.py:704
  647.7 7.8 collective-permute-start.55
  647.7 73.7 %collective-permute-start.59 = (bf16[768,2048]{1,0:T(8,128)(2,1)}, bf16[768,2048]{1,0:T(8,128)(2,1)}, u32[]{:S(2)}, u32[]{:S(2)}) collective-permute-start(bf16[768,2048]{1,0:T(8,128)(2,1)} %copy-done.41), channel_id=1, source_target_pairs={{0,4},{4,0},{8,12},{12,8},{16,20},{20,16},{24,28},{28,24},{1,5},{5... | collective-permute-start | bytes 9437192 | tf_op jit(solution)/shard_map/ppermute | solution.py:686
  662.8 148.6 %reduce-scatter.19.cloned.1.call-start = ((), (), s32[]{:S(2)}) async-start(), calls=%async_computation.20 | async-start | bytes 3932160 | tf_op jit(solution)/shard_map/reduce_scatter | solution.py:704
  662.8 7.3 collective-permute-start.56
  662.9 13.6 %collective-permute-start.57 = (bf16[128,1536]{1,0:T(8,128)(2,1)}, bf16[128,1536]{1,0:T(8,128)(2,1)S(1)}, u32[]{:S(2)}, u32[]{:S(2)}) collective-permute-start(bf16[128,1536]{1,0:T(8,128)(2,1)} %get-tuple-element.287), channel_id=1, source_target_pairs={{0,1},{1,0},{2,3},{3,2},{4,5},{5,4},{6,7},{7,6},{8,9},{9,8},{10,11... | collective-permute-start | bytes 1179656 | tf_op jit(solution)/shard_map/ppermute | solution.py:695
  728.0 103.1 %reduce-scatter.23.cloned.1.call-start = ((), (), s32[]{:S(2)}) async-start(), calls=%async_computation.22 | async-start | bytes 1474560 | tf_op jit(solution)/shard_map/reduce_scatter | solution.py:704
  730.6 27.5 %collective-permute-start.62 = (bf16[384,1536]{1,0:T(8,128)(2,1)}, bf16[384,1536]{1,0:T(8,128)(2,1)}, u32[]{:S(2)}, u32[]{:S(2)}) collective-permute-start(bf16[384,1536]{1,0:T(8,128)(2,1)} %copy-done.68), channel_id=1, source_target_pairs={{0,4},{4,0},{8,12},{12,8},{16,20},{20,16},{24,28},{28,24},{1,5},{5... | collective-permute-start | bytes 3538952 | tf_op jit(solution)/shard_map/ppermute | solution.py:686
  758.1 51.8 %collective-permute-start.65 = (bf16[768,1536]{1,0:T(8,128)(2,1)}, bf16[768,1536]{1,0:T(8,128)(2,1)}, u32[]{:S(2)}, u32[]{:S(2)}) collective-permute-start(bf16[768,1536]{1,0:T(8,128)(2,1)} %product_tn.29), channel_id=1, source_target_pairs={{0,4},{4,0},{8,12},{12,8},{16,20},{20,16},{24,28},{28,24},{1,5},{5... | collective-permute-start | bytes 7077896 | tf_op jit(solution)/shard_map/ppermute | solution.py:686
  771.9 101.0 %reduce-scatter.21.cloned.1.call-start = ((), (), s32[]{:S(2)}) async-start(), calls=%async_computation.21 | async-start | bytes 2949120 | tf_op jit(solution)/shard_map/reduce_scatter | solution.py:704
  775.4 10.5 %collective-permute-start.64 = (bf16[128,1536]{1,0:T(8,128)(2,1)S(1)}, bf16[128,1536]{1,0:T(8,128)(2,1)S(1)}, u32[]{:S(2)}, u32[]{:S(2)}) collective-permute-start(bf16[128,1536]{1,0:T(8,128)(2,1)S(1)} %fusion), channel_id=1, source_target_pairs={{0,2},{1,3},{2,0},{3,1},{4,6},{5,7},{6,4},{7,5},{8,10},{9,11},{10,... | collective-permute-start | bytes 1179656 | tf_op jit(solution)/shard_map/ppermute | solution.py:698
  829.0 12.6 %collective-permute-start.69 = (bf16[96,255]{1,0:T(8,128)(2,1)S(1)}, bf16[96,255]{1,0:T(8,128)(2,1)S(1)}, u32[]{:S(2)}, u32[]{:S(2)}) collective-permute-start(bf16[96,255]{1,0:T(8,128)(2,1)S(1)} %fusion.30), channel_id=1, source_target_pairs={{0,4},{4,0},{8,12},{12,8},{16,20},{20,16},{24,28},{28,24},{1,5},{5... | collective-permute-start | bytes 146888 | tf_op jit(solution)/shard_map/ppermute | solution.py:686
  841.8 10.8 %collective-permute-start.70 = (f32[4,192]{1,0:T(4,128)S(1)}, f32[4,192]{1,0:T(4,128)S(1)}, u32[]{:S(2)}, u32[]{:S(2)}) collective-permute-start(f32[4,192]{1,0:T(4,128)S(1)} %reshape.438), channel_id=1, source_target_pairs={{0,1},{1,0},{2,3},{3,2},{4,5},{5,4},{6,7},{7,6},{8,9},{9,8},{10,11... | collective-permute-start | bytes 9224 | tf_op jit(solution)/shard_map/ppermute | solution.py:695
  (201 other events, 1718.1 us)
Sparse Core Ops, SparseCore 0:
  12.9 56.4 all-gather.7
  71.6 41.1 all-gather.9
  114.9 61.2 all-gather.11
  178.2 36.9 all-gather.15
  217.2 39.0 all-gather.13
  257.7 61.2 all-gather.17
  321.2 36.9 all-gather.19
  492.8 38.3 reduce-scatter.8
  550.0 65.4 reduce-scatter.10
  618.2 18.9 reduce-scatter.12
  643.3 36.3 reduce-scatter.14
  681.9 34.3 reduce-scatter.16
  728.1 60.5 reduce-scatter.18
  791.6 27.5 reduce-scatter.22
  821.5 51.4 reduce-scatter.20

commit v7 on v6

--- a/solution.py
+++ b/solution.py
@@ -743,9 +743,9 @@
             self.y == 0, v, jnp.concatenate([v[:, half:], v[:, :half]], axis=1)
         )
 
-    def gather_rows(self, v):
+    def gather_rows(self, v, *order):
         x = self.swap_x(v)
-        core = self.swap_core(v)
+        core = self.swap_core(after(v, *order))
         return jnp.concatenate([v, x, core, self.swap_core(x)], axis=0)
 
     def scatter_rows(self, part, *order):
@@ -1012,8 +1012,8 @@
     done = b_in.finish(b_out.terms[0], d_n3, block_out)
     g2, gain_c = leave(g3, x2, r3, 2, d_n3, done, a_out.came)
 
-    dy2 = links.gather_rows(g2.astype(bf16))
-    dy2 = after(dy2, a_out.finish(g2), q_in.came)
+    dy2 = links.gather_rows(g2.astype(bf16), q_in.came)
+    dy2 = after(dy2, a_out.finish(g2))
     f_in, f_out, d_pair = ffn_backward(
         links, dy2, kept_a, ffn_a_out, q_in.came, finish=q_in
     )

time: 892 us -> 902 us (1.011)
  waiting for transfers between devices: 376 us -> 391 us
  transfers between devices with their start and end apart: 87 -> 87, of which waited for: 49 -> 49; matrix products, arithmetic and copies ran while one was open for 15% -> 15% of each run, Pallas kernels for 19% -> 18%
where the time goes in v7:
time: 902 us; the launch traced here: 892 us
  waiting for transfers between devices  391 us (43%)
  Pallas kernels  176 us (20%)
  starting transfers between devices  119 us (13%)
  local copies, waits for them, and re-layouts  118 us (13%)
  other arithmetic  52.8 us (6%)
  between operations  17.3 us (2%)
  matrix products  17.1 us (2%)
    ppermute x16, waiting for transfers between devices, swap_y(): return lax.ppermute(v, 'dp', [(i, i ^ 1) for i in range(self.dp)])  190 us
    ppermute x19, waiting for transfers between devices, swap_x(): return lax.ppermute(v, 'tensor', [(i, i ^ 2) for i in range(PIECES)])  91.3 us
    all_gather x7, waiting for transfers between devices, gather_z(): lax.all_gather(v, 'dp', axis=0, tiled=True, axis_index_groups=self.groups)  68 us
    ppermute x27, starting transfers between devices, swap_core(): return lax.ppermute(v, 'tensor', [(i, i ^ 1) for i in range(PIECES)])  65.6 us
    unnamed x362, local copies, waits for them, and re-layouts  52 us
    pallas_call x16, Pallas kernels, product_tn(): pl.pallas_call(lambda *refs: tn_kernel(len(rights), bool(adds), *refs), g...  40.9 us
    pallas_call x1, Pallas kernels, scan_backward(): pl.pallas_call(scan_bwd_kernel, grid_spec=grid, out_shape=[jax.ShapeDtype...  36.7 us
    pallas_call x6, Pallas kernels, product_nt(): pl.pallas_call(lambda *refs: nt_kernel(len(ds), steps, *refs), grid=(step...  28.2 us
  transfers between devices with their start and end apart: 87, of which 49 were waited for; matrix products, arithmetic and copies ran while one was open for 15% of the time, Pallas kernels for 18%

profile of v7, /device:TPU:9, one launch (start us, length us, event | category | flops | bytes accessed | tf_op | source)
XLA Modules:
  0.0 891.5 jit_solution(4306475601509612947)
XLA Ops:
  7.2 3.5 reshape.406
  37.1 3.5 collective-permute-done.3
  40.7 4.0 collective-permute-done.2
  48.9 20.6 %all-gather.8.cloned.1.call-done.refs_2_ = bf16[768,1536]{1,0:T(8,128)(2,1)} async-done(((bf16[192,1536]{1,0:T(8,128)(2,1)}), bf16[768,1536]{1,0:T(8,128)(2,1)}) %all-gather.8.cloned.1.call-update) | async-done | bytes 2359312 | tf_op jit(solution)/shard_map/all_gather | solution.py:701
  75.3 6.0 collective-permute-done.7
  84.2 28.5 %all-gather.10.cloned.1.call-done = bf16[576,1536]{1,0:T(8,128)(2,1)} async-done(((bf16[144,1536]{1,0:T(8,128)(2,1)}), bf16[576,1536]{1,0:T(8,128)(2,1)}) %all-gather.10.cloned.1.call-update) | async-done | bytes 1769488 | tf_op jit(solution)/shard_map/all_gather | solution.py:701
  112.7 9.4 %collective-permute-done.10.refs_3_ = bf16[768,1536]{1,0:T(8,128)(2,1)} collective-permute-done((bf16[768,1536]{1,0:T(8,128)(2,1)}, bf16[768,1536]{1,0:T(8,128)(2,1)}, u32[]{:S(2)}, u32[]{:S(2)}) %collective-permute-start.10) | collective-permute-done | bytes 2359328 | tf_op jit(solution)/shard_map/ppermute | solution.py:686
  123.6 3.2 fusion.38
  129.4 3.8 conv_forward.1
  145.1 23.2 %scan_forward.1 = (bf16[4,2,64,768]{3,2,1,0:T(8,128)(2,1)S(1)}, f32[4,2,64,768]{3,2,1,0:T(8,128)S(1)}, bf16[8,64,16,768]{3,2,1,0:T(8,128)(2,1)}) custom-call(s32[4]{0:T(128)S(1)} %pad_add_fusion.2.slot, bf16[4,2,64,128]{3,2,1,0:T(8,128)(2,1)S(1)} %bitcast.174, bf16[96,768]{1,0:T(8,128)(2,1)S(1)} %reshape.411.wdt_ref, bf16[4,2,64,768]{3,2,1,0:T(8,128)(2,1)S(1)} %copy-done.29, ...), custom_call_target="tpu_custom_call" | custom-call | flops 1 | bytes 1 | tf_op jit(solution)/shard_map/scan_forward/pallas_call | solution.py:395
  170.1 6.1 all-gather.12.cloned.1.call-done.own_g.own_u.refs_2_
  196.4 3.9 collective-permute-done.15
  202.3 12.9 %all-gather.16.cloned.1.call-done = bf16[512,1536]{1,0:T(8,128)(2,1)} async-done(((bf16[128,1536]{1,0:T(8,128)(2,1)}), bf16[512,1536]{1,0:T(8,128)(2,1)}) %all-gather.16.cloned.1.call-update) | async-done | bytes 1572880 | tf_op jit(solution)/shard_map/all_gather | solution.py:701
  215.2 31.6 %collective-permute-done.22.other_g.other_u.refs_3_ = bf16[768,2048]{1,0:T(8,128)(2,1)} collective-permute-done((bf16[768,2048]{1,0:T(8,128)(2,1)}, bf16[768,2048]{1,0:T(8,128)(2,1)}, u32[]{:S(2)}, u32[]{:S(2)}) %collective-permute-start.22) | collective-permute-done | bytes 3145760 | tf_op jit(solution)/shard_map/ppermute | solution.py:686
  252.3 4.9 collective-permute-done.16
  261.4 6.3 gate_forward.2
  270.8 10.5 %collective-permute-done.23 = bf16[512,1536]{1,0:T(8,128)(2,1)} collective-permute-done((bf16[512,1536]{1,0:T(8,128)(2,1)}, bf16[512,1536]{1,0:T(8,128)(2,1)}, u32[]{:S(2)}, u32[]{:S(2)}) %collective-permute-start.23) | collective-permute-done | bytes 1572896 | tf_op jit(solution)/shard_map/ppermute | solution.py:686
  282.6 3.3 maximum_select_fusion.w
  300.3 18.8 %collective-permute-done.25.refs_2_ = bf16[768,1152]{1,0:T(8,128)(2,1)} collective-permute-done((bf16[768,1152]{1,0:T(8,128)(2,1)}, bf16[768,1152]{1,0:T(8,128)(2,1)}, u32[]{:S(2)}, u32[]{:S(2)}) %collective-permute-start.25) | collective-permute-done | bytes 1769504 | tf_op jit(solution)/shard_map/ppermute | solution.py:686
  331.6 4.9 collective-permute-start.28
  336.4 5.2 collective-permute-start.29
  348.2 3.3 fusion.35
  352.7 3.1 attention_forward.1
  355.8 33.4 %collective-permute-done.30.other_g.other_u.refs_3_ = bf16[768,2048]{1,0:T(8,128)(2,1)} collective-permute-done((bf16[768,2048]{1,0:T(8,128)(2,1)}, bf16[768,2048]{1,0:T(8,128)(2,1)}, u32[]{:S(2)}, u32[]{:S(2)}) %collective-permute-start.30) | collective-permute-done | bytes 3145760 | tf_op jit(solution)/shard_map/ppermute | solution.py:686
  390.3 4.7 collective-permute-start.31
  402.0 7.8 collective-permute-done.32
  414.3 8.0 collective-permute-done.33
  427.7 6.2 gate_forward.3
  439.1 3.6 maximum_select_fusion.1.w
  442.7 4.7 gate_backward.2
  447.4 3.5 product_tn.17
  450.9 7.4 product_nt.6
  465.3 6.7 collective-permute-done.40.refs_2_
  475.1 5.2 collective-permute-done.41
  481.3 7.4 collective-permute-done.38
  494.2 3.5 collective-permute-start.43
  500.3 4.2 collective-permute-start.44
  512.0 4.0 attention_backward.1
  518.8 5.1 product_nt.8
  525.0 15.6 %collective-permute-done.46.refs_3_ = bf16[768,2048]{1,0:T(8,128)(2,1)} collective-permute-done((bf16[768,2048]{1,0:T(8,128)(2,1)}, bf16[768,2048]{1,0:T(8,128)(2,1)}, u32[]{:S(2)}, u32[]{:S(2)}) %collective-permute-start.46) | collective-permute-done | bytes 3145760 | tf_op jit(solution)/shard_map/ppermute | solution.py:686
  544.2 4.0 product_tn.21
  551.2 4.0 collective-permute-start.45
  557.4 13.0 %collective-permute-done.47.refs_2_ = bf16[192,1536]{1,0:T(8,128)(2,1)S(1)} collective-permute-done((bf16[192,1536]{1,0:T(8,128)(2,1)}, bf16[192,1536]{1,0:T(8,128)(2,1)S(1)}, u32[]{:S(2)}, u32[]{:S(2)}) %collective-permute-start.47) | collective-permute-done | bytes 589856 | tf_op jit(solution)/shard_map/ppermute | solution.py:686
  573.0 7.4 collective-permute-done.48
  585.7 6.6 collective-permute-done.49
  594.8 16.4 %collective-permute-done.50.refs_2_ = bf16[768,1152]{1,0:T(8,128)(2,1)} collective-permute-done((bf16[768,1152]{1,0:T(8,128)(2,1)}, bf16[768,1152]{1,0:T(8,128)(2,1)}, u32[]{:S(2)}, u32[]{:S(2)}) %collective-permute-start.50) | collective-permute-done | bytes 1769504 | tf_op jit(solution)/shard_map/ppermute | solution.py:686
  621.1 3.2 product_tn.24
  628.0 4.8 gate_backward.3
  636.8 7.2 product_nt.9
  650.2 4.8 collective-permute-done.54.refs_2_
  656.5 8.5 collective-permute-done.55
  674.3 7.4 collective-permute-done.56
  690.4 36.7 %scan_backward.1 = (bf16[4,2,64,768]{3,2,1,0:T(8,128)(2,1)S(1)}, f32[4,2,64,768]{3,2,1,0:T(8,128)S(1)}, bf16[4,2,64,768]{3,2,1,0:T(8,128)(2,1)S(1)}, f32[4,2,2,8...) custom-call(s32[4]{0:T(128)S(1)} %pad_add_fusion.2.slot, ...), custom_call_target="tpu_custom_call" | custom-call | flops 1 | bytes 1 | tf_op jit(solution)/shard_map/scan_backward/pallas_call | solution.py:441
  732.1 5.3 product_tn.28
  753.1 5.7 conv_backward.1
  759.4 3.1 product_tn.29
  762.5 5.0 collective-permute-done.62.refs_2_
  768.7 3.1 product_tn.30
  772.9 5.6 product_nt.11
  785.2 10.1 %collective-permute-done.64 = bf16[128,1536]{1,0:T(8,128)(2,1)S(1)} collective-permute-done((bf16[128,1536]{1,0:T(8,128)(2,1)S(1)}, bf16[128,1536]{1,0:T(8,128)(2,1)S(1)}, u32[]{:S(2)}, u32[]{:S(2)}) %collective-permute-start.64) | collective-permute-done | bytes 393248 | tf_op jit(solution)/shard_map/ppermute | solution.py:698
  795.4 23.8 %collective-permute-done.65.refs_3_ = bf16[768,1536]{1,0:T(8,128)(2,1)} collective-permute-done((bf16[768,1536]{1,0:T(8,128)(2,1)}, bf16[768,1536]{1,0:T(8,128)(2,1)}, u32[]{:S(2)}, u32[]{:S(2)}) %collective-permute-start.65) | collective-permute-done | bytes 2359328 | tf_op jit(solution)/shard_map/ppermute | solution.py:686
  820.7 4.7 product_tn.31
  852.0 9.4 %collective-permute-start.70 = (f32[4,192]{1,0:T(4,128)S(1)}, f32[4,192]{1,0:T(4,128)S(1)}, u32[]{:S(2)}, u32[]{:S(2)}) collective-permute-start(f32[4,192]{1,0:T(4,128)S(1)} %reshape.438), channel_id=1, source_target_pairs={{0,1},{1,0},{2,3},{3,2},{4,5},{5,4},{6,7},{7,6},{8,9},{9,8},{10,11... | collective-permute-start | bytes 9224 | tf_op jit(solution)/shard_map/ppermute | solution.py:695
  865.7 16.6 %reduce-scatter.21.cloned.1.call-done.refs_0_ = bf16[192,1536]{1,0:T(8,128)(2,1)} async-done(((bf16[768,1536]{1,0:T(8,128)(2,1)}), bf16[192,1536]{1,0:T(8,128)(2,1)}) %reduce-scatter.21.cloned.1.call-update) | async-done | bytes 589840 | tf_op jit(solution)/shard_map/reduce_scatter | solution.py:704
  (769 shorter events, 306.5 us)
Async XLA Ops:
  7.2 62.2 %all-gather.8.cloned.1.call-start = ((), (), s32[]{:S(2)}) async-start(), calls=%async_computation.8 | async-start | bytes 2949120 | tf_op jit(solution)/shard_map/all_gather | solution.py:701
  12.8 99.9 %all-gather.10.cloned.1.call-start = ((), (), s32[]{:S(2)}) async-start(), calls=%async_computation.9 | async-start | bytes 2211840 | tf_op jit(solution)/shard_map/all_gather | solution.py:701
  22.9 153.3 %all-gather.12.cloned.1.call-start = ((), (), s32[]{:S(2)}) async-start(), calls=%async_computation.10 | async-start | bytes 3932160 | tf_op jit(solution)/shard_map/all_gather | solution.py:701
  23.6 191.6 %all-gather.16.cloned.1.call-start = ((), (), s32[]{:S(2)}) async-start(), calls=%async_computation.12 | async-start | bytes 1966080 | tf_op jit(solution)/shard_map/all_gather | solution.py:701
  24.0 8.0 collective-permute-start.6
  25.3 8.3 collective-permute-start.5
  26.6 10.5 %collective-permute-start.4 = (bf16[24480]{0:T(1024)(128)(2,1)S(1)}, bf16[24480]{0:T(1024)(128)(2,1)S(1)}, u32[]{:S(2)}, u32[]{:S(2)}) collective-permute-start(bf16[24480]{0:T(1024)(128)(2,1)S(1)} %pad_maximum_fusion.19), channel_id=1, source_target_pairs={{0,12},{4,16},{8,20},{12,24},{16,28},{20,0},{24,4},{28,8},{1,13},{... | collective-permute-start | bytes 146888 | tf_op jit(solution)/shard_map/ppermute | solution.py:714
  27.7 12.9 %collective-permute-start.3 = (bf16[24480]{0:T(1024)(128)(2,1)S(1)}, bf16[24480]{0:T(1024)(128)(2,1)S(1)}, u32[]{:S(2)}, u32[]{:S(2)}) collective-permute-start(bf16[24480]{0:T(1024)(128)(2,1)S(1)} %pad_maximum_fusion.19), channel_id=1, source_target_pairs={{0,16},{4,20},{8,24},{12,28},{16,0},{20,4},{24,8},{28,12},{1,17},{... | collective-permute-start | bytes 146888 | tf_op jit(solution)/shard_map/ppermute | solution.py:714
  29.8 14.9 %collective-permute-start.2 = (bf16[24480]{0:T(1024)(128)(2,1)S(1)}, bf16[24480]{0:T(1024)(128)(2,1)S(1)}, u32[]{:S(2)}, u32[]{:S(2)}) collective-permute-start(bf16[24480]{0:T(1024)(128)(2,1)S(1)} %pad_maximum_fusion.19), channel_id=1, source_target_pairs={{0,20},{4,24},{8,28},{12,0},{16,4},{20,8},{24,12},{28,16},{1,21},{... | collective-permute-start | bytes 146888 | tf_op jit(solution)/shard_map/ppermute | solution.py:714
  31.8 239.0 %all-gather.14.cloned.1.call-start = ((), (), s32[]{:S(2)}) async-start(), calls=%async_computation.11 | async-start | bytes 2211840 | tf_op jit(solution)/shard_map/all_gather | solution.py:701
  32.0 12.7 %collective-permute-start.1 = (bf16[24480]{0:T(1024)(128)(2,1)S(1)}, bf16[24480]{0:T(1024)(128)(2,1)S(1)}, u32[]{:S(2)}, u32[]{:S(2)}) collective-permute-start(bf16[24480]{0:T(1024)(128)(2,1)S(1)} %pad_maximum_fusion.19), channel_id=1, source_target_pairs={{0,24},{4,28},{8,0},{12,4},{16,8},{20,12},{24,16},{28,20},{1,25},{... | collective-permute-start | bytes 146888 | tf_op jit(solution)/shard_map/ppermute | solution.py:714
  33.5 11.3 %collective-permute-start = (bf16[24480]{0:T(1024)(128)(2,1)S(1)}, bf16[24480]{0:T(1024)(128)(2,1)S(1)}, u32[]{:S(2)}, u32[]{:S(2)}) collective-permute-start(bf16[24480]{0:T(1024)(128)(2,1)S(1)} %pad_maximum_fusion.19), channel_id=1, source_target_pairs={{0,28},{4,0},{8,4},{12,8},{16,12},{20,16},{24,20},{28,24},{1,29},{... | collective-permute-start | bytes 146888 | tf_op jit(solution)/shard_map/ppermute | solution.py:714
  69.4 52.7 %collective-permute-start.10 = (bf16[768,1536]{1,0:T(8,128)(2,1)}, bf16[768,1536]{1,0:T(8,128)(2,1)}, u32[]{:S(2)}, u32[]{:S(2)}) collective-permute-start(bf16[768,1536]{1,0:T(8,128)(2,1)} %all-gather.8.cloned.1.call-done.refs_2_), channel_id=1, source_target_pairs={{0,4},{4,0},{8,12},{12,8},{16,20},{20,16},{24,28},{28,24},{1,5},{5... | collective-permute-start | bytes 7077896 | tf_op jit(solution)/shard_map/ppermute | solution.py:686
  71.2 10.1 %collective-permute-start.7 = (bf16[128,1536]{1,0:T(8,128)(2,1)S(1)}, bf16[128,1536]{1,0:T(8,128)(2,1)S(1)}, u32[]{:S(2)}, u32[]{:S(2)}) collective-permute-start(bf16[128,1536]{1,0:T(8,128)(2,1)S(1)} %maximum_select_fusion.8), channel_id=1, source_target_pairs={{0,2},{1,3},{2,0},{3,1},{4,6},{5,7},{6,4},{7,5},{8,10},{9,11},{10,... | collective-permute-start | bytes 1179656 | tf_op jit(solution)/shard_map/ppermute | solution.py:698
  74.3 9.8 %collective-permute-start.8 = (bf16[128,1536]{1,0:T(8,128)(2,1)S(1)}, bf16[128,1536]{1,0:T(8,128)(2,1)S(1)}, u32[]{:S(2)}, u32[]{:S(2)}) collective-permute-start(bf16[128,1536]{1,0:T(8,128)(2,1)S(1)} %maximum_select_fusion.8), channel_id=1, source_target_pairs={{0,1},{1,0},{2,3},{3,2},{4,5},{5,4},{6,7},{7,6},{8,9},{9,8},{10,11... | collective-permute-start | bytes 1179656 | tf_op jit(solution)/shard_map/ppermute | solution.py:695
  122.1 54.1 %collective-permute-start.13 = (bf16[576,1536]{1,0:T(8,128)(2,1)}, bf16[576,1536]{1,0:T(8,128)(2,1)}, u32[]{:S(2)}, u32[]{:S(2)}) collective-permute-start(bf16[576,1536]{1,0:T(8,128)(2,1)} %all-gather.10.cloned.1.call-done), channel_id=1, source_target_pairs={{0,4},{4,0},{8,12},{12,8},{16,20},{20,16},{24,28},{28,24},{1,5},{5... | collective-permute-start | bytes 5308424 | tf_op jit(solution)/shard_map/ppermute | solution.py:686
  137.0 186.0 %all-gather.18.cloned.1.call-start = ((), (), s32[]{:S(2)}) async-start(), calls=%async_computation.13 | async-start | bytes 3932160 | tf_op jit(solution)/shard_map/all_gather | solution.py:701
  177.6 69.2 %collective-permute-start.22 = (bf16[768,2048]{1,0:T(8,128)(2,1)}, bf16[768,2048]{1,0:T(8,128)(2,1)}, u32[]{:S(2)}, u32[]{:S(2)}) collective-permute-start(bf16[768,2048]{1,0:T(8,128)(2,1)} %all-gather.12.cloned.1.call-done.own_g.own_u.refs_2_), channel_id=1, source_target_pairs={{0,4},{4,0},{8,12},{12,8},{16,20},{20,16},{24,28},{28,24},{1,5},{5... | collective-permute-start | bytes 9437192 | tf_op jit(solution)/shard_map/ppermute | solution.py:686
  183.7 215.4 %all-gather.20.cloned.1.call-start = ((), (), s32[]{:S(2)}) async-start(), calls=%async_computation.14 | async-start | bytes 1966080 | tf_op jit(solution)/shard_map/all_gather | solution.py:701
  189.7 10.6 %collective-permute-start.15 = (bf16[128,1536]{1,0:T(8,128)(2,1)}, bf16[128,1536]{1,0:T(8,128)(2,1)}, u32[]{:S(2)}, u32[]{:S(2)}) collective-permute-start(bf16[128,1536]{1,0:T(8,128)(2,1)} %fusion.18), channel_id=1, source_target_pairs={{0,2},{1,3},{2,0},{3,1},{4,6},{5,7},{6,4},{7,5},{8,10},{9,11},{10,... | collective-permute-start | bytes 1179656 | tf_op jit(solution)/shard_map/ppermute | solution.py:698
  195.3 56.5 %collective-permute-start.19 = (bf16[128,1536]{1,0:T(8,128)(2,1)S(1)}, bf16[128,1536]{1,0:T(8,128)(2,1)}, u32[]{:S(2)}, u32[]{:S(2)}) collective-permute-start(bf16[128,1536]{1,0:T(8,128)(2,1)S(1)} %copy.296), channel_id=1, source_target_pairs={{0,2},{1,3},{2,0},{3,1},{4,6},{5,7},{6,4},{7,5},{8,10},{9,11},{10,... | collective-permute-start | bytes 1179656 | tf_op jit(solution)/shard_map/ppermute | solution.py:698
  246.8 34.5 %collective-permute-start.23 = (bf16[512,1536]{1,0:T(8,128)(2,1)}, bf16[512,1536]{1,0:T(8,128)(2,1)}, u32[]{:S(2)}, u32[]{:S(2)}) collective-permute-start(bf16[512,1536]{1,0:T(8,128)(2,1)} %all-gather.16.cloned.1.call-done), channel_id=1, source_target_pairs={{0,4},{4,0},{8,12},{12,8},{16,20},{20,16},{24,28},{28,24},{1,5},{5... | collective-permute-start | bytes 4718600 | tf_op jit(solution)/shard_map/ppermute | solution.py:686
  248.3 8.9 collective-permute-start.16
  249.6 10.3 %collective-permute-start.20 = (bf16[128,1536]{1,0:T(8,128)(2,1)S(1)}, bf16[128,1536]{1,0:T(8,128)(2,1)S(1)}, u32[]{:S(2)}, u32[]{:S(2)}) collective-permute-start(bf16[128,1536]{1,0:T(8,128)(2,1)S(1)} %copy.296), channel_id=1, source_target_pairs={{0,1},{1,0},{2,3},{3,2},{4,5},{5,4},{6,7},{7,6},{8,9},{9,8},{10,11... | collective-permute-start | bytes 1179656 | tf_op jit(solution)/shard_map/ppermute | solution.py:695
  251.8 8.1 collective-permute-start.21
  251.8 9.3 %collective-permute-start.17 = (bf16[128,1536]{1,0:T(8,128)(2,1)S(1)}, bf16[128,1536]{1,0:T(8,128)(2,1)S(1)}, u32[]{:S(2)}, u32[]{:S(2)}) collective-permute-start(bf16[128,1536]{1,0:T(8,128)(2,1)S(1)} %maximum_select_fusion.9), channel_id=1, source_target_pairs={{0,1},{1,0},{2,3},{3,2},{4,5},{5,4},{6,7},{7,6},{8,9},{9,8},{10,11... | collective-permute-start | bytes 1179656 | tf_op jit(solution)/shard_map/ppermute | solution.py:695
  281.3 37.8 %collective-permute-start.25 = (bf16[768,1152]{1,0:T(8,128)(2,1)}, bf16[768,1152]{1,0:T(8,128)(2,1)}, u32[]{:S(2)}, u32[]{:S(2)}) collective-permute-start(bf16[768,1152]{1,0:T(8,128)(2,1)} %all-gather.14.cloned.1.call-done.refs_1_), channel_id=1, source_target_pairs={{0,4},{4,0},{8,12},{12,8},{16,20},{20,16},{24,28},{28,24},{1,5},{5... | collective-permute-start | bytes 5308424 | tf_op jit(solution)/shard_map/ppermute | solution.py:686
  294.6 246.1 %reduce-scatter.9.cloned.1.call-start = ((), (), s32[]{:S(2)}) async-start(), calls=%async_computation.15 | async-start | bytes 1966080 | tf_op jit(solution)/shard_map/reduce_scatter | solution.py:704
  323.1 66.2 %collective-permute-start.30 = (bf16[768,2048]{1,0:T(8,128)(2,1)}, bf16[768,2048]{1,0:T(8,128)(2,1)}, u32[]{:S(2)}, u32[]{:S(2)}) collective-permute-start(bf16[768,2048]{1,0:T(8,128)(2,1)} %all-gather.18.cloned.1.call-done.own_g.own_u.refs_2_), channel_id=1, source_target_pairs={{0,4},{4,0},{8,12},{12,8},{16,20},{20,16},{24,28},{28,24},{1,5},{5... | collective-permute-start | bytes 9437192 | tf_op jit(solution)/shard_map/ppermute | solution.py:686
  331.6 14.8 %collective-permute-start.28 = (bf16[128,1536]{1,0:T(8,128)(2,1)S(1)}, bf16[128,1536]{1,0:T(8,128)(2,1)}, u32[]{:S(2)}, u32[]{:S(2)}) collective-permute-start(bf16[128,1536]{1,0:T(8,128)(2,1)S(1)} %maximum_select_fusion.10), channel_id=1, source_target_pairs={{0,1},{1,0},{2,3},{3,2},{4,5},{5,4},{6,7},{7,6},{8,9},{9,8},{10,11... | collective-permute-start | bytes 1179656 | tf_op jit(solution)/shard_map/ppermute | solution.py:695
  336.4 10.0 %collective-permute-start.29 = (bf16[128,1536]{1,0:T(8,128)(2,1)}, bf16[128,1536]{1,0:T(8,128)(2,1)}, u32[]{:S(2)}, u32[]{:S(2)}) collective-permute-start(bf16[128,1536]{1,0:T(8,128)(2,1)} %collective-permute-done.27), channel_id=1, source_target_pairs={{0,1},{1,0},{2,3},{3,2},{4,5},{5,4},{6,7},{7,6},{8,9},{9,8},{10,11... | collective-permute-start | bytes 1179656 | tf_op jit(solution)/shard_map/ppermute | solution.py:695
  399.2 10.6 %collective-permute-start.32 = (bf16[128,1536]{1,0:T(8,128)(2,1)}, bf16[128,1536]{1,0:T(8,128)(2,1)}, u32[]{:S(2)}, u32[]{:S(2)}) collective-permute-start(bf16[128,1536]{1,0:T(8,128)(2,1)} %fusion.12), channel_id=1, source_target_pairs={{0,2},{1,3},{2,0},{3,1},{4,6},{5,7},{6,4},{7,5},{8,10},{9,11},{10,... | collective-permute-start | bytes 1179656 | tf_op jit(solution)/shard_map/ppermute | solution.py:698
  400.6 35.6 %collective-permute-start.36 = (bf16[512,1536]{1,0:T(8,128)(2,1)}, bf16[512,1536]{1,0:T(8,128)(2,1)}, u32[]{:S(2)}, u32[]{:S(2)}) collective-permute-start(bf16[512,1536]{1,0:T(8,128)(2,1)} %all-gather.20.cloned.1.call-done), channel_id=1, source_target_pairs={{0,4},{4,0},{8,12},{12,8},{16,20},{20,16},{24,28},{28,24},{1,5},{5... | collective-permute-start | bytes 4718600 | tf_op jit(solution)/shard_map/ppermute | solution.py:686
  412.7 9.6 %collective-permute-start.33 = (bf16[128,1536]{1,0:T(8,128)(2,1)S(1)}, bf16[128,1536]{1,0:T(8,128)(2,1)}, u32[]{:S(2)}, u32[]{:S(2)}) collective-permute-start(bf16[128,1536]{1,0:T(8,128)(2,1)S(1)} %maximum_select_fusion.11), channel_id=1, source_target_pairs={{0,2},{1,3},{2,0},{3,1},{4,6},{5,7},{6,4},{7,5},{8,10},{9,11},{10,... | collective-permute-start | bytes 1179656 | tf_op jit(solution)/shard_map/ppermute | solution.py:698
  412.8 13.6 %collective-permute-start.34 = (bf16[128,1536]{1,0:T(8,128)(2,1)S(1)}, bf16[128,1536]{1,0:T(8,128)(2,1)}, u32[]{:S(2)}, u32[]{:S(2)}) collective-permute-start(bf16[128,1536]{1,0:T(8,128)(2,1)S(1)} %maximum_select_fusion.11), channel_id=1, source_target_pairs={{0,1},{1,0},{2,3},{3,2},{4,5},{5,4},{6,7},{7,6},{8,9},{9,8},{10,11... | collective-permute-start | bytes 1179656 | tf_op jit(solution)/shard_map/ppermute | solution.py:695
  437.6 34.4 %collective-permute-start.40 = (bf16[512,1536]{1,0:T(8,128)(2,1)S(1)}, bf16[512,1536]{1,0:T(8,128)(2,1)S(1)}, u32[]{:S(2)}, u32[]{:S(2)}) collective-permute-start(bf16[512,1536]{1,0:T(8,128)(2,1)S(1)} %product_tn.16), channel_id=1, source_target_pairs={{0,4},{4,0},{8,12},{12,8},{16,20},{20,16},{24,28},{28,24},{1,5},{5... | collective-permute-start | bytes 4718600 | tf_op jit(solution)/shard_map/ppermute | solution.py:686
  472.0 8.3 collective-permute-start.41
  473.6 15.2 %collective-permute-start.38 = (bf16[128,1536]{1,0:T(8,128)(2,1)S(1)}, bf16[128,1536]{1,0:T(8,128)(2,1)S(1)}, u32[]{:S(2)}, u32[]{:S(2)}) collective-permute-start(bf16[128,1536]{1,0:T(8,128)(2,1)S(1)} %fusion.8), channel_id=1, source_target_pairs={{0,2},{1,3},{2,0},{3,1},{4,6},{5,7},{6,4},{7,5},{8,10},{9,11},{10,... | collective-permute-start | bytes 1179656 | tf_op jit(solution)/shard_map/ppermute | solution.py:698
  473.7 66.9 %collective-permute-start.46 = (bf16[768,2048]{1,0:T(8,128)(2,1)}, bf16[768,2048]{1,0:T(8,128)(2,1)}, u32[]{:S(2)}, u32[]{:S(2)}) collective-permute-start(bf16[768,2048]{1,0:T(8,128)(2,1)} %product_tn.17), channel_id=1, source_target_pairs={{0,4},{4,0},{8,12},{12,8},{16,20},{20,16},{24,28},{28,24},{1,5},{5... | collective-permute-start | bytes 9437192 | tf_op jit(solution)/shard_map/ppermute | solution.py:686
  492.7 174.8 %reduce-scatter.11.cloned.1.call-start = ((), (), s32[]{:S(2)}) async-start(), calls=%async_computation.16 | async-start | bytes 3932160 | tf_op jit(solution)/shard_map/reduce_scatter | solution.py:704
  492.8 7.5 collective-permute-start.42
  494.2 13.6 %collective-permute-start.43 = (bf16[128,1536]{1,0:T(8,128)(2,1)S(1)}, bf16[128,1536]{1,0:T(8,128)(2,1)}, u32[]{:S(2)}, u32[]{:S(2)}) collective-permute-start(bf16[128,1536]{1,0:T(8,128)(2,1)S(1)} %copy-done.134), channel_id=1, source_target_pairs={{0,1},{1,0},{2,3},{3,2},{4,5},{5,4},{6,7},{7,6},{8,9},{9,8},{10,11... | collective-permute-start | bytes 1179656 | tf_op jit(solution)/shard_map/ppermute | solution.py:695
  500.3 7.5 collective-permute-start.44
  549.9 181.0 %reduce-scatter.13.cloned.1.call-start = ((), (), s32[]{:S(2)}) async-start(), calls=%async_computation.17 | async-start | bytes 737280 | tf_op jit(solution)/shard_map/reduce_scatter | solution.py:704
  555.2 15.2 %collective-permute-start.47 = (bf16[192,1536]{1,0:T(8,128)(2,1)}, bf16[192,1536]{1,0:T(8,128)(2,1)S(1)}, u32[]{:S(2)}, u32[]{:S(2)}) collective-permute-start(bf16[192,1536]{1,0:T(8,128)(2,1)} %copy-done.94), channel_id=1, source_target_pairs={{0,4},{4,0},{8,12},{12,8},{16,20},{20,16},{24,28},{28,24},{1,5},{5... | collective-permute-start | bytes 1769480 | tf_op jit(solution)/shard_map/ppermute | solution.py:686
  570.4 10.0 %collective-permute-start.48 = (bf16[128,1536]{1,0:T(8,128)(2,1)S(1)}, bf16[128,1536]{1,0:T(8,128)(2,1)S(1)}, u32[]{:S(2)}, u32[]{:S(2)}) collective-permute-start(bf16[128,1536]{1,0:T(8,128)(2,1)S(1)} %fusion.4), channel_id=1, source_target_pairs={{0,2},{1,3},{2,0},{3,1},{4,6},{5,7},{6,4},{7,5},{8,10},{9,11},{10,... | collective-permute-start | bytes 1179656 | tf_op jit(solution)/shard_map/ppermute | solution.py:698
  571.8 39.4 %collective-permute-start.50 = (bf16[768,1152]{1,0:T(8,128)(2,1)}, bf16[768,1152]{1,0:T(8,128)(2,1)}, u32[]{:S(2)}, u32[]{:S(2)}) collective-permute-start(bf16[768,1152]{1,0:T(8,128)(2,1)} %product_tn.20), channel_id=1, source_target_pairs={{0,4},{4,0},{8,12},{12,8},{16,20},{20,16},{24,28},{28,24},{1,5},{5... | collective-permute-start | bytes 5308424 | tf_op jit(solution)/shard_map/ppermute | solution.py:686
  582.9 9.4 %collective-permute-start.49 = (bf16[128,1536]{1,0:T(8,128)(2,1)}, bf16[128,1536]{1,0:T(8,128)(2,1)}, u32[]{:S(2)}, u32[]{:S(2)}) collective-permute-start(bf16[128,1536]{1,0:T(8,128)(2,1)} %get-tuple-element.150), channel_id=1, source_target_pairs={{0,2},{1,3},{2,0},{3,1},{4,6},{5,7},{6,4},{7,5},{8,10},{9,11},{10,... | collective-permute-start | bytes 1179656 | tf_op jit(solution)/shard_map/ppermute | solution.py:698
  585.7 145.2 %reduce-scatter.15.cloned.1.call-start = ((), (), s32[]{:S(2)}) async-start(), calls=%async_computation.18 | async-start | bytes 2211840 | tf_op jit(solution)/shard_map/reduce_scatter | solution.py:704
  592.3 22.9 %collective-permute-start.52 = (bf16[128,1536]{1,0:T(8,128)(2,1)}, bf16[128,1536]{1,0:T(8,128)(2,1)S(1)}, u32[]{:S(2)}, u32[]{:S(2)}) collective-permute-start(bf16[128,1536]{1,0:T(8,128)(2,1)} %collective-permute-done.49), channel_id=1, source_target_pairs={{0,1},{1,0},{2,3},{3,2},{4,5},{5,4},{6,7},{7,6},{8,9},{9,8},{10,11... | collective-permute-start | bytes 1179656 | tf_op jit(solution)/shard_map/ppermute | solution.py:695
  618.7 36.3 %collective-permute-start.54 = (bf16[512,1536]{1,0:T(8,128)(2,1)}, bf16[512,1536]{1,0:T(8,128)(2,1)}, u32[]{:S(2)}, u32[]{:S(2)}) collective-permute-start(bf16[512,1536]{1,0:T(8,128)(2,1)} %product_tn.23), channel_id=1, source_target_pairs={{0,4},{4,0},{8,12},{12,8},{16,20},{20,16},{24,28},{28,24},{1,5},{5... | collective-permute-start | bytes 4718600 | tf_op jit(solution)/shard_map/ppermute | solution.py:686
  646.5 84.4 %reduce-scatter.17.cloned.1.call-start = ((), (), s32[]{:S(2)}) async-start(), calls=%async_computation.19 | async-start | bytes 1966080 | tf_op jit(solution)/shard_map/reduce_scatter | solution.py:704
  655.0 9.9 %collective-permute-start.55 = (bf16[128,1536]{1,0:T(8,128)(2,1)S(1)}, bf16[128,1536]{1,0:T(8,128)(2,1)S(1)}, u32[]{:S(2)}, u32[]{:S(2)}) collective-permute-start(bf16[128,1536]{1,0:T(8,128)(2,1)S(1)} %fusion.2), channel_id=1, source_target_pairs={{0,2},{1,3},{2,0},{3,1},{4,6},{5,7},{6,4},{7,5},{8,10},{9,11},{10,... | collective-permute-start | bytes 1179656 | tf_op jit(solution)/shard_map/ppermute | solution.py:698
  655.1 75.8 %collective-permute-start.59 = (bf16[768,2048]{1,0:T(8,128)(2,1)}, bf16[768,2048]{1,0:T(8,128)(2,1)}, u32[]{:S(2)}, u32[]{:S(2)}) collective-permute-start(bf16[768,2048]{1,0:T(8,128)(2,1)} %copy-done.41), channel_id=1, source_target_pairs={{0,4},{4,0},{8,12},{12,8},{16,20},{20,16},{24,28},{28,24},{1,5},{5... | collective-permute-start | bytes 9437192 | tf_op jit(solution)/shard_map/ppermute | solution.py:686
  672.2 148.5 %reduce-scatter.19.cloned.1.call-start = ((), (), s32[]{:S(2)}) async-start(), calls=%async_computation.20 | async-start | bytes 3932160 | tf_op jit(solution)/shard_map/reduce_scatter | solution.py:704
  672.2 9.4 %collective-permute-start.56 = (bf16[128,1536]{1,0:T(8,128)(2,1)}, bf16[128,1536]{1,0:T(8,128)(2,1)S(1)}, u32[]{:S(2)}, u32[]{:S(2)}) collective-permute-start(bf16[128,1536]{1,0:T(8,128)(2,1)} %get-tuple-element.289), channel_id=1, source_target_pairs={{0,2},{1,3},{2,0},{3,1},{4,6},{5,7},{6,4},{7,5},{8,10},{9,11},{10,... | collective-permute-start | bytes 1179656 | tf_op jit(solution)/shard_map/ppermute | solution.py:698
  672.4 13.6 %collective-permute-start.57 = (bf16[128,1536]{1,0:T(8,128)(2,1)}, bf16[128,1536]{1,0:T(8,128)(2,1)S(1)}, u32[]{:S(2)}, u32[]{:S(2)}) collective-permute-start(bf16[128,1536]{1,0:T(8,128)(2,1)} %get-tuple-element.289), channel_id=1, source_target_pairs={{0,1},{1,0},{2,3},{3,2},{4,5},{5,4},{6,7},{7,6},{8,9},{9,8},{10,11... | collective-permute-start | bytes 1179656 | tf_op jit(solution)/shard_map/ppermute | solution.py:695
  737.4 103.9 %reduce-scatter.23.cloned.1.call-start = ((), (), s32[]{:S(2)}) async-start(), calls=%async_computation.22 | async-start | bytes 1474560 | tf_op jit(solution)/shard_map/reduce_scatter | solution.py:704
  740.0 27.5 %collective-permute-start.62 = (bf16[384,1536]{1,0:T(8,128)(2,1)}, bf16[384,1536]{1,0:T(8,128)(2,1)}, u32[]{:S(2)}, u32[]{:S(2)}) collective-permute-start(bf16[384,1536]{1,0:T(8,128)(2,1)} %copy-done.68), channel_id=1, source_target_pairs={{0,4},{4,0},{8,12},{12,8},{16,20},{20,16},{24,28},{28,24},{1,5},{5... | collective-permute-start | bytes 3538952 | tf_op jit(solution)/shard_map/ppermute | solution.py:686
  767.5 51.8 %collective-permute-start.65 = (bf16[768,1536]{1,0:T(8,128)(2,1)}, bf16[768,1536]{1,0:T(8,128)(2,1)}, u32[]{:S(2)}, u32[]{:S(2)}) collective-permute-start(bf16[768,1536]{1,0:T(8,128)(2,1)} %product_tn.29), channel_id=1, source_target_pairs={{0,4},{4,0},{8,12},{12,8},{16,20},{20,16},{24,28},{28,24},{1,5},{5... | collective-permute-start | bytes 7077896 | tf_op jit(solution)/shard_map/ppermute | solution.py:686
  781.3 101.0 %reduce-scatter.21.cloned.1.call-start = ((), (), s32[]{:S(2)}) async-start(), calls=%async_computation.21 | async-start | bytes 2949120 | tf_op jit(solution)/shard_map/reduce_scatter | solution.py:704
  784.8 10.5 %collective-permute-start.64 = (bf16[128,1536]{1,0:T(8,128)(2,1)S(1)}, bf16[128,1536]{1,0:T(8,128)(2,1)S(1)}, u32[]{:S(2)}, u32[]{:S(2)}) collective-permute-start(bf16[128,1536]{1,0:T(8,128)(2,1)S(1)} %fusion), channel_id=1, source_target_pairs={{0,2},{1,3},{2,0},{3,1},{4,6},{5,7},{6,4},{7,5},{8,10},{9,11},{10,... | collective-permute-start | bytes 1179656 | tf_op jit(solution)/shard_map/ppermute | solution.py:698
  838.8 13.1 %collective-permute-start.69 = (bf16[96,255]{1,0:T(8,128)(2,1)S(1)}, bf16[96,255]{1,0:T(8,128)(2,1)S(1)}, u32[]{:S(2)}, u32[]{:S(2)}) collective-permute-start(bf16[96,255]{1,0:T(8,128)(2,1)S(1)} %fusion.30), channel_id=1, source_target_pairs={{0,4},{4,0},{8,12},{12,8},{16,20},{20,16},{24,28},{28,24},{1,5},{5... | collective-permute-start | bytes 146888 | tf_op jit(solution)/shard_map/ppermute | solution.py:686
  852.0 10.2 %collective-permute-start.70 = (f32[4,192]{1,0:T(4,128)S(1)}, f32[4,192]{1,0:T(4,128)S(1)}, u32[]{:S(2)}, u32[]{:S(2)}) collective-permute-start(f32[4,192]{1,0:T(4,128)S(1)} %reshape.438), channel_id=1, source_target_pairs={{0,1},{1,0},{2,3},{3,2},{4,5},{5,4},{6,7},{7,6},{8,9},{9,8},{10,11... | collective-permute-start | bytes 9224 | tf_op jit(solution)/shard_map/ppermute | solution.py:695
  (201 other events, 1722.3 us)
Sparse Core Ops, SparseCore 0:
  12.9 56.4 all-gather.7
  71.6 41.1 all-gather.9
  114.9 61.2 all-gather.11
  178.2 36.9 all-gather.15
  217.2 39.0 all-gather.13
  257.7 61.2 all-gather.17
  321.2 36.9 all-gather.19
  492.8 38.3 reduce-scatter.8
  550.0 65.4 reduce-scatter.10
  618.2 18.9 reduce-scatter.12
  646.6 36.4 reduce-scatter.14
  685.4 34.3 reduce-scatter.16
  737.5 60.8 reduce-scatter.18
  801.3 27.6 reduce-scatter.22
  831.2 51.0 reduce-scatter.20
